TPU v7x, 256 devices: a whole 4x4x8 slice. The times are simulated.
256 devices in a mesh: dp: 16 (over z_hi, y, core), owner: 16 (over x, z_lo).
Axes of the slice: x: 4, y: 4, z: 8 (z_hi: 2, z_lo: 4; z = z_hi * 4 + z_lo), core: 2. Of those that a mesh axis runs over, the one named last changes fastest.
Arguments:
- activations: bfloat16 [32768, 4096], P(('dp', 'owner'))
- out_grads: bfloat16 [32768, 16384], P(('dp', 'owner'))
- sample_ids: int32 [4096], P(('dp', 'owner')), may hold values from 0 to 127
- damping: float32 [20], replicated, may hold values from 0.3 to 3
- weight_grad: bfloat16 [4096, 16384], P('dp', 'owner'), may hold values from -6 to 6
Outputs:
- preconditioned: bfloat16 [4096, 16384], P('dp', 'owner')
Inputs may be any that keep to these rules, and one draw needn't show every extreme that they name: Entry k names token (k // 16) * 128 + sample_ids[k], a token of the same device's rows.
All inputs are finite; a program needn't handle non-finite values.
Results may differ from a plain program's by a relative error of at most 0.014.
Values may be sent and summed in bfloat16 or wider, within the bound.
No kernel may reach another device: no remote copies, remote signals or barrier semaphores. Data moves between devices by JAX's collectives and lax.ppermute only.
A program may use at most 128 MiB of HBM per device.

v0:
```python
import jax
import jax.numpy as jnp
from jax import lax
from jax.sharding import PartitionSpec as P

B = 1024
DA = 4096
DG = 16384
ITERS = 5


def swapped(value, axis, apart):
    mask = 2**apart
    pairs = [(source, source ^ mask) for source in range(lax.axis_size(axis))]
    return lax.ppermute(value, axis, pairs)


def from_root(value, axis, root):
    mine = lax.axis_index(axis) == root
    return lax.psum(jnp.where(mine, value, jnp.zeros_like(value)), axis)


def collect_rows(piece):
    return lax.all_gather(piece, "dp", axis=1, tiled=True)


def on_device(activations, out_grads, sample_ids, damping, weight_grad):
    dp_count = lax.axis_size("dp")
    own_count = lax.axis_size("owner")
    dp_index = lax.axis_index("dp")
    own_index = lax.axis_index("owner")
    blocks_a = DA // B
    blocks_g = DG // B
    per_owner = blocks_g // own_count
    copies = own_count // blocks_a
    samp_count = sample_ids.shape[0]
    sample_total = samp_count * dp_count * own_count
    samp_x = activations[sample_ids]
    samp_g = out_grads[sample_ids]
    g_part = samp_g.reshape(samp_count, own_count, per_owner, B)
    x_part = jnp.tile(samp_x.reshape(samp_count, 1, blocks_a, B), (1, copies, 1, 1))
    x_part = x_part.reshape(samp_count, own_count, 1, B)
    outgoing = jnp.concatenate([g_part, x_part], axis=2)
    received = lax.all_to_all(outgoing, "owner", split_axis=1, concat_axis=0, tiled=True)
    summed = jnp.einsum("snkb,snkc->kbc", received, received, preferred_element_type=jnp.float32)
    partial_cov = summed / sample_total
    damp_g = lax.dynamic_slice_in_dim(damping, blocks_a + own_index * per_owner, per_owner, 0)
    damp_a = lax.dynamic_slice_in_dim(damping, own_index % blocks_a, 1, 0)
    damp_slots = jnp.concatenate([damp_g, damp_a])[:, None, None]
    identity = jnp.eye(B, dtype=jnp.float32)
    row_count = B // dp_count
    row_start = dp_index * row_count
    final_scale = 2.0**ITERS
    identity_rows = lax.dynamic_slice_in_dim(identity, row_start, row_count, 0)
    factor = (
        lax.psum(partial_cov.astype(jnp.bfloat16), "dp").astype(jnp.float32)
        + damp_slots * identity[None]
    )
    frob_norm = jnp.sqrt(jnp.sum(factor * factor, axis=(1, 2)))[:, None, None]
    own_rows = lax.dynamic_slice_in_dim(factor, row_start, row_count, 1)
    rows_bf = own_rows.astype(jnp.bfloat16)
    iterate = identity_rows[None] / frob_norm
    whole_bf = (identity[None] / frob_norm).astype(jnp.bfloat16)
    for round_index in range(ITERS):
        if round_index > 0:
            whole_bf = collect_rows(iterate.astype(jnp.bfloat16))
        product = jnp.einsum(
            "kab,kbc->kac", rows_bf, whole_bf, preferred_element_type=jnp.float32
        ).astype(jnp.bfloat16)
        iterate = 2.0 * iterate - jnp.einsum(
            "kab,kbc->kac", product, whole_bf, preferred_element_type=jnp.float32
        )
    inverse = collect_rows((iterate * (frob_norm / final_scale)).astype(jnp.bfloat16))
    w_rows = weight_grad.shape[0]
    mixed_cols = jnp.einsum(
        "rsb,sbc->rsc",
        weight_grad.reshape(w_rows, per_owner, B),
        inverse[:per_owner],
        preferred_element_type=jnp.float32,
    )
    mixed_cols = mixed_cols.astype(jnp.bfloat16).reshape(w_rows, per_owner * B)
    group_size = B // w_rows
    gathered = mixed_cols
    for bit_level in range(group_size.bit_length() - 1):
        partner = swapped(gathered, "dp", bit_level)
        upper_half = dp_index // (1 << bit_level) % 2
        gathered = jnp.where(
            upper_half == 1,
            jnp.concatenate([partner, gathered], axis=0),
            jnp.concatenate([gathered, partner], axis=0),
        )
    block_a = dp_index // group_size
    local_start = dp_index % group_size * w_rows
    root_owner = block_a + blocks_a * (dp_index % copies)
    a_piece = lax.dynamic_slice_in_dim(inverse[per_owner], local_start, w_rows, 0)
    a_rows = from_root(a_piece, "owner", root_owner)
    return jnp.dot(a_rows, gathered, preferred_element_type=jnp.float32).astype(jnp.bfloat16)


def solution(mesh):
    placed = (
        P(("dp", "owner"), None),
        P(("dp", "owner"), None),
        P(("dp", "owner")),
        P(),
        P("dp", "owner"),
    )
    return jax.shard_map(
        on_device, mesh=mesh, in_specs=placed, out_specs=P("dp", "owner"), check_vma=False
    )
```

profile of v0, /device:TPU:33, one launch (start us, length us, event | category | flops | bytes accessed | tf_op | source)
XLA Modules:
  0.0 815.7 jit_solution(14516170601314026116)
XLA Ops:
  6.5 0.7 compare_select_fusion
  7.3 4.1 gather_fusion
  11.4 0.3 copy.15
  11.7 0.3 copy.10
  12.0 0.6 gather_fusion.1
  12.8 31.8 %all_to_all.15 = bf16[16,16,2,1024]{3,0,2,1:T(8,128)(2,1)S(1)} all-to-all(bf16[16,16,2,1024]{3,0,2,1:T(8,128)(2,1)S(1)} %pad_maximum_fusion), channel_id=1, replica_groups=mesh['dp'=16,'owner'=16] {'owner'}, dimensions={1} | all-to-all | bytes 2097152 | tf_op jit(solution)/shard_map/all_to_all | solution.py:44
  44.7 3.3 multiply_convert_fusion
  48.1 0.7 fusion.19
  48.7 1.4 pad_maximum_fusion.1
  50.1 0.5 fusion
  50.6 2.0 copy-done.1
  52.6 190.0 %all-reduce.3.cloned.1.call-done = bf16[2,1024,1024]{2,1,0:T(8,128)(2,1)} async-done(((bf16[2,1024,1024]{2,1,0:T(8,128)(2,1)}), bf16[2,1024,1024]{2,1,0:T(8,128)(2,1)}) %all-reduce.3.cloned.1.call-update) | async-done | bytes 4194320 | tf_op jit(solution)/shard_map/psum | solution.py:56
  242.6 5.0 multiply_reduce_fusion
  247.6 5.9 fusion.20
  253.6 78.5 %all-gather.6.cloned.1.call-done = bf16[2,1024,1024]{2,1,0:T(8,128)(2,1)} async-done(((bf16[2,64,1024]{2,1,0:T(8,128)(2,1)}), bf16[2,1024,1024]{2,1,0:T(8,128)(2,1)}) %all-gather.6.cloned.1.call-update) | async-done | bytes 4194320 | tf_op jit(solution)/shard_map/all_gather | solution.py:24
  332.1 5.8 fusion.21
  337.9 72.9 %all-gather.8.cloned.1.call-done = bf16[2,1024,1024]{2,1,0:T(8,128)(2,1)} async-done(((bf16[2,64,1024]{2,1,0:T(8,128)(2,1)}), bf16[2,1024,1024]{2,1,0:T(8,128)(2,1)}) %all-gather.8.cloned.1.call-update) | async-done | bytes 4194320 | tf_op jit(solution)/shard_map/all_gather | solution.py:24
  410.8 5.8 fusion.22
  416.7 72.9 %all-gather.10.cloned.1.call-done = bf16[2,1024,1024]{2,1,0:T(8,128)(2,1)} async-done(((bf16[2,64,1024]{2,1,0:T(8,128)(2,1)}), bf16[2,1024,1024]{2,1,0:T(8,128)(2,1)}) %all-gather.10.cloned.1.call-update) | async-done | bytes 4194320 | tf_op jit(solution)/shard_map/all_gather | solution.py:24
  489.6 5.8 fusion.23
  495.4 0.2 all-gather.14.cloned.1.call-start
  495.6 72.8 %all-gather.12.cloned.1.call-done = bf16[2,1024,1024]{2,1,0:T(8,128)(2,1)} async-done(((bf16[2,64,1024]{2,1,0:T(8,128)(2,1)}), bf16[2,1024,1024]{2,1,0:T(8,128)(2,1)}) %all-gather.12.cloned.1.call-update) | async-done | bytes 4194320 | tf_op jit(solution)/shard_map/all_gather | solution.py:24
  568.4 5.8 fusion.16
  574.3 73.0 %all-gather.14.cloned.1.call-done = bf16[2,1024,1024]{2,1,0:T(8,128)(2,1)} async-done(((bf16[2,64,1024]{2,1,0:T(8,128)(2,1)}), bf16[2,1024,1024]{2,1,0:T(8,128)(2,1)}) %all-gather.14.cloned.1.call-update) | async-done | bytes 4194320 | tf_op jit(solution)/shard_map/all_gather | solution.py:24
  647.2 3.1 fusion.13
  650.3 0.3 collective-permute-start
  650.6 2.0 collective-permute-done
  652.6 3.1 maximum_select_fusion.4
  655.7 0.9 collective-permute-start.1
  656.6 0.9 select_bitcast_fusion
  657.5 147.4 %all-reduce.5.cloned.1.call-done = bf16[256,1024]{1,0:T(8,128)(2,1)} async-done(((bf16[256,1024]{1,0:T(8,128)(2,1)}), bf16[256,1024]{1,0:T(8,128)(2,1)}) %all-reduce.5.cloned.1.call-update) | async-done | bytes 524304 | tf_op jit(solution)/shard_map/psum | solution.py:20
  804.9 3.9 fusion.11
  (31 shorter events, 0.6 us)
Async XLA Ops:
  6.5 5.4 copy-start
  6.5 236.0 %all-reduce.3.cloned.1.call-start = ((), (), s32[]{:S(2)}) async-start(), calls=%async_computation.1 | async-start | bytes 8388608 | tf_op jit(solution)/shard_map/psum | solution.py:56
  44.6 3.4 copy-start.2
  48.0 284.1 %all-gather.6.cloned.1.call-start = ((), (), s32[]{:S(2)}) async-start(), calls=%async_computation.2 | async-start | bytes 4456448 | tf_op jit(solution)/shard_map/all_gather | solution.py:24
  50.6 2.0 copy-start.1
  253.5 157.3 %all-gather.8.cloned.1.call-start = ((), (), s32[]{:S(2)}) async-start(), calls=%async_computation.3 | async-start | bytes 4456448 | tf_op jit(solution)/shard_map/all_gather | solution.py:24
  337.9 151.8 %all-gather.10.cloned.1.call-start = ((), (), s32[]{:S(2)}) async-start(), calls=%async_computation.4 | async-start | bytes 4456448 | tf_op jit(solution)/shard_map/all_gather | solution.py:24
  416.6 151.8 %all-gather.12.cloned.1.call-start = ((), (), s32[]{:S(2)}) async-start(), calls=%async_computation.5 | async-start | bytes 4456448 | tf_op jit(solution)/shard_map/all_gather | solution.py:24
  495.4 151.8 %all-gather.14.cloned.1.call-start = ((), (), s32[]{:S(2)}) async-start(), calls=%async_computation.6 | async-start | bytes 4456448 | tf_op jit(solution)/shard_map/all_gather | solution.py:24
  568.4 78.8 %copy-start.3 = (bf16[256,1024]{1,0:T(8,128)(2,1)S(1)}, bf16[256,1024]{1,0:T(8,128)(2,1)}, u32[]{:S(2)}) copy-start(bf16[256,1024]{1,0:T(8,128)(2,1)} %param.9) | copy-start | bytes 1572868
  574.2 230.7 %all-reduce.5.cloned.1.call-start = ((), (), s32[]{:S(2)}) async-start(), calls=%async_computation.7 | async-start | bytes 1048576 | tf_op jit(solution)/shard_map/psum | solution.py:20
  650.3 6.3 slice-start
  650.3 2.3 collective-permute-start
  655.7 149.3 %collective-permute-start.1 = (bf16[512,1024]{1,0:T(8,128)(2,1)}, bf16[512,1024]{1,0:T(8,128)(2,1)}, u32[]{:S(2)}, u32[]{:S(2)}) collective-permute-start(bf16[512,1024]{1,0:T(8,128)(2,1)} %maximum_select_fusion.4), channel_id=1, source_target_pairs={{0,32},{16,48},{32,0},{48,16},{64,96},{80,112},{96,64},{112,80},{1... | collective-permute-start | bytes 3145736 | tf_op jit(solution)/shard_map/ppermute | solution.py:15
Sparse Core Ops, SparseCore 0:
  48.1 194.4 all-reduce.2
  253.6 78.4 all-gather.5
  338.0 72.8 all-gather.7
  416.7 72.8 all-gather.9
  495.5 72.8 all-gather.11
  574.3 72.8 all-gather.13
  657.6 147.2 all-reduce.4
where the time goes:
time: 827 us; the launch traced here: 816 us
  waiting for transfers between devices  710 us (86%)
  matrix products  39.2 us (5%)
  blocking collectives  31.8 us (4%)
  between operations  13.7 us (2%)
  other arithmetic  11.7 us (1%)
    all_gather x5, waiting for transfers between devices, collect_rows(): return lax.all_gather(piece, 'dp', axis=1, tiled=True)  370 us
    psum x1, waiting for transfers between devices, on_device(): lax.psum(partial_cov.astype(jnp.bfloat16), 'dp').astype(jnp.float32)  190 us
    psum x1, waiting for transfers between devices, from_root(): return lax.psum(jnp.where(mine, value, jnp.zeros_like(value)), axis)  147 us
    all_to_all x1, blocking collectives, on_device(): lax.all_to_all(outgoing, 'owner', split_axis=1, concat_axis=0, tiled=True)  31.8 us
    dot_general x5, matrix products, on_device(): jnp.einsum('kab,kbc->kac', product, whole_bf, preferred_element_type=jnp....  28.9 us
  transfers between devices with their start and end apart: 9, of which 8 were waited for; matrix products, arithmetic and copies ran while one was open for 0% of the time, Pallas kernels for 0%

commit v1 on v0

v1 whole, which is shorter than its diff:
```python
import jax
import jax.numpy as jnp
from jax import lax
from jax.experimental import pallas as pl
from jax.experimental.pallas import tpu as pltpu
from jax.sharding import PartitionSpec as P

BLOCKS_A = 4
ITERS = 5
BF16 = jnp.bfloat16
F32 = jnp.float32
MIB = 2 ** 20
UPPER = [(r, c) for r in range(4) for c in range(r, 4)]
SMEM = pl.BlockSpec(memory_space=pltpu.SMEM)
VMEM = pl.BlockSpec(memory_space=pltpu.VMEM)


def dot(a, b):
    return jnp.dot(a, b, preferred_element_type=F32)


def gram(a, b):
    return lax.dot_general(a, b, (((0,), (0,)), ((), ())), preferred_element_type=F32)


def linear(zh, y, c, x, zl):
    return ((zh * 4 + y) * 2 + c) * 16 + x * 4 + zl


def moved(value, where):
    pairs = []
    for source in range(256):
        c, x, zl = source // 16 % 2, source // 4 % 4, source % 4
        zh, y = source // 128, source // 32 % 4
        target = where(zh, y, c, x, zl)
        if target is not None:
            pairs.append((source, linear(*target)))
    return lax.ppermute(value, ("dp", "owner"), pairs)


def z_shift(zh, zl, k):
    z = zh * 4 + zl
    z = (z + {1: 1, 2: 2 if z % 2 == 0 else -2, 3: -1}[k]) % 8
    return z // 4, z % 4


def pack_kernel(place_ref, mine_ref, other_ref, *outs):
    count, size = mine_ref.shape[0], outs[0].shape[1]
    for k, out in enumerate(outs):
        for owner in range(4):
            index = owner * 4 + lax.rem(place_ref[0] + k, 4)
            cols = pl.ds(pl.multiple_of(index * size, size), size)
            out[owner * 2 * count:(owner * 2 + 1) * count, :] = mine_ref[:, cols]
            out[(owner * 2 + 1) * count:(owner * 2 + 2) * count, :] = other_ref[:, cols]


def pack(place, mine, other, size):
    return pl.pallas_call(
        pack_kernel,
        out_shape=(jax.ShapeDtypeStruct((8 * mine.shape[0], size), BF16),) * 4,
        in_specs=[SMEM, VMEM, VMEM],
        out_specs=(VMEM,) * 4,
        compiler_params=pltpu.CompilerParams(vmem_limit_bytes=8 * MIB),
    )(place, mine, other)


def deal_kernel(place_ref, h0, h1, h2, h3, *outs):
    rows = h0.shape[0] // 4
    for k, out in enumerate(outs):
        start = pl.multiple_of(lax.rem(place_ref[0] + k, 4) * rows, rows)
        for i, held in enumerate((h0, h1, h2, h3)):
            out[i * rows:(i + 1) * rows, :] = held[pl.ds(start, rows), :]


def deal(place, held):
    return pl.pallas_call(
        deal_kernel,
        out_shape=(jax.ShapeDtypeStruct(held[0].shape, BF16),) * 4,
        in_specs=[SMEM] + [VMEM] * 4,
        out_specs=(VMEM,) * 4,
        compiler_params=pltpu.CompilerParams(vmem_limit_bytes=8 * MIB),
    )(place, *held)


def cov_kernel(scale, place_ref, *refs):
    dealt, held, chunks, (all_ref, panel_ref) = refs[:4], refs[4:8], refs[8:12], refs[12:]
    count, size = held[0].shape
    tile, sub = size // 4, size // 16
    for role, pieces in enumerate((dealt, held)):
        @pl.when(place_ref[2] == role)
        def _():
            for k, piece in enumerate(pieces):
                all_ref[k * count:(k + 1) * count, :] = piece[...]
    for r in range(4):
        cols = all_ref[:, r * tile:(r + 1) * tile]
        panel_ref[:, r * tile:] = gram(cols, all_ref[:, r * tile:]) * scale
        for k, chunk in enumerate(chunks):
            start = pl.multiple_of(lax.rem(place_ref[0] + k * place_ref[1], 4) * sub, sub)
            for t, (row, c) in enumerate(UPPER):
                if row == r:
                    chunk[t * sub:(t + 1) * sub, :] = panel_ref[
                        pl.ds(start, sub), c * tile:(c + 1) * tile].astype(BF16)


def cov(place, dealt, held, scale):
    count, size = held[0].shape
    tile, sub = size // 4, size // 16
    return pl.pallas_call(
        lambda *refs: cov_kernel(scale, *refs),
        out_shape=(jax.ShapeDtypeStruct((len(UPPER) * sub, tile), BF16),) * 4,
        in_specs=[SMEM] + [VMEM] * 8,
        out_specs=(VMEM,) * 4,
        scratch_shapes=[pltpu.VMEM((4 * count, size), BF16), pltpu.VMEM((tile, size), F32)],
        compiler_params=pltpu.CompilerParams(vmem_limit_bytes=16 * MIB),
    )(place, *dealt, *held)


def rounds_kernel(place_ref, damp_ref, p0, p1, p2, p3, out_ref, a_ref, x_ref, xb_ref, p_ref):
    size = out_ref.shape[0]
    tile = size // 4
    sub = tile // 4
    base, damp = place_ref[0], damp_ref[0]
    for k, piece in enumerate((p0, p1, p2, p3)):
        start = pl.multiple_of(lax.rem(base + 4 - k, 4) * sub, sub)
        for t, (r, c) in enumerate(UPPER):
            a_ref[pl.ds(r * tile + start, sub), c * tile:(c + 1) * tile] = piece[t * sub:(t + 1) * sub, :]
    row = lax.broadcasted_iota(jnp.int32, (tile, tile), 0)
    col = lax.broadcasted_iota(jnp.int32, (tile, tile), 1)
    eye = row == col
    total = jnp.zeros((1, 1), F32)
    for r, c in UPPER:
        rows, cols = slice(r * tile, (r + 1) * tile), slice(c * tile, (c + 1) * tile)
        value = a_ref[rows, cols].astype(F32)
        if r == c:
            value = value + jnp.where(eye, damp, 0.0)
            a_ref[rows, cols] = value.astype(BF16)
            total += jnp.sum(value * value, keepdims=True)
        else:
            total += 2.0 * jnp.sum(value * value, keepdims=True)
            a_ref[cols, rows] = value.T.astype(BF16)
    frob = jnp.sqrt(total)
    inv = 1.0 / frob
    inv_bf = inv.astype(BF16).astype(F32)
    for r in range(4):
        rows = slice(r * tile, (r + 1) * tile)
        for c in range(4):
            cols = slice(c * tile, (c + 1) * tile)
            product = (a_ref[rows, cols].astype(F32) * inv_bf).astype(BF16).astype(F32)
            value = -product * inv_bf
            if r == c:
                value = value + jnp.where(eye, 2.0 * inv, 0.0)
            x_ref[rows, cols] = value
            xb_ref[0, rows, cols] = value.astype(BF16)
    for step in range(1, ITERS):
        now, later = (step - 1) % 2, step % 2
        for r in range(4):
            rows = slice(r * tile, (r + 1) * tile)
            p_ref[rows, :] = dot(a_ref[rows, :], xb_ref[now]).astype(BF16)
        for r in range(4):
            rows = slice(r * tile, (r + 1) * tile)
            value = 2.0 * x_ref[rows, :] - dot(p_ref[rows, :], xb_ref[now])
            if step < ITERS - 1:
                x_ref[rows, :] = value
                xb_ref[later, rows, :] = value.astype(BF16)
            else:
                out_ref[rows, :] = (value * (frob / 2.0 ** ITERS)).astype(BF16)


def rounds(place, damp, pieces):
    tile = pieces[0].shape[1]
    size = tile * 4
    return pl.pallas_call(
        rounds_kernel,
        out_shape=jax.ShapeDtypeStruct((size, size), BF16),
        in_specs=[SMEM, SMEM] + [VMEM] * 4,
        out_specs=VMEM,
        scratch_shapes=[
            pltpu.VMEM((size, size), BF16),
            pltpu.VMEM((size, size), F32),
            pltpu.VMEM((2, size, size), BF16),
            pltpu.VMEM((size, size), BF16),
        ],
        cost_estimate=pl.CostEstimate(flops=16 * size ** 3, transcendentals=0, bytes_accessed=4 * size * size),
        compiler_params=pltpu.CompilerParams(vmem_limit_bytes=24 * MIB),
    )(place, damp, *pieces)


def mix_kernel(place_ref, s_ref, w0, w1, w2, w3, t0_ref, t1_ref):
    tile, size = t0_ref.shape
    half = place_ref[2]

    @pl.when(place_ref[1] == 1)
    def _():
        for i, target in enumerate((t0_ref, t1_ref)):
            rows = pl.ds(pl.multiple_of((2 * half + i) * tile, tile), tile)
            value = jnp.zeros((tile, size), F32)
            for b, w in enumerate((w0, w1, w2, w3)):
                cols = pl.ds(pl.multiple_of(lax.rem(2 * half + b, 4) * tile, tile), tile)
                value += dot(s_ref[rows, cols], w[...])
            target[...] = value.astype(BF16)


def mix(place, inverse, weights):
    return pl.pallas_call(
        mix_kernel,
        out_shape=(jax.ShapeDtypeStruct(weights[0].shape, BF16),) * 2,
        in_specs=[SMEM] + [VMEM] * 5,
        out_specs=(VMEM,) * 2,
        compiler_params=pltpu.CompilerParams(vmem_limit_bytes=16 * MIB),
    )(place, inverse, *weights)


def last_kernel(place_ref, t0_ref, s_own, t1_ref, s_other, out_ref):
    @pl.when(place_ref[1] == 0)
    def _():
        out_ref[...] = dot(t0_ref[...], s_own[...]).astype(BF16)

    @pl.when(place_ref[1] == 1)
    def _():
        out_ref[...] = dot(t1_ref[...], s_other[...]).astype(BF16)


def last(place, t0, s_own, t1, s_other):
    return pl.pallas_call(
        last_kernel,
        out_shape=jax.ShapeDtypeStruct(t0.shape, BF16),
        in_specs=[SMEM] + [VMEM] * 4,
        out_specs=VMEM,
        compiler_params=pltpu.CompilerParams(vmem_limit_bytes=16 * MIB),
    )(place, t0, s_own, t1, s_other)


def pick(parts, index):
    return lax.dynamic_index_in_dim(parts, index, 0, keepdims=False)


def on_device(activations, out_grads, sample_ids, damping, weight_grad):
    d, o = lax.axis_index("dp"), lax.axis_index("owner")
    zh, y, core = d // 8, d // 2 % 4, d % 2
    x, zl = o // 4, o % 4
    size = weight_grad.shape[1]
    scale = 1.0 / (sample_ids.shape[0] * 256)
    is_g = core == 0

    hot = (sample_ids[:, None] == jnp.arange(activations.shape[0], dtype=jnp.int32)[None]).astype(BF16)
    samp_x = dot(hot, activations).astype(BF16)
    other_x = moved(samp_x, lambda zh, y, c, x, zl: (zh, y, 1, x, zl) if c == 0 else None)
    samp_g = dot(hot, out_grads).astype(BF16)
    other_g = moved(samp_g, lambda zh, y, c, x, zl: (zh, y, 0, x, zl) if c == 1 else None)

    both_x = jnp.concatenate([samp_x, other_x])
    mine_x = []
    for dz, dy in ((0, 0), (0, 1), (1, 0), (1, 1)):
        block = (zh ^ dz) * 2 + (y // 2 ^ dy)
        sent = lax.dynamic_slice_in_dim(both_x, block * size, size, 1)
        mine_x.append(sent if dz + dy == 0 else moved(
            sent, lambda zh, y, c, x, zl: (zh ^ dz, y ^ (2 * dy), 1, x, zl) if c == 1 else None))
    mine_x = jnp.concatenate(mine_x)

    packed = pack(((zl + 2) % 4).reshape(1), samp_g, other_g, size)
    own_w, *packed = lax.optimization_barrier((weight_grad, *packed))
    weights = [
        moved(own_w, lambda zh, y, c, x, zl: (zh, y, 1, x, zl) if c == 0 else None),
        moved(own_w, lambda zh, y, c, x, zl: (zh, y ^ 1, 1, x, zl) if c == 0 else None),
        moved(own_w, lambda zh, y, c, x, zl: (zh, y ^ 1, 1, x, zl) if c == 1 else None),
    ]
    held = [jnp.where(is_g, packed[0], mine_x)]
    for k in (1, 2, 3):
        held.append(moved(
            jnp.where(is_g, packed[k], mine_x),
            lambda zh, y, c, x, zl: (z_shift(zh, zl, k)[0], y, 0, x, z_shift(zh, zl, k)[1]) if c == 0
            else (zh, y, 1, (x + k) % 4, zl),
        ))

    dealt = list(deal(x.reshape(1), held))
    for k in (1, 2, 3):
        dealt[k] = moved(dealt[k], lambda zh, y, c, x, zl: (zh, y, 0, (x + k) % 4, zl) if c == 0 else None)

    weights, dealt = lax.optimization_barrier((weights, dealt))
    weights.insert(1, weight_grad)

    chunks = cov(jnp.stack([jnp.where(is_g, y, x), 1 - core, core]), dealt, held, scale)
    total = chunks[0].astype(F32)
    for k in (1, 2, 3):
        total += moved(
            chunks[k],
            lambda zh, y, c, x, zl: (zh, (y + k) % 4, 0, x, zl) if c == 0 else (zh, y, 1, x, (zl + k) % 4),
        ).astype(F32)
    part = total.astype(BF16)

    def beside(zh, zl, by):
        z = (zh * 4 + zl + by) % 8
        return z // 4, z % 4

    here = moved(part, lambda zh, y, c, x, zl: (beside(zh, zl, 2)[0], y, 0, x, beside(zh, zl, 2)[1]) if c == 0
                 else (zh, y ^ 1, 1, x, zl))
    there = moved(part, lambda zh, y, c, x, zl: (beside(zh, zl, -2)[0], y, 0, x, beside(zh, zl, -2)[1]) if c == 0
                  else None)
    piece = (here.astype(F32) + jnp.where(is_g, there, part).astype(F32)).astype(BF16)

    pieces = [piece]
    for k in (1, 2, 3):
        pieces.append(moved(
            piece,
            lambda zh, y, c, x, zl: (zh, (y + k) % 4, 0, x, zl) if c == 0 else (zh, y, 1, (x + k) % 4, zl),
        ))

    damp = pick(damping, jnp.where(is_g, BLOCKS_A + o, zh * 2 + y // 2)).reshape(1)
    place = jnp.stack([jnp.where(is_g, y, x), core, y % 2])
    inverse = rounds(place, damp, pieces)

    inv_g = moved(inverse, lambda zh, y, c, x, zl: (zh, y, 1, x, zl) if c == 0 else None)
    mixed_0, mixed_1 = mix(place, inverse, weights)
    mixed_0 = moved(mixed_0, lambda zh, y, c, x, zl: (zh, y, 0, x, zl) if c == 1 else None)
    return last(place, mixed_0, inverse, mixed_1, inv_g)


def solution(mesh):
    placed = (
        P(("dp", "owner"), None),
        P(("dp", "owner"), None),
        P(("dp", "owner")),
        P(),
        P("dp", "owner"),
    )
    return jax.shard_map(
        on_device, mesh=mesh, in_specs=placed, out_specs=P("dp", "owner"), check_vma=False
    )
```

time: 827 us -> 143 us (0.17); the launches traced: 816 us -> 141 us
  waiting for transfers between devices: 710 us -> 46.9 us
  starting transfers between devices: 1.6 us -> 56.6 us
  matrix products: 39.2 us -> 3.31 us
  blocking collectives: 31.8 us -> 0 us
  Pallas kernels: 0 us -> 28.7 us
  between operations: 13.7 us -> 0.36 us
    all_gather x5 -> x0, waiting for transfers between devices: 370 us -> none  [collect_rows(): return lax.all_gather(piece, 'dp', axis=1, tiled=True)]
    psum x2 -> x0, waiting for transfers between devices: 337 us -> none  [the longest x1 190 us: on_device(): lax.psum(partial_cov.astype(jnp.bfloat16), 'dp').astype(jnp.float32)]
    ppermute x2 -> x24, starting transfers between devices: 1.17 us -> 56.6 us  [moved(): return lax.ppermute(value, ('dp', 'owner'), pairs)]
    ppermute x2 -> x24, waiting for transfers between devices: 2 us -> 46.9 us  [moved(): return lax.ppermute(value, ('dp', 'owner'), pairs)]
    dot_general x8 -> x2, matrix products: 39.2 us -> 3.31 us  [dot(): return jnp.dot(a, b, preferred_element_type=F32)]
    all_to_all x1 -> x0, blocking collectives: 31.8 us -> none  [on_device(): lax.all_to_all(outgoing, 'owner', split_axis=1, concat_axis=0, tiled=True)]
    pallas_call x0 -> x6, Pallas kernels: none -> 28.7 us  [the longest x1 20.9 us: rounds(): pl.pallas_call(rounds_kernel, out_shape=jax.ShapeDtypeStruct((size, size)...]
  transfers between devices with their start and end apart: 9 -> 24, of which waited for: 8 -> 12; matrix products, arithmetic and copies ran while one was open for 0% -> 2% of each run, Pallas kernels for 0% -> 2%
where the time goes in v1:
time: 143 us; the launch traced here: 141 us
  starting transfers between devices  56.6 us (40%)
  waiting for transfers between devices  46.9 us (33%)
  Pallas kernels  28.7 us (20%)
  other arithmetic  3.97 us (3%)
  matrix products  3.31 us (2%)
    ppermute x24, starting transfers between devices, moved(): return lax.ppermute(value, ('dp', 'owner'), pairs)  56.6 us
    ppermute x24, waiting for transfers between devices, moved(): return lax.ppermute(value, ('dp', 'owner'), pairs)  46.9 us
    pallas_call x1, Pallas kernels, rounds(): pl.pallas_call(rounds_kernel, out_shape=jax.ShapeDtypeStruct((size, size)...  20.9 us
    dot_general x2, matrix products, dot(): return jnp.dot(a, b, preferred_element_type=F32)  3.31 us
  transfers between devices with their start and end apart: 24, of which 12 were waited for; matrix products, arithmetic and copies ran while one was open for 2% of the time, Pallas kernels for 2%

profile of v1, /device:TPU:33, one launch (start us, length us, event | category | flops | bytes accessed | tf_op | source)
XLA Modules:
  0.0 140.5 jit_solution(5523908479561311510)
XLA Ops:
  0.0 3.0 %convolution_convert_fusion.mine_ref = bf16[16,16384]{1,0:T(8,128)(2,1)S(1)} fusion(bf16[128,16384]{1,0:T(8,128)(2,1)} %param.6, s32[16]{0:T(128)} %param.7), kind=kOutput, calls=%fused_computation | convolution fusion | flops 67373056 | bytes 4718656 | tf_op jit(solution)/shard_map/dot_general | solution.py:19
  3.0 2.6 %collective-permute-start = (bf16[16,16384]{1,0:T(8,128)(2,1)S(1)}, bf16[16,16384]{1,0:T(8,128)(2,1)S(1)}, u32[]{:S(2)}, u32[]{:S(2)}) collective-permute-start(bf16[16,16384]{1,0:T(8,128)(2,1)S(1)} %convolution_convert_fusion.mine_ref), channel_id=1, source_target_pairs={{16,0},{17,1},{18,2},{19,3},{20,4},{21,5},{22,6},{23,7},{24,8},{25... | collective-permute-start | bytes 1572872 | tf_op jit(solution)/shard_map/ppermute | solution.py:38
  6.0 1.3 collective-permute-start.4
  7.4 1.9 %collective-permute-done.4 = bf16[16,4096]{1,0:T(8,128)(2,1)S(1)} collective-permute-done((bf16[16,4096]{1,0:T(8,128)(2,1)S(1)}, bf16[16,4096]{1,0:T(8,128)(2,1)S(1)}, u32[]{:S(2)}, u32[]{:S(2)}) %collective-permute-start.4) | collective-permute-done | bytes 131104 | tf_op jit(solution)/shard_map/ppermute | solution.py:38
  9.9 4.8 %collective-permute-start.5 = (bf16[32,1024]{1,0:T(8,128)(2,1)}, bf16[32,1024]{1,0:T(8,128)(2,1)S(1)}, u32[]{:S(2)}, u32[]{:S(2)}) collective-permute-start(bf16[32,1024]{1,0:T(8,128)(2,1)} %get-tuple-element.61), channel_id=1, source_target_pairs={{16,80},{17,81},{18,82},{19,83},{20,84},{21,85},{22,86},{23,87},{2... | collective-permute-start | bytes 196616 | tf_op jit(solution)/shard_map/ppermute | solution.py:38
  14.7 7.9 %collective-permute-start.6 = (bf16[32,1024]{1,0:T(8,128)(2,1)}, bf16[32,1024]{1,0:T(8,128)(2,1)}, u32[]{:S(2)}, u32[]{:S(2)}) collective-permute-start(bf16[32,1024]{1,0:T(8,128)(2,1)} %get-tuple-element.62), channel_id=1, source_target_pairs={{16,144},{17,145},{18,146},{19,147},{20,148},{21,149},{22,150},{23... | collective-permute-start | bytes 196616 | tf_op jit(solution)/shard_map/ppermute | solution.py:38
  22.6 1.9 %collective-permute-start.7 = (bf16[32,1024]{1,0:T(8,128)(2,1)}, bf16[32,1024]{1,0:T(8,128)(2,1)}, u32[]{:S(2)}, u32[]{:S(2)}) collective-permute-start(bf16[32,1024]{1,0:T(8,128)(2,1)} %get-tuple-element.63), channel_id=1, source_target_pairs={{16,208},{17,209},{18,210},{19,211},{20,212},{21,213},{22,214},{23... | collective-permute-start | bytes 196616 | tf_op jit(solution)/shard_map/ppermute | solution.py:38
  25.2 9.1 %collective-permute-done.7 = bf16[32,1024]{1,0:T(8,128)(2,1)} collective-permute-done((bf16[32,1024]{1,0:T(8,128)(2,1)}, bf16[32,1024]{1,0:T(8,128)(2,1)}, u32[]{:S(2)}, u32[]{:S(2)}) %collective-permute-start.7) | collective-permute-done | bytes 65568 | tf_op jit(solution)/shard_map/ppermute | solution.py:38
  34.3 1.9 %broadcast_select_fusion = (bf16[128,1024]{1,0:T(8,128)(2,1)S(1)}, bf16[128,1024]{1,0:T(8,128)(2,1)}, bf16[128,1024]{1,0:T(8,128)(2,1)}) fusion(bf16[128,1024]{1,0:T(8,128)(2,1)S(1)} %get-tuple-element.39, pred[]{:T(512)S(6)} %eq.22, bf16[32,1024]{1,0:T(8,128)(2,1)} %collective-permute-done.7, bf16[32,1024]{1,0:T(8,128)(2,1)} %collective-permute-done.6, ...), kind=kLoop, calls=%fused_computation.13 | loop fusion | flops 1441792 | bytes 1835009 | tf_op jit(solution)/shard_map/jit(_where)/select_n | solution.py:270
  36.2 2.5 %collective-permute-start.10 = (bf16[128,1024]{1,0:T(8,128)(2,1)S(1)}, bf16[128,1024]{1,0:T(8,128)(2,1)S(1)}, u32[]{:S(2)}, u32[]{:S(2)}) collective-permute-start(bf16[128,1024]{1,0:T(8,128)(2,1)S(1)} %get-tuple-element.57), channel_id=1, source_target_pairs={{0,131},{1,0},{2,1},{3,2},{4,135},{5,4},{6,5},{7,6},{8,139},{9,8},... | collective-permute-start | bytes 786440 | tf_op jit(solution)/shard_map/ppermute | solution.py:38
  38.7 2.3 %collective-permute-start.3 = (bf16[256,1024]{1,0:T(8,128)(2,1)S(1)}, bf16[256,1024]{1,0:T(8,128)(2,1)S(1)}, u32[]{:S(2)}, u32[]{:S(2)}) collective-permute-start(bf16[256,1024]{1,0:T(8,128)(2,1)S(1)} %copy-done.1), channel_id=1, source_target_pairs={{16,48},{17,49},{18,50},{19,51},{20,52},{21,53},{22,54},{23,55},{2... | collective-permute-start | bytes 1572872 | tf_op jit(solution)/shard_map/ppermute | solution.py:38
  41.0 1.7 %collective-permute-start.9 = (bf16[128,1024]{1,0:T(8,128)(2,1)}, bf16[128,1024]{1,0:T(8,128)(2,1)S(1)}, u32[]{:S(2)}, u32[]{:S(2)}) collective-permute-start(bf16[128,1024]{1,0:T(8,128)(2,1)} %get-tuple-element.59), channel_id=1, source_target_pairs={{0,2},{1,131},{2,128},{3,1},{4,6},{5,135},{6,132},{7,5},{8,10},{9,... | collective-permute-start | bytes 786440 | tf_op jit(solution)/shard_map/ppermute | solution.py:38
  44.1 1.3 collective-permute-start.1
  46.3 4.2 %collective-permute-done.8.h1.refs_6_ = bf16[128,1024]{1,0:T(8,128)(2,1)S(1)} collective-permute-done((bf16[128,1024]{1,0:T(8,128)(2,1)}, bf16[128,1024]{1,0:T(8,128)(2,1)S(1)}, u32[]{:S(2)}, u32[]{:S(2)}) %collective-permute-start.8) | collective-permute-done | bytes 262176 | tf_op jit(solution)/shard_map/ppermute | solution.py:38
  51.4 1.4 collective-permute-start.11
  52.8 1.4 collective-permute-start.12
  54.2 1.4 collective-permute-start.13
  55.7 2.3 %shard_map.57 = (bf16[640,256]{1,0:T(8,128)(2,1)S(1)}, bf16[640,256]{1,0:T(8,128)(2,1)S(1)}, bf16[640,256]{1,0:T(8,128)(2,1)S(1)}, bf16[640,256]{1,0:T(8,128)(2,1)S(1)}) custom-call(s32[3]{0:T(128)S(1)} %pad_add_fusion.1.refs_0_, bf16[128,1024]{1,0:T(8,128)(2,1)S(1)} %get-tuple-element.44.refs_1_, bf16[128,1024]{1,0:T(8,128)(2,1)} %collective-permute-done.11.refs_2_, ...), custom_call_target="tpu_custom_call" | custom-call | tf_op jit(solution)/shard_map/pallas_call | solution.py:108
  59.1 2.8 %collective-permute-start.15 = (bf16[640,256]{1,0:T(8,128)(2,1)S(1)}, bf16[640,256]{1,0:T(8,128)(2,1)S(1)}, u32[]{:S(2)}, u32[]{:S(2)}) collective-permute-start(bf16[640,256]{1,0:T(8,128)(2,1)S(1)} %get-tuple-element.50), channel_id=1, source_target_pairs={{0,64},{1,65},{2,66},{3,67},{4,68},{5,69},{6,70},{7,71},{8,72},{9,... | collective-permute-start | bytes 983048 | tf_op jit(solution)/shard_map/ppermute | solution.py:38
  62.0 2.8 %collective-permute-done.14 = bf16[640,256]{1,0:T(8,128)(2,1)S(1)} collective-permute-done((bf16[640,256]{1,0:T(8,128)(2,1)S(1)}, bf16[640,256]{1,0:T(8,128)(2,1)S(1)}, u32[]{:S(2)}, u32[]{:S(2)}) %collective-permute-start.14) | collective-permute-done | bytes 327712 | tf_op jit(solution)/shard_map/ppermute | solution.py:38
  64.7 8.9 %collective-permute-done.15 = bf16[640,256]{1,0:T(8,128)(2,1)S(1)} collective-permute-done((bf16[640,256]{1,0:T(8,128)(2,1)S(1)}, bf16[640,256]{1,0:T(8,128)(2,1)S(1)}, u32[]{:S(2)}, u32[]{:S(2)}) %collective-permute-start.15) | collective-permute-done | bytes 327712 | tf_op jit(solution)/shard_map/ppermute | solution.py:38
  73.7 2.8 %collective-permute-done.16 = bf16[640,256]{1,0:T(8,128)(2,1)S(1)} collective-permute-done((bf16[640,256]{1,0:T(8,128)(2,1)S(1)}, bf16[640,256]{1,0:T(8,128)(2,1)S(1)}, u32[]{:S(2)}, u32[]{:S(2)}) %collective-permute-start.16) | collective-permute-done | bytes 327712 | tf_op jit(solution)/shard_map/ppermute | solution.py:38
  78.5 5.7 %collective-permute-done.17 = bf16[640,256]{1,0:T(8,128)(2,1)S(1)} collective-permute-done((bf16[640,256]{1,0:T(8,128)(2,1)S(1)}, bf16[640,256]{1,0:T(8,128)(2,1)S(1)}, u32[]{:S(2)}, u32[]{:S(2)}) %collective-permute-start.17) | collective-permute-done | bytes 327712 | tf_op jit(solution)/shard_map/ppermute | solution.py:38
  84.3 2.5 %collective-permute-start.21 = (bf16[640,256]{1,0:T(8,128)(2,1)S(1)}, bf16[640,256]{1,0:T(8,128)(2,1)S(1)}, u32[]{:S(2)}, u32[]{:S(2)}) collective-permute-start(bf16[640,256]{1,0:T(8,128)(2,1)S(1)} %add_convert_fusion.p0), channel_id=1, source_target_pairs={{0,96},{1,97},{2,98},{3,99},{4,100},{5,101},{6,102},{7,103},{8,104... | collective-permute-start | bytes 983048 | tf_op jit(solution)/shard_map/ppermute | solution.py:38
  88.2 6.2 %collective-permute-done.21.p3 = bf16[640,256]{1,0:T(8,128)(2,1)S(1)} collective-permute-done((bf16[640,256]{1,0:T(8,128)(2,1)S(1)}, bf16[640,256]{1,0:T(8,128)(2,1)S(1)}, u32[]{:S(2)}, u32[]{:S(2)}) %collective-permute-start.21) | collective-permute-done | bytes 327712 | tf_op jit(solution)/shard_map/ppermute | solution.py:38
  94.7 3.2 %collective-permute-done.19.p1 = bf16[640,256]{1,0:T(8,128)(2,1)S(1)} collective-permute-done((bf16[640,256]{1,0:T(8,128)(2,1)S(1)}, bf16[640,256]{1,0:T(8,128)(2,1)S(1)}, u32[]{:S(2)}, u32[]{:S(2)}) %collective-permute-start.19) | collective-permute-done | bytes 327712 | tf_op jit(solution)/shard_map/ppermute | solution.py:38
  97.8 20.9 %shard_map.58.s_ref.s_own = bf16[1024,1024]{1,0:T(8,128)(2,1)S(1)} custom-call(s32[3]{0:T(128)S(1)} %pad_add_fusion.place_ref, f32[1]{0:T(128)} %dynamic_slice.16.damp_ref, bf16[640,256]{1,0:T(8,128)(2,1)S(1)} %add_convert_fusion.p0, bf16[640,256]{1,0:T(8,128)(2,1)S(1)} %collective-permute-done.19.p1, bf16[640,256]{1,0:T(8,128)(2,1)S(1)} %collective-permute-done.20.p2, ...), custom_call_target="tpu_custom_call" | custom-call | flops 17179869184 | bytes 4194304 | tf_op jit(solution)/shard_map/pallas_call | solution.py:172
  118.7 1.3 collective-permute-start.23
  120.0 2.5 %shard_map.59 = (bf16[256,1024]{1,0:T(8,128)(2,1)S(1)}, bf16[256,1024]{1,0:T(8,128)(2,1)S(1)}) custom-call(s32[3]{0:T(128)S(1)} %pad_add_fusion.place_ref, bf16[1024,1024]{1,0:T(8,128)(2,1)S(1)} %shard_map.58.s_ref.s_own, bf16[256,1024]{1,0:T(8,128)(2,1)} %collective-permute-done.1.w0, bf16[256,1024]{1,0:T(8,128)(2,1)S(1)} %copy-done.1, ...), custom_call_target="tpu_custom_call" | custom-call | tf_op jit(solution)/shard_map/pallas_call | solution.py:204
  122.5 14.5 %collective-permute-start.22 = (bf16[256,1024]{1,0:T(8,128)(2,1)S(1)}, bf16[256,1024]{1,0:T(8,128)(2,1)S(1)}, u32[]{:S(2)}, u32[]{:S(2)}) collective-permute-start(bf16[256,1024]{1,0:T(8,128)(2,1)S(1)} %get-tuple-element.55), channel_id=1, source_target_pairs={{16,0},{17,1},{18,2},{19,3},{20,4},{21,5},{22,6},{23,7},{24,8},{25... | collective-permute-start | bytes 1572872 | tf_op jit(solution)/shard_map/ppermute | solution.py:38
  137.0 1.5 %collective-permute-done.22.t0_ref = bf16[256,1024]{1,0:T(8,128)(2,1)S(1)} collective-permute-done((bf16[256,1024]{1,0:T(8,128)(2,1)S(1)}, bf16[256,1024]{1,0:T(8,128)(2,1)S(1)}, u32[]{:S(2)}, u32[]{:S(2)}) %collective-permute-start.22) | collective-permute-done | bytes 524320 | tf_op jit(solution)/shard_map/ppermute | solution.py:38
  138.5 2.1 %shard_map.60 = bf16[256,1024]{1,0:T(8,128)(2,1)} custom-call(s32[3]{0:T(128)S(1)} %pad_add_fusion.place_ref, bf16[256,1024]{1,0:T(8,128)(2,1)S(1)} %collective-permute-done.22.t0_ref, bf16[1024,1024]{1,0:T(8,128)(2,1)S(1)} %shard_map.58.s_ref.s_own, bf16[256,1024]{1,0:T(8,128)(2,1)S(1)} %get-tuple-element.56.t1_ref, ...), custom_call_target="tpu_custom_call" | custom-call | tf_op jit(solution)/shard_map/pallas_call | solution.py:224
  (40 shorter events, 9.7 us)
Async XLA Ops:
  0.0 5.7 %copy-start = (bf16[128,4096]{1,0:T(8,128)(2,1)S(1)}, bf16[128,4096]{1,0:T(8,128)(2,1)}, u32[]{:S(2)}) copy-start(bf16[128,4096]{1,0:T(8,128)(2,1)} %param.5) | copy-start | bytes 3145732
  0.0 5.7 %copy-start.2 = (s32[16]{0:T(128)S(1)}, s32[16]{0:T(128)}, u32[]{:S(2)}) copy-start(s32[16]{0:T(128)} %param.7) | copy-start | bytes 196
  0.0 38.6 %copy-start.1 = (bf16[256,1024]{1,0:T(8,128)(2,1)S(1)}, bf16[256,1024]{1,0:T(8,128)(2,1)}, u32[]{:S(2)}) copy-start(bf16[256,1024]{1,0:T(8,128)(2,1)} %w1.1) | copy-start | bytes 1572868
  3.0 21.6 %collective-permute-start = (bf16[16,16384]{1,0:T(8,128)(2,1)S(1)}, bf16[16,16384]{1,0:T(8,128)(2,1)S(1)}, u32[]{:S(2)}, u32[]{:S(2)}) collective-permute-start(bf16[16,16384]{1,0:T(8,128)(2,1)S(1)} %convolution_convert_fusion.mine_ref), channel_id=1, source_target_pairs={{16,0},{17,1},{18,2},{19,3},{20,4},{21,5},{22,6},{23,7},{24,8},{25... | collective-permute-start | bytes 1572872 | tf_op jit(solution)/shard_map/ppermute | solution.py:38
  6.0 3.2 %collective-permute-start.4 = (bf16[16,4096]{1,0:T(8,128)(2,1)S(1)}, bf16[16,4096]{1,0:T(8,128)(2,1)S(1)}, u32[]{:S(2)}, u32[]{:S(2)}) collective-permute-start(bf16[16,4096]{1,0:T(8,128)(2,1)S(1)} %convolution_convert_fusion.1), channel_id=1, source_target_pairs={{0,16},{1,17},{2,18},{3,19},{4,20},{5,21},{6,22},{7,23},{8,24},{9,... | collective-permute-start | bytes 393224 | tf_op jit(solution)/shard_map/ppermute | solution.py:38
  9.9 14.8 %collective-permute-start.5 = (bf16[32,1024]{1,0:T(8,128)(2,1)}, bf16[32,1024]{1,0:T(8,128)(2,1)S(1)}, u32[]{:S(2)}, u32[]{:S(2)}) collective-permute-start(bf16[32,1024]{1,0:T(8,128)(2,1)} %get-tuple-element.61), channel_id=1, source_target_pairs={{16,80},{17,81},{18,82},{19,83},{20,84},{21,85},{22,86},{23,87},{2... | collective-permute-start | bytes 196616 | tf_op jit(solution)/shard_map/ppermute | solution.py:38
  14.7 10.5 %collective-permute-start.6 = (bf16[32,1024]{1,0:T(8,128)(2,1)}, bf16[32,1024]{1,0:T(8,128)(2,1)}, u32[]{:S(2)}, u32[]{:S(2)}) collective-permute-start(bf16[32,1024]{1,0:T(8,128)(2,1)} %get-tuple-element.62), channel_id=1, source_target_pairs={{16,144},{17,145},{18,146},{19,147},{20,148},{21,149},{22,150},{23... | collective-permute-start | bytes 196616 | tf_op jit(solution)/shard_map/ppermute | solution.py:38
  22.6 11.6 %collective-permute-start.7 = (bf16[32,1024]{1,0:T(8,128)(2,1)}, bf16[32,1024]{1,0:T(8,128)(2,1)}, u32[]{:S(2)}, u32[]{:S(2)}) collective-permute-start(bf16[32,1024]{1,0:T(8,128)(2,1)} %get-tuple-element.63), channel_id=1, source_target_pairs={{16,208},{17,209},{18,210},{19,211},{20,212},{21,213},{22,214},{23... | collective-permute-start | bytes 196616 | tf_op jit(solution)/shard_map/ppermute | solution.py:38
  34.3 53.3 %copy-start.3 = (f32[20]{0:T(128)S(1)}, f32[20]{0:T(128)}, u32[]{:S(2)}) copy-start(f32[20]{0:T(128)} %param.8) | copy-start | bytes 244
  36.2 7.9 %collective-permute-start.10 = (bf16[128,1024]{1,0:T(8,128)(2,1)S(1)}, bf16[128,1024]{1,0:T(8,128)(2,1)S(1)}, u32[]{:S(2)}, u32[]{:S(2)}) collective-permute-start(bf16[128,1024]{1,0:T(8,128)(2,1)S(1)} %get-tuple-element.57), channel_id=1, source_target_pairs={{0,131},{1,0},{2,1},{3,2},{4,135},{5,4},{6,5},{7,6},{8,139},{9,8},... | collective-permute-start | bytes 786440 | tf_op jit(solution)/shard_map/ppermute | solution.py:38
  38.7 15.5 %collective-permute-start.3 = (bf16[256,1024]{1,0:T(8,128)(2,1)S(1)}, bf16[256,1024]{1,0:T(8,128)(2,1)S(1)}, u32[]{:S(2)}, u32[]{:S(2)}) collective-permute-start(bf16[256,1024]{1,0:T(8,128)(2,1)S(1)} %copy-done.1), channel_id=1, source_target_pairs={{16,48},{17,49},{18,50},{19,51},{20,52},{21,53},{22,54},{23,55},{2... | collective-permute-start | bytes 1572872 | tf_op jit(solution)/shard_map/ppermute | solution.py:38
  41.0 9.5 %collective-permute-start.8 = (bf16[128,1024]{1,0:T(8,128)(2,1)}, bf16[128,1024]{1,0:T(8,128)(2,1)S(1)}, u32[]{:S(2)}, u32[]{:S(2)}) collective-permute-start(bf16[128,1024]{1,0:T(8,128)(2,1)} %get-tuple-element.58), channel_id=1, source_target_pairs={{0,1},{1,2},{2,3},{3,128},{4,5},{5,6},{6,7},{7,132},{8,9},{9,10},{... | collective-permute-start | bytes 786440 | tf_op jit(solution)/shard_map/ppermute | solution.py:38
  41.0 9.4 %collective-permute-start.9 = (bf16[128,1024]{1,0:T(8,128)(2,1)}, bf16[128,1024]{1,0:T(8,128)(2,1)S(1)}, u32[]{:S(2)}, u32[]{:S(2)}) collective-permute-start(bf16[128,1024]{1,0:T(8,128)(2,1)} %get-tuple-element.59), channel_id=1, source_target_pairs={{0,2},{1,131},{2,128},{3,1},{4,6},{5,135},{6,132},{7,5},{8,10},{9,... | collective-permute-start | bytes 786440 | tf_op jit(solution)/shard_map/ppermute | solution.py:38
  42.8 12.9 %collective-permute-start.2 = (bf16[256,1024]{1,0:T(8,128)(2,1)S(1)}, bf16[256,1024]{1,0:T(8,128)(2,1)}, u32[]{:S(2)}, u32[]{:S(2)}) collective-permute-start(bf16[256,1024]{1,0:T(8,128)(2,1)S(1)} %copy-done.1), channel_id=1, source_target_pairs={{0,48},{1,49},{2,50},{3,51},{4,52},{5,53},{6,54},{7,55},{8,56},{9,... | collective-permute-start | bytes 1572872 | tf_op jit(solution)/shard_map/ppermute | solution.py:38
  44.1 11.6 %collective-permute-start.1 = (bf16[256,1024]{1,0:T(8,128)(2,1)S(1)}, bf16[256,1024]{1,0:T(8,128)(2,1)}, u32[]{:S(2)}, u32[]{:S(2)}) collective-permute-start(bf16[256,1024]{1,0:T(8,128)(2,1)S(1)} %copy-done.1), channel_id=1, source_target_pairs={{0,16},{1,17},{2,18},{3,19},{4,20},{5,21},{6,22},{7,23},{8,24},{9,... | collective-permute-start | bytes 1572872 | tf_op jit(solution)/shard_map/ppermute | solution.py:38
  51.4 4.2 %collective-permute-start.11 = (bf16[128,1024]{1,0:T(8,128)(2,1)}, bf16[128,1024]{1,0:T(8,128)(2,1)}, u32[]{:S(2)}, u32[]{:S(2)}) collective-permute-start(bf16[128,1024]{1,0:T(8,128)(2,1)} %get-tuple-element.41), channel_id=1, source_target_pairs={{0,4},{1,5},{2,6},{3,7},{4,8},{5,9},{6,10},{7,11},{8,12},{9,13},{1... | collective-permute-start | bytes 786440 | tf_op jit(solution)/shard_map/ppermute | solution.py:38
  52.8 2.8 %collective-permute-start.12 = (bf16[128,1024]{1,0:T(8,128)(2,1)}, bf16[128,1024]{1,0:T(8,128)(2,1)}, u32[]{:S(2)}, u32[]{:S(2)}) collective-permute-start(bf16[128,1024]{1,0:T(8,128)(2,1)} %get-tuple-element.42), channel_id=1, source_target_pairs={{0,8},{1,9},{2,10},{3,11},{4,12},{5,13},{6,14},{7,15},{8,0},{9,1},... | collective-permute-start | bytes 786440 | tf_op jit(solution)/shard_map/ppermute | solution.py:38
  54.2 1.5 %collective-permute-start.13 = (bf16[128,1024]{1,0:T(8,128)(2,1)}, bf16[128,1024]{1,0:T(8,128)(2,1)}, u32[]{:S(2)}, u32[]{:S(2)}) collective-permute-start(bf16[128,1024]{1,0:T(8,128)(2,1)} %get-tuple-element.43), channel_id=1, source_target_pairs={{0,12},{1,13},{2,14},{3,15},{4,0},{5,1},{6,2},{7,3},{8,4},{9,5},{1... | collective-permute-start | bytes 786440 | tf_op jit(solution)/shard_map/ppermute | solution.py:38
  58.0 6.7 %collective-permute-start.14 = (bf16[640,256]{1,0:T(8,128)(2,1)S(1)}, bf16[640,256]{1,0:T(8,128)(2,1)S(1)}, u32[]{:S(2)}, u32[]{:S(2)}) collective-permute-start(bf16[640,256]{1,0:T(8,128)(2,1)S(1)} %get-tuple-element.49), channel_id=1, source_target_pairs={{0,32},{1,33},{2,34},{3,35},{4,36},{5,37},{6,38},{7,39},{8,40},{9,... | collective-permute-start | bytes 983048 | tf_op jit(solution)/shard_map/ppermute | solution.py:38
  59.1 14.6 %collective-permute-start.15 = (bf16[640,256]{1,0:T(8,128)(2,1)S(1)}, bf16[640,256]{1,0:T(8,128)(2,1)S(1)}, u32[]{:S(2)}, u32[]{:S(2)}) collective-permute-start(bf16[640,256]{1,0:T(8,128)(2,1)S(1)} %get-tuple-element.50), channel_id=1, source_target_pairs={{0,64},{1,65},{2,66},{3,67},{4,68},{5,69},{6,70},{7,71},{8,72},{9,... | collective-permute-start | bytes 983048 | tf_op jit(solution)/shard_map/ppermute | solution.py:38
  62.0 14.5 %collective-permute-start.16 = (bf16[640,256]{1,0:T(8,128)(2,1)S(1)}, bf16[640,256]{1,0:T(8,128)(2,1)S(1)}, u32[]{:S(2)}, u32[]{:S(2)}) collective-permute-start(bf16[640,256]{1,0:T(8,128)(2,1)S(1)} %get-tuple-element.51), channel_id=1, source_target_pairs={{0,96},{1,97},{2,98},{3,99},{4,100},{5,101},{6,102},{7,103},{8,104... | collective-permute-start | bytes 983048 | tf_op jit(solution)/shard_map/ppermute | solution.py:38
  76.7 1.9 %collective-permute-start.18 = (bf16[640,256]{1,0:T(8,128)(2,1)S(1)}, bf16[640,256]{1,0:T(8,128)(2,1)S(1)}, u32[]{:S(2)}, u32[]{:S(2)}) collective-permute-start(bf16[640,256]{1,0:T(8,128)(2,1)S(1)} %add_convert_fusion.1), channel_id=1, source_target_pairs={{0,130},{1,131},{2,0},{3,1},{4,134},{5,135},{6,4},{7,5},{8,138},{9... | collective-permute-start | bytes 983048 | tf_op jit(solution)/shard_map/ppermute | solution.py:38
  77.4 6.8 %collective-permute-start.17 = (bf16[640,256]{1,0:T(8,128)(2,1)S(1)}, bf16[640,256]{1,0:T(8,128)(2,1)S(1)}, u32[]{:S(2)}, u32[]{:S(2)}) collective-permute-start(bf16[640,256]{1,0:T(8,128)(2,1)S(1)} %add_convert_fusion.1), channel_id=1, source_target_pairs={{0,2},{1,3},{2,128},{3,129},{4,6},{5,7},{6,132},{7,133},{8,10},{9,... | collective-permute-start | bytes 983048 | tf_op jit(solution)/shard_map/ppermute | solution.py:38
  84.3 10.1 %collective-permute-start.21 = (bf16[640,256]{1,0:T(8,128)(2,1)S(1)}, bf16[640,256]{1,0:T(8,128)(2,1)S(1)}, u32[]{:S(2)}, u32[]{:S(2)}) collective-permute-start(bf16[640,256]{1,0:T(8,128)(2,1)S(1)} %add_convert_fusion.p0), channel_id=1, source_target_pairs={{0,96},{1,97},{2,98},{3,99},{4,100},{5,101},{6,102},{7,103},{8,104... | collective-permute-start | bytes 983048 | tf_op jit(solution)/shard_map/ppermute | solution.py:38
  86.9 7.8 %collective-permute-start.20 = (bf16[640,256]{1,0:T(8,128)(2,1)S(1)}, bf16[640,256]{1,0:T(8,128)(2,1)S(1)}, u32[]{:S(2)}, u32[]{:S(2)}) collective-permute-start(bf16[640,256]{1,0:T(8,128)(2,1)S(1)} %add_convert_fusion.p0), channel_id=1, source_target_pairs={{0,64},{1,65},{2,66},{3,67},{4,68},{5,69},{6,70},{7,71},{8,72},{9,... | collective-permute-start | bytes 983048 | tf_op jit(solution)/shard_map/ppermute | solution.py:38
  87.2 10.6 %collective-permute-start.19 = (bf16[640,256]{1,0:T(8,128)(2,1)S(1)}, bf16[640,256]{1,0:T(8,128)(2,1)S(1)}, u32[]{:S(2)}, u32[]{:S(2)}) collective-permute-start(bf16[640,256]{1,0:T(8,128)(2,1)S(1)} %add_convert_fusion.p0), channel_id=1, source_target_pairs={{0,32},{1,33},{2,34},{3,35},{4,36},{5,37},{6,38},{7,39},{8,40},{9,... | collective-permute-start | bytes 983048 | tf_op jit(solution)/shard_map/ppermute | solution.py:38
  118.7 19.7 %collective-permute-start.23 = (bf16[1024,1024]{1,0:T(8,128)(2,1)S(1)}, bf16[1024,1024]{1,0:T(8,128)(2,1)S(1)}, u32[]{:S(2)}, u32[]{:S(2)}) collective-permute-start(bf16[1024,1024]{1,0:T(8,128)(2,1)S(1)} %shard_map.58.s_ref.s_own), channel_id=1, source_target_pairs={{0,16},{1,17},{2,18},{3,19},{4,20},{5,21},{6,22},{7,23},{8,24},{9,... | collective-permute-start | bytes 6291464 | tf_op jit(solution)/shard_map/ppermute | solution.py:38
  122.5 16.0 %collective-permute-start.22 = (bf16[256,1024]{1,0:T(8,128)(2,1)S(1)}, bf16[256,1024]{1,0:T(8,128)(2,1)S(1)}, u32[]{:S(2)}, u32[]{:S(2)}) collective-permute-start(bf16[256,1024]{1,0:T(8,128)(2,1)S(1)} %get-tuple-element.55), channel_id=1, source_target_pairs={{16,0},{17,1},{18,2},{19,3},{20,4},{21,5},{22,6},{23,7},{24,8},{25... | collective-permute-start | bytes 1572872 | tf_op jit(solution)/shard_map/ppermute | solution.py:38

commit v2 on v1

--- a/solution.py
+++ b/solution.py
@@ -42,6 +42,11 @@
     z = zh * 4 + zl
     z = (z + {1: 1, 2: 2 if z % 2 == 0 else -2, 3: -1}[k]) % 8
     return z // 4, z % 4
+
+
+def across(zh, y, x, zl, dz, dy):
+    z = (zh * 4 + zl + dz * (-2 if zl < 2 else 2)) % 8
+    return z // 4, 3 - y if dy else y, 1, x, z % 4
 
 
 def pack_kernel(place_ref, mine_ref, other_ref, *outs):
@@ -254,16 +259,10 @@
         block = (zh ^ dz) * 2 + (y // 2 ^ dy)
         sent = lax.dynamic_slice_in_dim(both_x, block * size, size, 1)
         mine_x.append(sent if dz + dy == 0 else moved(
-            sent, lambda zh, y, c, x, zl: (zh ^ dz, y ^ (2 * dy), 1, x, zl) if c == 1 else None))
+            sent, lambda zh, y, c, x, zl: across(zh, y, x, zl, dz, dy) if c == 1 else None))
     mine_x = jnp.concatenate(mine_x)
 
     packed = pack(((zl + 2) % 4).reshape(1), samp_g, other_g, size)
-    own_w, *packed = lax.optimization_barrier((weight_grad, *packed))
-    weights = [
-        moved(own_w, lambda zh, y, c, x, zl: (zh, y, 1, x, zl) if c == 0 else None),
-        moved(own_w, lambda zh, y, c, x, zl: (zh, y ^ 1, 1, x, zl) if c == 0 else None),
-        moved(own_w, lambda zh, y, c, x, zl: (zh, y ^ 1, 1, x, zl) if c == 1 else None),
-    ]
     held = [jnp.where(is_g, packed[0], mine_x)]
     for k in (1, 2, 3):
         held.append(moved(
@@ -275,9 +274,6 @@
     dealt = list(deal(x.reshape(1), held))
     for k in (1, 2, 3):
         dealt[k] = moved(dealt[k], lambda zh, y, c, x, zl: (zh, y, 0, (x + k) % 4, zl) if c == 0 else None)
-
-    weights, dealt = lax.optimization_barrier((weights, dealt))
-    weights.insert(1, weight_grad)
 
     chunks = cov(jnp.stack([jnp.where(is_g, y, x), 1 - core, core]), dealt, held, scale)
     total = chunks[0].astype(F32)
@@ -305,9 +301,16 @@
             lambda zh, y, c, x, zl: (zh, (y + k) % 4, 0, x, zl) if c == 0 else (zh, y, 1, (x + k) % 4, zl),
         ))
 
+    own_w, _ = lax.optimization_barrier((weight_grad, piece))
+    weights = [
+        moved(own_w, lambda zh, y, c, x, zl: (zh, y, 1, x, zl) if c == 0 else None),
+        moved(own_w, lambda zh, y, c, x, zl: (zh, y ^ 1, 1, x, zl) if c == 0 else None),
+        moved(own_w, lambda zh, y, c, x, zl: (zh, y ^ 1, 1, x, zl) if c == 1 else None),
+    ]
     damp = pick(damping, jnp.where(is_g, BLOCKS_A + o, zh * 2 + y // 2)).reshape(1)
     place = jnp.stack([jnp.where(is_g, y, x), core, y % 2])
-    inverse = rounds(place, damp, pieces)
+    inverse, *weights = lax.optimization_barrier((rounds(place, damp, pieces), *weights))
+    weights.insert(1, weight_grad)
 
     inv_g = moved(inverse, lambda zh, y, c, x, zl: (zh, y, 1, x, zl) if c == 0 else None)
     mixed_0, mixed_1 = mix(place, inverse, weights)

time: 143 us -> 130 us (0.909); the launches traced: 141 us -> 130 us
  starting transfers between devices: 56.6 us -> 40 us
  waiting for transfers between devices: 46.9 us -> 53.9 us
    ppermute x24, starting transfers between devices: 56.6 us -> 40 us  [moved(): return lax.ppermute(value, ('dp', 'owner'), pairs)]
    ppermute x24, waiting for transfers between devices: 46.9 us -> 53.9 us  [moved(): return lax.ppermute(value, ('dp', 'owner'), pairs)]
  transfers between devices with their start and end apart: 24 -> 24, of which waited for: 12 -> 12; matrix products, arithmetic and copies ran while one was open for 2% -> 2% of each run, Pallas kernels for 2% -> 18%
where the time goes in v2:
time: 130 us
  waiting for transfers between devices  53.9 us (41%)
  starting transfers between devices  40 us (31%)
  Pallas kernels  28.4 us (22%)
  matrix products  3.28 us (3%)
  other arithmetic  3.28 us (3%)
    ppermute x24, waiting for transfers between devices, moved(): return lax.ppermute(value, ('dp', 'owner'), pairs)  53.9 us
    ppermute x24, starting transfers between devices, moved(): return lax.ppermute(value, ('dp', 'owner'), pairs)  40 us
    pallas_call x1, Pallas kernels, rounds(): pl.pallas_call(rounds_kernel, out_shape=jax.ShapeDtypeStruct((size, size)...  21.4 us
    dot_general x2, matrix products, dot(): return jnp.dot(a, b, preferred_element_type=F32)  3.28 us
  transfers between devices with their start and end apart: 24, of which 12 were waited for; matrix products, arithmetic and copies ran while one was open for 2% of the time, Pallas kernels for 18%

profile of v2, /device:TPU:33, one launch (start us, length us, event | category | flops | bytes accessed | tf_op | source)
XLA Modules:
  0.0 129.9 jit_solution(9741071180164893229)
XLA Ops:
  0.0 3.0 %convolution_convert_fusion.mine_ref = bf16[16,16384]{1,0:T(8,128)(2,1)S(1)} fusion(bf16[128,16384]{1,0:T(8,128)(2,1)} %param.6, s32[16]{0:T(128)} %param.7), kind=kOutput, calls=%fused_computation | convolution fusion | flops 67373056 | bytes 4718656 | tf_op jit(solution)/shard_map/dot_general | solution.py:19
  3.0 2.6 %collective-permute-start = (bf16[16,16384]{1,0:T(8,128)(2,1)S(1)}, bf16[16,16384]{1,0:T(8,128)(2,1)S(1)}, u32[]{:S(2)}, u32[]{:S(2)}) collective-permute-start(bf16[16,16384]{1,0:T(8,128)(2,1)S(1)} %convolution_convert_fusion.mine_ref), channel_id=1, source_target_pairs={{16,0},{17,1},{18,2},{19,3},{20,4},{21,5},{22,6},{23,7},{24,8},{25... | collective-permute-start | bytes 1572872 | tf_op jit(solution)/shard_map/ppermute | solution.py:38
  5.9 1.3 collective-permute-start.1
  7.3 1.9 %collective-permute-done.1 = bf16[16,4096]{1,0:T(8,128)(2,1)S(1)} collective-permute-done((bf16[16,4096]{1,0:T(8,128)(2,1)S(1)}, bf16[16,4096]{1,0:T(8,128)(2,1)S(1)}, u32[]{:S(2)}, u32[]{:S(2)}) %collective-permute-start.1) | collective-permute-done | bytes 131104 | tf_op jit(solution)/shard_map/ppermute | solution.py:38
  9.2 4.6 %collective-permute-start.2 = (bf16[32,1024]{1,0:T(8,128)(2,1)S(1)}, bf16[32,1024]{1,0:T(8,128)(2,1)S(1)}, u32[]{:S(2)}, u32[]{:S(2)}) collective-permute-start(bf16[32,1024]{1,0:T(8,128)(2,1)S(1)} %get-tuple-element.47), channel_id=1, source_target_pairs={{16,112},{17,113},{18,114},{19,115},{20,116},{21,117},{22,118},{23... | collective-permute-start | bytes 196616 | tf_op jit(solution)/shard_map/ppermute | solution.py:38
  13.8 7.0 %collective-permute-start.3 = (bf16[32,1024]{1,0:T(8,128)(2,1)S(1)}, bf16[32,1024]{1,0:T(8,128)(2,1)}, u32[]{:S(2)}, u32[]{:S(2)}) collective-permute-start(bf16[32,1024]{1,0:T(8,128)(2,1)S(1)} %get-tuple-element.48), channel_id=1, source_target_pairs={{16,146},{17,147},{18,144},{19,145},{20,150},{21,151},{22,148},{23... | collective-permute-start | bytes 196616 | tf_op jit(solution)/shard_map/ppermute | solution.py:38
  20.9 1.9 %collective-permute-start.4 = (bf16[32,1024]{1,0:T(8,128)(2,1)S(1)}, bf16[32,1024]{1,0:T(8,128)(2,1)}, u32[]{:S(2)}, u32[]{:S(2)}) collective-permute-start(bf16[32,1024]{1,0:T(8,128)(2,1)S(1)} %get-tuple-element.49), channel_id=1, source_target_pairs={{16,242},{17,243},{18,240},{19,241},{20,246},{21,247},{22,244},{23... | collective-permute-start | bytes 196616 | tf_op jit(solution)/shard_map/ppermute | solution.py:38
  23.4 10.2 %collective-permute-done.4 = bf16[32,1024]{1,0:T(8,128)(2,1)} collective-permute-done((bf16[32,1024]{1,0:T(8,128)(2,1)S(1)}, bf16[32,1024]{1,0:T(8,128)(2,1)}, u32[]{:S(2)}, u32[]{:S(2)}) %collective-permute-start.4) | collective-permute-done | bytes 65568 | tf_op jit(solution)/shard_map/ppermute | solution.py:38
  33.6 1.9 %broadcast_select_fusion = (bf16[128,1024]{1,0:T(8,128)(2,1)}, bf16[128,1024]{1,0:T(8,128)(2,1)S(1)}, bf16[128,1024]{1,0:T(8,128)(2,1)S(1)}) fusion(bf16[128,1024]{1,0:T(8,128)(2,1)S(1)} %get-tuple-element.27, pred[]{:T(512)S(6)} %eq.22, bf16[32,1024]{1,0:T(8,128)(2,1)} %collective-permute-done.4, bf16[32,1024]{1,0:T(8,128)(2,1)} %collective-permute-done.3, ...), kind=kLoop, calls=%fused_computation.13 | loop fusion | flops 1441792 | bytes 1835009 | tf_op jit(solution)/shard_map/jit(_where)/select_n | solution.py:269
  35.5 2.5 %collective-permute-start.7 = (bf16[128,1024]{1,0:T(8,128)(2,1)}, bf16[128,1024]{1,0:T(8,128)(2,1)S(1)}, u32[]{:S(2)}, u32[]{:S(2)}) collective-permute-start(bf16[128,1024]{1,0:T(8,128)(2,1)} %get-tuple-element.43), channel_id=1, source_target_pairs={{0,131},{1,0},{2,1},{3,2},{4,135},{5,4},{6,5},{7,6},{8,139},{9,8},... | collective-permute-start | bytes 786440 | tf_op jit(solution)/shard_map/ppermute | solution.py:38
  38.0 1.7 %collective-permute-start.6 = (bf16[128,1024]{1,0:T(8,128)(2,1)S(1)}, bf16[128,1024]{1,0:T(8,128)(2,1)S(1)}, u32[]{:S(2)}, u32[]{:S(2)}) collective-permute-start(bf16[128,1024]{1,0:T(8,128)(2,1)S(1)} %get-tuple-element.45), channel_id=1, source_target_pairs={{0,2},{1,131},{2,128},{3,1},{4,6},{5,135},{6,132},{7,5},{8,10},{9,... | collective-permute-start | bytes 786440 | tf_op jit(solution)/shard_map/ppermute | solution.py:38
  40.7 5.0 %collective-permute-done.7.h3.refs_8_ = bf16[128,1024]{1,0:T(8,128)(2,1)S(1)} collective-permute-done((bf16[128,1024]{1,0:T(8,128)(2,1)}, bf16[128,1024]{1,0:T(8,128)(2,1)S(1)}, u32[]{:S(2)}, u32[]{:S(2)}) %collective-permute-start.7) | collective-permute-done | bytes 262176 | tf_op jit(solution)/shard_map/ppermute | solution.py:38
  45.7 1.6 %collective-permute-done.5.h1.refs_6_ = bf16[128,1024]{1,0:T(8,128)(2,1)S(1)} collective-permute-done((bf16[128,1024]{1,0:T(8,128)(2,1)S(1)}, bf16[128,1024]{1,0:T(8,128)(2,1)S(1)}, u32[]{:S(2)}, u32[]{:S(2)}) %collective-permute-start.5) | collective-permute-done | bytes 262176 | tf_op jit(solution)/shard_map/ppermute | solution.py:38
  49.5 1.4 %collective-permute-start.10 = (bf16[128,1024]{1,0:T(8,128)(2,1)}, bf16[128,1024]{1,0:T(8,128)(2,1)}, u32[]{:S(2)}, u32[]{:S(2)}) collective-permute-start(bf16[128,1024]{1,0:T(8,128)(2,1)} %get-tuple-element.31), channel_id=1, source_target_pairs={{0,12},{1,13},{2,14},{3,15},{4,0},{5,1},{6,2},{7,3},{8,4},{9,5},{1... | collective-permute-start | bytes 786440 | tf_op jit(solution)/shard_map/ppermute | solution.py:38
  51.0 2.2 %shard_map.57 = (bf16[640,256]{1,0:T(8,128)(2,1)S(1)}, bf16[640,256]{1,0:T(8,128)(2,1)S(1)}, bf16[640,256]{1,0:T(8,128)(2,1)S(1)}, bf16[640,256]{1,0:T(8,128)(2,1)S(1)}) custom-call(s32[3]{0:T(128)S(1)} %pad_add_fusion.1.refs_0_, bf16[128,1024]{1,0:T(8,128)(2,1)S(1)} %get-tuple-element.28.refs_1_, bf16[128,1024]{1,0:T(8,128)(2,1)S(1)} %collective-permute-done.8.refs_2_, ...), custom_call_target="tpu_custom_call" | custom-call | tf_op jit(solution)/shard_map/pallas_call | solution.py:113
  53.2 2.0 %collective-permute-start.11 = (bf16[640,256]{1,0:T(8,128)(2,1)S(1)}, bf16[640,256]{1,0:T(8,128)(2,1)S(1)}, u32[]{:S(2)}, u32[]{:S(2)}) collective-permute-start(bf16[640,256]{1,0:T(8,128)(2,1)S(1)} %get-tuple-element.33), channel_id=1, source_target_pairs={{0,32},{1,33},{2,34},{3,35},{4,36},{5,37},{6,38},{7,39},{8,40},{9,... | collective-permute-start | bytes 983048 | tf_op jit(solution)/shard_map/ppermute | solution.py:38
  55.2 3.3 %collective-permute-start.12 = (bf16[640,256]{1,0:T(8,128)(2,1)S(1)}, bf16[640,256]{1,0:T(8,128)(2,1)S(1)}, u32[]{:S(2)}, u32[]{:S(2)}) collective-permute-start(bf16[640,256]{1,0:T(8,128)(2,1)S(1)} %get-tuple-element.34), channel_id=1, source_target_pairs={{0,64},{1,65},{2,66},{3,67},{4,68},{5,69},{6,70},{7,71},{8,72},{9,... | collective-permute-start | bytes 983048 | tf_op jit(solution)/shard_map/ppermute | solution.py:38
  58.5 2.7 %collective-permute-done.11 = bf16[640,256]{1,0:T(8,128)(2,1)S(1)} collective-permute-done((bf16[640,256]{1,0:T(8,128)(2,1)S(1)}, bf16[640,256]{1,0:T(8,128)(2,1)S(1)}, u32[]{:S(2)}, u32[]{:S(2)}) %collective-permute-start.11) | collective-permute-done | bytes 327712 | tf_op jit(solution)/shard_map/ppermute | solution.py:38
  61.2 8.6 %collective-permute-done.12 = bf16[640,256]{1,0:T(8,128)(2,1)S(1)} collective-permute-done((bf16[640,256]{1,0:T(8,128)(2,1)S(1)}, bf16[640,256]{1,0:T(8,128)(2,1)S(1)}, u32[]{:S(2)}, u32[]{:S(2)}) %collective-permute-start.12) | collective-permute-done | bytes 327712 | tf_op jit(solution)/shard_map/ppermute | solution.py:38
  69.8 9.3 %collective-permute-done.13 = bf16[640,256]{1,0:T(8,128)(2,1)S(1)} collective-permute-done((bf16[640,256]{1,0:T(8,128)(2,1)S(1)}, bf16[640,256]{1,0:T(8,128)(2,1)S(1)}, u32[]{:S(2)}, u32[]{:S(2)}) %collective-permute-start.13) | collective-permute-done | bytes 327712 | tf_op jit(solution)/shard_map/ppermute | solution.py:38
  80.1 8.4 %collective-permute-done.14 = bf16[640,256]{1,0:T(8,128)(2,1)S(1)} collective-permute-done((bf16[640,256]{1,0:T(8,128)(2,1)S(1)}, bf16[640,256]{1,0:T(8,128)(2,1)S(1)}, u32[]{:S(2)}, u32[]{:S(2)}) %collective-permute-start.14) | collective-permute-done | bytes 327712 | tf_op jit(solution)/shard_map/ppermute | solution.py:38
  88.8 1.4 %collective-permute-start.16 = (bf16[640,256]{1,0:T(8,128)(2,1)S(1)}, bf16[640,256]{1,0:T(8,128)(2,1)}, u32[]{:S(2)}, u32[]{:S(2)}) collective-permute-start(bf16[640,256]{1,0:T(8,128)(2,1)S(1)} %add_convert_fusion.p0), channel_id=1, source_target_pairs={{0,32},{1,33},{2,34},{3,35},{4,36},{5,37},{6,38},{7,39},{8,40},{9,... | collective-permute-start | bytes 983048 | tf_op jit(solution)/shard_map/ppermute | solution.py:38
  90.9 1.9 %collective-permute-start.21 = (bf16[256,1024]{1,0:T(8,128)(2,1)S(1)}, bf16[256,1024]{1,0:T(8,128)(2,1)S(1)}, u32[]{:S(2)}, u32[]{:S(2)}) collective-permute-start(bf16[256,1024]{1,0:T(8,128)(2,1)S(1)} %copy-done.1), channel_id=1, source_target_pairs={{16,48},{17,49},{18,50},{19,51},{20,52},{21,53},{22,54},{23,55},{2... | collective-permute-start | bytes 1572872 | tf_op jit(solution)/shard_map/ppermute | solution.py:38
  92.8 1.3 collective-permute-start.20
  95.0 1.5 %collective-permute-start.19 = (bf16[256,1024]{1,0:T(8,128)(2,1)S(1)}, bf16[256,1024]{1,0:T(8,128)(2,1)S(1)}, u32[]{:S(2)}, u32[]{:S(2)}) collective-permute-start(bf16[256,1024]{1,0:T(8,128)(2,1)S(1)} %copy-done.1), channel_id=1, source_target_pairs={{0,16},{1,17},{2,18},{3,19},{4,20},{5,21},{6,22},{7,23},{8,24},{9,... | collective-permute-start | bytes 1572872 | tf_op jit(solution)/shard_map/ppermute | solution.py:38
  96.5 3.3 %collective-permute-done.16.p1 = bf16[640,256]{1,0:T(8,128)(2,1)} collective-permute-done((bf16[640,256]{1,0:T(8,128)(2,1)S(1)}, bf16[640,256]{1,0:T(8,128)(2,1)}, u32[]{:S(2)}, u32[]{:S(2)}) %collective-permute-start.16) | collective-permute-done | bytes 327712 | tf_op jit(solution)/shard_map/ppermute | solution.py:38
  99.8 21.4 %shard_map.58.s_ref.s_own = bf16[1024,1024]{1,0:T(8,128)(2,1)S(1)} custom-call(s32[3]{0:T(128)S(1)} %pad_add_fusion.place_ref, f32[1]{0:T(128)} %dynamic_slice.16.damp_ref, bf16[640,256]{1,0:T(8,128)(2,1)S(1)} %add_convert_fusion.p0, bf16[640,256]{1,0:T(8,128)(2,1)} %collective-permute-done.16.p1, bf16[640,256]{1,0:T(8,128)(2,1)} %collective-permute-done.17.p2, ...), custom_call_target="tpu_custom_call" | custom-call | flops 17179869184 | bytes 4194304 | tf_op jit(solution)/shard_map/pallas_call | solution.py:177
  121.3 1.3 collective-permute-start.23
  122.6 1.8 %shard_map.59 = (bf16[256,1024]{1,0:T(8,128)(2,1)S(1)}, bf16[256,1024]{1,0:T(8,128)(2,1)S(1)}) custom-call(s32[3]{0:T(128)S(1)} %pad_add_fusion.place_ref, bf16[1024,1024]{1,0:T(8,128)(2,1)S(1)} %shard_map.58.s_ref.s_own, bf16[256,1024]{1,0:T(8,128)(2,1)S(1)} %collective-permute-done.19.w0, bf16[256,1024]{1,0:T(8,128)(2,1)S(1)} %copy-done.1, ...), custom_call_target="tpu_custom_call" | custom-call | tf_op jit(solution)/shard_map/pallas_call | solution.py:209
  124.4 2.0 %collective-permute-start.22 = (bf16[256,1024]{1,0:T(8,128)(2,1)S(1)}, bf16[256,1024]{1,0:T(8,128)(2,1)S(1)}, u32[]{:S(2)}, u32[]{:S(2)}) collective-permute-start(bf16[256,1024]{1,0:T(8,128)(2,1)S(1)} %get-tuple-element.41), channel_id=1, source_target_pairs={{16,0},{17,1},{18,2},{19,3},{20,4},{21,5},{22,6},{23,7},{24,8},{25... | collective-permute-start | bytes 1572872 | tf_op jit(solution)/shard_map/ppermute | solution.py:38
  126.4 1.5 %collective-permute-done.22.t0_ref = bf16[256,1024]{1,0:T(8,128)(2,1)S(1)} collective-permute-done((bf16[256,1024]{1,0:T(8,128)(2,1)S(1)}, bf16[256,1024]{1,0:T(8,128)(2,1)S(1)}, u32[]{:S(2)}, u32[]{:S(2)}) %collective-permute-start.22) | collective-permute-done | bytes 524320 | tf_op jit(solution)/shard_map/ppermute | solution.py:38
  127.9 2.1 %shard_map.60 = bf16[256,1024]{1,0:T(8,128)(2,1)} custom-call(s32[3]{0:T(128)S(1)} %pad_add_fusion.place_ref, bf16[256,1024]{1,0:T(8,128)(2,1)S(1)} %collective-permute-done.22.t0_ref, bf16[1024,1024]{1,0:T(8,128)(2,1)S(1)} %shard_map.58.s_ref.s_own, bf16[256,1024]{1,0:T(8,128)(2,1)S(1)} %get-tuple-element.42.t1_ref, ...), custom_call_target="tpu_custom_call" | custom-call | tf_op jit(solution)/shard_map/pallas_call | solution.py:229
  (40 shorter events, 7.1 us)
Async XLA Ops:
  0.0 5.6 %copy-start = (bf16[128,4096]{1,0:T(8,128)(2,1)S(1)}, bf16[128,4096]{1,0:T(8,128)(2,1)}, u32[]{:S(2)}) copy-start(bf16[128,4096]{1,0:T(8,128)(2,1)} %param.5) | copy-start | bytes 3145732
  0.0 5.6 %copy-start.2 = (s32[16]{0:T(128)S(1)}, s32[16]{0:T(128)}, u32[]{:S(2)}) copy-start(s32[16]{0:T(128)} %param.7) | copy-start | bytes 196
  3.0 19.9 %collective-permute-start = (bf16[16,16384]{1,0:T(8,128)(2,1)S(1)}, bf16[16,16384]{1,0:T(8,128)(2,1)S(1)}, u32[]{:S(2)}, u32[]{:S(2)}) collective-permute-start(bf16[16,16384]{1,0:T(8,128)(2,1)S(1)} %convolution_convert_fusion.mine_ref), channel_id=1, source_target_pairs={{16,0},{17,1},{18,2},{19,3},{20,4},{21,5},{22,6},{23,7},{24,8},{25... | collective-permute-start | bytes 1572872 | tf_op jit(solution)/shard_map/ppermute | solution.py:38
  5.9 3.2 %collective-permute-start.1 = (bf16[16,4096]{1,0:T(8,128)(2,1)S(1)}, bf16[16,4096]{1,0:T(8,128)(2,1)S(1)}, u32[]{:S(2)}, u32[]{:S(2)}) collective-permute-start(bf16[16,4096]{1,0:T(8,128)(2,1)S(1)} %convolution_convert_fusion.1), channel_id=1, source_target_pairs={{0,16},{1,17},{2,18},{3,19},{4,20},{5,21},{6,22},{7,23},{8,24},{9,... | collective-permute-start | bytes 393224 | tf_op jit(solution)/shard_map/ppermute | solution.py:38
  9.2 13.8 %collective-permute-start.2 = (bf16[32,1024]{1,0:T(8,128)(2,1)S(1)}, bf16[32,1024]{1,0:T(8,128)(2,1)S(1)}, u32[]{:S(2)}, u32[]{:S(2)}) collective-permute-start(bf16[32,1024]{1,0:T(8,128)(2,1)S(1)} %get-tuple-element.47), channel_id=1, source_target_pairs={{16,112},{17,113},{18,114},{19,115},{20,116},{21,117},{22,118},{23... | collective-permute-start | bytes 196616 | tf_op jit(solution)/shard_map/ppermute | solution.py:38
  13.8 9.6 %collective-permute-start.3 = (bf16[32,1024]{1,0:T(8,128)(2,1)S(1)}, bf16[32,1024]{1,0:T(8,128)(2,1)}, u32[]{:S(2)}, u32[]{:S(2)}) collective-permute-start(bf16[32,1024]{1,0:T(8,128)(2,1)S(1)} %get-tuple-element.48), channel_id=1, source_target_pairs={{16,146},{17,147},{18,144},{19,145},{20,150},{21,151},{22,148},{23... | collective-permute-start | bytes 196616 | tf_op jit(solution)/shard_map/ppermute | solution.py:38
  20.9 12.8 %collective-permute-start.4 = (bf16[32,1024]{1,0:T(8,128)(2,1)S(1)}, bf16[32,1024]{1,0:T(8,128)(2,1)}, u32[]{:S(2)}, u32[]{:S(2)}) collective-permute-start(bf16[32,1024]{1,0:T(8,128)(2,1)S(1)} %get-tuple-element.49), channel_id=1, source_target_pairs={{16,242},{17,243},{18,240},{19,241},{20,246},{21,247},{22,244},{23... | collective-permute-start | bytes 196616 | tf_op jit(solution)/shard_map/ppermute | solution.py:38
  33.6 56.5 %copy-start.3 = (f32[20]{0:T(128)S(1)}, f32[20]{0:T(128)}, u32[]{:S(2)}) copy-start(f32[20]{0:T(128)} %param.8) | copy-start | bytes 244
  33.6 57.2 %copy-start.1 = (bf16[256,1024]{1,0:T(8,128)(2,1)S(1)}, bf16[256,1024]{1,0:T(8,128)(2,1)}, u32[]{:S(2)}) copy-start(bf16[256,1024]{1,0:T(8,128)(2,1)} %w1.1) | copy-start | bytes 1572868
  35.5 10.1 %collective-permute-start.7 = (bf16[128,1024]{1,0:T(8,128)(2,1)}, bf16[128,1024]{1,0:T(8,128)(2,1)S(1)}, u32[]{:S(2)}, u32[]{:S(2)}) collective-permute-start(bf16[128,1024]{1,0:T(8,128)(2,1)} %get-tuple-element.43), channel_id=1, source_target_pairs={{0,131},{1,0},{2,1},{3,2},{4,135},{5,4},{6,5},{7,6},{8,139},{9,8},... | collective-permute-start | bytes 786440 | tf_op jit(solution)/shard_map/ppermute | solution.py:38
  38.0 9.2 %collective-permute-start.5 = (bf16[128,1024]{1,0:T(8,128)(2,1)S(1)}, bf16[128,1024]{1,0:T(8,128)(2,1)S(1)}, u32[]{:S(2)}, u32[]{:S(2)}) collective-permute-start(bf16[128,1024]{1,0:T(8,128)(2,1)S(1)} %get-tuple-element.44), channel_id=1, source_target_pairs={{0,1},{1,2},{2,3},{3,128},{4,5},{5,6},{6,7},{7,132},{8,9},{9,10},{... | collective-permute-start | bytes 786440 | tf_op jit(solution)/shard_map/ppermute | solution.py:38
  38.0 9.2 %collective-permute-start.6 = (bf16[128,1024]{1,0:T(8,128)(2,1)S(1)}, bf16[128,1024]{1,0:T(8,128)(2,1)S(1)}, u32[]{:S(2)}, u32[]{:S(2)}) collective-permute-start(bf16[128,1024]{1,0:T(8,128)(2,1)S(1)} %get-tuple-element.45), channel_id=1, source_target_pairs={{0,2},{1,131},{2,128},{3,1},{4,6},{5,135},{6,132},{7,5},{8,10},{9,... | collective-permute-start | bytes 786440 | tf_op jit(solution)/shard_map/ppermute | solution.py:38
  48.2 2.8 %collective-permute-start.8 = (bf16[128,1024]{1,0:T(8,128)(2,1)}, bf16[128,1024]{1,0:T(8,128)(2,1)S(1)}, u32[]{:S(2)}, u32[]{:S(2)}) collective-permute-start(bf16[128,1024]{1,0:T(8,128)(2,1)} %get-tuple-element.29), channel_id=1, source_target_pairs={{0,4},{1,5},{2,6},{3,7},{4,8},{5,9},{6,10},{7,11},{8,12},{9,13},{1... | collective-permute-start | bytes 786440 | tf_op jit(solution)/shard_map/ppermute | solution.py:38
  48.8 2.2 %collective-permute-start.9 = (bf16[128,1024]{1,0:T(8,128)(2,1)}, bf16[128,1024]{1,0:T(8,128)(2,1)S(1)}, u32[]{:S(2)}, u32[]{:S(2)}) collective-permute-start(bf16[128,1024]{1,0:T(8,128)(2,1)} %get-tuple-element.30), channel_id=1, source_target_pairs={{0,8},{1,9},{2,10},{3,11},{4,12},{5,13},{6,14},{7,15},{8,0},{9,1},... | collective-permute-start | bytes 786440 | tf_op jit(solution)/shard_map/ppermute | solution.py:38
  49.5 1.5 %collective-permute-start.10 = (bf16[128,1024]{1,0:T(8,128)(2,1)}, bf16[128,1024]{1,0:T(8,128)(2,1)}, u32[]{:S(2)}, u32[]{:S(2)}) collective-permute-start(bf16[128,1024]{1,0:T(8,128)(2,1)} %get-tuple-element.31), channel_id=1, source_target_pairs={{0,12},{1,13},{2,14},{3,15},{4,0},{5,1},{6,2},{7,3},{8,4},{9,5},{1... | collective-permute-start | bytes 786440 | tf_op jit(solution)/shard_map/ppermute | solution.py:38
  53.2 8.0 %collective-permute-start.11 = (bf16[640,256]{1,0:T(8,128)(2,1)S(1)}, bf16[640,256]{1,0:T(8,128)(2,1)S(1)}, u32[]{:S(2)}, u32[]{:S(2)}) collective-permute-start(bf16[640,256]{1,0:T(8,128)(2,1)S(1)} %get-tuple-element.33), channel_id=1, source_target_pairs={{0,32},{1,33},{2,34},{3,35},{4,36},{5,37},{6,38},{7,39},{8,40},{9,... | collective-permute-start | bytes 983048 | tf_op jit(solution)/shard_map/ppermute | solution.py:38
  55.2 14.6 %collective-permute-start.12 = (bf16[640,256]{1,0:T(8,128)(2,1)S(1)}, bf16[640,256]{1,0:T(8,128)(2,1)S(1)}, u32[]{:S(2)}, u32[]{:S(2)}) collective-permute-start(bf16[640,256]{1,0:T(8,128)(2,1)S(1)} %get-tuple-element.34), channel_id=1, source_target_pairs={{0,64},{1,65},{2,66},{3,67},{4,68},{5,69},{6,70},{7,71},{8,72},{9,... | collective-permute-start | bytes 983048 | tf_op jit(solution)/shard_map/ppermute | solution.py:38
  58.5 20.6 %collective-permute-start.13 = (bf16[640,256]{1,0:T(8,128)(2,1)S(1)}, bf16[640,256]{1,0:T(8,128)(2,1)S(1)}, u32[]{:S(2)}, u32[]{:S(2)}) collective-permute-start(bf16[640,256]{1,0:T(8,128)(2,1)S(1)} %get-tuple-element.35), channel_id=1, source_target_pairs={{0,96},{1,97},{2,98},{3,99},{4,100},{5,101},{6,102},{7,103},{8,104... | collective-permute-start | bytes 983048 | tf_op jit(solution)/shard_map/ppermute | solution.py:38
  79.3 0.8 collective-permute-start.15
  80.0 8.5 %collective-permute-start.14 = (bf16[640,256]{1,0:T(8,128)(2,1)S(1)}, bf16[640,256]{1,0:T(8,128)(2,1)S(1)}, u32[]{:S(2)}, u32[]{:S(2)}) collective-permute-start(bf16[640,256]{1,0:T(8,128)(2,1)S(1)} %add_convert_fusion.1), channel_id=1, source_target_pairs={{0,2},{1,3},{2,128},{3,129},{4,6},{5,7},{6,132},{7,133},{8,10},{9,... | collective-permute-start | bytes 983048 | tf_op jit(solution)/shard_map/ppermute | solution.py:38
  88.6 6.4 %collective-permute-start.18 = (bf16[640,256]{1,0:T(8,128)(2,1)S(1)}, bf16[640,256]{1,0:T(8,128)(2,1)S(1)}, u32[]{:S(2)}, u32[]{:S(2)}) collective-permute-start(bf16[640,256]{1,0:T(8,128)(2,1)S(1)} %add_convert_fusion.p0), channel_id=1, source_target_pairs={{0,96},{1,97},{2,98},{3,99},{4,100},{5,101},{6,102},{7,103},{8,104... | collective-permute-start | bytes 983048 | tf_op jit(solution)/shard_map/ppermute | solution.py:38
  88.7 7.8 %collective-permute-start.17 = (bf16[640,256]{1,0:T(8,128)(2,1)S(1)}, bf16[640,256]{1,0:T(8,128)(2,1)}, u32[]{:S(2)}, u32[]{:S(2)}) collective-permute-start(bf16[640,256]{1,0:T(8,128)(2,1)S(1)} %add_convert_fusion.p0), channel_id=1, source_target_pairs={{0,64},{1,65},{2,66},{3,67},{4,68},{5,69},{6,70},{7,71},{8,72},{9,... | collective-permute-start | bytes 983048 | tf_op jit(solution)/shard_map/ppermute | solution.py:38
  88.8 11.0 %collective-permute-start.16 = (bf16[640,256]{1,0:T(8,128)(2,1)S(1)}, bf16[640,256]{1,0:T(8,128)(2,1)}, u32[]{:S(2)}, u32[]{:S(2)}) collective-permute-start(bf16[640,256]{1,0:T(8,128)(2,1)S(1)} %add_convert_fusion.p0), channel_id=1, source_target_pairs={{0,32},{1,33},{2,34},{3,35},{4,36},{5,37},{6,38},{7,39},{8,40},{9,... | collective-permute-start | bytes 983048 | tf_op jit(solution)/shard_map/ppermute | solution.py:38
  90.9 30.4 %collective-permute-start.21 = (bf16[256,1024]{1,0:T(8,128)(2,1)S(1)}, bf16[256,1024]{1,0:T(8,128)(2,1)S(1)}, u32[]{:S(2)}, u32[]{:S(2)}) collective-permute-start(bf16[256,1024]{1,0:T(8,128)(2,1)S(1)} %copy-done.1), channel_id=1, source_target_pairs={{16,48},{17,49},{18,50},{19,51},{20,52},{21,53},{22,54},{23,55},{2... | collective-permute-start | bytes 1572872 | tf_op jit(solution)/shard_map/ppermute | solution.py:38
  92.8 28.5 %collective-permute-start.20 = (bf16[256,1024]{1,0:T(8,128)(2,1)S(1)}, bf16[256,1024]{1,0:T(8,128)(2,1)S(1)}, u32[]{:S(2)}, u32[]{:S(2)}) collective-permute-start(bf16[256,1024]{1,0:T(8,128)(2,1)S(1)} %copy-done.1), channel_id=1, source_target_pairs={{0,48},{1,49},{2,50},{3,51},{4,52},{5,53},{6,54},{7,55},{8,56},{9,... | collective-permute-start | bytes 1572872 | tf_op jit(solution)/shard_map/ppermute | solution.py:38
  95.0 26.3 %collective-permute-start.19 = (bf16[256,1024]{1,0:T(8,128)(2,1)S(1)}, bf16[256,1024]{1,0:T(8,128)(2,1)S(1)}, u32[]{:S(2)}, u32[]{:S(2)}) collective-permute-start(bf16[256,1024]{1,0:T(8,128)(2,1)S(1)} %copy-done.1), channel_id=1, source_target_pairs={{0,16},{1,17},{2,18},{3,19},{4,20},{5,21},{6,22},{7,23},{8,24},{9,... | collective-permute-start | bytes 1572872 | tf_op jit(solution)/shard_map/ppermute | solution.py:38
  121.3 6.5 %collective-permute-start.23 = (bf16[1024,1024]{1,0:T(8,128)(2,1)S(1)}, bf16[1024,1024]{1,0:T(8,128)(2,1)S(1)}, u32[]{:S(2)}, u32[]{:S(2)}) collective-permute-start(bf16[1024,1024]{1,0:T(8,128)(2,1)S(1)} %shard_map.58.s_ref.s_own), channel_id=1, source_target_pairs={{0,16},{1,17},{2,18},{3,19},{4,20},{5,21},{6,22},{7,23},{8,24},{9,... | collective-permute-start | bytes 6291464 | tf_op jit(solution)/shard_map/ppermute | solution.py:38
  124.4 3.4 %collective-permute-start.22 = (bf16[256,1024]{1,0:T(8,128)(2,1)S(1)}, bf16[256,1024]{1,0:T(8,128)(2,1)S(1)}, u32[]{:S(2)}, u32[]{:S(2)}) collective-permute-start(bf16[256,1024]{1,0:T(8,128)(2,1)S(1)} %get-tuple-element.41), channel_id=1, source_target_pairs={{16,0},{17,1},{18,2},{19,3},{20,4},{21,5},{22,6},{23,7},{24,8},{25... | collective-permute-start | bytes 1572872 | tf_op jit(solution)/shard_map/ppermute | solution.py:38

commit v3 on v2

--- a/solution.py
+++ b/solution.py
@@ -44,19 +44,14 @@
     return z // 4, z % 4
 
 
-def across(zh, y, x, zl, dz, dy):
-    z = (zh * 4 + zl + dz * (-2 if zl < 2 else 2)) % 8
-    return z // 4, 3 - y if dy else y, 1, x, z % 4
-
-
 def pack_kernel(place_ref, mine_ref, other_ref, *outs):
     count, size = mine_ref.shape[0], outs[0].shape[1]
     for k, out in enumerate(outs):
-        for owner in range(4):
-            index = owner * 4 + lax.rem(place_ref[0] + k, 4)
+        for zl in range(4):
+            index = lax.rem(place_ref[0] + k, 4) * 4 + zl
             cols = pl.ds(pl.multiple_of(index * size, size), size)
-            out[owner * 2 * count:(owner * 2 + 1) * count, :] = mine_ref[:, cols]
-            out[(owner * 2 + 1) * count:(owner * 2 + 2) * count, :] = other_ref[:, cols]
+            out[zl * 2 * count:(zl * 2 + 1) * count, :] = mine_ref[:, cols]
+            out[(zl * 2 + 1) * count:(zl * 2 + 2) * count, :] = other_ref[:, cols]
 
 
 def pack(place, mine, other, size):
@@ -69,33 +64,40 @@
     )(place, mine, other)
 
 
-def deal_kernel(place_ref, h0, h1, h2, h3, *outs):
+def deal_kernel(place_ref, h0, h1, h2, h3, kept_ref, come_ref, *outs):
     rows = h0.shape[0] // 4
-    for k, out in enumerate(outs):
-        start = pl.multiple_of(lax.rem(place_ref[0] + k, 4) * rows, rows)
-        for i, held in enumerate((h0, h1, h2, h3)):
-            out[i * rows:(i + 1) * rows, :] = held[pl.ds(start, rows), :]
-
-
-def deal(place, held):
+    half = kept_ref.shape[0]
+
+    @pl.when(place_ref[1] == 0)
+    def _():
+        for k, out in enumerate(outs):
+            start = pl.multiple_of(lax.rem(place_ref[0] + k, 4) * rows, rows)
+            for i, held in enumerate((h0, h1, h2, h3)):
+                out[i * rows:(i + 1) * rows, :] = held[pl.ds(start, rows), :]
+
+    @pl.when(place_ref[1] == 1)
+    def _():
+        for out in outs:
+            out[:half, :] = kept_ref[...]
+            out[half:, :] = come_ref[...]
+
+
+def deal(place, held, kept, come):
     return pl.pallas_call(
         deal_kernel,
         out_shape=(jax.ShapeDtypeStruct(held[0].shape, BF16),) * 4,
-        in_specs=[SMEM] + [VMEM] * 4,
+        in_specs=[SMEM] + [VMEM] * 6,
         out_specs=(VMEM,) * 4,
         compiler_params=pltpu.CompilerParams(vmem_limit_bytes=8 * MIB),
-    )(place, *held)
+    )(place, *held, kept, come)
 
 
 def cov_kernel(scale, place_ref, *refs):
-    dealt, held, chunks, (all_ref, panel_ref) = refs[:4], refs[4:8], refs[8:12], refs[12:]
-    count, size = held[0].shape
+    pieces, chunks, (all_ref, panel_ref) = refs[:4], refs[4:8], refs[8:]
+    count, size = pieces[0].shape
     tile, sub = size // 4, size // 16
-    for role, pieces in enumerate((dealt, held)):
-        @pl.when(place_ref[2] == role)
-        def _():
-            for k, piece in enumerate(pieces):
-                all_ref[k * count:(k + 1) * count, :] = piece[...]
+    for k, piece in enumerate(pieces):
+        all_ref[k * count:(k + 1) * count, :] = piece[...]
     for r in range(4):
         cols = all_ref[:, r * tile:(r + 1) * tile]
         panel_ref[:, r * tile:] = gram(cols, all_ref[:, r * tile:]) * scale
@@ -107,17 +109,17 @@
                         pl.ds(start, sub), c * tile:(c + 1) * tile].astype(BF16)
 
 
-def cov(place, dealt, held, scale):
-    count, size = held[0].shape
+def cov(place, pieces, scale):
+    count, size = pieces[0].shape
     tile, sub = size // 4, size // 16
     return pl.pallas_call(
         lambda *refs: cov_kernel(scale, *refs),
         out_shape=(jax.ShapeDtypeStruct((len(UPPER) * sub, tile), BF16),) * 4,
-        in_specs=[SMEM] + [VMEM] * 8,
+        in_specs=[SMEM] + [VMEM] * 4,
         out_specs=(VMEM,) * 4,
         scratch_shapes=[pltpu.VMEM((4 * count, size), BF16), pltpu.VMEM((tile, size), F32)],
         compiler_params=pltpu.CompilerParams(vmem_limit_bytes=16 * MIB),
-    )(place, *dealt, *held)
+    )(place, *pieces)
 
 
 def rounds_kernel(place_ref, damp_ref, p0, p1, p2, p3, out_ref, a_ref, x_ref, xb_ref, p_ref):
@@ -253,29 +255,33 @@
     samp_g = dot(hot, out_grads).astype(BF16)
     other_g = moved(samp_g, lambda zh, y, c, x, zl: (zh, y, 0, x, zl) if c == 1 else None)
 
+    packed = pack(x.reshape(1), samp_g, other_g, size)
+    held = [packed[0]]
+    for k in (2, 1, 3):
+        held.append(moved(packed[k], lambda zh, y, c, x, zl: (zh, y, 0, (x + k) % 4, zl) if c == 0 else None))
+
     both_x = jnp.concatenate([samp_x, other_x])
-    mine_x = []
-    for dz, dy in ((0, 0), (0, 1), (1, 0), (1, 1)):
-        block = (zh ^ dz) * 2 + (y // 2 ^ dy)
-        sent = lax.dynamic_slice_in_dim(both_x, block * size, size, 1)
-        mine_x.append(sent if dz + dy == 0 else moved(
-            sent, lambda zh, y, c, x, zl: across(zh, y, x, zl, dz, dy) if c == 1 else None))
-    mine_x = jnp.concatenate(mine_x)
-
-    packed = pack(((zl + 2) % 4).reshape(1), samp_g, other_g, size)
-    held = [jnp.where(is_g, packed[0], mine_x)]
-    for k in (1, 2, 3):
-        held.append(moved(
-            jnp.where(is_g, packed[k], mine_x),
+
+    def over_z(zh, y, c, x, zl):
+        z = (zh * 4 + zl + (-2 if zl < 2 else 2)) % 8
+        return (z // 4, y, 1, x, z % 4) if c == 1 else None
+
+    def columns(value, start, count):
+        return lax.dynamic_slice_in_dim(value, start * size, count * size, 1)
+
+    halves = jnp.concatenate([columns(both_x, zh * 2, 2), moved(columns(both_x, (1 - zh) * 2, 2), over_z)])
+    kept = columns(halves, y // 2, 1)
+    come = moved(columns(halves, 1 - y // 2, 1), lambda zh, y, c, x, zl: (zh, 3 - y, 1, x, zl) if c == 1 else None)
+
+    samples = list(deal(jnp.stack([(zl + 2) % 4, core]), held, kept, come))
+    for k in (2, 1, 3):
+        samples[k] = moved(
+            samples[k],
             lambda zh, y, c, x, zl: (z_shift(zh, zl, k)[0], y, 0, x, z_shift(zh, zl, k)[1]) if c == 0
             else (zh, y, 1, (x + k) % 4, zl),
-        ))
-
-    dealt = list(deal(x.reshape(1), held))
-    for k in (1, 2, 3):
-        dealt[k] = moved(dealt[k], lambda zh, y, c, x, zl: (zh, y, 0, (x + k) % 4, zl) if c == 0 else None)
-
-    chunks = cov(jnp.stack([jnp.where(is_g, y, x), 1 - core, core]), dealt, held, scale)
+        )
+
+    chunks = cov(jnp.stack([jnp.where(is_g, y, x), 1 - core]), samples, scale)
     total = chunks[0].astype(F32)
     for k in (1, 2, 3):
         total += moved(

time: 130 us -> 121 us (0.931); the launches traced: 130 us -> 120 us
  waiting for transfers between devices: 53.9 us -> 38.4 us
  starting transfers between devices: 40 us -> 45.7 us
    ppermute x24 -> x23, waiting for transfers between devices: 53.9 us -> 38.4 us  [moved(): return lax.ppermute(value, ('dp', 'owner'), pairs)]
    ppermute x24 -> x23, starting transfers between devices: 40 us -> 45.7 us  [moved(): return lax.ppermute(value, ('dp', 'owner'), pairs)]
    select_n x2 -> x0, other arithmetic: 2.81 us -> none  [the longest x1 1.87 us: on_device(): jnp.where(is_g, packed[k], mine_x)]
    concatenate x0 -> x1, other arithmetic: none -> 1.54 us  [on_device(): jnp.concatenate([columns(both_x, zh * 2, 2), moved(columns(both_x, (1 - z...]
  transfers between devices with their start and end apart: 24 -> 23, of which waited for: 12 -> 12; matrix products, arithmetic and copies ran while one was open for 2% -> 3% of each run, Pallas kernels for 18% -> 20%
where the time goes in v3:
time: 121 us; the launch traced here: 120 us
  starting transfers between devices  45.7 us (38%)
  waiting for transfers between devices  38.4 us (32%)
  Pallas kernels  28.6 us (24%)
  matrix products  3.28 us (3%)
  other arithmetic  2.74 us (2%)
    ppermute x23, starting transfers between devices, moved(): return lax.ppermute(value, ('dp', 'owner'), pairs)  45.7 us
    ppermute x23, waiting for transfers between devices, moved(): return lax.ppermute(value, ('dp', 'owner'), pairs)  38.4 us
    pallas_call x1, Pallas kernels, rounds(): pl.pallas_call(rounds_kernel, out_shape=jax.ShapeDtypeStruct((size, size)...  20.8 us
    dot_general x2, matrix products, dot(): return jnp.dot(a, b, preferred_element_type=F32)  3.28 us
  transfers between devices with their start and end apart: 23, of which 12 were waited for; matrix products, arithmetic and copies ran while one was open for 3% of the time, Pallas kernels for 20%

profile of v3, /device:TPU:33, one launch (start us, length us, event | category | flops | bytes accessed | tf_op | source)
XLA Modules:
  0.0 119.6 jit_solution(1527945770599293409)
XLA Ops:
  0.0 3.0 %convolution_convert_fusion.mine_ref = bf16[16,16384]{1,0:T(8,128)(2,1)S(1)} fusion(bf16[128,16384]{1,0:T(8,128)(2,1)} %param.6, s32[16]{0:T(128)} %param.7), kind=kOutput, calls=%fused_computation | convolution fusion | flops 67373056 | bytes 4718656 | tf_op jit(solution)/shard_map/dot_general | solution.py:19
  3.0 2.7 %collective-permute-start = (bf16[16,16384]{1,0:T(8,128)(2,1)S(1)}, bf16[16,16384]{1,0:T(8,128)(2,1)S(1)}, u32[]{:S(2)}, u32[]{:S(2)}) collective-permute-start(bf16[16,16384]{1,0:T(8,128)(2,1)S(1)} %convolution_convert_fusion.mine_ref), channel_id=1, source_target_pairs={{16,0},{17,1},{18,2},{19,3},{20,4},{21,5},{22,6},{23,7},{24,8},{25... | collective-permute-start | bytes 1572872 | tf_op jit(solution)/shard_map/ppermute | solution.py:38
  6.1 1.3 %collective-permute-start.4 = (bf16[16,4096]{1,0:T(8,128)(2,1)S(1)}, bf16[16,4096]{1,0:T(8,128)(2,1)S(1)}, u32[]{:S(2)}, u32[]{:S(2)}) collective-permute-start(bf16[16,4096]{1,0:T(8,128)(2,1)S(1)} %convolution_convert_fusion.1), channel_id=1, source_target_pairs={{0,16},{1,17},{2,18},{3,19},{4,20},{5,21},{6,22},{7,23},{8,24},{9,... | collective-permute-start | bytes 393224 | tf_op jit(solution)/shard_map/ppermute | solution.py:38
  7.4 1.9 %collective-permute-done.4 = bf16[16,4096]{1,0:T(8,128)(2,1)S(1)} collective-permute-done((bf16[16,4096]{1,0:T(8,128)(2,1)S(1)}, bf16[16,4096]{1,0:T(8,128)(2,1)S(1)}, u32[]{:S(2)}, u32[]{:S(2)}) %collective-permute-start.4) | collective-permute-done | bytes 131104 | tf_op jit(solution)/shard_map/ppermute | solution.py:38
  10.0 7.0 %collective-permute-start.5 = (bf16[32,2048]{1,0:T(8,128)(2,1)}, bf16[32,2048]{1,0:T(8,128)(2,1)}, u32[]{:S(2)}, u32[]{:S(2)}) collective-permute-start(bf16[32,2048]{1,0:T(8,128)(2,1)} %get-tuple-element.45), channel_id=1, source_target_pairs={{16,146},{17,147},{18,144},{19,145},{20,150},{21,151},{22,148},{23... | collective-permute-start | bytes 393224 | tf_op jit(solution)/shard_map/ppermute | solution.py:38
  19.9 1.3 %collective-permute-done.5 = bf16[32,2048]{1,0:T(8,128)(2,1)} collective-permute-done((bf16[32,2048]{1,0:T(8,128)(2,1)}, bf16[32,2048]{1,0:T(8,128)(2,1)}, u32[]{:S(2)}, u32[]{:S(2)}) %collective-permute-start.5) | collective-permute-done | bytes 131104 | tf_op jit(solution)/shard_map/ppermute | solution.py:38
  21.3 1.5 %fusion = (bf16[64,1024]{1,0:T(8,128)(2,1)}, bf16[64,1024]{1,0:T(8,128)(2,1)S(1)}) fusion(s32[]{:T(128)S(6)} %select_n.84, bf16[32,2048]{1,0:T(8,128)(2,1)S(1)} %get-tuple-element.46, bf16[32,2048]{1,0:T(8,128)(2,1)} %collective-permute-done.5, s32[]{:T(128)S(6)} %select_n.83), kind=kLoop, calls=%fused_computation.12 | loop fusion | flops 524288 | bytes 524296 | tf_op jit(solution)/shard_map/concatenate | solution.py:272
  22.8 4.6 %collective-permute-start.6 = (bf16[64,1024]{1,0:T(8,128)(2,1)}, bf16[64,1024]{1,0:T(8,128)(2,1)S(1)}, u32[]{:S(2)}, u32[]{:S(2)}) collective-permute-start(bf16[64,1024]{1,0:T(8,128)(2,1)} %get-tuple-element.43), channel_id=1, source_target_pairs={{16,112},{17,113},{18,114},{19,115},{20,116},{21,117},{22,118},{23... | collective-permute-start | bytes 393224 | tf_op jit(solution)/shard_map/ppermute | solution.py:38
  27.6 2.4 %collective-permute-done.6.come_ref = bf16[64,1024]{1,0:T(8,128)(2,1)S(1)} collective-permute-done((bf16[64,1024]{1,0:T(8,128)(2,1)}, bf16[64,1024]{1,0:T(8,128)(2,1)S(1)}, u32[]{:S(2)}, u32[]{:S(2)}) %collective-permute-start.6) | collective-permute-done | bytes 131104 | tf_op jit(solution)/shard_map/ppermute | solution.py:38
  30.0 1.4 %shard_map.56 = (bf16[128,1024]{1,0:T(8,128)(2,1)S(1)}, bf16[128,1024]{1,0:T(8,128)(2,1)}, bf16[128,1024]{1,0:T(8,128)(2,1)}, bf16[128,1024]{1,0:T(8,128)(2,1)S(1)}) custom-call(s32[2]{0:T(128)S(1)} %pad_add_fusion.2.place_ref, bf16[128,1024]{1,0:T(8,128)(2,1)S(1)} %get-tuple-element.24.h0, bf16[128,1024]{1,0:T(8,128)(2,1)S(1)} %collective-permute-done.1.h1, ...), custom_call_target="tpu_custom_call" | custom-call | tf_op jit(solution)/shard_map/pallas_call | solution.py:86
  31.4 1.0 collective-permute-start.7
  32.4 2.6 %collective-permute-start.8 = (bf16[128,1024]{1,0:T(8,128)(2,1)}, bf16[128,1024]{1,0:T(8,128)(2,1)S(1)}, u32[]{:S(2)}, u32[]{:S(2)}) collective-permute-start(bf16[128,1024]{1,0:T(8,128)(2,1)} %get-tuple-element.30), channel_id=1, source_target_pairs={{0,2},{1,131},{2,128},{3,1},{4,6},{5,135},{6,132},{7,5},{8,10},{9,... | collective-permute-start | bytes 786440 | tf_op jit(solution)/shard_map/ppermute | solution.py:38
  36.1 2.1 %collective-permute-done.7.refs_2_ = bf16[128,1024]{1,0:T(8,128)(2,1)S(1)} collective-permute-done((bf16[128,1024]{1,0:T(8,128)(2,1)}, bf16[128,1024]{1,0:T(8,128)(2,1)S(1)}, u32[]{:S(2)}, u32[]{:S(2)}) %collective-permute-start.7) | collective-permute-done | bytes 262176 | tf_op jit(solution)/shard_map/ppermute | solution.py:38
  38.2 3.7 %collective-permute-done.8.refs_3_ = bf16[128,1024]{1,0:T(8,128)(2,1)S(1)} collective-permute-done((bf16[128,1024]{1,0:T(8,128)(2,1)}, bf16[128,1024]{1,0:T(8,128)(2,1)S(1)}, u32[]{:S(2)}, u32[]{:S(2)}) %collective-permute-start.8) | collective-permute-done | bytes 262176 | tf_op jit(solution)/shard_map/ppermute | solution.py:38
  41.9 1.7 %shard_map.57 = (bf16[640,256]{1,0:T(8,128)(2,1)S(1)}, bf16[640,256]{1,0:T(8,128)(2,1)S(1)}, bf16[640,256]{1,0:T(8,128)(2,1)S(1)}, bf16[640,256]{1,0:T(8,128)(2,1)S(1)}) custom-call(s32[2]{0:T(128)S(1)} %pad_add_fusion.1.refs_0_, bf16[128,1024]{1,0:T(8,128)(2,1)S(1)} %get-tuple-element.28.refs_1_, bf16[128,1024]{1,0:T(8,128)(2,1)S(1)} %collective-permute-done.7.refs_2_, ...), custom_call_target="tpu_custom_call" | custom-call | tf_op jit(solution)/shard_map/pallas_call | solution.py:115
  44.4 1.8 %collective-permute-start.11 = (bf16[640,256]{1,0:T(8,128)(2,1)S(1)}, bf16[640,256]{1,0:T(8,128)(2,1)S(1)}, u32[]{:S(2)}, u32[]{:S(2)}) collective-permute-start(bf16[640,256]{1,0:T(8,128)(2,1)S(1)} %get-tuple-element.34), channel_id=1, source_target_pairs={{0,64},{1,65},{2,66},{3,67},{4,68},{5,69},{6,70},{7,71},{8,72},{9,... | collective-permute-start | bytes 983048 | tf_op jit(solution)/shard_map/ppermute | solution.py:38
  46.3 3.6 %collective-permute-done.10 = bf16[640,256]{1,0:T(8,128)(2,1)S(1)} collective-permute-done((bf16[640,256]{1,0:T(8,128)(2,1)S(1)}, bf16[640,256]{1,0:T(8,128)(2,1)S(1)}, u32[]{:S(2)}, u32[]{:S(2)}) %collective-permute-start.10) | collective-permute-done | bytes 327712 | tf_op jit(solution)/shard_map/ppermute | solution.py:38
  49.9 9.0 %collective-permute-done.11 = bf16[640,256]{1,0:T(8,128)(2,1)S(1)} collective-permute-done((bf16[640,256]{1,0:T(8,128)(2,1)S(1)}, bf16[640,256]{1,0:T(8,128)(2,1)S(1)}, u32[]{:S(2)}, u32[]{:S(2)}) %collective-permute-start.11) | collective-permute-done | bytes 327712 | tf_op jit(solution)/shard_map/ppermute | solution.py:38
  58.9 2.3 %collective-permute-done.12 = bf16[640,256]{1,0:T(8,128)(2,1)S(1)} collective-permute-done((bf16[640,256]{1,0:T(8,128)(2,1)S(1)}, bf16[640,256]{1,0:T(8,128)(2,1)S(1)}, u32[]{:S(2)}, u32[]{:S(2)}) %collective-permute-start.12) | collective-permute-done | bytes 327712 | tf_op jit(solution)/shard_map/ppermute | solution.py:38
  62.1 6.2 %collective-permute-done.13 = bf16[640,256]{1,0:T(8,128)(2,1)S(1)} collective-permute-done((bf16[640,256]{1,0:T(8,128)(2,1)S(1)}, bf16[640,256]{1,0:T(8,128)(2,1)S(1)}, u32[]{:S(2)}, u32[]{:S(2)}) %collective-permute-start.13) | collective-permute-done | bytes 327712 | tf_op jit(solution)/shard_map/ppermute | solution.py:38
  68.5 2.1 %collective-permute-start.17 = (bf16[640,256]{1,0:T(8,128)(2,1)S(1)}, bf16[640,256]{1,0:T(8,128)(2,1)S(1)}, u32[]{:S(2)}, u32[]{:S(2)}) collective-permute-start(bf16[640,256]{1,0:T(8,128)(2,1)S(1)} %add_convert_fusion.p0), channel_id=1, source_target_pairs={{0,96},{1,97},{2,98},{3,99},{4,100},{5,101},{6,102},{7,103},{8,104... | collective-permute-start | bytes 983048 | tf_op jit(solution)/shard_map/ppermute | solution.py:38
  72.5 1.9 %collective-permute-start.20 = (bf16[256,1024]{1,0:T(8,128)(2,1)S(1)}, bf16[256,1024]{1,0:T(8,128)(2,1)S(1)}, u32[]{:S(2)}, u32[]{:S(2)}) collective-permute-start(bf16[256,1024]{1,0:T(8,128)(2,1)S(1)} %copy-done.1), channel_id=1, source_target_pairs={{16,48},{17,49},{18,50},{19,51},{20,52},{21,53},{22,54},{23,55},{2... | collective-permute-start | bytes 1572872 | tf_op jit(solution)/shard_map/ppermute | solution.py:38
  74.4 1.3 %collective-permute-start.19 = (bf16[256,1024]{1,0:T(8,128)(2,1)S(1)}, bf16[256,1024]{1,0:T(8,128)(2,1)S(1)}, u32[]{:S(2)}, u32[]{:S(2)}) collective-permute-start(bf16[256,1024]{1,0:T(8,128)(2,1)S(1)} %copy-done.1), channel_id=1, source_target_pairs={{0,48},{1,49},{2,50},{3,51},{4,52},{5,53},{6,54},{7,55},{8,56},{9,... | collective-permute-start | bytes 1572872 | tf_op jit(solution)/shard_map/ppermute | solution.py:38
  75.7 2.4 %collective-permute-done.17.p3 = bf16[640,256]{1,0:T(8,128)(2,1)S(1)} collective-permute-done((bf16[640,256]{1,0:T(8,128)(2,1)S(1)}, bf16[640,256]{1,0:T(8,128)(2,1)S(1)}, u32[]{:S(2)}, u32[]{:S(2)}) %collective-permute-start.17) | collective-permute-done | bytes 327712 | tf_op jit(solution)/shard_map/ppermute | solution.py:38
  78.1 1.5 %collective-permute-start.18 = (bf16[256,1024]{1,0:T(8,128)(2,1)S(1)}, bf16[256,1024]{1,0:T(8,128)(2,1)S(1)}, u32[]{:S(2)}, u32[]{:S(2)}) collective-permute-start(bf16[256,1024]{1,0:T(8,128)(2,1)S(1)} %copy-done.1), channel_id=1, source_target_pairs={{0,16},{1,17},{2,18},{3,19},{4,20},{5,21},{6,22},{7,23},{8,24},{9,... | collective-permute-start | bytes 1572872 | tf_op jit(solution)/shard_map/ppermute | solution.py:38
  79.6 1.9 %collective-permute-done.15.p1 = bf16[640,256]{1,0:T(8,128)(2,1)S(1)} collective-permute-done((bf16[640,256]{1,0:T(8,128)(2,1)S(1)}, bf16[640,256]{1,0:T(8,128)(2,1)S(1)}, u32[]{:S(2)}, u32[]{:S(2)}) %collective-permute-start.15) | collective-permute-done | bytes 327712 | tf_op jit(solution)/shard_map/ppermute | solution.py:38
  81.5 20.8 %shard_map.58.s_ref.s_own = bf16[1024,1024]{1,0:T(8,128)(2,1)S(1)} custom-call(s32[3]{0:T(128)S(1)} %pad_add_fusion.place_ref, f32[1]{0:T(128)} %dynamic_slice.16.damp_ref, bf16[640,256]{1,0:T(8,128)(2,1)S(1)} %add_convert_fusion.p0, bf16[640,256]{1,0:T(8,128)(2,1)S(1)} %collective-permute-done.15.p1, bf16[640,256]{1,0:T(8,128)(2,1)S(1)} %collective-permute-done.16.p2, ...), custom_call_target="tpu_custom_call" | custom-call | flops 17179869184 | bytes 4194304 | tf_op jit(solution)/shard_map/pallas_call | solution.py:179
  102.3 1.3 %collective-permute-start.22 = (bf16[1024,1024]{1,0:T(8,128)(2,1)S(1)}, bf16[1024,1024]{1,0:T(8,128)(2,1)S(1)}, u32[]{:S(2)}, u32[]{:S(2)}) collective-permute-start(bf16[1024,1024]{1,0:T(8,128)(2,1)S(1)} %shard_map.58.s_ref.s_own), channel_id=1, source_target_pairs={{0,16},{1,17},{2,18},{3,19},{4,20},{5,21},{6,22},{7,23},{8,24},{9,... | collective-permute-start | bytes 6291464 | tf_op jit(solution)/shard_map/ppermute | solution.py:38
  103.6 1.8 %shard_map.59 = (bf16[256,1024]{1,0:T(8,128)(2,1)S(1)}, bf16[256,1024]{1,0:T(8,128)(2,1)S(1)}) custom-call(s32[3]{0:T(128)S(1)} %pad_add_fusion.place_ref, bf16[1024,1024]{1,0:T(8,128)(2,1)S(1)} %shard_map.58.s_ref.s_own, bf16[256,1024]{1,0:T(8,128)(2,1)S(1)} %collective-permute-done.18.w0, bf16[256,1024]{1,0:T(8,128)(2,1)S(1)} %copy-done.1, ...), custom_call_target="tpu_custom_call" | custom-call | tf_op jit(solution)/shard_map/pallas_call | solution.py:211
  105.4 10.6 %collective-permute-start.21 = (bf16[256,1024]{1,0:T(8,128)(2,1)S(1)}, bf16[256,1024]{1,0:T(8,128)(2,1)S(1)}, u32[]{:S(2)}, u32[]{:S(2)}) collective-permute-start(bf16[256,1024]{1,0:T(8,128)(2,1)S(1)} %get-tuple-element.41), channel_id=1, source_target_pairs={{16,0},{17,1},{18,2},{19,3},{20,4},{21,5},{22,6},{23,7},{24,8},{25... | collective-permute-start | bytes 1572872 | tf_op jit(solution)/shard_map/ppermute | solution.py:38
  116.1 1.5 %collective-permute-done.21.t0_ref = bf16[256,1024]{1,0:T(8,128)(2,1)S(1)} collective-permute-done((bf16[256,1024]{1,0:T(8,128)(2,1)S(1)}, bf16[256,1024]{1,0:T(8,128)(2,1)S(1)}, u32[]{:S(2)}, u32[]{:S(2)}) %collective-permute-start.21) | collective-permute-done | bytes 524320 | tf_op jit(solution)/shard_map/ppermute | solution.py:38
  117.5 2.1 %shard_map.60 = bf16[256,1024]{1,0:T(8,128)(2,1)} custom-call(s32[3]{0:T(128)S(1)} %pad_add_fusion.place_ref, bf16[256,1024]{1,0:T(8,128)(2,1)S(1)} %collective-permute-done.21.t0_ref, bf16[1024,1024]{1,0:T(8,128)(2,1)S(1)} %shard_map.58.s_ref.s_own, bf16[256,1024]{1,0:T(8,128)(2,1)S(1)} %get-tuple-element.42.t1_ref, ...), custom_call_target="tpu_custom_call" | custom-call | tf_op jit(solution)/shard_map/pallas_call | solution.py:231
  (38 shorter events, 8.8 us)
Async XLA Ops:
  0.0 5.8 %copy-start = (bf16[128,4096]{1,0:T(8,128)(2,1)S(1)}, bf16[128,4096]{1,0:T(8,128)(2,1)}, u32[]{:S(2)}) copy-start(bf16[128,4096]{1,0:T(8,128)(2,1)} %param.5) | copy-start | bytes 3145732
  0.0 5.8 %copy-start.2 = (s32[16]{0:T(128)S(1)}, s32[16]{0:T(128)}, u32[]{:S(2)}) copy-start(s32[16]{0:T(128)} %param.7) | copy-start | bytes 196
  3.0 68.8 %copy-start.3 = (f32[20]{0:T(128)S(1)}, f32[20]{0:T(128)}, u32[]{:S(2)}) copy-start(f32[20]{0:T(128)} %param.8) | copy-start | bytes 244
  3.0 69.5 %copy-start.1 = (bf16[256,1024]{1,0:T(8,128)(2,1)S(1)}, bf16[256,1024]{1,0:T(8,128)(2,1)}, u32[]{:S(2)}) copy-start(bf16[256,1024]{1,0:T(8,128)(2,1)} %w1.1) | copy-start | bytes 1572868
  3.0 14.0 %collective-permute-start = (bf16[16,16384]{1,0:T(8,128)(2,1)S(1)}, bf16[16,16384]{1,0:T(8,128)(2,1)S(1)}, u32[]{:S(2)}, u32[]{:S(2)}) collective-permute-start(bf16[16,16384]{1,0:T(8,128)(2,1)S(1)} %convolution_convert_fusion.mine_ref), channel_id=1, source_target_pairs={{16,0},{17,1},{18,2},{19,3},{20,4},{21,5},{22,6},{23,7},{24,8},{25... | collective-permute-start | bytes 1572872 | tf_op jit(solution)/shard_map/ppermute | solution.py:38
  6.1 3.2 %collective-permute-start.4 = (bf16[16,4096]{1,0:T(8,128)(2,1)S(1)}, bf16[16,4096]{1,0:T(8,128)(2,1)S(1)}, u32[]{:S(2)}, u32[]{:S(2)}) collective-permute-start(bf16[16,4096]{1,0:T(8,128)(2,1)S(1)} %convolution_convert_fusion.1), channel_id=1, source_target_pairs={{0,16},{1,17},{2,18},{3,19},{4,20},{5,21},{6,22},{7,23},{8,24},{9,... | collective-permute-start | bytes 393224 | tf_op jit(solution)/shard_map/ppermute | solution.py:38
  10.0 11.3 %collective-permute-start.5 = (bf16[32,2048]{1,0:T(8,128)(2,1)}, bf16[32,2048]{1,0:T(8,128)(2,1)}, u32[]{:S(2)}, u32[]{:S(2)}) collective-permute-start(bf16[32,2048]{1,0:T(8,128)(2,1)} %get-tuple-element.45), channel_id=1, source_target_pairs={{16,146},{17,147},{18,144},{19,145},{20,150},{21,151},{22,148},{23... | collective-permute-start | bytes 393224 | tf_op jit(solution)/shard_map/ppermute | solution.py:38
  17.8 12.2 %collective-permute-start.1 = (bf16[128,1024]{1,0:T(8,128)(2,1)}, bf16[128,1024]{1,0:T(8,128)(2,1)S(1)}, u32[]{:S(2)}, u32[]{:S(2)}) collective-permute-start(bf16[128,1024]{1,0:T(8,128)(2,1)} %get-tuple-element.25), channel_id=1, source_target_pairs={{0,8},{1,9},{2,10},{3,11},{4,12},{5,13},{6,14},{7,15},{8,0},{9,1},... | collective-permute-start | bytes 786440 | tf_op jit(solution)/shard_map/ppermute | solution.py:38
  18.5 11.5 %collective-permute-start.2 = (bf16[128,1024]{1,0:T(8,128)(2,1)S(1)}, bf16[128,1024]{1,0:T(8,128)(2,1)S(1)}, u32[]{:S(2)}, u32[]{:S(2)}) collective-permute-start(bf16[128,1024]{1,0:T(8,128)(2,1)S(1)} %get-tuple-element.26), channel_id=1, source_target_pairs={{0,4},{1,5},{2,6},{3,7},{4,8},{5,9},{6,10},{7,11},{8,12},{9,13},{1... | collective-permute-start | bytes 786440 | tf_op jit(solution)/shard_map/ppermute | solution.py:38
  19.2 10.8 %collective-permute-start.3 = (bf16[128,1024]{1,0:T(8,128)(2,1)S(1)}, bf16[128,1024]{1,0:T(8,128)(2,1)S(1)}, u32[]{:S(2)}, u32[]{:S(2)}) collective-permute-start(bf16[128,1024]{1,0:T(8,128)(2,1)S(1)} %get-tuple-element.27), channel_id=1, source_target_pairs={{0,12},{1,13},{2,14},{3,15},{4,0},{5,1},{6,2},{7,3},{8,4},{9,5},{1... | collective-permute-start | bytes 786440 | tf_op jit(solution)/shard_map/ppermute | solution.py:38
  22.8 7.2 %collective-permute-start.6 = (bf16[64,1024]{1,0:T(8,128)(2,1)}, bf16[64,1024]{1,0:T(8,128)(2,1)S(1)}, u32[]{:S(2)}, u32[]{:S(2)}) collective-permute-start(bf16[64,1024]{1,0:T(8,128)(2,1)} %get-tuple-element.43), channel_id=1, source_target_pairs={{16,112},{17,113},{18,114},{19,115},{20,116},{21,117},{22,118},{23... | collective-permute-start | bytes 393224 | tf_op jit(solution)/shard_map/ppermute | solution.py:38
  31.4 6.8 %collective-permute-start.7 = (bf16[128,1024]{1,0:T(8,128)(2,1)}, bf16[128,1024]{1,0:T(8,128)(2,1)S(1)}, u32[]{:S(2)}, u32[]{:S(2)}) collective-permute-start(bf16[128,1024]{1,0:T(8,128)(2,1)} %get-tuple-element.29), channel_id=1, source_target_pairs={{0,1},{1,2},{2,3},{3,128},{4,5},{5,6},{6,7},{7,132},{8,9},{9,10},{... | collective-permute-start | bytes 786440 | tf_op jit(solution)/shard_map/ppermute | solution.py:38
  32.4 9.4 %collective-permute-start.8 = (bf16[128,1024]{1,0:T(8,128)(2,1)}, bf16[128,1024]{1,0:T(8,128)(2,1)S(1)}, u32[]{:S(2)}, u32[]{:S(2)}) collective-permute-start(bf16[128,1024]{1,0:T(8,128)(2,1)} %get-tuple-element.30), channel_id=1, source_target_pairs={{0,2},{1,131},{2,128},{3,1},{4,6},{5,135},{6,132},{7,5},{8,10},{9,... | collective-permute-start | bytes 786440 | tf_op jit(solution)/shard_map/ppermute | solution.py:38
  35.1 6.8 %collective-permute-start.9 = (bf16[128,1024]{1,0:T(8,128)(2,1)S(1)}, bf16[128,1024]{1,0:T(8,128)(2,1)S(1)}, u32[]{:S(2)}, u32[]{:S(2)}) collective-permute-start(bf16[128,1024]{1,0:T(8,128)(2,1)S(1)} %get-tuple-element.31), channel_id=1, source_target_pairs={{0,131},{1,0},{2,1},{3,2},{4,135},{5,4},{6,5},{7,6},{8,139},{9,8},... | collective-permute-start | bytes 786440 | tf_op jit(solution)/shard_map/ppermute | solution.py:38
  43.6 6.3 %collective-permute-start.10 = (bf16[640,256]{1,0:T(8,128)(2,1)S(1)}, bf16[640,256]{1,0:T(8,128)(2,1)S(1)}, u32[]{:S(2)}, u32[]{:S(2)}) collective-permute-start(bf16[640,256]{1,0:T(8,128)(2,1)S(1)} %get-tuple-element.33), channel_id=1, source_target_pairs={{0,32},{1,33},{2,34},{3,35},{4,36},{5,37},{6,38},{7,39},{8,40},{9,... | collective-permute-start | bytes 983048 | tf_op jit(solution)/shard_map/ppermute | solution.py:38
  44.4 14.6 %collective-permute-start.11 = (bf16[640,256]{1,0:T(8,128)(2,1)S(1)}, bf16[640,256]{1,0:T(8,128)(2,1)S(1)}, u32[]{:S(2)}, u32[]{:S(2)}) collective-permute-start(bf16[640,256]{1,0:T(8,128)(2,1)S(1)} %get-tuple-element.34), channel_id=1, source_target_pairs={{0,64},{1,65},{2,66},{3,67},{4,68},{5,69},{6,70},{7,71},{8,72},{9,... | collective-permute-start | bytes 983048 | tf_op jit(solution)/shard_map/ppermute | solution.py:38
  46.1 15.0 %collective-permute-start.12 = (bf16[640,256]{1,0:T(8,128)(2,1)S(1)}, bf16[640,256]{1,0:T(8,128)(2,1)S(1)}, u32[]{:S(2)}, u32[]{:S(2)}) collective-permute-start(bf16[640,256]{1,0:T(8,128)(2,1)S(1)} %get-tuple-element.35), channel_id=1, source_target_pairs={{0,96},{1,97},{2,98},{3,99},{4,100},{5,101},{6,102},{7,103},{8,104... | collective-permute-start | bytes 983048 | tf_op jit(solution)/shard_map/ppermute | solution.py:38
  61.4 0.8 collective-permute-start.14
  62.0 6.3 %collective-permute-start.13 = (bf16[640,256]{1,0:T(8,128)(2,1)S(1)}, bf16[640,256]{1,0:T(8,128)(2,1)S(1)}, u32[]{:S(2)}, u32[]{:S(2)}) collective-permute-start(bf16[640,256]{1,0:T(8,128)(2,1)S(1)} %add_convert_fusion.1), channel_id=1, source_target_pairs={{0,2},{1,3},{2,128},{3,129},{4,6},{5,7},{6,132},{7,133},{8,10},{9,... | collective-permute-start | bytes 983048 | tf_op jit(solution)/shard_map/ppermute | solution.py:38
  68.5 9.6 %collective-permute-start.17 = (bf16[640,256]{1,0:T(8,128)(2,1)S(1)}, bf16[640,256]{1,0:T(8,128)(2,1)S(1)}, u32[]{:S(2)}, u32[]{:S(2)}) collective-permute-start(bf16[640,256]{1,0:T(8,128)(2,1)S(1)} %add_convert_fusion.p0), channel_id=1, source_target_pairs={{0,96},{1,97},{2,98},{3,99},{4,100},{5,101},{6,102},{7,103},{8,104... | collective-permute-start | bytes 983048 | tf_op jit(solution)/shard_map/ppermute | solution.py:38
  70.5 9.0 %collective-permute-start.16 = (bf16[640,256]{1,0:T(8,128)(2,1)S(1)}, bf16[640,256]{1,0:T(8,128)(2,1)S(1)}, u32[]{:S(2)}, u32[]{:S(2)}) collective-permute-start(bf16[640,256]{1,0:T(8,128)(2,1)S(1)} %add_convert_fusion.p0), channel_id=1, source_target_pairs={{0,64},{1,65},{2,66},{3,67},{4,68},{5,69},{6,70},{7,71},{8,72},{9,... | collective-permute-start | bytes 983048 | tf_op jit(solution)/shard_map/ppermute | solution.py:38
  71.2 10.3 %collective-permute-start.15 = (bf16[640,256]{1,0:T(8,128)(2,1)S(1)}, bf16[640,256]{1,0:T(8,128)(2,1)S(1)}, u32[]{:S(2)}, u32[]{:S(2)}) collective-permute-start(bf16[640,256]{1,0:T(8,128)(2,1)S(1)} %add_convert_fusion.p0), channel_id=1, source_target_pairs={{0,32},{1,33},{2,34},{3,35},{4,36},{5,37},{6,38},{7,39},{8,40},{9,... | collective-permute-start | bytes 983048 | tf_op jit(solution)/shard_map/ppermute | solution.py:38
  72.5 29.9 %collective-permute-start.20 = (bf16[256,1024]{1,0:T(8,128)(2,1)S(1)}, bf16[256,1024]{1,0:T(8,128)(2,1)S(1)}, u32[]{:S(2)}, u32[]{:S(2)}) collective-permute-start(bf16[256,1024]{1,0:T(8,128)(2,1)S(1)} %copy-done.1), channel_id=1, source_target_pairs={{16,48},{17,49},{18,50},{19,51},{20,52},{21,53},{22,54},{23,55},{2... | collective-permute-start | bytes 1572872 | tf_op jit(solution)/shard_map/ppermute | solution.py:38
  74.4 28.0 %collective-permute-start.19 = (bf16[256,1024]{1,0:T(8,128)(2,1)S(1)}, bf16[256,1024]{1,0:T(8,128)(2,1)S(1)}, u32[]{:S(2)}, u32[]{:S(2)}) collective-permute-start(bf16[256,1024]{1,0:T(8,128)(2,1)S(1)} %copy-done.1), channel_id=1, source_target_pairs={{0,48},{1,49},{2,50},{3,51},{4,52},{5,53},{6,54},{7,55},{8,56},{9,... | collective-permute-start | bytes 1572872 | tf_op jit(solution)/shard_map/ppermute | solution.py:38
  78.1 24.3 %collective-permute-start.18 = (bf16[256,1024]{1,0:T(8,128)(2,1)S(1)}, bf16[256,1024]{1,0:T(8,128)(2,1)S(1)}, u32[]{:S(2)}, u32[]{:S(2)}) collective-permute-start(bf16[256,1024]{1,0:T(8,128)(2,1)S(1)} %copy-done.1), channel_id=1, source_target_pairs={{0,16},{1,17},{2,18},{3,19},{4,20},{5,21},{6,22},{7,23},{8,24},{9,... | collective-permute-start | bytes 1572872 | tf_op jit(solution)/shard_map/ppermute | solution.py:38
  102.3 15.2 %collective-permute-start.22 = (bf16[1024,1024]{1,0:T(8,128)(2,1)S(1)}, bf16[1024,1024]{1,0:T(8,128)(2,1)S(1)}, u32[]{:S(2)}, u32[]{:S(2)}) collective-permute-start(bf16[1024,1024]{1,0:T(8,128)(2,1)S(1)} %shard_map.58.s_ref.s_own), channel_id=1, source_target_pairs={{0,16},{1,17},{2,18},{3,19},{4,20},{5,21},{6,22},{7,23},{8,24},{9,... | collective-permute-start | bytes 6291464 | tf_op jit(solution)/shard_map/ppermute | solution.py:38
  105.4 12.1 %collective-permute-start.21 = (bf16[256,1024]{1,0:T(8,128)(2,1)S(1)}, bf16[256,1024]{1,0:T(8,128)(2,1)S(1)}, u32[]{:S(2)}, u32[]{:S(2)}) collective-permute-start(bf16[256,1024]{1,0:T(8,128)(2,1)S(1)} %get-tuple-element.41), channel_id=1, source_target_pairs={{16,0},{17,1},{18,2},{19,3},{20,4},{21,5},{22,6},{23,7},{24,8},{25... | collective-permute-start | bytes 1572872 | tf_op jit(solution)/shard_map/ppermute | solution.py:38

commit v4 on v3

--- a/solution.py
+++ b/solution.py
@@ -127,50 +127,54 @@
     tile = size // 4
     sub = tile // 4
     base, damp = place_ref[0], damp_ref[0]
+    blocks = [slice(i * tile, (i + 1) * tile) for i in range(4)]
+
+    def mirrored(ref, c, value):
+        ref[:(c + 1) * tile, blocks[c]] = value
+        for r in range(c):
+            ref[blocks[c], blocks[r]] = value[blocks[r], :].T
+
     for k, piece in enumerate((p0, p1, p2, p3)):
         start = pl.multiple_of(lax.rem(base + 4 - k, 4) * sub, sub)
         for t, (r, c) in enumerate(UPPER):
-            a_ref[pl.ds(r * tile + start, sub), c * tile:(c + 1) * tile] = piece[t * sub:(t + 1) * sub, :]
+            a_ref[pl.ds(r * tile + start, sub), blocks[c]] = piece[t * sub:(t + 1) * sub, :]
     row = lax.broadcasted_iota(jnp.int32, (tile, tile), 0)
     col = lax.broadcasted_iota(jnp.int32, (tile, tile), 1)
     eye = row == col
     total = jnp.zeros((1, 1), F32)
     for r, c in UPPER:
-        rows, cols = slice(r * tile, (r + 1) * tile), slice(c * tile, (c + 1) * tile)
-        value = a_ref[rows, cols].astype(F32)
+        value = a_ref[blocks[r], blocks[c]].astype(F32)
         if r == c:
             value = value + jnp.where(eye, damp, 0.0)
-            a_ref[rows, cols] = value.astype(BF16)
+            a_ref[blocks[r], blocks[c]] = value.astype(BF16)
             total += jnp.sum(value * value, keepdims=True)
         else:
             total += 2.0 * jnp.sum(value * value, keepdims=True)
-            a_ref[cols, rows] = value.T.astype(BF16)
+            a_ref[blocks[c], blocks[r]] = a_ref[blocks[r], blocks[c]].T
     frob = jnp.sqrt(total)
     inv = 1.0 / frob
     inv_bf = inv.astype(BF16).astype(F32)
     for r in range(4):
-        rows = slice(r * tile, (r + 1) * tile)
         for c in range(4):
-            cols = slice(c * tile, (c + 1) * tile)
-            product = (a_ref[rows, cols].astype(F32) * inv_bf).astype(BF16).astype(F32)
+            product = (a_ref[blocks[r], blocks[c]].astype(F32) * inv_bf).astype(BF16).astype(F32)
             value = -product * inv_bf
             if r == c:
                 value = value + jnp.where(eye, 2.0 * inv, 0.0)
-            x_ref[rows, cols] = value
-            xb_ref[0, rows, cols] = value.astype(BF16)
+            if r <= c:
+                x_ref[blocks[r], blocks[c]] = value
+            xb_ref[0, blocks[r], blocks[c]] = value.astype(BF16)
     for step in range(1, ITERS):
-        now, later = (step - 1) % 2, step % 2
-        for r in range(4):
-            rows = slice(r * tile, (r + 1) * tile)
-            p_ref[rows, :] = dot(a_ref[rows, :], xb_ref[now]).astype(BF16)
-        for r in range(4):
-            rows = slice(r * tile, (r + 1) * tile)
-            value = 2.0 * x_ref[rows, :] - dot(p_ref[rows, :], xb_ref[now])
+        now, later = xb_ref.at[(step - 1) % 2], xb_ref.at[step % 2]
+        for c in (3, 2, 1, 0):
+            mirrored(p_ref, c, dot(a_ref[:(c + 1) * tile, :], now[:, blocks[c]]).astype(BF16))
+        for c in range(4):
+            rows = slice(0, (c + 1) * tile)
+            value = 2.0 * x_ref[rows, blocks[c]] - dot(p_ref[rows, :], now[:, blocks[c]])
             if step < ITERS - 1:
-                x_ref[rows, :] = value
-                xb_ref[later, rows, :] = value.astype(BF16)
+                x_ref[rows, blocks[c]] = value
+                mirrored(later, c, value.astype(BF16))
             else:
-                out_ref[rows, :] = (value * (frob / 2.0 ** ITERS)).astype(BF16)
+                mirrored(out_ref, c, (value * (frob / 2.0 ** ITERS)).astype(BF16))
 
 
 def rounds(place, damp, pieces):
@@ -192,49 +196,55 @@
     )(place, damp, *pieces)
 
 
-def mix_kernel(place_ref, s_ref, w0, w1, w2, w3, t0_ref, t1_ref):
-    tile, size = t0_ref.shape
+def mix_kernel(place_ref, s_ref, w0, w1, w2, w3, out_ref, t_ref):
+    tile, size = w0.shape
     half = place_ref[2]
 
     @pl.when(place_ref[1] == 1)
     def _():
-        for i, target in enumerate((t0_ref, t1_ref)):
+        for i in range(2):
             rows = pl.ds(pl.multiple_of((2 * half + i) * tile, tile), tile)
             value = jnp.zeros((tile, size), F32)
             for b, w in enumerate((w0, w1, w2, w3)):
                 cols = pl.ds(pl.multiple_of(lax.rem(2 * half + b, 4) * tile, tile), tile)
                 value += dot(s_ref[rows, cols], w[...])
-            target[...] = value.astype(BF16)
+            t_ref[i * tile:(i + 1) * tile, :] = value.astype(BF16)
+        out_ref[:2 * tile, :] = t_ref[...]
 
 
 def mix(place, inverse, weights):
+    tile, size = weights[0].shape
     return pl.pallas_call(
         mix_kernel,
-        out_shape=(jax.ShapeDtypeStruct(weights[0].shape, BF16),) * 2,
+        out_shape=jax.ShapeDtypeStruct(inverse.shape, BF16),
         in_specs=[SMEM] + [VMEM] * 5,
-        out_specs=(VMEM,) * 2,
+        out_specs=VMEM,
+        scratch_shapes=[pltpu.VMEM((2 * tile, size), BF16)],
+        input_output_aliases={1: 0},
         compiler_params=pltpu.CompilerParams(vmem_limit_bytes=16 * MIB),
     )(place, inverse, *weights)
 
 
-def last_kernel(place_ref, t0_ref, s_own, t1_ref, s_other, out_ref):
+def last_kernel(place_ref, mine_ref, other_ref, out_ref):
+    tile = out_ref.shape[0]
+
     @pl.when(place_ref[1] == 0)
     def _():
-        out_ref[...] = dot(t0_ref[...], s_own[...]).astype(BF16)
+        out_ref[...] = dot(other_ref[:tile, :], mine_ref[...]).astype(BF16)
 
     @pl.when(place_ref[1] == 1)
     def _():
-        out_ref[...] = dot(t1_ref[...], s_other[...]).astype(BF16)
-
-
-def last(place, t0, s_own, t1, s_other):
+        out_ref[...] = dot(mine_ref[tile:2 * tile, :], other_ref[...]).astype(BF16)
+
+
+def last(place, mine, other, rows):
     return pl.pallas_call(
         last_kernel,
-        out_shape=jax.ShapeDtypeStruct(t0.shape, BF16),
-        in_specs=[SMEM] + [VMEM] * 4,
+        out_shape=jax.ShapeDtypeStruct((rows, mine.shape[1]), BF16),
+        in_specs=[SMEM] + [VMEM] * 2,
         out_specs=VMEM,
         compiler_params=pltpu.CompilerParams(vmem_limit_bytes=16 * MIB),
-    )(place, t0, s_own, t1, s_other)
+    )(place, mine, other)
 
 
 def pick(parts, index):
@@ -252,12 +262,13 @@
     hot = (sample_ids[:, None] == jnp.arange(activations.shape[0], dtype=jnp.int32)[None]).astype(BF16)
     samp_x = dot(hot, activations).astype(BF16)
     other_x = moved(samp_x, lambda zh, y, c, x, zl: (zh, y, 1, x, zl) if c == 0 else None)
+    out_grads, _ = lax.optimization_barrier((out_grads, samp_x))
     samp_g = dot(hot, out_grads).astype(BF16)
     other_g = moved(samp_g, lambda zh, y, c, x, zl: (zh, y, 0, x, zl) if c == 1 else None)
 
     packed = pack(x.reshape(1), samp_g, other_g, size)
     held = [packed[0]]
-    for k in (2, 1, 3):
+    for k in (1, 2, 3):
         held.append(moved(packed[k], lambda zh, y, c, x, zl: (zh, y, 0, (x + k) % 4, zl) if c == 0 else None))
 
     both_x = jnp.concatenate([samp_x, other_x])
@@ -274,7 +285,7 @@
     come = moved(columns(halves, 1 - y // 2, 1), lambda zh, y, c, x, zl: (zh, 3 - y, 1, x, zl) if c == 1 else None)
 
     samples = list(deal(jnp.stack([(zl + 2) % 4, core]), held, kept, come))
-    for k in (2, 1, 3):
+    for k in (1, 2, 3):
         samples[k] = moved(
             samples[k],
             lambda zh, y, c, x, zl: (z_shift(zh, zl, k)[0], y, 0, x, z_shift(zh, zl, k)[1]) if c == 0
@@ -318,10 +329,9 @@
     inverse, *weights = lax.optimization_barrier((rounds(place, damp, pieces), *weights))
     weights.insert(1, weight_grad)
 
-    inv_g = moved(inverse, lambda zh, y, c, x, zl: (zh, y, 1, x, zl) if c == 0 else None)
-    mixed_0, mixed_1 = mix(place, inverse, weights)
-    mixed_0 = moved(mixed_0, lambda zh, y, c, x, zl: (zh, y, 0, x, zl) if c == 1 else None)
-    return last(place, mixed_0, inverse, mixed_1, inv_g)
+    mine = mix(place, inverse, weights)
+    other = moved(mine, lambda zh, y, c, x, zl: (zh, y, 1 - c, x, zl))
+    return last(place, mine, other, weight_grad.shape[0])
 
 
 def solution(mesh):

time: 121 us -> 115 us (0.950)
  Pallas kernels: 28.6 us -> 22.5 us
  starting transfers between devices: 45.7 us -> 43 us
  waiting for transfers between devices: 38.4 us -> 40.4 us
  local copies, waits for them, and re-layouts: 0.59 us -> 1.84 us
    pallas_call x1, Pallas kernels: 20.8 us -> 14.7 us  [rounds(): pl.pallas_call(rounds_kernel, out_shape=jax.ShapeDtypeStruct((size, size)...]
    ppermute x23 -> x22, starting transfers between devices: 45.7 us -> 43 us  [moved(): return lax.ppermute(value, ('dp', 'owner'), pairs)]
    ppermute x23 -> x22, waiting for transfers between devices: 38.4 us -> 40.4 us  [moved(): return lax.ppermute(value, ('dp', 'owner'), pairs)]
    unnamed x8 -> x6, local copies, waits for them, and re-layouts: 0.02 us -> 1.23 us
  transfers between devices with their start and end apart: 23 -> 22, of which waited for: 12 -> 12; matrix products, arithmetic and copies ran while one was open for 3% -> 3% of each run, Pallas kernels for 20% -> 13%
where the time goes in v4:
time: 115 us
  starting transfers between devices  43 us (37%)
  waiting for transfers between devices  40.4 us (35%)
  Pallas kernels  22.5 us (20%)
  matrix products  3.86 us (3%)
  other arithmetic  2.74 us (2%)
  local copies, waits for them, and re-layouts  1.84 us (2%)
    ppermute x22, starting transfers between devices, moved(): return lax.ppermute(value, ('dp', 'owner'), pairs)  43 us
    ppermute x22, waiting for transfers between devices, moved(): return lax.ppermute(value, ('dp', 'owner'), pairs)  40.4 us
    pallas_call x1, Pallas kernels, rounds(): pl.pallas_call(rounds_kernel, out_shape=jax.ShapeDtypeStruct((size, size)...  14.7 us
    dot_general x2, matrix products, dot(): return jnp.dot(a, b, preferred_element_type=F32)  3.86 us
  transfers between devices with their start and end apart: 22, of which 12 were waited for; matrix products, arithmetic and copies ran while one was open for 3% of the time, Pallas kernels for 13%

profile of v4, /device:TPU:33, one launch (start us, length us, event | category | flops | bytes accessed | tf_op | source)
XLA Modules:
  0.0 114.7 jit_solution(1878417569470743756)
XLA Ops:
  0.0 1.2 %copy-done = bf16[128,4096]{1,0:T(8,128)(2,1)S(1)} copy-done((bf16[128,4096]{1,0:T(8,128)(2,1)S(1)}, bf16[128,4096]{1,0:T(8,128)(2,1)}, u32[]{:S(2)}) %copy-start) | copy-done | bytes 1048600
  2.2 2.9 %convolution_convert_fusion.mine_ref = bf16[16,16384]{1,0:T(8,128)(2,1)S(1)} fusion(bf16[128,16384]{1,0:T(8,128)(2,1)} %param.6, s32[16]{0:T(128)} %param.7), kind=kOutput, calls=%fused_computation | convolution fusion | flops 67373056 | bytes 4718656 | tf_op jit(solution)/shard_map/dot_general | solution.py:19
  5.1 2.7 %collective-permute-start = (bf16[16,16384]{1,0:T(8,128)(2,1)S(1)}, bf16[16,16384]{1,0:T(8,128)(2,1)S(1)}, u32[]{:S(2)}, u32[]{:S(2)}) collective-permute-start(bf16[16,16384]{1,0:T(8,128)(2,1)S(1)} %convolution_convert_fusion.mine_ref), channel_id=1, source_target_pairs={{16,0},{17,1},{18,2},{19,3},{20,4},{21,5},{22,6},{23,7},{24,8},{25... | collective-permute-start | bytes 1572872 | tf_op jit(solution)/shard_map/ppermute | solution.py:38
  7.9 1.3 %collective-permute-start.4 = (bf16[16,4096]{1,0:T(8,128)(2,1)S(1)}, bf16[16,4096]{1,0:T(8,128)(2,1)S(1)}, u32[]{:S(2)}, u32[]{:S(2)}) collective-permute-start(bf16[16,4096]{1,0:T(8,128)(2,1)S(1)} %convolution_convert_fusion.1), channel_id=1, source_target_pairs={{0,16},{1,17},{2,18},{3,19},{4,20},{5,21},{6,22},{7,23},{8,24},{9,... | collective-permute-start | bytes 393224 | tf_op jit(solution)/shard_map/ppermute | solution.py:38
  9.2 1.9 %collective-permute-done.4 = bf16[16,4096]{1,0:T(8,128)(2,1)S(1)} collective-permute-done((bf16[16,4096]{1,0:T(8,128)(2,1)S(1)}, bf16[16,4096]{1,0:T(8,128)(2,1)S(1)}, u32[]{:S(2)}, u32[]{:S(2)}) %collective-permute-start.4) | collective-permute-done | bytes 131104 | tf_op jit(solution)/shard_map/ppermute | solution.py:38
  11.8 7.0 %collective-permute-start.5 = (bf16[32,2048]{1,0:T(8,128)(2,1)}, bf16[32,2048]{1,0:T(8,128)(2,1)}, u32[]{:S(2)}, u32[]{:S(2)}) collective-permute-start(bf16[32,2048]{1,0:T(8,128)(2,1)} %get-tuple-element.43), channel_id=1, source_target_pairs={{16,146},{17,147},{18,144},{19,145},{20,150},{21,151},{22,148},{23... | collective-permute-start | bytes 393224 | tf_op jit(solution)/shard_map/ppermute | solution.py:38
  21.7 1.2 %collective-permute-done.5 = bf16[32,2048]{1,0:T(8,128)(2,1)} collective-permute-done((bf16[32,2048]{1,0:T(8,128)(2,1)}, bf16[32,2048]{1,0:T(8,128)(2,1)}, u32[]{:S(2)}, u32[]{:S(2)}) %collective-permute-start.5) | collective-permute-done | bytes 131104 | tf_op jit(solution)/shard_map/ppermute | solution.py:38
  22.9 1.5 %fusion = (bf16[64,1024]{1,0:T(8,128)(2,1)}, bf16[64,1024]{1,0:T(8,128)(2,1)S(1)}) fusion(s32[]{:T(128)S(6)} %select_n.84, bf16[32,2048]{1,0:T(8,128)(2,1)S(1)} %get-tuple-element.44, bf16[32,2048]{1,0:T(8,128)(2,1)} %collective-permute-done.5, s32[]{:T(128)S(6)} %select_n.83), kind=kLoop, calls=%fused_computation.12 | loop fusion | flops 524288 | bytes 524296 | tf_op jit(solution)/shard_map/concatenate | solution.py:283
  24.4 4.6 %collective-permute-start.6 = (bf16[64,1024]{1,0:T(8,128)(2,1)}, bf16[64,1024]{1,0:T(8,128)(2,1)S(1)}, u32[]{:S(2)}, u32[]{:S(2)}) collective-permute-start(bf16[64,1024]{1,0:T(8,128)(2,1)} %get-tuple-element.41), channel_id=1, source_target_pairs={{16,112},{17,113},{18,114},{19,115},{20,116},{21,117},{22,118},{23... | collective-permute-start | bytes 393224 | tf_op jit(solution)/shard_map/ppermute | solution.py:38
  29.1 2.4 %collective-permute-done.6.come_ref = bf16[64,1024]{1,0:T(8,128)(2,1)S(1)} collective-permute-done((bf16[64,1024]{1,0:T(8,128)(2,1)}, bf16[64,1024]{1,0:T(8,128)(2,1)S(1)}, u32[]{:S(2)}, u32[]{:S(2)}) %collective-permute-start.6) | collective-permute-done | bytes 131104 | tf_op jit(solution)/shard_map/ppermute | solution.py:38
  31.6 1.4 %shard_map.56 = (bf16[128,1024]{1,0:T(8,128)(2,1)S(1)}, bf16[128,1024]{1,0:T(8,128)(2,1)}, bf16[128,1024]{1,0:T(8,128)(2,1)}, bf16[128,1024]{1,0:T(8,128)(2,1)S(1)}) custom-call(s32[2]{0:T(128)S(1)} %pad_add_fusion.2.place_ref, bf16[128,1024]{1,0:T(8,128)(2,1)S(1)} %get-tuple-element.24.h0, bf16[128,1024]{1,0:T(8,128)(2,1)S(1)} %collective-permute-done.1.h1, ...), custom_call_target="tpu_custom_call" | custom-call | tf_op jit(solution)/shard_map/pallas_call | solution.py:86
  33.0 1.2 %collective-permute-start.7 = (bf16[128,1024]{1,0:T(8,128)(2,1)}, bf16[128,1024]{1,0:T(8,128)(2,1)S(1)}, u32[]{:S(2)}, u32[]{:S(2)}) collective-permute-start(bf16[128,1024]{1,0:T(8,128)(2,1)} %get-tuple-element.29), channel_id=1, source_target_pairs={{0,1},{1,2},{2,3},{3,128},{4,5},{5,6},{6,7},{7,132},{8,9},{9,10},{... | collective-permute-start | bytes 786440 | tf_op jit(solution)/shard_map/ppermute | solution.py:38
  34.2 2.6 %collective-permute-start.8 = (bf16[128,1024]{1,0:T(8,128)(2,1)}, bf16[128,1024]{1,0:T(8,128)(2,1)S(1)}, u32[]{:S(2)}, u32[]{:S(2)}) collective-permute-start(bf16[128,1024]{1,0:T(8,128)(2,1)} %get-tuple-element.30), channel_id=1, source_target_pairs={{0,2},{1,131},{2,128},{3,1},{4,6},{5,135},{6,132},{7,5},{8,10},{9,... | collective-permute-start | bytes 786440 | tf_op jit(solution)/shard_map/ppermute | solution.py:38
  37.9 1.9 %collective-permute-done.7.refs_2_ = bf16[128,1024]{1,0:T(8,128)(2,1)S(1)} collective-permute-done((bf16[128,1024]{1,0:T(8,128)(2,1)}, bf16[128,1024]{1,0:T(8,128)(2,1)S(1)}, u32[]{:S(2)}, u32[]{:S(2)}) %collective-permute-start.7) | collective-permute-done | bytes 262176 | tf_op jit(solution)/shard_map/ppermute | solution.py:38
  39.8 3.8 %collective-permute-done.8.refs_3_ = bf16[128,1024]{1,0:T(8,128)(2,1)S(1)} collective-permute-done((bf16[128,1024]{1,0:T(8,128)(2,1)}, bf16[128,1024]{1,0:T(8,128)(2,1)S(1)}, u32[]{:S(2)}, u32[]{:S(2)}) %collective-permute-start.8) | collective-permute-done | bytes 262176 | tf_op jit(solution)/shard_map/ppermute | solution.py:38
  43.6 1.7 %shard_map.57 = (bf16[640,256]{1,0:T(8,128)(2,1)S(1)}, bf16[640,256]{1,0:T(8,128)(2,1)S(1)}, bf16[640,256]{1,0:T(8,128)(2,1)S(1)}, bf16[640,256]{1,0:T(8,128)(2,1)S(1)}) custom-call(s32[2]{0:T(128)S(1)} %pad_add_fusion.1.refs_0_, bf16[128,1024]{1,0:T(8,128)(2,1)S(1)} %get-tuple-element.28.refs_1_, bf16[128,1024]{1,0:T(8,128)(2,1)S(1)} %collective-permute-done.7.refs_2_, ...), custom_call_target="tpu_custom_call" | custom-call | tf_op jit(solution)/shard_map/pallas_call | solution.py:115
  45.9 2.0 %collective-permute-start.11 = (bf16[640,256]{1,0:T(8,128)(2,1)S(1)}, bf16[640,256]{1,0:T(8,128)(2,1)S(1)}, u32[]{:S(2)}, u32[]{:S(2)}) collective-permute-start(bf16[640,256]{1,0:T(8,128)(2,1)S(1)} %get-tuple-element.34), channel_id=1, source_target_pairs={{0,64},{1,65},{2,66},{3,67},{4,68},{5,69},{6,70},{7,71},{8,72},{9,... | collective-permute-start | bytes 983048 | tf_op jit(solution)/shard_map/ppermute | solution.py:38
  48.0 3.6 %collective-permute-done.10 = bf16[640,256]{1,0:T(8,128)(2,1)S(1)} collective-permute-done((bf16[640,256]{1,0:T(8,128)(2,1)S(1)}, bf16[640,256]{1,0:T(8,128)(2,1)S(1)}, u32[]{:S(2)}, u32[]{:S(2)}) %collective-permute-start.10) | collective-permute-done | bytes 327712 | tf_op jit(solution)/shard_map/ppermute | solution.py:38
  51.6 8.9 %collective-permute-done.11 = bf16[640,256]{1,0:T(8,128)(2,1)S(1)} collective-permute-done((bf16[640,256]{1,0:T(8,128)(2,1)S(1)}, bf16[640,256]{1,0:T(8,128)(2,1)S(1)}, u32[]{:S(2)}, u32[]{:S(2)}) %collective-permute-start.11) | collective-permute-done | bytes 327712 | tf_op jit(solution)/shard_map/ppermute | solution.py:38
  60.5 2.5 %collective-permute-done.12 = bf16[640,256]{1,0:T(8,128)(2,1)S(1)} collective-permute-done((bf16[640,256]{1,0:T(8,128)(2,1)S(1)}, bf16[640,256]{1,0:T(8,128)(2,1)S(1)}, u32[]{:S(2)}, u32[]{:S(2)}) %collective-permute-start.12) | collective-permute-done | bytes 327712 | tf_op jit(solution)/shard_map/ppermute | solution.py:38
  63.9 6.2 %collective-permute-done.13 = bf16[640,256]{1,0:T(8,128)(2,1)S(1)} collective-permute-done((bf16[640,256]{1,0:T(8,128)(2,1)S(1)}, bf16[640,256]{1,0:T(8,128)(2,1)S(1)}, u32[]{:S(2)}, u32[]{:S(2)}) %collective-permute-start.13) | collective-permute-done | bytes 327712 | tf_op jit(solution)/shard_map/ppermute | solution.py:38
  70.3 2.0 %collective-permute-start.17 = (bf16[640,256]{1,0:T(8,128)(2,1)S(1)}, bf16[640,256]{1,0:T(8,128)(2,1)S(1)}, u32[]{:S(2)}, u32[]{:S(2)}) collective-permute-start(bf16[640,256]{1,0:T(8,128)(2,1)S(1)} %add_convert_fusion.p0), channel_id=1, source_target_pairs={{0,96},{1,97},{2,98},{3,99},{4,100},{5,101},{6,102},{7,103},{8,104... | collective-permute-start | bytes 983048 | tf_op jit(solution)/shard_map/ppermute | solution.py:38
  74.3 1.9 %collective-permute-start.20 = (bf16[256,1024]{1,0:T(8,128)(2,1)S(1)}, bf16[256,1024]{1,0:T(8,128)(2,1)S(1)}, u32[]{:S(2)}, u32[]{:S(2)}) collective-permute-start(bf16[256,1024]{1,0:T(8,128)(2,1)S(1)} %copy-done.1), channel_id=1, source_target_pairs={{16,48},{17,49},{18,50},{19,51},{20,52},{21,53},{22,54},{23,55},{2... | collective-permute-start | bytes 1572872 | tf_op jit(solution)/shard_map/ppermute | solution.py:38
  76.2 1.3 %collective-permute-start.19 = (bf16[256,1024]{1,0:T(8,128)(2,1)S(1)}, bf16[256,1024]{1,0:T(8,128)(2,1)S(1)}, u32[]{:S(2)}, u32[]{:S(2)}) collective-permute-start(bf16[256,1024]{1,0:T(8,128)(2,1)S(1)} %copy-done.1), channel_id=1, source_target_pairs={{0,48},{1,49},{2,50},{3,51},{4,52},{5,53},{6,54},{7,55},{8,56},{9,... | collective-permute-start | bytes 1572872 | tf_op jit(solution)/shard_map/ppermute | solution.py:38
  77.5 2.3 %collective-permute-done.17.p3 = bf16[640,256]{1,0:T(8,128)(2,1)S(1)} collective-permute-done((bf16[640,256]{1,0:T(8,128)(2,1)S(1)}, bf16[640,256]{1,0:T(8,128)(2,1)S(1)}, u32[]{:S(2)}, u32[]{:S(2)}) %collective-permute-start.17) | collective-permute-done | bytes 327712 | tf_op jit(solution)/shard_map/ppermute | solution.py:38
  79.8 1.5 %collective-permute-start.18 = (bf16[256,1024]{1,0:T(8,128)(2,1)S(1)}, bf16[256,1024]{1,0:T(8,128)(2,1)S(1)}, u32[]{:S(2)}, u32[]{:S(2)}) collective-permute-start(bf16[256,1024]{1,0:T(8,128)(2,1)S(1)} %copy-done.1), channel_id=1, source_target_pairs={{0,16},{1,17},{2,18},{3,19},{4,20},{5,21},{6,22},{7,23},{8,24},{9,... | collective-permute-start | bytes 1572872 | tf_op jit(solution)/shard_map/ppermute | solution.py:38
  81.3 1.9 %collective-permute-done.15.p1 = bf16[640,256]{1,0:T(8,128)(2,1)S(1)} collective-permute-done((bf16[640,256]{1,0:T(8,128)(2,1)S(1)}, bf16[640,256]{1,0:T(8,128)(2,1)S(1)}, u32[]{:S(2)}, u32[]{:S(2)}) %collective-permute-start.15) | collective-permute-done | bytes 327712 | tf_op jit(solution)/shard_map/ppermute | solution.py:38
  83.2 14.7 %shard_map.58.s_ref = bf16[1024,1024]{1,0:T(8,128)(2,1)S(1)} custom-call(s32[3]{0:T(128)S(1)} %pad_add_fusion.place_ref, f32[1]{0:T(128)} %dynamic_slice.16.damp_ref, bf16[640,256]{1,0:T(8,128)(2,1)S(1)} %add_convert_fusion.p0, bf16[640,256]{1,0:T(8,128)(2,1)S(1)} %collective-permute-done.15.p1, bf16[640,256]{1,0:T(8,128)(2,1)S(1)} %collective-permute-done.16.p2, ...), custom_call_target="tpu_custom_call" | custom-call | flops 17179869184 | bytes 4194304 | tf_op jit(solution)/shard_map/pallas_call | solution.py:183
  97.9 1.8 %shard_map.59.mine_ref = bf16[1024,1024]{1,0:T(8,128)(2,1)S(1)} custom-call(s32[3]{0:T(128)S(1)} %pad_add_fusion.place_ref, bf16[1024,1024]{1,0:T(8,128)(2,1)S(1)} %shard_map.58.s_ref, bf16[256,1024]{1,0:T(8,128)(2,1)S(1)} %collective-permute-done.18.w0, bf16[256,1024]{1,0:T(8,128)(2,1)S(1)} %copy-done.1, ...), custom_call_target="tpu_custom_call", output_to_operand_aliasing={{}: (1, {})} | custom-call | tf_op jit(solution)/shard_map/pallas_call | solution.py:217
  99.8 9.0 %collective-permute-start.21 = (bf16[1024,1024]{1,0:T(8,128)(2,1)S(1)}, bf16[1024,1024]{1,0:T(8,128)(2,1)S(1)}, u32[]{:S(2)}, u32[]{:S(2)}) collective-permute-start(bf16[1024,1024]{1,0:T(8,128)(2,1)S(1)} %shard_map.59.mine_ref), channel_id=1, source_target_pairs={{0,16},{1,17},{2,18},{3,19},{4,20},{5,21},{6,22},{7,23},{8,24},{9,... | collective-permute-start | bytes 6291464 | tf_op jit(solution)/shard_map/ppermute | solution.py:38
  108.8 3.8 %collective-permute-done.21.other_ref = bf16[1024,1024]{1,0:T(8,128)(2,1)S(1)} collective-permute-done((bf16[1024,1024]{1,0:T(8,128)(2,1)S(1)}, bf16[1024,1024]{1,0:T(8,128)(2,1)S(1)}, u32[]{:S(2)}, u32[]{:S(2)}) %collective-permute-start.21) | collective-permute-done | bytes 2097184 | tf_op jit(solution)/shard_map/ppermute | solution.py:38
  112.6 2.1 %shard_map.60 = bf16[256,1024]{1,0:T(8,128)(2,1)} custom-call(s32[3]{0:T(128)S(1)} %pad_add_fusion.place_ref, bf16[1024,1024]{1,0:T(8,128)(2,1)S(1)} %shard_map.59.mine_ref, bf16[1024,1024]{1,0:T(8,128)(2,1)S(1)} %collective-permute-done.21.other_ref), custom_call_target="tpu_custom_call" | custom-call | tf_op jit(solution)/shard_map/pallas_call | solution.py:241
  (34 shorter events, 9.3 us)
Async XLA Ops:
  0.0 1.2 %copy-start = (bf16[128,4096]{1,0:T(8,128)(2,1)S(1)}, bf16[128,4096]{1,0:T(8,128)(2,1)}, u32[]{:S(2)}) copy-start(bf16[128,4096]{1,0:T(8,128)(2,1)} %param.5) | copy-start | bytes 3145732
  5.1 68.5 %copy-start.2 = (f32[20]{0:T(128)S(1)}, f32[20]{0:T(128)}, u32[]{:S(2)}) copy-start(f32[20]{0:T(128)} %param.8) | copy-start | bytes 244
  5.1 69.2 %copy-start.1 = (bf16[256,1024]{1,0:T(8,128)(2,1)S(1)}, bf16[256,1024]{1,0:T(8,128)(2,1)}, u32[]{:S(2)}) copy-start(bf16[256,1024]{1,0:T(8,128)(2,1)} %w1.1) | copy-start | bytes 1572868
  5.1 13.7 %collective-permute-start = (bf16[16,16384]{1,0:T(8,128)(2,1)S(1)}, bf16[16,16384]{1,0:T(8,128)(2,1)S(1)}, u32[]{:S(2)}, u32[]{:S(2)}) collective-permute-start(bf16[16,16384]{1,0:T(8,128)(2,1)S(1)} %convolution_convert_fusion.mine_ref), channel_id=1, source_target_pairs={{16,0},{17,1},{18,2},{19,3},{20,4},{21,5},{22,6},{23,7},{24,8},{25... | collective-permute-start | bytes 1572872 | tf_op jit(solution)/shard_map/ppermute | solution.py:38
  7.9 3.2 %collective-permute-start.4 = (bf16[16,4096]{1,0:T(8,128)(2,1)S(1)}, bf16[16,4096]{1,0:T(8,128)(2,1)S(1)}, u32[]{:S(2)}, u32[]{:S(2)}) collective-permute-start(bf16[16,4096]{1,0:T(8,128)(2,1)S(1)} %convolution_convert_fusion.1), channel_id=1, source_target_pairs={{0,16},{1,17},{2,18},{3,19},{4,20},{5,21},{6,22},{7,23},{8,24},{9,... | collective-permute-start | bytes 393224 | tf_op jit(solution)/shard_map/ppermute | solution.py:38
  11.8 11.1 %collective-permute-start.5 = (bf16[32,2048]{1,0:T(8,128)(2,1)}, bf16[32,2048]{1,0:T(8,128)(2,1)}, u32[]{:S(2)}, u32[]{:S(2)}) collective-permute-start(bf16[32,2048]{1,0:T(8,128)(2,1)} %get-tuple-element.43), channel_id=1, source_target_pairs={{16,146},{17,147},{18,144},{19,145},{20,150},{21,151},{22,148},{23... | collective-permute-start | bytes 393224 | tf_op jit(solution)/shard_map/ppermute | solution.py:38
  19.6 12.0 %collective-permute-start.1 = (bf16[128,1024]{1,0:T(8,128)(2,1)}, bf16[128,1024]{1,0:T(8,128)(2,1)S(1)}, u32[]{:S(2)}, u32[]{:S(2)}) collective-permute-start(bf16[128,1024]{1,0:T(8,128)(2,1)} %get-tuple-element.25), channel_id=1, source_target_pairs={{0,4},{1,5},{2,6},{3,7},{4,8},{5,9},{6,10},{7,11},{8,12},{9,13},{1... | collective-permute-start | bytes 786440 | tf_op jit(solution)/shard_map/ppermute | solution.py:38
  20.3 11.3 %collective-permute-start.2 = (bf16[128,1024]{1,0:T(8,128)(2,1)S(1)}, bf16[128,1024]{1,0:T(8,128)(2,1)S(1)}, u32[]{:S(2)}, u32[]{:S(2)}) collective-permute-start(bf16[128,1024]{1,0:T(8,128)(2,1)S(1)} %get-tuple-element.26), channel_id=1, source_target_pairs={{0,8},{1,9},{2,10},{3,11},{4,12},{5,13},{6,14},{7,15},{8,0},{9,1},... | collective-permute-start | bytes 786440 | tf_op jit(solution)/shard_map/ppermute | solution.py:38
  21.0 10.6 %collective-permute-start.3 = (bf16[128,1024]{1,0:T(8,128)(2,1)S(1)}, bf16[128,1024]{1,0:T(8,128)(2,1)S(1)}, u32[]{:S(2)}, u32[]{:S(2)}) collective-permute-start(bf16[128,1024]{1,0:T(8,128)(2,1)S(1)} %get-tuple-element.27), channel_id=1, source_target_pairs={{0,12},{1,13},{2,14},{3,15},{4,0},{5,1},{6,2},{7,3},{8,4},{9,5},{1... | collective-permute-start | bytes 786440 | tf_op jit(solution)/shard_map/ppermute | solution.py:38
  24.4 7.2 %collective-permute-start.6 = (bf16[64,1024]{1,0:T(8,128)(2,1)}, bf16[64,1024]{1,0:T(8,128)(2,1)S(1)}, u32[]{:S(2)}, u32[]{:S(2)}) collective-permute-start(bf16[64,1024]{1,0:T(8,128)(2,1)} %get-tuple-element.41), channel_id=1, source_target_pairs={{16,112},{17,113},{18,114},{19,115},{20,116},{21,117},{22,118},{23... | collective-permute-start | bytes 393224 | tf_op jit(solution)/shard_map/ppermute | solution.py:38
  33.0 6.8 %collective-permute-start.7 = (bf16[128,1024]{1,0:T(8,128)(2,1)}, bf16[128,1024]{1,0:T(8,128)(2,1)S(1)}, u32[]{:S(2)}, u32[]{:S(2)}) collective-permute-start(bf16[128,1024]{1,0:T(8,128)(2,1)} %get-tuple-element.29), channel_id=1, source_target_pairs={{0,1},{1,2},{2,3},{3,128},{4,5},{5,6},{6,7},{7,132},{8,9},{9,10},{... | collective-permute-start | bytes 786440 | tf_op jit(solution)/shard_map/ppermute | solution.py:38
  34.2 9.4 %collective-permute-start.8 = (bf16[128,1024]{1,0:T(8,128)(2,1)}, bf16[128,1024]{1,0:T(8,128)(2,1)S(1)}, u32[]{:S(2)}, u32[]{:S(2)}) collective-permute-start(bf16[128,1024]{1,0:T(8,128)(2,1)} %get-tuple-element.30), channel_id=1, source_target_pairs={{0,2},{1,131},{2,128},{3,1},{4,6},{5,135},{6,132},{7,5},{8,10},{9,... | collective-permute-start | bytes 786440 | tf_op jit(solution)/shard_map/ppermute | solution.py:38
  36.9 6.8 %collective-permute-start.9 = (bf16[128,1024]{1,0:T(8,128)(2,1)S(1)}, bf16[128,1024]{1,0:T(8,128)(2,1)S(1)}, u32[]{:S(2)}, u32[]{:S(2)}) collective-permute-start(bf16[128,1024]{1,0:T(8,128)(2,1)S(1)} %get-tuple-element.31), channel_id=1, source_target_pairs={{0,131},{1,0},{2,1},{3,2},{4,135},{5,4},{6,5},{7,6},{8,139},{9,8},... | collective-permute-start | bytes 786440 | tf_op jit(solution)/shard_map/ppermute | solution.py:38
  45.3 6.3 %collective-permute-start.10 = (bf16[640,256]{1,0:T(8,128)(2,1)S(1)}, bf16[640,256]{1,0:T(8,128)(2,1)S(1)}, u32[]{:S(2)}, u32[]{:S(2)}) collective-permute-start(bf16[640,256]{1,0:T(8,128)(2,1)S(1)} %get-tuple-element.33), channel_id=1, source_target_pairs={{0,32},{1,33},{2,34},{3,35},{4,36},{5,37},{6,38},{7,39},{8,40},{9,... | collective-permute-start | bytes 983048 | tf_op jit(solution)/shard_map/ppermute | solution.py:38
  45.9 14.6 %collective-permute-start.11 = (bf16[640,256]{1,0:T(8,128)(2,1)S(1)}, bf16[640,256]{1,0:T(8,128)(2,1)S(1)}, u32[]{:S(2)}, u32[]{:S(2)}) collective-permute-start(bf16[640,256]{1,0:T(8,128)(2,1)S(1)} %get-tuple-element.34), channel_id=1, source_target_pairs={{0,64},{1,65},{2,66},{3,67},{4,68},{5,69},{6,70},{7,71},{8,72},{9,... | collective-permute-start | bytes 983048 | tf_op jit(solution)/shard_map/ppermute | solution.py:38
  47.9 15.0 %collective-permute-start.12 = (bf16[640,256]{1,0:T(8,128)(2,1)S(1)}, bf16[640,256]{1,0:T(8,128)(2,1)S(1)}, u32[]{:S(2)}, u32[]{:S(2)}) collective-permute-start(bf16[640,256]{1,0:T(8,128)(2,1)S(1)} %get-tuple-element.35), channel_id=1, source_target_pairs={{0,96},{1,97},{2,98},{3,99},{4,100},{5,101},{6,102},{7,103},{8,104... | collective-permute-start | bytes 983048 | tf_op jit(solution)/shard_map/ppermute | solution.py:38
  63.1 0.8 collective-permute-start.14
  63.8 6.3 %collective-permute-start.13 = (bf16[640,256]{1,0:T(8,128)(2,1)S(1)}, bf16[640,256]{1,0:T(8,128)(2,1)S(1)}, u32[]{:S(2)}, u32[]{:S(2)}) collective-permute-start(bf16[640,256]{1,0:T(8,128)(2,1)S(1)} %add_convert_fusion.1), channel_id=1, source_target_pairs={{0,2},{1,3},{2,128},{3,129},{4,6},{5,7},{6,132},{7,133},{8,10},{9,... | collective-permute-start | bytes 983048 | tf_op jit(solution)/shard_map/ppermute | solution.py:38
  70.3 9.6 %collective-permute-start.17 = (bf16[640,256]{1,0:T(8,128)(2,1)S(1)}, bf16[640,256]{1,0:T(8,128)(2,1)S(1)}, u32[]{:S(2)}, u32[]{:S(2)}) collective-permute-start(bf16[640,256]{1,0:T(8,128)(2,1)S(1)} %add_convert_fusion.p0), channel_id=1, source_target_pairs={{0,96},{1,97},{2,98},{3,99},{4,100},{5,101},{6,102},{7,103},{8,104... | collective-permute-start | bytes 983048 | tf_op jit(solution)/shard_map/ppermute | solution.py:38
  72.3 9.0 %collective-permute-start.16 = (bf16[640,256]{1,0:T(8,128)(2,1)S(1)}, bf16[640,256]{1,0:T(8,128)(2,1)S(1)}, u32[]{:S(2)}, u32[]{:S(2)}) collective-permute-start(bf16[640,256]{1,0:T(8,128)(2,1)S(1)} %add_convert_fusion.p0), channel_id=1, source_target_pairs={{0,64},{1,65},{2,66},{3,67},{4,68},{5,69},{6,70},{7,71},{8,72},{9,... | collective-permute-start | bytes 983048 | tf_op jit(solution)/shard_map/ppermute | solution.py:38
  73.0 10.3 %collective-permute-start.15 = (bf16[640,256]{1,0:T(8,128)(2,1)S(1)}, bf16[640,256]{1,0:T(8,128)(2,1)S(1)}, u32[]{:S(2)}, u32[]{:S(2)}) collective-permute-start(bf16[640,256]{1,0:T(8,128)(2,1)S(1)} %add_convert_fusion.p0), channel_id=1, source_target_pairs={{0,32},{1,33},{2,34},{3,35},{4,36},{5,37},{6,38},{7,39},{8,40},{9,... | collective-permute-start | bytes 983048 | tf_op jit(solution)/shard_map/ppermute | solution.py:38
  74.3 23.7 %collective-permute-start.20 = (bf16[256,1024]{1,0:T(8,128)(2,1)S(1)}, bf16[256,1024]{1,0:T(8,128)(2,1)S(1)}, u32[]{:S(2)}, u32[]{:S(2)}) collective-permute-start(bf16[256,1024]{1,0:T(8,128)(2,1)S(1)} %copy-done.1), channel_id=1, source_target_pairs={{16,48},{17,49},{18,50},{19,51},{20,52},{21,53},{22,54},{23,55},{2... | collective-permute-start | bytes 1572872 | tf_op jit(solution)/shard_map/ppermute | solution.py:38
  76.2 21.8 %collective-permute-start.19 = (bf16[256,1024]{1,0:T(8,128)(2,1)S(1)}, bf16[256,1024]{1,0:T(8,128)(2,1)S(1)}, u32[]{:S(2)}, u32[]{:S(2)}) collective-permute-start(bf16[256,1024]{1,0:T(8,128)(2,1)S(1)} %copy-done.1), channel_id=1, source_target_pairs={{0,48},{1,49},{2,50},{3,51},{4,52},{5,53},{6,54},{7,55},{8,56},{9,... | collective-permute-start | bytes 1572872 | tf_op jit(solution)/shard_map/ppermute | solution.py:38
  79.8 18.1 %collective-permute-start.18 = (bf16[256,1024]{1,0:T(8,128)(2,1)S(1)}, bf16[256,1024]{1,0:T(8,128)(2,1)S(1)}, u32[]{:S(2)}, u32[]{:S(2)}) collective-permute-start(bf16[256,1024]{1,0:T(8,128)(2,1)S(1)} %copy-done.1), channel_id=1, source_target_pairs={{0,16},{1,17},{2,18},{3,19},{4,20},{5,21},{6,22},{7,23},{8,24},{9,... | collective-permute-start | bytes 1572872 | tf_op jit(solution)/shard_map/ppermute | solution.py:38
  99.8 12.8 %collective-permute-start.21 = (bf16[1024,1024]{1,0:T(8,128)(2,1)S(1)}, bf16[1024,1024]{1,0:T(8,128)(2,1)S(1)}, u32[]{:S(2)}, u32[]{:S(2)}) collective-permute-start(bf16[1024,1024]{1,0:T(8,128)(2,1)S(1)} %shard_map.59.mine_ref), channel_id=1, source_target_pairs={{0,16},{1,17},{2,18},{3,19},{4,20},{5,21},{6,22},{7,23},{8,24},{9,... | collective-permute-start | bytes 6291464 | tf_op jit(solution)/shard_map/ppermute | solution.py:38

commit v5 on v4

--- a/solution.py
+++ b/solution.py
@@ -33,8 +33,8 @@
         c, x, zl = source // 16 % 2, source // 4 % 4, source % 4
         zh, y = source // 128, source // 32 % 4
         target = where(zh, y, c, x, zl)
-        if target is not None:
-            pairs.append((source, linear(*target)))
+        pairs.append((source, source if target is None else linear(*target)))
+    assert len({target for _, target in pairs}) == 256
     return lax.ppermute(value, ("dp", "owner"), pairs)
 
 
@@ -42,6 +42,27 @@
     z = zh * 4 + zl
     z = (z + {1: 1, 2: 2 if z % 2 == 0 else -2, 3: -1}[k]) % 8
     return z // 4, z % 4
+
+
+def offer_kernel(core_ref, x_ref, g_ref, out_ref):
+    @pl.when(core_ref[0] == 0)
+    def _():
+        out_ref[:, :x_ref.shape[1]] = x_ref[...]
+        out_ref[:, x_ref.shape[1]:] = jnp.zeros((x_ref.shape[0], out_ref.shape[1] - x_ref.shape[1]), BF16)
+
+    @pl.when(core_ref[0] == 1)
+    def _():
+        out_ref[...] = g_ref[...]
+
+
+def offer(core, samp_x, samp_g):
+    return pl.pallas_call(
+        offer_kernel,
+        out_shape=jax.ShapeDtypeStruct(samp_g.shape, BF16),
+        in_specs=[SMEM, VMEM, VMEM],
+        out_specs=VMEM,
+        compiler_params=pltpu.CompilerParams(vmem_limit_bytes=8 * MIB),
+    )(core, samp_x, samp_g)
 
 
 def pack_kernel(place_ref, mine_ref, other_ref, *outs):
@@ -260,18 +281,17 @@
     is_g = core == 0
 
     hot = (sample_ids[:, None] == jnp.arange(activations.shape[0], dtype=jnp.int32)[None]).astype(BF16)
+    samp_g = dot(hot, out_grads).astype(BF16)
+    activations, _ = lax.optimization_barrier((activations, samp_g))
     samp_x = dot(hot, activations).astype(BF16)
-    other_x = moved(samp_x, lambda zh, y, c, x, zl: (zh, y, 1, x, zl) if c == 0 else None)
-    out_grads, _ = lax.optimization_barrier((out_grads, samp_x))
-    samp_g = dot(hot, out_grads).astype(BF16)
-    other_g = moved(samp_g, lambda zh, y, c, x, zl: (zh, y, 0, x, zl) if c == 1 else None)
-
-    packed = pack(x.reshape(1), samp_g, other_g, size)
+    other = moved(offer(core.reshape(1), samp_x, samp_g), lambda zh, y, c, x, zl: (zh, y, 1 - c, x, zl))
+
+    packed = pack(x.reshape(1), samp_g, other, size)
     held = [packed[0]]
     for k in (1, 2, 3):
         held.append(moved(packed[k], lambda zh, y, c, x, zl: (zh, y, 0, (x + k) % 4, zl) if c == 0 else None))
 
-    both_x = jnp.concatenate([samp_x, other_x])
+    both_x = jnp.concatenate([samp_x, other[:, :4 * size]])
 
     def over_z(zh, y, c, x, zl):
         z = (zh * 4 + zl + (-2 if zl < 2 else 2)) % 8
@@ -309,7 +329,7 @@
                  else (zh, y ^ 1, 1, x, zl))
     there = moved(part, lambda zh, y, c, x, zl: (beside(zh, zl, -2)[0], y, 0, x, beside(zh, zl, -2)[1]) if c == 0
                   else None)
-    piece = (here.astype(F32) + jnp.where(is_g, there, part).astype(F32)).astype(BF16)
+    piece = (here.astype(F32) + there.astype(F32)).astype(BF16)
 
     pieces = [piece]
     for k in (1, 2, 3):
@@ -320,8 +340,8 @@
 
     own_w, _ = lax.optimization_barrier((weight_grad, piece))
     weights = [
-        moved(own_w, lambda zh, y, c, x, zl: (zh, y, 1, x, zl) if c == 0 else None),
-        moved(own_w, lambda zh, y, c, x, zl: (zh, y ^ 1, 1, x, zl) if c == 0 else None),
+        moved(own_w, lambda zh, y, c, x, zl: (zh, y, 1 - c, x, zl)),
+        moved(own_w, lambda zh, y, c, x, zl: (zh, y ^ 1, 1, x, zl) if c == 0 else (zh, y, 0, x, zl)),
         moved(own_w, lambda zh, y, c, x, zl: (zh, y ^ 1, 1, x, zl) if c == 1 else None),
     ]
     damp = pick(damping, jnp.where(is_g, BLOCKS_A + o, zh * 2 + y // 2)).reshape(1)

time: 115 us -> 110 us (0.957)
  waiting for transfers between devices: 40.4 us -> 33.8 us
  starting transfers between devices: 43 us -> 47 us
  other arithmetic: 2.74 us -> 1.41 us
  local copies, waits for them, and re-layouts: 1.84 us -> 0.68 us
    ppermute x22 -> x21, waiting for transfers between devices: 40.4 us -> 33.8 us  [moved(): return lax.ppermute(value, ('dp', 'owner'), pairs)]
    ppermute x22 -> x21, starting transfers between devices: 43 us -> 47 us  [moved(): return lax.ppermute(value, ('dp', 'owner'), pairs)]
    unnamed x6 -> x8, local copies, waits for them, and re-layouts: 1.23 us -> 0.02 us
  transfers between devices with their start and end apart: 22 -> 21, of which waited for: 12 -> 9; matrix products, arithmetic and copies ran while one was open for 3% -> 2% of each run, Pallas kernels for 13% -> 15%
where the time goes in v5:
time: 110 us
  starting transfers between devices  47 us (43%)
  waiting for transfers between devices  33.8 us (31%)
  Pallas kernels  23.1 us (21%)
  matrix products  3.28 us (3%)
  other arithmetic  1.41 us (1%)
    ppermute x21, starting transfers between devices, moved(): return lax.ppermute(value, ('dp', 'owner'), pairs)  47 us
    ppermute x21, waiting for transfers between devices, moved(): return lax.ppermute(value, ('dp', 'owner'), pairs)  33.8 us
    pallas_call x1, Pallas kernels, rounds(): pl.pallas_call(rounds_kernel, out_shape=jax.ShapeDtypeStruct((size, size)...  15.2 us
    dot_general x2, matrix products, dot(): return jnp.dot(a, b, preferred_element_type=F32)  3.28 us
  transfers between devices with their start and end apart: 21, of which 9 were waited for; matrix products, arithmetic and copies ran while one was open for 2% of the time, Pallas kernels for 15%

profile of v5, /device:TPU:33, one launch (start us, length us, event | category | flops | bytes accessed | tf_op | source)
XLA Modules:
  0.0 109.6 jit_solution(4475169973807766249)
XLA Ops:
  0.0 3.0 %convolution_convert_fusion.g_ref.mine_ref = bf16[16,16384]{1,0:T(8,128)(2,1)S(1)} fusion(bf16[128,16384]{1,0:T(8,128)(2,1)} %param.6, s32[16]{0:T(128)} %param.7), kind=kOutput, calls=%fused_computation | convolution fusion | flops 67373056 | bytes 4718656 | tf_op jit(solution)/shard_map/dot_general | solution.py:19
  4.1 1.5 %collective-permute-done.other_ref = bf16[16,16384]{1,0:T(8,128)(2,1)S(1)} collective-permute-done((bf16[16,16384]{1,0:T(8,128)(2,1)S(1)}, bf16[16,16384]{1,0:T(8,128)(2,1)S(1)}, u32[]{:S(2)}, u32[]{:S(2)}) %collective-permute-start) | collective-permute-done | bytes 524320 | tf_op jit(solution)/shard_map/ppermute | solution.py:38
  5.7 7.0 %collective-permute-start.4 = (bf16[32,2048]{1,0:T(8,128)(2,1)S(1)}, bf16[32,2048]{1,0:T(8,128)(2,1)}, u32[]{:S(2)}, u32[]{:S(2)}) collective-permute-start(bf16[32,2048]{1,0:T(8,128)(2,1)S(1)} %get-tuple-element.43), channel_id=1, source_target_pairs={{0,0},{1,1},{2,2},{3,3},{4,4},{5,5},{6,6},{7,7},{8,8},{9,9},{10,10... | collective-permute-start | bytes 393224 | tf_op jit(solution)/shard_map/ppermute | solution.py:38
  12.8 0.9 shard_map.56
  13.7 1.6 %collective-permute-start.1 = (bf16[128,1024]{1,0:T(8,128)(2,1)}, bf16[128,1024]{1,0:T(8,128)(2,1)S(1)}, u32[]{:S(2)}, u32[]{:S(2)}) collective-permute-start(bf16[128,1024]{1,0:T(8,128)(2,1)} %get-tuple-element.25), channel_id=1, source_target_pairs={{0,4},{1,5},{2,6},{3,7},{4,8},{5,9},{6,10},{7,11},{8,12},{9,13},{1... | collective-permute-start | bytes 786440 | tf_op jit(solution)/shard_map/ppermute | solution.py:38
  15.2 1.6 %collective-permute-start.2 = (bf16[128,1024]{1,0:T(8,128)(2,1)}, bf16[128,1024]{1,0:T(8,128)(2,1)S(1)}, u32[]{:S(2)}, u32[]{:S(2)}) collective-permute-start(bf16[128,1024]{1,0:T(8,128)(2,1)} %get-tuple-element.26), channel_id=1, source_target_pairs={{0,8},{1,9},{2,10},{3,11},{4,12},{5,13},{6,14},{7,15},{8,0},{9,1},... | collective-permute-start | bytes 786440 | tf_op jit(solution)/shard_map/ppermute | solution.py:38
  17.6 0.9 fusion
  18.5 4.6 %collective-permute-start.5 = (bf16[64,1024]{1,0:T(8,128)(2,1)S(1)}, bf16[64,1024]{1,0:T(8,128)(2,1)S(1)}, u32[]{:S(2)}, u32[]{:S(2)}) collective-permute-start(bf16[64,1024]{1,0:T(8,128)(2,1)S(1)} %get-tuple-element.41), channel_id=1, source_target_pairs={{0,0},{1,1},{2,2},{3,3},{4,4},{5,5},{6,6},{7,7},{8,8},{9,9},{10,10... | collective-permute-start | bytes 393224 | tf_op jit(solution)/shard_map/ppermute | solution.py:38
  23.3 2.2 %collective-permute-done.5.come_ref = bf16[64,1024]{1,0:T(8,128)(2,1)S(1)} collective-permute-done((bf16[64,1024]{1,0:T(8,128)(2,1)S(1)}, bf16[64,1024]{1,0:T(8,128)(2,1)S(1)}, u32[]{:S(2)}, u32[]{:S(2)}) %collective-permute-start.5) | collective-permute-done | bytes 131104 | tf_op jit(solution)/shard_map/ppermute | solution.py:38
  25.5 1.4 %shard_map.57 = (bf16[128,1024]{1,0:T(8,128)(2,1)S(1)}, bf16[128,1024]{1,0:T(8,128)(2,1)}, bf16[128,1024]{1,0:T(8,128)(2,1)}, bf16[128,1024]{1,0:T(8,128)(2,1)S(1)}) custom-call(s32[2]{0:T(128)S(1)} %pad_add_fusion.2.place_ref, bf16[128,1024]{1,0:T(8,128)(2,1)S(1)} %get-tuple-element.24.h0, bf16[128,1024]{1,0:T(8,128)(2,1)S(1)} %collective-permute-done.1.h1, ...), custom_call_target="tpu_custom_call" | custom-call | tf_op jit(solution)/shard_map/pallas_call | solution.py:107
  26.9 1.2 %collective-permute-start.6 = (bf16[128,1024]{1,0:T(8,128)(2,1)}, bf16[128,1024]{1,0:T(8,128)(2,1)S(1)}, u32[]{:S(2)}, u32[]{:S(2)}) collective-permute-start(bf16[128,1024]{1,0:T(8,128)(2,1)} %get-tuple-element.29), channel_id=1, source_target_pairs={{0,1},{1,2},{2,3},{3,128},{4,5},{5,6},{6,7},{7,132},{8,9},{9,10},{... | collective-permute-start | bytes 786440 | tf_op jit(solution)/shard_map/ppermute | solution.py:38
  28.1 2.5 %collective-permute-start.7 = (bf16[128,1024]{1,0:T(8,128)(2,1)}, bf16[128,1024]{1,0:T(8,128)(2,1)S(1)}, u32[]{:S(2)}, u32[]{:S(2)}) collective-permute-start(bf16[128,1024]{1,0:T(8,128)(2,1)} %get-tuple-element.30), channel_id=1, source_target_pairs={{0,2},{1,131},{2,128},{3,1},{4,6},{5,135},{6,132},{7,5},{8,10},{9,... | collective-permute-start | bytes 786440 | tf_op jit(solution)/shard_map/ppermute | solution.py:38
  30.6 1.2 %collective-permute-start.8 = (bf16[128,1024]{1,0:T(8,128)(2,1)S(1)}, bf16[128,1024]{1,0:T(8,128)(2,1)S(1)}, u32[]{:S(2)}, u32[]{:S(2)}) collective-permute-start(bf16[128,1024]{1,0:T(8,128)(2,1)S(1)} %get-tuple-element.31), channel_id=1, source_target_pairs={{0,131},{1,0},{2,1},{3,2},{4,135},{5,4},{6,5},{7,6},{8,139},{9,8},... | collective-permute-start | bytes 786440 | tf_op jit(solution)/shard_map/ppermute | solution.py:38
  31.8 1.8 %collective-permute-done.6.refs_2_ = bf16[128,1024]{1,0:T(8,128)(2,1)S(1)} collective-permute-done((bf16[128,1024]{1,0:T(8,128)(2,1)}, bf16[128,1024]{1,0:T(8,128)(2,1)S(1)}, u32[]{:S(2)}, u32[]{:S(2)}) %collective-permute-start.6) | collective-permute-done | bytes 262176 | tf_op jit(solution)/shard_map/ppermute | solution.py:38
  33.5 3.8 %collective-permute-done.7.refs_3_ = bf16[128,1024]{1,0:T(8,128)(2,1)S(1)} collective-permute-done((bf16[128,1024]{1,0:T(8,128)(2,1)}, bf16[128,1024]{1,0:T(8,128)(2,1)S(1)}, u32[]{:S(2)}, u32[]{:S(2)}) %collective-permute-start.7) | collective-permute-done | bytes 262176 | tf_op jit(solution)/shard_map/ppermute | solution.py:38
  37.3 1.7 %shard_map.58 = (bf16[640,256]{1,0:T(8,128)(2,1)S(1)}, bf16[640,256]{1,0:T(8,128)(2,1)S(1)}, bf16[640,256]{1,0:T(8,128)(2,1)S(1)}, bf16[640,256]{1,0:T(8,128)(2,1)S(1)}) custom-call(s32[2]{0:T(128)S(1)} %pad_add_fusion.1.refs_0_, bf16[128,1024]{1,0:T(8,128)(2,1)S(1)} %get-tuple-element.28.refs_1_, bf16[128,1024]{1,0:T(8,128)(2,1)S(1)} %collective-permute-done.6.refs_2_, ...), custom_call_target="tpu_custom_call" | custom-call | tf_op jit(solution)/shard_map/pallas_call | solution.py:136
  39.0 0.8 collective-permute-start.9
  39.8 2.4 %collective-permute-start.10 = (bf16[640,256]{1,0:T(8,128)(2,1)S(1)}, bf16[640,256]{1,0:T(8,128)(2,1)S(1)}, u32[]{:S(2)}, u32[]{:S(2)}) collective-permute-start(bf16[640,256]{1,0:T(8,128)(2,1)S(1)} %get-tuple-element.34), channel_id=1, source_target_pairs={{0,64},{1,65},{2,66},{3,67},{4,68},{5,69},{6,70},{7,71},{8,72},{9,... | collective-permute-start | bytes 983048 | tf_op jit(solution)/shard_map/ppermute | solution.py:38
  42.3 2.7 %collective-permute-done.9 = bf16[640,256]{1,0:T(8,128)(2,1)S(1)} collective-permute-done((bf16[640,256]{1,0:T(8,128)(2,1)S(1)}, bf16[640,256]{1,0:T(8,128)(2,1)S(1)}, u32[]{:S(2)}, u32[]{:S(2)}) %collective-permute-start.9) | collective-permute-done | bytes 327712 | tf_op jit(solution)/shard_map/ppermute | solution.py:38
  45.0 9.3 %collective-permute-done.10 = bf16[640,256]{1,0:T(8,128)(2,1)S(1)} collective-permute-done((bf16[640,256]{1,0:T(8,128)(2,1)S(1)}, bf16[640,256]{1,0:T(8,128)(2,1)S(1)}, u32[]{:S(2)}, u32[]{:S(2)}) %collective-permute-start.10) | collective-permute-done | bytes 327712 | tf_op jit(solution)/shard_map/ppermute | solution.py:38
  54.4 2.4 %collective-permute-done.11 = bf16[640,256]{1,0:T(8,128)(2,1)S(1)} collective-permute-done((bf16[640,256]{1,0:T(8,128)(2,1)S(1)}, bf16[640,256]{1,0:T(8,128)(2,1)S(1)}, u32[]{:S(2)}, u32[]{:S(2)}) %collective-permute-start.11) | collective-permute-done | bytes 327712 | tf_op jit(solution)/shard_map/ppermute | solution.py:38
  57.8 6.2 %collective-permute-done.12 = bf16[640,256]{1,0:T(8,128)(2,1)S(1)} collective-permute-done((bf16[640,256]{1,0:T(8,128)(2,1)S(1)}, bf16[640,256]{1,0:T(8,128)(2,1)S(1)}, u32[]{:S(2)}, u32[]{:S(2)}) %collective-permute-start.12) | collective-permute-done | bytes 327712 | tf_op jit(solution)/shard_map/ppermute | solution.py:38
  64.1 2.1 %collective-permute-start.16 = (bf16[640,256]{1,0:T(8,128)(2,1)S(1)}, bf16[640,256]{1,0:T(8,128)(2,1)S(1)}, u32[]{:S(2)}, u32[]{:S(2)}) collective-permute-start(bf16[640,256]{1,0:T(8,128)(2,1)S(1)} %add_convert_fusion.p0), channel_id=1, source_target_pairs={{0,96},{1,97},{2,98},{3,99},{4,100},{5,101},{6,102},{7,103},{8,104... | collective-permute-start | bytes 983048 | tf_op jit(solution)/shard_map/ppermute | solution.py:38
  66.1 0.9 collective-permute-start.15
  68.4 1.9 %collective-permute-start.19 = (bf16[256,1024]{1,0:T(8,128)(2,1)S(1)}, bf16[256,1024]{1,0:T(8,128)(2,1)S(1)}, u32[]{:S(2)}, u32[]{:S(2)}) collective-permute-start(bf16[256,1024]{1,0:T(8,128)(2,1)S(1)} %copy-done.1), channel_id=1, source_target_pairs={{0,0},{1,1},{2,2},{3,3},{4,4},{5,5},{6,6},{7,7},{8,8},{9,9},{10,10... | collective-permute-start | bytes 1572872 | tf_op jit(solution)/shard_map/ppermute | solution.py:38
  70.3 8.2 %collective-permute-start.18 = (bf16[256,1024]{1,0:T(8,128)(2,1)S(1)}, bf16[256,1024]{1,0:T(8,128)(2,1)S(1)}, u32[]{:S(2)}, u32[]{:S(2)}) collective-permute-start(bf16[256,1024]{1,0:T(8,128)(2,1)S(1)} %copy-done.1), channel_id=1, source_target_pairs={{0,48},{1,49},{2,50},{3,51},{4,52},{5,53},{6,54},{7,55},{8,56},{9,... | collective-permute-start | bytes 1572872 | tf_op jit(solution)/shard_map/ppermute | solution.py:38
  78.5 4.0 %collective-permute-start.17 = (bf16[256,1024]{1,0:T(8,128)(2,1)S(1)}, bf16[256,1024]{1,0:T(8,128)(2,1)S(1)}, u32[]{:S(2)}, u32[]{:S(2)}) collective-permute-start(bf16[256,1024]{1,0:T(8,128)(2,1)S(1)} %copy-done.1), channel_id=1, source_target_pairs={{0,16},{1,17},{2,18},{3,19},{4,20},{5,21},{6,22},{7,23},{8,24},{9,... | collective-permute-start | bytes 1572872 | tf_op jit(solution)/shard_map/ppermute | solution.py:38
  82.5 15.2 %shard_map.59.s_ref = bf16[1024,1024]{1,0:T(8,128)(2,1)S(1)} custom-call(s32[3]{0:T(128)S(1)} %pad_add_fusion.place_ref, f32[1]{0:T(128)} %dynamic_slice.16.damp_ref, bf16[640,256]{1,0:T(8,128)(2,1)S(1)} %add_convert_fusion.p0, bf16[640,256]{1,0:T(8,128)(2,1)} %collective-permute-done.14.p1, bf16[640,256]{1,0:T(8,128)(2,1)} %collective-permute-done.15.p2, ...), custom_call_target="tpu_custom_call" | custom-call | flops 17179869184 | bytes 4194304 | tf_op jit(solution)/shard_map/pallas_call | solution.py:204
  97.8 1.8 %shard_map.60.mine_ref = bf16[1024,1024]{1,0:T(8,128)(2,1)S(1)} custom-call(s32[3]{0:T(128)S(1)} %pad_add_fusion.place_ref, bf16[1024,1024]{1,0:T(8,128)(2,1)S(1)} %shard_map.59.s_ref, bf16[256,1024]{1,0:T(8,128)(2,1)S(1)} %collective-permute-done.17.w0, bf16[256,1024]{1,0:T(8,128)(2,1)S(1)} %copy-done.1, ...), custom_call_target="tpu_custom_call", output_to_operand_aliasing={{}: (1, {})} | custom-call | tf_op jit(solution)/shard_map/pallas_call | solution.py:238
  99.6 4.1 %collective-permute-start.20 = (bf16[1024,1024]{1,0:T(8,128)(2,1)S(1)}, bf16[1024,1024]{1,0:T(8,128)(2,1)S(1)}, u32[]{:S(2)}, u32[]{:S(2)}) collective-permute-start(bf16[1024,1024]{1,0:T(8,128)(2,1)S(1)} %shard_map.60.mine_ref), channel_id=1, source_target_pairs={{0,16},{1,17},{2,18},{3,19},{4,20},{5,21},{6,22},{7,23},{8,24},{9,... | collective-permute-start | bytes 6291464 | tf_op jit(solution)/shard_map/ppermute | solution.py:38
  103.7 3.8 %collective-permute-done.20.other_ref = bf16[1024,1024]{1,0:T(8,128)(2,1)S(1)} collective-permute-done((bf16[1024,1024]{1,0:T(8,128)(2,1)S(1)}, bf16[1024,1024]{1,0:T(8,128)(2,1)S(1)}, u32[]{:S(2)}, u32[]{:S(2)}) %collective-permute-start.20) | collective-permute-done | bytes 2097184 | tf_op jit(solution)/shard_map/ppermute | solution.py:38
  107.5 2.1 %shard_map.61 = bf16[256,1024]{1,0:T(8,128)(2,1)} custom-call(s32[3]{0:T(128)S(1)} %pad_add_fusion.place_ref, bf16[1024,1024]{1,0:T(8,128)(2,1)S(1)} %shard_map.60.mine_ref, bf16[1024,1024]{1,0:T(8,128)(2,1)S(1)} %collective-permute-done.20.other_ref), custom_call_target="tpu_custom_call" | custom-call | tf_op jit(solution)/shard_map/pallas_call | solution.py:262
  (36 shorter events, 4.5 us)
Async XLA Ops:
  0.0 3.0 %copy-start = (bf16[128,4096]{1,0:T(8,128)(2,1)S(1)}, bf16[128,4096]{1,0:T(8,128)(2,1)}, u32[]{:S(2)}) copy-start(bf16[128,4096]{1,0:T(8,128)(2,1)} %param.5) | copy-start | bytes 3145732
  0.0 3.0 %copy-start.2 = (s32[16]{0:T(128)S(1)}, s32[16]{0:T(128)}, u32[]{:S(2)}) copy-start(s32[16]{0:T(128)} %param.7) | copy-start | bytes 196
  3.3 64.4 %copy-start.3 = (f32[20]{0:T(128)S(1)}, f32[20]{0:T(128)}, u32[]{:S(2)}) copy-start(f32[20]{0:T(128)} %param.8) | copy-start | bytes 244
  3.3 65.1 %copy-start.1 = (bf16[256,1024]{1,0:T(8,128)(2,1)S(1)}, bf16[256,1024]{1,0:T(8,128)(2,1)}, u32[]{:S(2)}) copy-start(bf16[256,1024]{1,0:T(8,128)(2,1)} %w1.1) | copy-start | bytes 1572868
  3.4 2.3 %collective-permute-start = (bf16[16,16384]{1,0:T(8,128)(2,1)S(1)}, bf16[16,16384]{1,0:T(8,128)(2,1)S(1)}, u32[]{:S(2)}, u32[]{:S(2)}) collective-permute-start(bf16[16,16384]{1,0:T(8,128)(2,1)S(1)} %shard_map.55), channel_id=1, source_target_pairs={{0,16},{1,17},{2,18},{3,19},{4,20},{5,21},{6,22},{7,23},{8,24},{9,... | collective-permute-start | bytes 1572872 | tf_op jit(solution)/shard_map/ppermute | solution.py:38
  5.7 11.8 %collective-permute-start.4 = (bf16[32,2048]{1,0:T(8,128)(2,1)S(1)}, bf16[32,2048]{1,0:T(8,128)(2,1)}, u32[]{:S(2)}, u32[]{:S(2)}) collective-permute-start(bf16[32,2048]{1,0:T(8,128)(2,1)S(1)} %get-tuple-element.43), channel_id=1, source_target_pairs={{0,0},{1,1},{2,2},{3,3},{4,4},{5,5},{6,6},{7,7},{8,8},{9,9},{10,10... | collective-permute-start | bytes 393224 | tf_op jit(solution)/shard_map/ppermute | solution.py:38
  13.7 9.6 %collective-permute-start.1 = (bf16[128,1024]{1,0:T(8,128)(2,1)}, bf16[128,1024]{1,0:T(8,128)(2,1)S(1)}, u32[]{:S(2)}, u32[]{:S(2)}) collective-permute-start(bf16[128,1024]{1,0:T(8,128)(2,1)} %get-tuple-element.25), channel_id=1, source_target_pairs={{0,4},{1,5},{2,6},{3,7},{4,8},{5,9},{6,10},{7,11},{8,12},{9,13},{1... | collective-permute-start | bytes 786440 | tf_op jit(solution)/shard_map/ppermute | solution.py:38
  15.2 8.0 %collective-permute-start.2 = (bf16[128,1024]{1,0:T(8,128)(2,1)}, bf16[128,1024]{1,0:T(8,128)(2,1)S(1)}, u32[]{:S(2)}, u32[]{:S(2)}) collective-permute-start(bf16[128,1024]{1,0:T(8,128)(2,1)} %get-tuple-element.26), channel_id=1, source_target_pairs={{0,8},{1,9},{2,10},{3,11},{4,12},{5,13},{6,14},{7,15},{8,0},{9,1},... | collective-permute-start | bytes 786440 | tf_op jit(solution)/shard_map/ppermute | solution.py:38
  16.8 6.4 %collective-permute-start.3 = (bf16[128,1024]{1,0:T(8,128)(2,1)S(1)}, bf16[128,1024]{1,0:T(8,128)(2,1)S(1)}, u32[]{:S(2)}, u32[]{:S(2)}) collective-permute-start(bf16[128,1024]{1,0:T(8,128)(2,1)S(1)} %get-tuple-element.27), channel_id=1, source_target_pairs={{0,12},{1,13},{2,14},{3,15},{4,0},{5,1},{6,2},{7,3},{8,4},{9,5},{1... | collective-permute-start | bytes 786440 | tf_op jit(solution)/shard_map/ppermute | solution.py:38
  18.5 7.0 %collective-permute-start.5 = (bf16[64,1024]{1,0:T(8,128)(2,1)S(1)}, bf16[64,1024]{1,0:T(8,128)(2,1)S(1)}, u32[]{:S(2)}, u32[]{:S(2)}) collective-permute-start(bf16[64,1024]{1,0:T(8,128)(2,1)S(1)} %get-tuple-element.41), channel_id=1, source_target_pairs={{0,0},{1,1},{2,2},{3,3},{4,4},{5,5},{6,6},{7,7},{8,8},{9,9},{10,10... | collective-permute-start | bytes 393224 | tf_op jit(solution)/shard_map/ppermute | solution.py:38
  26.9 6.6 %collective-permute-start.6 = (bf16[128,1024]{1,0:T(8,128)(2,1)}, bf16[128,1024]{1,0:T(8,128)(2,1)S(1)}, u32[]{:S(2)}, u32[]{:S(2)}) collective-permute-start(bf16[128,1024]{1,0:T(8,128)(2,1)} %get-tuple-element.29), channel_id=1, source_target_pairs={{0,1},{1,2},{2,3},{3,128},{4,5},{5,6},{6,7},{7,132},{8,9},{9,10},{... | collective-permute-start | bytes 786440 | tf_op jit(solution)/shard_map/ppermute | solution.py:38
  28.1 9.2 %collective-permute-start.7 = (bf16[128,1024]{1,0:T(8,128)(2,1)}, bf16[128,1024]{1,0:T(8,128)(2,1)S(1)}, u32[]{:S(2)}, u32[]{:S(2)}) collective-permute-start(bf16[128,1024]{1,0:T(8,128)(2,1)} %get-tuple-element.30), channel_id=1, source_target_pairs={{0,2},{1,131},{2,128},{3,1},{4,6},{5,135},{6,132},{7,5},{8,10},{9,... | collective-permute-start | bytes 786440 | tf_op jit(solution)/shard_map/ppermute | solution.py:38
  30.6 6.8 %collective-permute-start.8 = (bf16[128,1024]{1,0:T(8,128)(2,1)S(1)}, bf16[128,1024]{1,0:T(8,128)(2,1)S(1)}, u32[]{:S(2)}, u32[]{:S(2)}) collective-permute-start(bf16[128,1024]{1,0:T(8,128)(2,1)S(1)} %get-tuple-element.31), channel_id=1, source_target_pairs={{0,131},{1,0},{2,1},{3,2},{4,135},{5,4},{6,5},{7,6},{8,139},{9,8},... | collective-permute-start | bytes 786440 | tf_op jit(solution)/shard_map/ppermute | solution.py:38
  39.0 6.0 %collective-permute-start.9 = (bf16[640,256]{1,0:T(8,128)(2,1)S(1)}, bf16[640,256]{1,0:T(8,128)(2,1)S(1)}, u32[]{:S(2)}, u32[]{:S(2)}) collective-permute-start(bf16[640,256]{1,0:T(8,128)(2,1)S(1)} %get-tuple-element.33), channel_id=1, source_target_pairs={{0,32},{1,33},{2,34},{3,35},{4,36},{5,37},{6,38},{7,39},{8,40},{9,... | collective-permute-start | bytes 983048 | tf_op jit(solution)/shard_map/ppermute | solution.py:38
  39.8 14.6 %collective-permute-start.10 = (bf16[640,256]{1,0:T(8,128)(2,1)S(1)}, bf16[640,256]{1,0:T(8,128)(2,1)S(1)}, u32[]{:S(2)}, u32[]{:S(2)}) collective-permute-start(bf16[640,256]{1,0:T(8,128)(2,1)S(1)} %get-tuple-element.34), channel_id=1, source_target_pairs={{0,64},{1,65},{2,66},{3,67},{4,68},{5,69},{6,70},{7,71},{8,72},{9,... | collective-permute-start | bytes 983048 | tf_op jit(solution)/shard_map/ppermute | solution.py:38
  42.2 14.6 %collective-permute-start.11 = (bf16[640,256]{1,0:T(8,128)(2,1)S(1)}, bf16[640,256]{1,0:T(8,128)(2,1)S(1)}, u32[]{:S(2)}, u32[]{:S(2)}) collective-permute-start(bf16[640,256]{1,0:T(8,128)(2,1)S(1)} %get-tuple-element.35), channel_id=1, source_target_pairs={{0,96},{1,97},{2,98},{3,99},{4,100},{5,101},{6,102},{7,103},{8,104... | collective-permute-start | bytes 983048 | tf_op jit(solution)/shard_map/ppermute | solution.py:38
  57.0 0.8 collective-permute-start.13
  57.7 6.3 %collective-permute-start.12 = (bf16[640,256]{1,0:T(8,128)(2,1)S(1)}, bf16[640,256]{1,0:T(8,128)(2,1)S(1)}, u32[]{:S(2)}, u32[]{:S(2)}) collective-permute-start(bf16[640,256]{1,0:T(8,128)(2,1)S(1)} %add_convert_fusion.1), channel_id=1, source_target_pairs={{0,2},{1,3},{2,128},{3,129},{4,6},{5,7},{6,132},{7,133},{8,10},{9,... | collective-permute-start | bytes 983048 | tf_op jit(solution)/shard_map/ppermute | solution.py:38
  64.1 14.4 %collective-permute-start.16 = (bf16[640,256]{1,0:T(8,128)(2,1)S(1)}, bf16[640,256]{1,0:T(8,128)(2,1)S(1)}, u32[]{:S(2)}, u32[]{:S(2)}) collective-permute-start(bf16[640,256]{1,0:T(8,128)(2,1)S(1)} %add_convert_fusion.p0), channel_id=1, source_target_pairs={{0,96},{1,97},{2,98},{3,99},{4,100},{5,101},{6,102},{7,103},{8,104... | collective-permute-start | bytes 983048 | tf_op jit(solution)/shard_map/ppermute | solution.py:38
  66.1 16.4 %collective-permute-start.15 = (bf16[640,256]{1,0:T(8,128)(2,1)S(1)}, bf16[640,256]{1,0:T(8,128)(2,1)}, u32[]{:S(2)}, u32[]{:S(2)}) collective-permute-start(bf16[640,256]{1,0:T(8,128)(2,1)S(1)} %add_convert_fusion.p0), channel_id=1, source_target_pairs={{0,64},{1,65},{2,66},{3,67},{4,68},{5,69},{6,70},{7,71},{8,72},{9,... | collective-permute-start | bytes 983048 | tf_op jit(solution)/shard_map/ppermute | solution.py:38
  67.1 15.5 %collective-permute-start.14 = (bf16[640,256]{1,0:T(8,128)(2,1)S(1)}, bf16[640,256]{1,0:T(8,128)(2,1)}, u32[]{:S(2)}, u32[]{:S(2)}) collective-permute-start(bf16[640,256]{1,0:T(8,128)(2,1)S(1)} %add_convert_fusion.p0), channel_id=1, source_target_pairs={{0,32},{1,33},{2,34},{3,35},{4,36},{5,37},{6,38},{7,39},{8,40},{9,... | collective-permute-start | bytes 983048 | tf_op jit(solution)/shard_map/ppermute | solution.py:38
  68.4 29.3 %collective-permute-start.19 = (bf16[256,1024]{1,0:T(8,128)(2,1)S(1)}, bf16[256,1024]{1,0:T(8,128)(2,1)S(1)}, u32[]{:S(2)}, u32[]{:S(2)}) collective-permute-start(bf16[256,1024]{1,0:T(8,128)(2,1)S(1)} %copy-done.1), channel_id=1, source_target_pairs={{0,0},{1,1},{2,2},{3,3},{4,4},{5,5},{6,6},{7,7},{8,8},{9,9},{10,10... | collective-permute-start | bytes 1572872 | tf_op jit(solution)/shard_map/ppermute | solution.py:38
  70.3 27.4 %collective-permute-start.18 = (bf16[256,1024]{1,0:T(8,128)(2,1)S(1)}, bf16[256,1024]{1,0:T(8,128)(2,1)S(1)}, u32[]{:S(2)}, u32[]{:S(2)}) collective-permute-start(bf16[256,1024]{1,0:T(8,128)(2,1)S(1)} %copy-done.1), channel_id=1, source_target_pairs={{0,48},{1,49},{2,50},{3,51},{4,52},{5,53},{6,54},{7,55},{8,56},{9,... | collective-permute-start | bytes 1572872 | tf_op jit(solution)/shard_map/ppermute | solution.py:38
  78.5 19.2 %collective-permute-start.17 = (bf16[256,1024]{1,0:T(8,128)(2,1)S(1)}, bf16[256,1024]{1,0:T(8,128)(2,1)S(1)}, u32[]{:S(2)}, u32[]{:S(2)}) collective-permute-start(bf16[256,1024]{1,0:T(8,128)(2,1)S(1)} %copy-done.1), channel_id=1, source_target_pairs={{0,16},{1,17},{2,18},{3,19},{4,20},{5,21},{6,22},{7,23},{8,24},{9,... | collective-permute-start | bytes 1572872 | tf_op jit(solution)/shard_map/ppermute | solution.py:38
  99.6 7.9 %collective-permute-start.20 = (bf16[1024,1024]{1,0:T(8,128)(2,1)S(1)}, bf16[1024,1024]{1,0:T(8,128)(2,1)S(1)}, u32[]{:S(2)}, u32[]{:S(2)}) collective-permute-start(bf16[1024,1024]{1,0:T(8,128)(2,1)S(1)} %shard_map.60.mine_ref), channel_id=1, source_target_pairs={{0,16},{1,17},{2,18},{3,19},{4,20},{5,21},{6,22},{7,23},{8,24},{9,... | collective-permute-start | bytes 6291464 | tf_op jit(solution)/shard_map/ppermute | solution.py:38

commit v6 on v5

--- a/solution.py
+++ b/solution.py
@@ -38,6 +38,37 @@
     return lax.ppermute(value, ("dp", "owner"), pairs)
 
 
+def dealt(value, group_of):
+    groups = []
+    for device in range(256):
+        c, x, zl = device // 16 % 2, device // 4 % 4, device % 4
+        members = [linear(*member) for member in group_of(device // 128, device // 32 % 4, c, x, zl)]
+        assert device in members
+        if device == min(members):
+            groups.append(members)
+    assert sorted(sum(groups, [])) == list(range(256))
+    return lax.all_to_all(
+        value, ("dp", "owner"), split_axis=0, concat_axis=0, tiled=True, axis_index_groups=groups)
+
+
+def over_x(zh, y, c, x, zl):
+    return [(zh, y, c, i, zl) for i in range(4)]
+
+
+def over_y(zh, y, c, x, zl):
+    return [(zh, i, c, x, zl) for i in range(4)]
+
+
+def over_zl(zh, y, c, x, zl):
+    return [(zh, y, c, x, i) for i in range(4)]
+
+
+def over_blocks(zh, y, c, x, zl):
+    z = (zh * 4 + zl + (-2 if zl < 2 else 2)) % 8
+    places = {zh: (zh, zl), 1 - zh: (z // 4, z % 4)}
+    return [(places[h][0], y if y // 2 == g else 3 - y, c, x, places[h][1]) for h in range(2) for g in range(2)]
+
+
 def z_shift(zh, zl, k):
     z = zh * 4 + zl
     z = (z + {1: 1, 2: 2 if z % 2 == 0 else -2, 3: -1}[k]) % 8
@@ -65,56 +96,56 @@
     )(core, samp_x, samp_g)
 
 
-def pack_kernel(place_ref, mine_ref, other_ref, *outs):
-    count, size = mine_ref.shape[0], outs[0].shape[1]
+def pack_kernel(core_ref, x_ref, g_ref, other_ref, out_ref):
+    count, size = x_ref.shape[0], out_ref.shape[2]
+
+    @pl.when(core_ref[0] == 0)
+    def _():
+        for i in range(4):
+            for zl in range(4):
+                cols = slice((i * 4 + zl) * size, (i * 4 + zl + 1) * size)
+                out_ref[i, zl * 2 * count:(zl * 2 + 1) * count, :] = g_ref[:, cols]
+                out_ref[i, (zl * 2 + 1) * count:(zl * 2 + 2) * count, :] = other_ref[:, cols]
+
+    @pl.when(core_ref[0] == 1)
+    def _():
+        for i in range(4):
+            cols = slice(i * size, (i + 1) * size)
+            out_ref[i, :count, :] = x_ref[:, cols]
+            out_ref[i, count:2 * count, :] = other_ref[:, cols]
+            out_ref[i, 2 * count:, :] = jnp.zeros((6 * count, size), BF16)
+
+
+def pack(core, samp_x, samp_g, other, size):
+    return pl.pallas_call(
+        pack_kernel,
+        out_shape=jax.ShapeDtypeStruct((4, 8 * samp_x.shape[0], size), BF16),
+        in_specs=[SMEM] + [VMEM] * 3,
+        out_specs=VMEM,
+        compiler_params=pltpu.CompilerParams(vmem_limit_bytes=8 * MIB),
+    )(core, samp_x, samp_g, other)
+
+
+def deal_kernel(place_ref, held_ref, *outs):
+    rows = held_ref.shape[1] // 4
     for k, out in enumerate(outs):
-        for zl in range(4):
-            index = lax.rem(place_ref[0] + k, 4) * 4 + zl
-            cols = pl.ds(pl.multiple_of(index * size, size), size)
-            out[zl * 2 * count:(zl * 2 + 1) * count, :] = mine_ref[:, cols]
-            out[(zl * 2 + 1) * count:(zl * 2 + 2) * count, :] = other_ref[:, cols]
-
-
-def pack(place, mine, other, size):
-    return pl.pallas_call(
-        pack_kernel,
-        out_shape=(jax.ShapeDtypeStruct((8 * mine.shape[0], size), BF16),) * 4,
-        in_specs=[SMEM, VMEM, VMEM],
+        start = pl.multiple_of(lax.rem(place_ref[0] + k * place_ref[1], 4) * rows, rows)
+        for i in range(4):
+            out[i * rows:(i + 1) * rows, :] = held_ref[i, pl.ds(start, rows), :]
+
+
+def deal(place, held):
+    return pl.pallas_call(
+        deal_kernel,
+        out_shape=(jax.ShapeDtypeStruct(held.shape[1:], BF16),) * 4,
+        in_specs=[SMEM, VMEM],
         out_specs=(VMEM,) * 4,
         compiler_params=pltpu.CompilerParams(vmem_limit_bytes=8 * MIB),
-    )(place, mine, other)
-
-
-def deal_kernel(place_ref, h0, h1, h2, h3, kept_ref, come_ref, *outs):
-    rows = h0.shape[0] // 4
-    half = kept_ref.shape[0]
-
-    @pl.when(place_ref[1] == 0)
-    def _():
-        for k, out in enumerate(outs):
-            start = pl.multiple_of(lax.rem(place_ref[0] + k, 4) * rows, rows)
-            for i, held in enumerate((h0, h1, h2, h3)):
-                out[i * rows:(i + 1) * rows, :] = held[pl.ds(start, rows), :]
-
-    @pl.when(place_ref[1] == 1)
-    def _():
-        for out in outs:
-            out[:half, :] = kept_ref[...]
-            out[half:, :] = come_ref[...]
-
-
-def deal(place, held, kept, come):
-    return pl.pallas_call(
-        deal_kernel,
-        out_shape=(jax.ShapeDtypeStruct(held[0].shape, BF16),) * 4,
-        in_specs=[SMEM] + [VMEM] * 6,
-        out_specs=(VMEM,) * 4,
-        compiler_params=pltpu.CompilerParams(vmem_limit_bytes=8 * MIB),
-    )(place, *held, kept, come)
+    )(place, held)
 
 
 def cov_kernel(scale, place_ref, *refs):
-    pieces, chunks, (all_ref, panel_ref) = refs[:4], refs[4:8], refs[8:]
+    pieces, chunks, (all_ref, panel_ref) = refs[:4], [refs[4].at[i] for i in range(4)], refs[5:]
     count, size = pieces[0].shape
     tile, sub = size // 4, size // 16
     for k, piece in enumerate(pieces):
@@ -135,19 +166,19 @@
     tile, sub = size // 4, size // 16
     return pl.pallas_call(
         lambda *refs: cov_kernel(scale, *refs),
-        out_shape=(jax.ShapeDtypeStruct((len(UPPER) * sub, tile), BF16),) * 4,
+        out_shape=jax.ShapeDtypeStruct((4, len(UPPER) * sub, tile), BF16),
         in_specs=[SMEM] + [VMEM] * 4,
-        out_specs=(VMEM,) * 4,
+        out_specs=VMEM,
         scratch_shapes=[pltpu.VMEM((4 * count, size), BF16), pltpu.VMEM((tile, size), F32)],
         compiler_params=pltpu.CompilerParams(vmem_limit_bytes=16 * MIB),
     )(place, *pieces)
 
 
-def rounds_kernel(place_ref, damp_ref, p0, p1, p2, p3, out_ref, a_ref, x_ref, xb_ref, p_ref):
+def rounds_kernel(damp_ref, pieces_ref, out_ref, a_ref, x_ref, xb_ref, p_ref):
     size = out_ref.shape[0]
     tile = size // 4
     sub = tile // 4
-    base, damp = place_ref[0], damp_ref[0]
+    damp = damp_ref[0]
     blocks = [slice(i * tile, (i + 1) * tile) for i in range(4)]
 
     def mirrored(ref, c, value):
@@ -155,10 +186,9 @@
         for r in range(c):
             ref[blocks[c], blocks[r]] = value[blocks[r], :].T
 
-    for k, piece in enumerate((p0, p1, p2, p3)):
-        start = pl.multiple_of(lax.rem(base + 4 - k, 4) * sub, sub)
+    for i in range(4):
         for t, (r, c) in enumerate(UPPER):
-            a_ref[pl.ds(r * tile + start, sub), blocks[c]] = piece[t * sub:(t + 1) * sub, :]
+            a_ref[r * tile + i * sub:r * tile + (i + 1) * sub, blocks[c]] = pieces_ref[i, t * sub:(t + 1) * sub, :]
     row = lax.broadcasted_iota(jnp.int32, (tile, tile), 0)
     col = lax.broadcasted_iota(jnp.int32, (tile, tile), 1)
     eye = row == col
@@ -198,13 +228,13 @@
                 mirrored(out_ref, c, (value * (frob / 2.0 ** ITERS)).astype(BF16))
 
 
-def rounds(place, damp, pieces):
-    tile = pieces[0].shape[1]
+def rounds(damp, pieces):
+    tile = pieces.shape[2]
     size = tile * 4
     return pl.pallas_call(
         rounds_kernel,
         out_shape=jax.ShapeDtypeStruct((size, size), BF16),
-        in_specs=[SMEM, SMEM] + [VMEM] * 4,
+        in_specs=[SMEM, VMEM],
         out_specs=VMEM,
         scratch_shapes=[
             pltpu.VMEM((size, size), BF16),
@@ -214,14 +244,14 @@
         ],
         cost_estimate=pl.CostEstimate(flops=16 * size ** 3, transcendentals=0, bytes_accessed=4 * size * size),
         compiler_params=pltpu.CompilerParams(vmem_limit_bytes=24 * MIB),
-    )(place, damp, *pieces)
+    )(damp, pieces)
 
 
 def mix_kernel(place_ref, s_ref, w0, w1, w2, w3, out_ref, t_ref):
     tile, size = w0.shape
-    half = place_ref[2]
-
-    @pl.when(place_ref[1] == 1)
+    half = place_ref[1]
+
+    @pl.when(place_ref[0] == 1)
     def _():
         for i in range(2):
             rows = pl.ds(pl.multiple_of((2 * half + i) * tile, tile), tile)
@@ -249,11 +279,11 @@
 def last_kernel(place_ref, mine_ref, other_ref, out_ref):
     tile = out_ref.shape[0]
 
-    @pl.when(place_ref[1] == 0)
+    @pl.when(place_ref[0] == 0)
     def _():
         out_ref[...] = dot(other_ref[:tile, :], mine_ref[...]).astype(BF16)
 
-    @pl.when(place_ref[1] == 1)
+    @pl.when(place_ref[0] == 1)
     def _():
         out_ref[...] = dot(mine_ref[tile:2 * tile, :], other_ref[...]).astype(BF16)
 
@@ -286,25 +316,12 @@
     samp_x = dot(hot, activations).astype(BF16)
     other = moved(offer(core.reshape(1), samp_x, samp_g), lambda zh, y, c, x, zl: (zh, y, 1 - c, x, zl))
 
-    packed = pack(x.reshape(1), samp_g, other, size)
-    held = [packed[0]]
-    for k in (1, 2, 3):
-        held.append(moved(packed[k], lambda zh, y, c, x, zl: (zh, y, 0, (x + k) % 4, zl) if c == 0 else None))
-
-    both_x = jnp.concatenate([samp_x, other[:, :4 * size]])
-
-    def over_z(zh, y, c, x, zl):
-        z = (zh * 4 + zl + (-2 if zl < 2 else 2)) % 8
-        return (z // 4, y, 1, x, z % 4) if c == 1 else None
-
-    def columns(value, start, count):
-        return lax.dynamic_slice_in_dim(value, start * size, count * size, 1)
-
-    halves = jnp.concatenate([columns(both_x, zh * 2, 2), moved(columns(both_x, (1 - zh) * 2, 2), over_z)])
-    kept = columns(halves, y // 2, 1)
-    come = moved(columns(halves, 1 - y // 2, 1), lambda zh, y, c, x, zl: (zh, 3 - y, 1, x, zl) if c == 1 else None)
-
-    samples = list(deal(jnp.stack([(zl + 2) % 4, core]), held, kept, come))
+    held = dealt(
+        pack(core.reshape(1), samp_x, samp_g, other, size),
+        lambda *place: over_x(*place) if place[2] == 0 else over_blocks(*place),
+    )
+
+    samples = list(deal(jnp.stack([jnp.where(is_g, (zl + 2) % 4, 0), 1 - core]), held))
     for k in (1, 2, 3):
         samples[k] = moved(
             samples[k],
@@ -312,14 +329,9 @@
             else (zh, y, 1, (x + k) % 4, zl),
         )
 
-    chunks = cov(jnp.stack([jnp.where(is_g, y, x), 1 - core]), samples, scale)
-    total = chunks[0].astype(F32)
-    for k in (1, 2, 3):
-        total += moved(
-            chunks[k],
-            lambda zh, y, c, x, zl: (zh, (y + k) % 4, 0, x, zl) if c == 0 else (zh, y, 1, x, (zl + k) % 4),
-        ).astype(F32)
-    part = total.astype(BF16)
+    chunks = cov(jnp.stack([jnp.where(is_g, 0, x), 1 - core]), samples, scale)
+    chunks = dealt(chunks, lambda *place: over_y(*place) if place[2] == 0 else over_zl(*place))
+    part = jnp.sum(chunks.astype(F32), axis=0).astype(BF16)
 
     def beside(zh, zl, by):
         z = (zh * 4 + zl + by) % 8
@@ -331,12 +343,10 @@
                   else None)
     piece = (here.astype(F32) + there.astype(F32)).astype(BF16)
 
-    pieces = [piece]
-    for k in (1, 2, 3):
-        pieces.append(moved(
-            piece,
-            lambda zh, y, c, x, zl: (zh, (y + k) % 4, 0, x, zl) if c == 0 else (zh, y, 1, (x + k) % 4, zl),
-        ))
+    pieces = dealt(
+        jnp.broadcast_to(piece, (4,) + piece.shape),
+        lambda *place: over_y(*place) if place[2] == 0 else over_x(*place),
+    )
 
     own_w, _ = lax.optimization_barrier((weight_grad, piece))
     weights = [
@@ -345,8 +355,8 @@
         moved(own_w, lambda zh, y, c, x, zl: (zh, y ^ 1, 1, x, zl) if c == 1 else None),
     ]
     damp = pick(damping, jnp.where(is_g, BLOCKS_A + o, zh * 2 + y // 2)).reshape(1)
-    place = jnp.stack([jnp.where(is_g, y, x), core, y % 2])
-    inverse, *weights = lax.optimization_barrier((rounds(place, damp, pieces), *weights))
+    place = jnp.stack([core, y % 2])
+    inverse, *weights = lax.optimization_barrier((rounds(damp, pieces), *weights))
     weights.insert(1, weight_grad)
 
     mine = mix(place, inverse, weights)

time: 110 us -> 124 us (1.13)
  blocking collectives: 0 us -> 25.6 us
  starting transfers between devices: 47 us -> 24.3 us
  waiting for transfers between devices: 33.8 us -> 45.4 us
    ppermute x21 -> x10, starting transfers between devices: 47 us -> 10.8 us  [moved(): return lax.ppermute(value, ('dp', 'owner'), pairs)]
    all_to_all x0 -> x2, waiting for transfers between devices: none -> 27.6 us  [dealt(): lax.all_to_all(value, ('dp', 'owner'), split_axis=0, concat_axis=0, tiled...]
    all_to_all x0 -> x1, blocking collectives: none -> 25.6 us  [dealt(): lax.all_to_all(value, ('dp', 'owner'), split_axis=0, concat_axis=0, tiled...]
    ppermute x21 -> x10, waiting for transfers between devices: 33.8 us -> 17.8 us  [moved(): return lax.ppermute(value, ('dp', 'owner'), pairs)]
    all_to_all x0 -> x2, starting transfers between devices: none -> 13.5 us  [dealt(): lax.all_to_all(value, ('dp', 'owner'), split_axis=0, concat_axis=0, tiled...]
    pallas_call x1, Pallas kernels: 15.2 us -> 14 us  [rounds(): pl.pallas_call(rounds_kernel, out_shape=jax.ShapeDtypeStruct((size, size)...]
  transfers between devices with their start and end apart: 21 -> 12, of which waited for: 9 -> 7; matrix products, arithmetic and copies ran while one was open for 2% -> 1% of each run, Pallas kernels for 15% -> 11%
where the time goes in v6:
time: 124 us; the launch traced here: 123 us
  waiting for transfers between devices  45.4 us (37%)
  blocking collectives  25.6 us (21%)
  starting transfers between devices  24.3 us (20%)
  Pallas kernels  21.9 us (18%)
  matrix products  3.28 us (3%)
  local copies, waits for them, and re-layouts  1.83 us (1%)
    all_to_all x2, waiting for transfers between devices, dealt(): lax.all_to_all(value, ('dp', 'owner'), split_axis=0, concat_axis=0, tiled...  27.6 us
    all_to_all x1, blocking collectives, dealt(): lax.all_to_all(value, ('dp', 'owner'), split_axis=0, concat_axis=0, tiled...  25.6 us
    ppermute x10, waiting for transfers between devices, moved(): return lax.ppermute(value, ('dp', 'owner'), pairs)  17.8 us
    pallas_call x1, Pallas kernels, rounds(): pl.pallas_call(rounds_kernel, out_shape=jax.ShapeDtypeStruct((size, size)...  14 us
    all_to_all x2, starting transfers between devices, dealt(): lax.all_to_all(value, ('dp', 'owner'), split_axis=0, concat_axis=0, tiled...  13.5 us
    ppermute x10, starting transfers between devices, moved(): return lax.ppermute(value, ('dp', 'owner'), pairs)  10.8 us
    dot_general x2, matrix products, dot(): return jnp.dot(a, b, preferred_element_type=F32)  3.28 us
    pallas_call x1, Pallas kernels, mix(): pl.pallas_call(mix_kernel, out_shape=jax.ShapeDtypeStruct(inverse.shape,...  2.51 us
  transfers between devices with their start and end apart: 12, of which 7 were waited for; matrix products, arithmetic and copies ran while one was open for 1% of the time, Pallas kernels for 11%

profile of v6, /device:TPU:33, one launch (start us, length us, event | category | flops | bytes accessed | tf_op | source)
XLA Modules:
  0.0 123.1 jit_solution(15996698060125260573)
XLA Ops:
  0.0 3.0 %convolution_convert_fusion.g_ref = bf16[16,16384]{1,0:T(8,128)(2,1)S(1)} fusion(bf16[128,16384]{1,0:T(8,128)(2,1)} %param.6, s32[16]{0:T(128)} %param.7), kind=kOutput, calls=%fused_computation | convolution fusion | flops 67373056 | bytes 4718656 | tf_op jit(solution)/shard_map/dot_general | solution.py:19
  3.0 0.3 convolution_convert_fusion.1.x_ref
  3.4 0.8 collective-permute-start
  4.1 1.5 %collective-permute-done.other_ref = bf16[16,16384]{1,0:T(8,128)(2,1)S(1)} collective-permute-done((bf16[16,16384]{1,0:T(8,128)(2,1)S(1)}, bf16[16,16384]{1,0:T(8,128)(2,1)S(1)}, u32[]{:S(2)}, u32[]{:S(2)}) %collective-permute-start) | collective-permute-done | bytes 524320 | tf_op jit(solution)/shard_map/ppermute | solution.py:38
  5.7 1.0 shard_map.56
  6.7 8.8 %all-to-all-start = ((bf16[4,128,1024]{2,1,0:T(8,128)(2,1)}), bf16[4,128,1024]{2,1,0:T(8,128)(2,1)S(1)}, u32[]{:S(2)}, u32[]{:S(2)}) async-start(bf16[4,128,1024]{2,1,0:T(8,128)(2,1)} %shard_map.56), calls=%async_computation | async-start | bytes 2097152 | tf_op jit(solution)/shard_map/all_to_all | solution.py:50
  15.6 21.0 %all-to-all-done.held_ref = bf16[4,128,1024]{2,1,0:T(8,128)(2,1)S(1)} async-done(((bf16[4,128,1024]{2,1,0:T(8,128)(2,1)}), bf16[4,128,1024]{2,1,0:T(8,128)(2,1)S(1)}, u32[]{:S(2)}, u32[]{:S(2)}) %all-to-all-start) | async-done | bytes 1048608 | tf_op jit(solution)/shard_map/all_to_all | solution.py:50
  36.6 0.6 shard_map.57
  37.3 1.8 %collective-permute-start.1 = (bf16[128,1024]{1,0:T(8,128)(2,1)S(1)}, bf16[128,1024]{1,0:T(8,128)(2,1)S(1)}, u32[]{:S(2)}, u32[]{:S(2)}) collective-permute-start(bf16[128,1024]{1,0:T(8,128)(2,1)S(1)} %get-tuple-element.17), channel_id=1, source_target_pairs={{0,1},{1,2},{2,3},{3,128},{4,5},{5,6},{6,7},{7,132},{8,9},{9,10},{... | collective-permute-start | bytes 786440 | tf_op jit(solution)/shard_map/ppermute | solution.py:38
  39.1 2.5 %collective-permute-start.2 = (bf16[128,1024]{1,0:T(8,128)(2,1)S(1)}, bf16[128,1024]{1,0:T(8,128)(2,1)S(1)}, u32[]{:S(2)}, u32[]{:S(2)}) collective-permute-start(bf16[128,1024]{1,0:T(8,128)(2,1)S(1)} %get-tuple-element.18), channel_id=1, source_target_pairs={{0,2},{1,131},{2,128},{3,1},{4,6},{5,135},{6,132},{7,5},{8,10},{9,... | collective-permute-start | bytes 786440 | tf_op jit(solution)/shard_map/ppermute | solution.py:38
  41.5 1.2 collective-permute-start.3
  42.7 1.3 %collective-permute-done.1.refs_2_ = bf16[128,1024]{1,0:T(8,128)(2,1)S(1)} collective-permute-done((bf16[128,1024]{1,0:T(8,128)(2,1)S(1)}, bf16[128,1024]{1,0:T(8,128)(2,1)S(1)}, u32[]{:S(2)}, u32[]{:S(2)}) %collective-permute-start.1) | collective-permute-done | bytes 262176 | tf_op jit(solution)/shard_map/ppermute | solution.py:38
  44.1 4.0 %collective-permute-done.2.refs_3_ = bf16[128,1024]{1,0:T(8,128)(2,1)S(1)} collective-permute-done((bf16[128,1024]{1,0:T(8,128)(2,1)S(1)}, bf16[128,1024]{1,0:T(8,128)(2,1)S(1)}, u32[]{:S(2)}, u32[]{:S(2)}) %collective-permute-start.2) | collective-permute-done | bytes 262176 | tf_op jit(solution)/shard_map/ppermute | solution.py:38
  48.1 1.7 %shard_map.58 = bf16[4,640,256]{2,1,0:T(8,128)(2,1)S(1)} custom-call(s32[2]{0:T(128)S(1)} %pad_add_fusion.1.refs_0_, bf16[128,1024]{1,0:T(8,128)(2,1)S(1)} %get-tuple-element.16.refs_1_, bf16[128,1024]{1,0:T(8,128)(2,1)S(1)} %collective-permute-done.1.refs_2_, bf16[128,1024]{1,0:T(8,128)(2,1)S(1)} %collective-permute-done.2.refs_3_, ...), custom_call_target="tpu_custom_call" | custom-call | tf_op jit(solution)/shard_map/pallas_call | solution.py:167
  49.8 25.6 %all_to_all.15 = bf16[4,640,256]{2,1,0:T(8,128)(2,1)S(1)} all-to-all(bf16[4,640,256]{2,1,0:T(8,128)(2,1)S(1)} %shard_map.58), channel_id=1, replica_groups={{0,32,64,96},{1,33,65,97},{2,34,66,98},{3,35,67,99},{4,36,68,100},{5,37..., dimensions={0} | all-to-all | bytes 2621440 | tf_op jit(solution)/shard_map/all_to_all | solution.py:50
  75.4 0.4 reduce_sum.12
  75.7 0.7 collective-permute-start.5
  76.4 0.1 collective-permute-start.4
  76.5 6.8 %collective-permute-done.4 = bf16[640,256]{1,0:T(8,128)(2,1)S(1)} collective-permute-done((bf16[640,256]{1,0:T(8,128)(2,1)S(1)}, bf16[640,256]{1,0:T(8,128)(2,1)S(1)}, u32[]{:S(2)}, u32[]{:S(2)}) %collective-permute-start.4) | collective-permute-done | bytes 327712 | tf_op jit(solution)/shard_map/ppermute | solution.py:38
  83.3 0.1 add_convert_fusion
  83.4 1.2 broadcast_in_dim.2
  84.5 4.6 %all-to-all-start.2 = ((bf16[4,640,256]{2,1,0:T(8,128)(2,1)}), bf16[4,640,256]{2,1,0:T(8,128)(2,1)S(1)}, u32[]{:S(2)}, u32[]{:S(2)}) async-start(bf16[4,640,256]{2,1,0:T(8,128)(2,1)} %broadcast_in_dim.2), calls=%async_computation.2 | async-start | bytes 2621440 | tf_op jit(solution)/shard_map/all_to_all | solution.py:50
  89.2 0.6 dynamic_slice.4.damp_ref
  89.9 2.2 %collective-permute-start.8 = (bf16[256,1024]{1,0:T(8,128)(2,1)S(1)}, bf16[256,1024]{1,0:T(8,128)(2,1)S(1)}, u32[]{:S(2)}, u32[]{:S(2)}) collective-permute-start(bf16[256,1024]{1,0:T(8,128)(2,1)S(1)} %copy-done.1), channel_id=1, source_target_pairs={{0,0},{1,1},{2,2},{3,3},{4,4},{5,5},{6,6},{7,7},{8,8},{9,9},{10,10... | collective-permute-start | bytes 1572872 | tf_op jit(solution)/shard_map/ppermute | solution.py:38
  92.1 0.1 collective-permute-start.7
  92.2 1.6 %collective-permute-start.6 = (bf16[256,1024]{1,0:T(8,128)(2,1)S(1)}, bf16[256,1024]{1,0:T(8,128)(2,1)}, u32[]{:S(2)}, u32[]{:S(2)}) collective-permute-start(bf16[256,1024]{1,0:T(8,128)(2,1)S(1)} %copy-done.1), channel_id=1, source_target_pairs={{0,16},{1,17},{2,18},{3,19},{4,20},{5,21},{6,22},{7,23},{8,24},{9,... | collective-permute-start | bytes 1572872 | tf_op jit(solution)/shard_map/ppermute | solution.py:38
  93.8 6.6 %all-to-all-done.2.pieces_ref = bf16[4,640,256]{2,1,0:T(8,128)(2,1)S(1)} async-done(((bf16[4,640,256]{2,1,0:T(8,128)(2,1)}), bf16[4,640,256]{2,1,0:T(8,128)(2,1)S(1)}, u32[]{:S(2)}, u32[]{:S(2)}) %all-to-all-start.2) | async-done | bytes 1310752 | tf_op jit(solution)/shard_map/all_to_all | solution.py:50
  100.3 14.0 %shard_map.59.s_ref = bf16[1024,1024]{1,0:T(8,128)(2,1)S(1)} custom-call(f32[1]{0:T(128)} %dynamic_slice.4.damp_ref, bf16[4,640,256]{2,1,0:T(8,128)(2,1)S(1)} %all-to-all-done.2.pieces_ref), custom_call_target="tpu_custom_call" | custom-call | flops 17179869184 | bytes 4194304 | tf_op jit(solution)/shard_map/pallas_call | solution.py:234
  114.3 2.5 %shard_map.60.mine_ref = bf16[1024,1024]{1,0:T(8,128)(2,1)S(1)} custom-call(s32[2]{0:T(128)S(1)} %pad_add_fusion.place_ref, bf16[1024,1024]{1,0:T(8,128)(2,1)S(1)} %shard_map.59.s_ref, bf16[256,1024]{1,0:T(8,128)(2,1)} %collective-permute-done.6.w0, bf16[256,1024]{1,0:T(8,128)(2,1)S(1)} %copy-done.1, ...), custom_call_target="tpu_custom_call", output_to_operand_aliasing={{}: (1, {})} | custom-call | tf_op jit(solution)/shard_map/pallas_call | solution.py:268
  116.8 0.1 collective-permute-start.9
  116.9 4.1 %collective-permute-done.9.other_ref = bf16[1024,1024]{1,0:T(8,128)(2,1)S(1)} collective-permute-done((bf16[1024,1024]{1,0:T(8,128)(2,1)S(1)}, bf16[1024,1024]{1,0:T(8,128)(2,1)S(1)}, u32[]{:S(2)}, u32[]{:S(2)}) %collective-permute-start.9) | collective-permute-done | bytes 2097184 | tf_op jit(solution)/shard_map/ppermute | solution.py:38
  121.1 2.1 %shard_map.61 = bf16[256,1024]{1,0:T(8,128)(2,1)} custom-call(s32[2]{0:T(128)S(1)} %pad_add_fusion.place_ref, bf16[1024,1024]{1,0:T(8,128)(2,1)S(1)} %shard_map.60.mine_ref, bf16[1024,1024]{1,0:T(8,128)(2,1)S(1)} %collective-permute-done.9.other_ref), custom_call_target="tpu_custom_call" | custom-call | tf_op jit(solution)/shard_map/pallas_call | solution.py:292
  (17 shorter events, 0.3 us)
Async XLA Ops:
  0.0 3.0 %copy-start = (bf16[128,4096]{1,0:T(8,128)(2,1)S(1)}, bf16[128,4096]{1,0:T(8,128)(2,1)}, u32[]{:S(2)}) copy-start(bf16[128,4096]{1,0:T(8,128)(2,1)} %param.5) | copy-start | bytes 3145732
  0.0 3.0 %copy-start.2 = (s32[16]{0:T(128)S(1)}, s32[16]{0:T(128)}, u32[]{:S(2)}) copy-start(s32[16]{0:T(128)} %param.7) | copy-start | bytes 196
  3.4 2.3 %collective-permute-start = (bf16[16,16384]{1,0:T(8,128)(2,1)S(1)}, bf16[16,16384]{1,0:T(8,128)(2,1)S(1)}, u32[]{:S(2)}, u32[]{:S(2)}) collective-permute-start(bf16[16,16384]{1,0:T(8,128)(2,1)S(1)} %shard_map.55), channel_id=1, source_target_pairs={{0,16},{1,17},{2,18},{3,19},{4,20},{5,21},{6,22},{7,23},{8,24},{9,... | collective-permute-start | bytes 1572872 | tf_op jit(solution)/shard_map/ppermute | solution.py:38
  6.7 29.9 %all-to-all-start = ((bf16[4,128,1024]{2,1,0:T(8,128)(2,1)}), bf16[4,128,1024]{2,1,0:T(8,128)(2,1)S(1)}, u32[]{:S(2)}, u32[]{:S(2)}) async-start(bf16[4,128,1024]{2,1,0:T(8,128)(2,1)} %shard_map.56), calls=%async_computation | async-start | bytes 2097152 | tf_op jit(solution)/shard_map/all_to_all | solution.py:50
  37.3 6.8 %collective-permute-start.1 = (bf16[128,1024]{1,0:T(8,128)(2,1)S(1)}, bf16[128,1024]{1,0:T(8,128)(2,1)S(1)}, u32[]{:S(2)}, u32[]{:S(2)}) collective-permute-start(bf16[128,1024]{1,0:T(8,128)(2,1)S(1)} %get-tuple-element.17), channel_id=1, source_target_pairs={{0,1},{1,2},{2,3},{3,128},{4,5},{5,6},{6,7},{7,132},{8,9},{9,10},{... | collective-permute-start | bytes 786440 | tf_op jit(solution)/shard_map/ppermute | solution.py:38
  39.1 9.0 %collective-permute-start.2 = (bf16[128,1024]{1,0:T(8,128)(2,1)S(1)}, bf16[128,1024]{1,0:T(8,128)(2,1)S(1)}, u32[]{:S(2)}, u32[]{:S(2)}) collective-permute-start(bf16[128,1024]{1,0:T(8,128)(2,1)S(1)} %get-tuple-element.18), channel_id=1, source_target_pairs={{0,2},{1,131},{2,128},{3,1},{4,6},{5,135},{6,132},{7,5},{8,10},{9,... | collective-permute-start | bytes 786440 | tf_op jit(solution)/shard_map/ppermute | solution.py:38
  41.5 6.6 %collective-permute-start.3 = (bf16[128,1024]{1,0:T(8,128)(2,1)S(1)}, bf16[128,1024]{1,0:T(8,128)(2,1)S(1)}, u32[]{:S(2)}, u32[]{:S(2)}) collective-permute-start(bf16[128,1024]{1,0:T(8,128)(2,1)S(1)} %get-tuple-element.19), channel_id=1, source_target_pairs={{0,131},{1,0},{2,1},{3,2},{4,135},{5,4},{6,5},{7,6},{8,139},{9,8},... | collective-permute-start | bytes 786440 | tf_op jit(solution)/shard_map/ppermute | solution.py:38
  75.7 0.8 collective-permute-start.5
  76.4 6.9 %collective-permute-start.4 = (bf16[640,256]{1,0:T(8,128)(2,1)S(1)}, bf16[640,256]{1,0:T(8,128)(2,1)S(1)}, u32[]{:S(2)}, u32[]{:S(2)}) collective-permute-start(bf16[640,256]{1,0:T(8,128)(2,1)S(1)} %reduce_sum.12), channel_id=1, source_target_pairs={{0,2},{1,3},{2,128},{3,129},{4,6},{5,7},{6,132},{7,133},{8,10},{9,... | collective-permute-start | bytes 983048 | tf_op jit(solution)/shard_map/ppermute | solution.py:38
  83.4 5.8 %copy-start.3 = (f32[20]{0:T(128)S(1)}, f32[20]{0:T(128)}, u32[]{:S(2)}) copy-start(f32[20]{0:T(128)} %param.8) | copy-start | bytes 244
  83.4 6.5 %copy-start.1 = (bf16[256,1024]{1,0:T(8,128)(2,1)S(1)}, bf16[256,1024]{1,0:T(8,128)(2,1)}, u32[]{:S(2)}) copy-start(bf16[256,1024]{1,0:T(8,128)(2,1)} %w1.1) | copy-start | bytes 1572868
  84.5 15.8 %all-to-all-start.2 = ((bf16[4,640,256]{2,1,0:T(8,128)(2,1)}), bf16[4,640,256]{2,1,0:T(8,128)(2,1)S(1)}, u32[]{:S(2)}, u32[]{:S(2)}) async-start(bf16[4,640,256]{2,1,0:T(8,128)(2,1)} %broadcast_in_dim.2), calls=%async_computation.2 | async-start | bytes 2621440 | tf_op jit(solution)/shard_map/all_to_all | solution.py:50
  89.9 24.4 %collective-permute-start.8 = (bf16[256,1024]{1,0:T(8,128)(2,1)S(1)}, bf16[256,1024]{1,0:T(8,128)(2,1)S(1)}, u32[]{:S(2)}, u32[]{:S(2)}) collective-permute-start(bf16[256,1024]{1,0:T(8,128)(2,1)S(1)} %copy-done.1), channel_id=1, source_target_pairs={{0,0},{1,1},{2,2},{3,3},{4,4},{5,5},{6,6},{7,7},{8,8},{9,9},{10,10... | collective-permute-start | bytes 1572872 | tf_op jit(solution)/shard_map/ppermute | solution.py:38
  92.1 22.2 %collective-permute-start.7 = (bf16[256,1024]{1,0:T(8,128)(2,1)S(1)}, bf16[256,1024]{1,0:T(8,128)(2,1)}, u32[]{:S(2)}, u32[]{:S(2)}) collective-permute-start(bf16[256,1024]{1,0:T(8,128)(2,1)S(1)} %copy-done.1), channel_id=1, source_target_pairs={{0,48},{1,49},{2,50},{3,51},{4,52},{5,53},{6,54},{7,55},{8,56},{9,... | collective-permute-start | bytes 1572872 | tf_op jit(solution)/shard_map/ppermute | solution.py:38
  92.2 22.1 %collective-permute-start.6 = (bf16[256,1024]{1,0:T(8,128)(2,1)S(1)}, bf16[256,1024]{1,0:T(8,128)(2,1)}, u32[]{:S(2)}, u32[]{:S(2)}) collective-permute-start(bf16[256,1024]{1,0:T(8,128)(2,1)S(1)} %copy-done.1), channel_id=1, source_target_pairs={{0,16},{1,17},{2,18},{3,19},{4,20},{5,21},{6,22},{7,23},{8,24},{9,... | collective-permute-start | bytes 1572872 | tf_op jit(solution)/shard_map/ppermute | solution.py:38
  116.8 4.2 %collective-permute-start.9 = (bf16[1024,1024]{1,0:T(8,128)(2,1)S(1)}, bf16[1024,1024]{1,0:T(8,128)(2,1)S(1)}, u32[]{:S(2)}, u32[]{:S(2)}) collective-permute-start(bf16[1024,1024]{1,0:T(8,128)(2,1)S(1)} %shard_map.60.mine_ref), channel_id=1, source_target_pairs={{0,16},{1,17},{2,18},{3,19},{4,20},{5,21},{6,22},{7,23},{8,24},{9,... | collective-permute-start | bytes 6291464 | tf_op jit(solution)/shard_map/ppermute | solution.py:38

commit v7 on v5

--- a/solution.py
+++ b/solution.py
@@ -11,6 +11,7 @@
 F32 = jnp.float32
 MIB = 2 ** 20
 UPPER = [(r, c) for r in range(4) for c in range(r, 4)]
+FIRST, SECOND = UPPER[:5], UPPER[5:]
 SMEM = pl.BlockSpec(memory_space=pltpu.SMEM)
 VMEM = pl.BlockSpec(memory_space=pltpu.VMEM)
 
@@ -114,20 +115,35 @@
 
 
 def cov_kernel(scale, place_ref, *refs):
-    pieces, chunks, (all_ref, panel_ref) = refs[:4], refs[4:8], refs[8:]
+    pieces, (keep_a, send_a, keep_b, send_b), (all_ref, full_ref) = refs[:4], refs[4:8], refs[8:]
     count, size = pieces[0].shape
     tile, sub = size // 4, size // 16
     for k, piece in enumerate(pieces):
         all_ref[k * count:(k + 1) * count, :] = piece[...]
     for r in range(4):
         cols = all_ref[:, r * tile:(r + 1) * tile]
-        panel_ref[:, r * tile:] = gram(cols, all_ref[:, r * tile:]) * scale
-        for k, chunk in enumerate(chunks):
-            start = pl.multiple_of(lax.rem(place_ref[0] + k * place_ref[1], 4) * sub, sub)
-            for t, (row, c) in enumerate(UPPER):
-                if row == r:
-                    chunk[t * sub:(t + 1) * sub, :] = panel_ref[
-                        pl.ds(start, sub), c * tile:(c + 1) * tile].astype(BF16)
+        full_ref[r * tile:(r + 1) * tile, r * tile:] = (gram(cols, all_ref[:, r * tile:]) * scale).astype(BF16)
+    mine = place_ref[1]
+
+    def put(out, slot, quarter, tiles):
+        start = pl.multiple_of(quarter * sub, sub)
+        for i, (r, c) in enumerate(tiles):
+            at = (slot * len(tiles) + i) * sub
+            out[at:at + sub, :] = full_ref[pl.ds(r * tile + start, sub), c * tile:(c + 1) * tile]
+
+    @pl.when(place_ref[0] == 0)
+    def _():
+        for out, masks, tiles in (
+            (keep_a, (0, 3), FIRST), (send_a, (1, 2), FIRST), (keep_b, (0, 1), SECOND), (send_b, (3, 2), SECOND)
+        ):
+            for slot, mask in enumerate(masks):
+                put(out, slot, lax.bitwise_xor(mine, jnp.int32(mask)), tiles)
+
+    @pl.when(place_ref[0] == 1)
+    def _():
+        for out in (keep_a, send_a, keep_b, send_b):
+            for slot, tiles in enumerate((FIRST, SECOND)):
+                put(out, slot, mine, tiles)
 
 
 def cov(place, pieces, scale):
@@ -138,12 +154,12 @@
         out_shape=(jax.ShapeDtypeStruct((len(UPPER) * sub, tile), BF16),) * 4,
         in_specs=[SMEM] + [VMEM] * 4,
         out_specs=(VMEM,) * 4,
-        scratch_shapes=[pltpu.VMEM((4 * count, size), BF16), pltpu.VMEM((tile, size), F32)],
+        scratch_shapes=[pltpu.VMEM((4 * count, size), BF16), pltpu.VMEM((size, size), BF16)],
         compiler_params=pltpu.CompilerParams(vmem_limit_bytes=16 * MIB),
     )(place, *pieces)
 
 
-def rounds_kernel(place_ref, damp_ref, p0, p1, p2, p3, out_ref, a_ref, x_ref, xb_ref, p_ref):
+def rounds_kernel(place_ref, damp_ref, piece, r1a, r1b, r2a, r2b, out_ref, a_ref, x_ref, xb_ref, p_ref):
     size = out_ref.shape[0]
     tile = size // 4
     sub = tile // 4
@@ -155,10 +171,14 @@
         for r in range(c):
             ref[blocks[c], blocks[r]] = value[blocks[r], :].T
 
-    for k, piece in enumerate((p0, p1, p2, p3)):
-        start = pl.multiple_of(lax.rem(base + 4 - k, 4) * sub, sub)
-        for t, (r, c) in enumerate(UPPER):
-            a_ref[pl.ds(r * tile + start, sub), blocks[c]] = piece[t * sub:(t + 1) * sub, :]
+    for source, part, mask, tiles in (
+        (piece, 0, 0, FIRST), (r1a, 0, 3, FIRST), (r2a, 0, 1, FIRST), (r2a, 1, 2, FIRST),
+        (piece, 1, 0, SECOND), (r1b, 0, 1, SECOND), (r2b, 0, 3, SECOND), (r2b, 1, 2, SECOND),
+    ):
+        start = pl.multiple_of(lax.bitwise_xor(base, jnp.int32(mask)) * sub, sub)
+        for i, (r, c) in enumerate(tiles):
+            at = (part * 5 + i) * sub
+            a_ref[pl.ds(r * tile + start, sub), blocks[c]] = source[at:at + sub, :]
     row = lax.broadcasted_iota(jnp.int32, (tile, tile), 0)
     col = lax.broadcasted_iota(jnp.int32, (tile, tile), 1)
     eye = row == col
@@ -204,7 +224,7 @@
     return pl.pallas_call(
         rounds_kernel,
         out_shape=jax.ShapeDtypeStruct((size, size), BF16),
-        in_specs=[SMEM, SMEM] + [VMEM] * 4,
+        in_specs=[SMEM, SMEM] + [VMEM] * 5,
         out_specs=VMEM,
         scratch_shapes=[
             pltpu.VMEM((size, size), BF16),
@@ -219,9 +239,9 @@
 
 def mix_kernel(place_ref, s_ref, w0, w1, w2, w3, out_ref, t_ref):
     tile, size = w0.shape
-    half = place_ref[2]
-
-    @pl.when(place_ref[1] == 1)
+    half = place_ref[1]
+
+    @pl.when(place_ref[0] == 1)
     def _():
         for i in range(2):
             rows = pl.ds(pl.multiple_of((2 * half + i) * tile, tile), tile)
@@ -249,11 +269,11 @@
 def last_kernel(place_ref, mine_ref, other_ref, out_ref):
     tile = out_ref.shape[0]
 
-    @pl.when(place_ref[1] == 0)
+    @pl.when(place_ref[0] == 0)
     def _():
         out_ref[...] = dot(other_ref[:tile, :], mine_ref[...]).astype(BF16)
 
-    @pl.when(place_ref[1] == 1)
+    @pl.when(place_ref[0] == 1)
     def _():
         out_ref[...] = dot(mine_ref[tile:2 * tile, :], other_ref[...]).astype(BF16)
 
@@ -312,14 +332,22 @@
             else (zh, y, 1, (x + k) % 4, zl),
         )
 
-    chunks = cov(jnp.stack([jnp.where(is_g, y, x), 1 - core]), samples, scale)
-    total = chunks[0].astype(F32)
-    for k in (1, 2, 3):
-        total += moved(
-            chunks[k],
-            lambda zh, y, c, x, zl: (zh, (y + k) % 4, 0, x, zl) if c == 0 else (zh, y, 1, x, (zl + k) % 4),
-        ).astype(F32)
-    part = total.astype(BF16)
+    keep_a, send_a, keep_b, send_b = cov(jnp.stack([core, jnp.where(is_g, y, x)]), samples, scale)
+    half = keep_a.shape[0] // 2
+    sum_a = keep_a.astype(F32) + moved(
+        send_a, lambda zh, y, c, x, zl: (zh, y ^ 1, 0, x, zl) if c == 0 else (zh, y, 1, x, zl ^ 1)).astype(F32)
+    sum_b = keep_b.astype(F32) + moved(
+        send_b, lambda zh, y, c, x, zl: (zh, y ^ 3, 0, x, zl) if c == 0 else None).astype(F32)
+    on_a = moved(
+        jnp.where(is_g, sum_a[half:], sum_a[:half]).astype(BF16),
+        lambda zh, y, c, x, zl: (zh, y ^ 3, 0, x, zl) if c == 0 else (zh, y, 1, x, zl ^ 2))
+    on_b = moved(
+        jnp.where(is_g, sum_b[half:], sum_a[half:]).astype(BF16),
+        lambda zh, y, c, x, zl: (zh, y ^ 1, 0, x, zl) if c == 0 else (zh, y, 1, x, zl ^ 2))
+    part = jnp.concatenate([
+        sum_a[:half] + on_a.astype(F32),
+        jnp.where(is_g, sum_b[:half], sum_a[half:]) + on_b.astype(F32),
+    ]).astype(BF16)
 
     def beside(zh, zl, by):
         z = (zh * 4 + zl + by) % 8
@@ -331,12 +359,14 @@
                   else None)
     piece = (here.astype(F32) + there.astype(F32)).astype(BF16)
 
-    pieces = [piece]
-    for k in (1, 2, 3):
-        pieces.append(moved(
-            piece,
-            lambda zh, y, c, x, zl: (zh, (y + k) % 4, 0, x, zl) if c == 0 else (zh, y, 1, (x + k) % 4, zl),
-        ))
+    def swapped(value, mask):
+        return moved(
+            value, lambda zh, y, c, x, zl: (zh, y ^ mask, 0, x, zl) if c == 0 else (zh, y, 1, x ^ mask, zl))
+
+    r1a, r1b = swapped(piece[:half], 3), swapped(piece[half:], 1)
+    r2a = swapped(jnp.concatenate([piece[:half], r1a]), 1)
+    r2b = swapped(jnp.concatenate([piece[half:], r1b]), 3)
+    pieces = [piece, r1a, r1b, r2a, r2b]
 
     own_w, _ = lax.optimization_barrier((weight_grad, piece))
     weights = [
@@ -345,8 +375,8 @@
         moved(own_w, lambda zh, y, c, x, zl: (zh, y ^ 1, 1, x, zl) if c == 1 else None),
     ]
     damp = pick(damping, jnp.where(is_g, BLOCKS_A + o, zh * 2 + y // 2)).reshape(1)
-    place = jnp.stack([jnp.where(is_g, y, x), core, y % 2])
-    inverse, *weights = lax.optimization_barrier((rounds(place, damp, pieces), *weights))
+    place = jnp.stack([core, y % 2])
+    inverse, *weights = lax.optimization_barrier((rounds(jnp.where(is_g, y, x).astype(jnp.int32).reshape(1), damp, pieces), *weights))
     weights.insert(1, weight_grad)
 
     mine = mix(place, inverse, weights)

time: 110 us -> 117 us (1.064)
  starting transfers between devices: 47 us -> 51.8 us
  waiting for transfers between devices: 33.8 us -> 37.7 us
  Pallas kernels: 23.1 us -> 20.4 us
    ppermute x21 -> x23, starting transfers between devices: 47 us -> 51.8 us  [moved(): return lax.ppermute(value, ('dp', 'owner'), pairs)]
    ppermute x21 -> x23, waiting for transfers between devices: 33.8 us -> 37.7 us  [moved(): return lax.ppermute(value, ('dp', 'owner'), pairs)]
  transfers between devices with their start and end apart: 21 -> 23, of which waited for: 9 -> 11; matrix products, arithmetic and copies ran while one was open for 2% -> 2% of each run, Pallas kernels for 15% -> 12%
where the time goes in v7:
time: 117 us; the launch traced here: 116 us
  starting transfers between devices  51.8 us (44%)
  waiting for transfers between devices  37.7 us (32%)
  Pallas kernels  20.4 us (17%)
  matrix products  3.28 us (3%)
  other arithmetic  2.23 us (2%)
    ppermute x23, starting transfers between devices, moved(): return lax.ppermute(value, ('dp', 'owner'), pairs)  51.8 us
    ppermute x23, waiting for transfers between devices, moved(): return lax.ppermute(value, ('dp', 'owner'), pairs)  37.7 us
    pallas_call x1, Pallas kernels, rounds(): pl.pallas_call(rounds_kernel, out_shape=jax.ShapeDtypeStruct((size, size)...  14.2 us
    dot_general x2, matrix products, dot(): return jnp.dot(a, b, preferred_element_type=F32)  3.28 us
  transfers between devices with their start and end apart: 23, of which 11 were waited for; matrix products, arithmetic and copies ran while one was open for 2% of the time, Pallas kernels for 12%

profile of v7, /device:TPU:33, one launch (start us, length us, event | category | flops | bytes accessed | tf_op | source)
XLA Modules:
  0.0 116.4 jit_solution(1392120356497214590)
XLA Ops:
  0.0 3.0 %convolution_convert_fusion.g_ref.mine_ref = bf16[16,16384]{1,0:T(8,128)(2,1)S(1)} fusion(bf16[128,16384]{1,0:T(8,128)(2,1)} %param.6, s32[16]{0:T(128)} %param.7), kind=kOutput, calls=%fused_computation | convolution fusion | flops 67373056 | bytes 4718656 | tf_op jit(solution)/shard_map/dot_general | solution.py:20
  3.4 0.8 collective-permute-start
  4.1 1.5 %collective-permute-done.other_ref = bf16[16,16384]{1,0:T(8,128)(2,1)S(1)} collective-permute-done((bf16[16,16384]{1,0:T(8,128)(2,1)S(1)}, bf16[16,16384]{1,0:T(8,128)(2,1)S(1)}, u32[]{:S(2)}, u32[]{:S(2)}) %collective-permute-start) | collective-permute-done | bytes 524320 | tf_op jit(solution)/shard_map/ppermute | solution.py:39
  5.7 0.7 fusion.5
  6.4 7.0 %collective-permute-start.4 = (bf16[32,2048]{1,0:T(8,128)(2,1)}, bf16[32,2048]{1,0:T(8,128)(2,1)}, u32[]{:S(2)}, u32[]{:S(2)}) collective-permute-start(bf16[32,2048]{1,0:T(8,128)(2,1)} %get-tuple-element.49), channel_id=1, source_target_pairs={{0,0},{1,1},{2,2},{3,3},{4,4},{5,5},{6,6},{7,7},{8,8},{9,9},{10,10... | collective-permute-start | bytes 393224 | tf_op jit(solution)/shard_map/ppermute | solution.py:39
  15.6 1.8 %collective-permute-done.4 = bf16[32,2048]{1,0:T(8,128)(2,1)} collective-permute-done((bf16[32,2048]{1,0:T(8,128)(2,1)}, bf16[32,2048]{1,0:T(8,128)(2,1)}, u32[]{:S(2)}, u32[]{:S(2)}) %collective-permute-start.4) | collective-permute-done | bytes 131104 | tf_op jit(solution)/shard_map/ppermute | solution.py:39
  17.5 0.9 fusion.3
  18.3 4.6 %collective-permute-start.5 = (bf16[64,1024]{1,0:T(8,128)(2,1)S(1)}, bf16[64,1024]{1,0:T(8,128)(2,1)S(1)}, u32[]{:S(2)}, u32[]{:S(2)}) collective-permute-start(bf16[64,1024]{1,0:T(8,128)(2,1)S(1)} %get-tuple-element.47), channel_id=1, source_target_pairs={{0,0},{1,1},{2,2},{3,3},{4,4},{5,5},{6,6},{7,7},{8,8},{9,9},{10,10... | collective-permute-start | bytes 393224 | tf_op jit(solution)/shard_map/ppermute | solution.py:39
  23.1 2.2 %collective-permute-done.5.come_ref = bf16[64,1024]{1,0:T(8,128)(2,1)S(1)} collective-permute-done((bf16[64,1024]{1,0:T(8,128)(2,1)S(1)}, bf16[64,1024]{1,0:T(8,128)(2,1)S(1)}, u32[]{:S(2)}, u32[]{:S(2)}) %collective-permute-start.5) | collective-permute-done | bytes 131104 | tf_op jit(solution)/shard_map/ppermute | solution.py:39
  26.0 1.3 %collective-permute-start.6 = (bf16[128,1024]{1,0:T(8,128)(2,1)S(1)}, bf16[128,1024]{1,0:T(8,128)(2,1)S(1)}, u32[]{:S(2)}, u32[]{:S(2)}) collective-permute-start(bf16[128,1024]{1,0:T(8,128)(2,1)S(1)} %get-tuple-element.29), channel_id=1, source_target_pairs={{0,1},{1,2},{2,3},{3,128},{4,5},{5,6},{6,7},{7,132},{8,9},{9,10},{... | collective-permute-start | bytes 786440 | tf_op jit(solution)/shard_map/ppermute | solution.py:39
  27.3 2.5 %collective-permute-start.7 = (bf16[128,1024]{1,0:T(8,128)(2,1)S(1)}, bf16[128,1024]{1,0:T(8,128)(2,1)S(1)}, u32[]{:S(2)}, u32[]{:S(2)}) collective-permute-start(bf16[128,1024]{1,0:T(8,128)(2,1)S(1)} %get-tuple-element.30), channel_id=1, source_target_pairs={{0,2},{1,131},{2,128},{3,1},{4,6},{5,135},{6,132},{7,5},{8,10},{9,... | collective-permute-start | bytes 786440 | tf_op jit(solution)/shard_map/ppermute | solution.py:39
  29.7 1.2 collective-permute-start.8
  30.9 1.5 %collective-permute-done.6.refs_2_ = bf16[128,1024]{1,0:T(8,128)(2,1)S(1)} collective-permute-done((bf16[128,1024]{1,0:T(8,128)(2,1)S(1)}, bf16[128,1024]{1,0:T(8,128)(2,1)S(1)}, u32[]{:S(2)}, u32[]{:S(2)}) %collective-permute-start.6) | collective-permute-done | bytes 262176 | tf_op jit(solution)/shard_map/ppermute | solution.py:39
  32.5 3.8 %collective-permute-done.7.refs_3_ = bf16[128,1024]{1,0:T(8,128)(2,1)S(1)} collective-permute-done((bf16[128,1024]{1,0:T(8,128)(2,1)S(1)}, bf16[128,1024]{1,0:T(8,128)(2,1)S(1)}, u32[]{:S(2)}, u32[]{:S(2)}) %collective-permute-start.7) | collective-permute-done | bytes 262176 | tf_op jit(solution)/shard_map/ppermute | solution.py:39
  36.3 1.5 %shard_map.58 = (bf16[640,256]{1,0:T(8,128)(2,1)S(1)}, bf16[640,256]{1,0:T(8,128)(2,1)S(1)}, bf16[640,256]{1,0:T(8,128)(2,1)S(1)}, bf16[640,256]{1,0:T(8,128)(2,1)S(1)}) custom-call(s32[2]{0:T(128)S(1)} %pad_add_fusion.1.refs_0_, bf16[128,1024]{1,0:T(8,128)(2,1)S(1)} %get-tuple-element.28.refs_1_, bf16[128,1024]{1,0:T(8,128)(2,1)S(1)} %collective-permute-done.6.refs_2_, ...), custom_call_target="tpu_custom_call" | custom-call | tf_op jit(solution)/shard_map/pallas_call | solution.py:152
  38.9 4.9 %collective-permute-done.9 = bf16[640,256]{1,0:T(8,128)(2,1)S(1)} collective-permute-done((bf16[640,256]{1,0:T(8,128)(2,1)S(1)}, bf16[640,256]{1,0:T(8,128)(2,1)S(1)}, u32[]{:S(2)}, u32[]{:S(2)}) %collective-permute-start.9) | collective-permute-done | bytes 327712 | tf_op jit(solution)/shard_map/ppermute | solution.py:39
  44.0 1.4 %collective-permute-start.10 = (bf16[320,256]{1,0:T(8,128)(2,1)S(1)}, bf16[320,256]{1,0:T(8,128)(2,1)S(1)}, u32[]{:S(2)}, u32[]{:S(2)}) collective-permute-start(bf16[320,256]{1,0:T(8,128)(2,1)S(1)} %get-tuple-element.43), channel_id=1, source_target_pairs={{0,96},{1,97},{2,98},{3,99},{4,100},{5,101},{6,102},{7,103},{8,104... | collective-permute-start | bytes 491528 | tf_op jit(solution)/shard_map/ppermute | solution.py:39
  45.5 1.0 collective-permute-start.12
  46.5 4.8 %collective-permute-done.10 = bf16[320,256]{1,0:T(8,128)(2,1)S(1)} collective-permute-done((bf16[320,256]{1,0:T(8,128)(2,1)S(1)}, bf16[320,256]{1,0:T(8,128)(2,1)S(1)}, u32[]{:S(2)}, u32[]{:S(2)}) %collective-permute-start.10) | collective-permute-done | bytes 163872 | tf_op jit(solution)/shard_map/ppermute | solution.py:39
  51.2 1.8 %collective-permute-done.12 = bf16[320,256]{1,0:T(8,128)(2,1)S(1)} collective-permute-done((bf16[320,256]{1,0:T(8,128)(2,1)S(1)}, bf16[320,256]{1,0:T(8,128)(2,1)S(1)}, u32[]{:S(2)}, u32[]{:S(2)}) %collective-permute-start.12) | collective-permute-done | bytes 163872 | tf_op jit(solution)/shard_map/ppermute | solution.py:39
  53.1 0.7 collective-permute-start.14
  53.9 7.7 %collective-permute-done.13 = bf16[640,256]{1,0:T(8,128)(2,1)S(1)} collective-permute-done((bf16[640,256]{1,0:T(8,128)(2,1)S(1)}, bf16[640,256]{1,0:T(8,128)(2,1)S(1)}, u32[]{:S(2)}, u32[]{:S(2)}) %collective-permute-start.13) | collective-permute-done | bytes 327712 | tf_op jit(solution)/shard_map/ppermute | solution.py:39
  61.8 1.5 %collective-permute-start.15 = (bf16[320,256]{1,0:T(8,128)(2,1)S(1)}, bf16[320,256]{1,0:T(8,128)(2,1)S(1)}, u32[]{:S(2)}, u32[]{:S(2)}) collective-permute-start(bf16[320,256]{1,0:T(8,128)(2,1)S(1)} %get-tuple-element.46), channel_id=1, source_target_pairs={{0,96},{1,97},{2,98},{3,99},{4,100},{5,101},{6,102},{7,103},{8,104... | collective-permute-start | bytes 491528 | tf_op jit(solution)/shard_map/ppermute | solution.py:39
  63.5 3.7 %collective-permute-done.15.r1a = bf16[320,256]{1,0:T(8,128)(2,1)S(1)} collective-permute-done((bf16[320,256]{1,0:T(8,128)(2,1)S(1)}, bf16[320,256]{1,0:T(8,128)(2,1)S(1)}, u32[]{:S(2)}, u32[]{:S(2)}) %collective-permute-start.15) | collective-permute-done | bytes 163872 | tf_op jit(solution)/shard_map/ppermute | solution.py:39
  67.4 1.4 %collective-permute-start.18 = (bf16[640,256]{1,0:T(8,128)(2,1)S(1)}, bf16[640,256]{1,0:T(8,128)(2,1)S(1)}, u32[]{:S(2)}, u32[]{:S(2)}) collective-permute-start(bf16[640,256]{1,0:T(8,128)(2,1)S(1)} %pad_maximum_fusion.2), channel_id=1, source_target_pairs={{0,96},{1,97},{2,98},{3,99},{4,100},{5,101},{6,102},{7,103},{8,104... | collective-permute-start | bytes 983048 | tf_op jit(solution)/shard_map/ppermute | solution.py:39
  69.6 2.2 %collective-permute-start.21 = (bf16[256,1024]{1,0:T(8,128)(2,1)S(1)}, bf16[256,1024]{1,0:T(8,128)(2,1)S(1)}, u32[]{:S(2)}, u32[]{:S(2)}) collective-permute-start(bf16[256,1024]{1,0:T(8,128)(2,1)S(1)} %copy-done.1), channel_id=1, source_target_pairs={{0,0},{1,1},{2,2},{3,3},{4,4},{5,5},{6,6},{7,7},{8,8},{9,9},{10,10... | collective-permute-start | bytes 1572872 | tf_op jit(solution)/shard_map/ppermute | solution.py:39
  71.8 19.0 %collective-permute-start.20 = (bf16[256,1024]{1,0:T(8,128)(2,1)S(1)}, bf16[256,1024]{1,0:T(8,128)(2,1)S(1)}, u32[]{:S(2)}, u32[]{:S(2)}) collective-permute-start(bf16[256,1024]{1,0:T(8,128)(2,1)S(1)} %copy-done.1), channel_id=1, source_target_pairs={{0,48},{1,49},{2,50},{3,51},{4,52},{5,53},{6,54},{7,55},{8,56},{9,... | collective-permute-start | bytes 1572872 | tf_op jit(solution)/shard_map/ppermute | solution.py:39
  91.0 14.2 %shard_map.59.s_ref = bf16[1024,1024]{1,0:T(8,128)(2,1)S(1)} custom-call(s32[1]{0:T(128)} %bitcast.2.place_ref, f32[1]{0:T(128)} %dynamic_slice.16.damp_ref, bf16[640,256]{1,0:T(8,128)(2,1)S(1)} %add_convert_fusion.piece, bf16[320,256]{1,0:T(8,128)(2,1)S(1)} %collective-permute-done.15.r1a, bf16[320,256]{1,0:T(8,128)(2,1)S(1)} %collective-permute-done.16.r1b, ...), custom_call_target="tpu_custom_call" | custom-call | flops 17179869184 | bytes 4194304 | tf_op jit(solution)/shard_map/pallas_call | solution.py:224
  105.3 1.8 %shard_map.60.mine_ref = bf16[1024,1024]{1,0:T(8,128)(2,1)S(1)} custom-call(s32[2]{0:T(128)S(1)} %pad_add_fusion.place_ref, bf16[1024,1024]{1,0:T(8,128)(2,1)S(1)} %shard_map.59.s_ref, bf16[256,1024]{1,0:T(8,128)(2,1)S(1)} %collective-permute-done.19.w0, bf16[256,1024]{1,0:T(8,128)(2,1)S(1)} %copy-done.1, ...), custom_call_target="tpu_custom_call", output_to_operand_aliasing={{}: (1, {})} | custom-call | tf_op jit(solution)/shard_map/pallas_call | solution.py:258
  107.1 3.4 %collective-permute-start.22 = (bf16[1024,1024]{1,0:T(8,128)(2,1)S(1)}, bf16[1024,1024]{1,0:T(8,128)(2,1)S(1)}, u32[]{:S(2)}, u32[]{:S(2)}) collective-permute-start(bf16[1024,1024]{1,0:T(8,128)(2,1)S(1)} %shard_map.60.mine_ref), channel_id=1, source_target_pairs={{0,16},{1,17},{2,18},{3,19},{4,20},{5,21},{6,22},{7,23},{8,24},{9,... | collective-permute-start | bytes 6291464 | tf_op jit(solution)/shard_map/ppermute | solution.py:39
  110.6 3.8 %collective-permute-done.22.other_ref = bf16[1024,1024]{1,0:T(8,128)(2,1)S(1)} collective-permute-done((bf16[1024,1024]{1,0:T(8,128)(2,1)S(1)}, bf16[1024,1024]{1,0:T(8,128)(2,1)S(1)}, u32[]{:S(2)}, u32[]{:S(2)}) %collective-permute-start.22) | collective-permute-done | bytes 2097184 | tf_op jit(solution)/shard_map/ppermute | solution.py:39
  114.4 2.1 %shard_map.61 = bf16[256,1024]{1,0:T(8,128)(2,1)} custom-call(s32[2]{0:T(128)S(1)} %pad_add_fusion.place_ref, bf16[1024,1024]{1,0:T(8,128)(2,1)S(1)} %shard_map.60.mine_ref, bf16[1024,1024]{1,0:T(8,128)(2,1)S(1)} %collective-permute-done.22.other_ref), custom_call_target="tpu_custom_call" | custom-call | tf_op jit(solution)/shard_map/pallas_call | solution.py:282
  (47 shorter events, 6.3 us)
Async XLA Ops:
  0.0 3.0 %copy-start = (bf16[128,4096]{1,0:T(8,128)(2,1)S(1)}, bf16[128,4096]{1,0:T(8,128)(2,1)}, u32[]{:S(2)}) copy-start(bf16[128,4096]{1,0:T(8,128)(2,1)} %param.5) | copy-start | bytes 3145732
  0.0 3.0 %copy-start.2 = (s32[16]{0:T(128)S(1)}, s32[16]{0:T(128)}, u32[]{:S(2)}) copy-start(s32[16]{0:T(128)} %param.7) | copy-start | bytes 196
  3.4 2.3 %collective-permute-start = (bf16[16,16384]{1,0:T(8,128)(2,1)S(1)}, bf16[16,16384]{1,0:T(8,128)(2,1)S(1)}, u32[]{:S(2)}, u32[]{:S(2)}) collective-permute-start(bf16[16,16384]{1,0:T(8,128)(2,1)S(1)} %shard_map.55), channel_id=1, source_target_pairs={{0,16},{1,17},{2,18},{3,19},{4,20},{5,21},{6,22},{7,23},{8,24},{9,... | collective-permute-start | bytes 1572872 | tf_op jit(solution)/shard_map/ppermute | solution.py:39
  6.4 11.1 %collective-permute-start.4 = (bf16[32,2048]{1,0:T(8,128)(2,1)}, bf16[32,2048]{1,0:T(8,128)(2,1)}, u32[]{:S(2)}, u32[]{:S(2)}) collective-permute-start(bf16[32,2048]{1,0:T(8,128)(2,1)} %get-tuple-element.49), channel_id=1, source_target_pairs={{0,0},{1,1},{2,2},{3,3},{4,4},{5,5},{6,6},{7,7},{8,8},{9,9},{10,10... | collective-permute-start | bytes 393224 | tf_op jit(solution)/shard_map/ppermute | solution.py:39
  13.5 9.6 %collective-permute-start.1 = (bf16[128,1024]{1,0:T(8,128)(2,1)S(1)}, bf16[128,1024]{1,0:T(8,128)(2,1)S(1)}, u32[]{:S(2)}, u32[]{:S(2)}) collective-permute-start(bf16[128,1024]{1,0:T(8,128)(2,1)S(1)} %get-tuple-element.25), channel_id=1, source_target_pairs={{0,4},{1,5},{2,6},{3,7},{4,8},{5,9},{6,10},{7,11},{8,12},{9,13},{1... | collective-permute-start | bytes 786440 | tf_op jit(solution)/shard_map/ppermute | solution.py:39
  14.2 8.9 %collective-permute-start.2 = (bf16[128,1024]{1,0:T(8,128)(2,1)S(1)}, bf16[128,1024]{1,0:T(8,128)(2,1)S(1)}, u32[]{:S(2)}, u32[]{:S(2)}) collective-permute-start(bf16[128,1024]{1,0:T(8,128)(2,1)S(1)} %get-tuple-element.26), channel_id=1, source_target_pairs={{0,8},{1,9},{2,10},{3,11},{4,12},{5,13},{6,14},{7,15},{8,0},{9,1},... | collective-permute-start | bytes 786440 | tf_op jit(solution)/shard_map/ppermute | solution.py:39
  14.9 8.2 %collective-permute-start.3 = (bf16[128,1024]{1,0:T(8,128)(2,1)S(1)}, bf16[128,1024]{1,0:T(8,128)(2,1)S(1)}, u32[]{:S(2)}, u32[]{:S(2)}) collective-permute-start(bf16[128,1024]{1,0:T(8,128)(2,1)S(1)} %get-tuple-element.27), channel_id=1, source_target_pairs={{0,12},{1,13},{2,14},{3,15},{4,0},{5,1},{6,2},{7,3},{8,4},{9,5},{1... | collective-permute-start | bytes 786440 | tf_op jit(solution)/shard_map/ppermute | solution.py:39
  18.3 7.0 %collective-permute-start.5 = (bf16[64,1024]{1,0:T(8,128)(2,1)S(1)}, bf16[64,1024]{1,0:T(8,128)(2,1)S(1)}, u32[]{:S(2)}, u32[]{:S(2)}) collective-permute-start(bf16[64,1024]{1,0:T(8,128)(2,1)S(1)} %get-tuple-element.47), channel_id=1, source_target_pairs={{0,0},{1,1},{2,2},{3,3},{4,4},{5,5},{6,6},{7,7},{8,8},{9,9},{10,10... | collective-permute-start | bytes 393224 | tf_op jit(solution)/shard_map/ppermute | solution.py:39
  26.0 6.5 %collective-permute-start.6 = (bf16[128,1024]{1,0:T(8,128)(2,1)S(1)}, bf16[128,1024]{1,0:T(8,128)(2,1)S(1)}, u32[]{:S(2)}, u32[]{:S(2)}) collective-permute-start(bf16[128,1024]{1,0:T(8,128)(2,1)S(1)} %get-tuple-element.29), channel_id=1, source_target_pairs={{0,1},{1,2},{2,3},{3,128},{4,5},{5,6},{6,7},{7,132},{8,9},{9,10},{... | collective-permute-start | bytes 786440 | tf_op jit(solution)/shard_map/ppermute | solution.py:39
  27.3 9.0 %collective-permute-start.7 = (bf16[128,1024]{1,0:T(8,128)(2,1)S(1)}, bf16[128,1024]{1,0:T(8,128)(2,1)S(1)}, u32[]{:S(2)}, u32[]{:S(2)}) collective-permute-start(bf16[128,1024]{1,0:T(8,128)(2,1)S(1)} %get-tuple-element.30), channel_id=1, source_target_pairs={{0,2},{1,131},{2,128},{3,1},{4,6},{5,135},{6,132},{7,5},{8,10},{9,... | collective-permute-start | bytes 786440 | tf_op jit(solution)/shard_map/ppermute | solution.py:39
  29.7 6.6 %collective-permute-start.8 = (bf16[128,1024]{1,0:T(8,128)(2,1)S(1)}, bf16[128,1024]{1,0:T(8,128)(2,1)S(1)}, u32[]{:S(2)}, u32[]{:S(2)}) collective-permute-start(bf16[128,1024]{1,0:T(8,128)(2,1)S(1)} %get-tuple-element.31), channel_id=1, source_target_pairs={{0,131},{1,0},{2,1},{3,2},{4,135},{5,4},{6,5},{7,6},{8,139},{9,8},... | collective-permute-start | bytes 786440 | tf_op jit(solution)/shard_map/ppermute | solution.py:39
  37.8 6.0 %collective-permute-start.9 = (bf16[640,256]{1,0:T(8,128)(2,1)S(1)}, bf16[640,256]{1,0:T(8,128)(2,1)S(1)}, u32[]{:S(2)}, u32[]{:S(2)}) collective-permute-start(bf16[640,256]{1,0:T(8,128)(2,1)S(1)} %get-tuple-element.33), channel_id=1, source_target_pairs={{0,32},{1,33},{2,34},{3,35},{4,36},{5,37},{6,38},{7,39},{8,40},{9,... | collective-permute-start | bytes 983048 | tf_op jit(solution)/shard_map/ppermute | solution.py:39
  38.2 5.7 %collective-permute-start.11 = (bf16[640,256]{1,0:T(8,128)(2,1)S(1)}, bf16[640,256]{1,0:T(8,128)(2,1)S(1)}, u32[]{:S(2)}, u32[]{:S(2)}) collective-permute-start(bf16[640,256]{1,0:T(8,128)(2,1)S(1)} %get-tuple-element.35), channel_id=1, source_target_pairs={{0,96},{1,97},{2,98},{3,99},{4,100},{5,101},{6,102},{7,103},{8,104... | collective-permute-start | bytes 983048 | tf_op jit(solution)/shard_map/ppermute | solution.py:39
  43.8 25.1 %copy-start.3 = (f32[20]{0:T(128)S(1)}, f32[20]{0:T(128)}, u32[]{:S(2)}) copy-start(f32[20]{0:T(128)} %param.8) | copy-start | bytes 244
  43.8 25.8 %copy-start.1 = (bf16[256,1024]{1,0:T(8,128)(2,1)S(1)}, bf16[256,1024]{1,0:T(8,128)(2,1)}, u32[]{:S(2)}) copy-start(bf16[256,1024]{1,0:T(8,128)(2,1)} %w1.1) | copy-start | bytes 1572868
  44.0 7.2 %collective-permute-start.10 = (bf16[320,256]{1,0:T(8,128)(2,1)S(1)}, bf16[320,256]{1,0:T(8,128)(2,1)S(1)}, u32[]{:S(2)}, u32[]{:S(2)}) collective-permute-start(bf16[320,256]{1,0:T(8,128)(2,1)S(1)} %get-tuple-element.43), channel_id=1, source_target_pairs={{0,96},{1,97},{2,98},{3,99},{4,100},{5,101},{6,102},{7,103},{8,104... | collective-permute-start | bytes 491528 | tf_op jit(solution)/shard_map/ppermute | solution.py:39
  45.5 7.5 %collective-permute-start.12 = (bf16[320,256]{1,0:T(8,128)(2,1)S(1)}, bf16[320,256]{1,0:T(8,128)(2,1)S(1)}, u32[]{:S(2)}, u32[]{:S(2)}) collective-permute-start(bf16[320,256]{1,0:T(8,128)(2,1)S(1)} %get-tuple-element.44), channel_id=1, source_target_pairs={{0,32},{1,33},{2,34},{3,35},{4,36},{5,37},{6,38},{7,39},{8,40},{9,... | collective-permute-start | bytes 491528 | tf_op jit(solution)/shard_map/ppermute | solution.py:39
  53.1 0.8 collective-permute-start.14
  53.8 7.8 %collective-permute-start.13 = (bf16[640,256]{1,0:T(8,128)(2,1)S(1)}, bf16[640,256]{1,0:T(8,128)(2,1)S(1)}, u32[]{:S(2)}, u32[]{:S(2)}) collective-permute-start(bf16[640,256]{1,0:T(8,128)(2,1)S(1)} %pad_maximum_fusion), channel_id=1, source_target_pairs={{0,2},{1,3},{2,128},{3,129},{4,6},{5,7},{6,132},{7,133},{8,10},{9,... | collective-permute-start | bytes 983048 | tf_op jit(solution)/shard_map/ppermute | solution.py:39
  61.8 5.5 %collective-permute-start.15 = (bf16[320,256]{1,0:T(8,128)(2,1)S(1)}, bf16[320,256]{1,0:T(8,128)(2,1)S(1)}, u32[]{:S(2)}, u32[]{:S(2)}) collective-permute-start(bf16[320,256]{1,0:T(8,128)(2,1)S(1)} %get-tuple-element.46), channel_id=1, source_target_pairs={{0,96},{1,97},{2,98},{3,99},{4,100},{5,101},{6,102},{7,103},{8,104... | collective-permute-start | bytes 491528 | tf_op jit(solution)/shard_map/ppermute | solution.py:39
  63.2 4.2 %collective-permute-start.16 = (bf16[320,256]{1,0:T(8,128)(2,1)S(1)}, bf16[320,256]{1,0:T(8,128)(2,1)S(1)}, u32[]{:S(2)}, u32[]{:S(2)}) collective-permute-start(bf16[320,256]{1,0:T(8,128)(2,1)S(1)} %get-tuple-element.45), channel_id=1, source_target_pairs={{0,32},{1,33},{2,34},{3,35},{4,36},{5,37},{6,38},{7,39},{8,40},{9,... | collective-permute-start | bytes 491528 | tf_op jit(solution)/shard_map/ppermute | solution.py:39
  67.3 23.8 %collective-permute-start.17 = (bf16[640,256]{1,0:T(8,128)(2,1)S(1)}, bf16[640,256]{1,0:T(8,128)(2,1)S(1)}, u32[]{:S(2)}, u32[]{:S(2)}) collective-permute-start(bf16[640,256]{1,0:T(8,128)(2,1)S(1)} %pad_maximum_fusion.1), channel_id=1, source_target_pairs={{0,32},{1,33},{2,34},{3,35},{4,36},{5,37},{6,38},{7,39},{8,40},{9,... | collective-permute-start | bytes 983048 | tf_op jit(solution)/shard_map/ppermute | solution.py:39
  67.4 23.6 %collective-permute-start.18 = (bf16[640,256]{1,0:T(8,128)(2,1)S(1)}, bf16[640,256]{1,0:T(8,128)(2,1)S(1)}, u32[]{:S(2)}, u32[]{:S(2)}) collective-permute-start(bf16[640,256]{1,0:T(8,128)(2,1)S(1)} %pad_maximum_fusion.2), channel_id=1, source_target_pairs={{0,96},{1,97},{2,98},{3,99},{4,100},{5,101},{6,102},{7,103},{8,104... | collective-permute-start | bytes 983048 | tf_op jit(solution)/shard_map/ppermute | solution.py:39
  69.6 35.7 %collective-permute-start.21 = (bf16[256,1024]{1,0:T(8,128)(2,1)S(1)}, bf16[256,1024]{1,0:T(8,128)(2,1)S(1)}, u32[]{:S(2)}, u32[]{:S(2)}) collective-permute-start(bf16[256,1024]{1,0:T(8,128)(2,1)S(1)} %copy-done.1), channel_id=1, source_target_pairs={{0,0},{1,1},{2,2},{3,3},{4,4},{5,5},{6,6},{7,7},{8,8},{9,9},{10,10... | collective-permute-start | bytes 1572872 | tf_op jit(solution)/shard_map/ppermute | solution.py:39
  71.8 33.5 %collective-permute-start.20 = (bf16[256,1024]{1,0:T(8,128)(2,1)S(1)}, bf16[256,1024]{1,0:T(8,128)(2,1)S(1)}, u32[]{:S(2)}, u32[]{:S(2)}) collective-permute-start(bf16[256,1024]{1,0:T(8,128)(2,1)S(1)} %copy-done.1), channel_id=1, source_target_pairs={{0,48},{1,49},{2,50},{3,51},{4,52},{5,53},{6,54},{7,55},{8,56},{9,... | collective-permute-start | bytes 1572872 | tf_op jit(solution)/shard_map/ppermute | solution.py:39
  90.8 14.5 %collective-permute-start.19 = (bf16[256,1024]{1,0:T(8,128)(2,1)S(1)}, bf16[256,1024]{1,0:T(8,128)(2,1)S(1)}, u32[]{:S(2)}, u32[]{:S(2)}) collective-permute-start(bf16[256,1024]{1,0:T(8,128)(2,1)S(1)} %copy-done.1), channel_id=1, source_target_pairs={{0,16},{1,17},{2,18},{3,19},{4,20},{5,21},{6,22},{7,23},{8,24},{9,... | collective-permute-start | bytes 1572872 | tf_op jit(solution)/shard_map/ppermute | solution.py:39
  107.1 7.2 %collective-permute-start.22 = (bf16[1024,1024]{1,0:T(8,128)(2,1)S(1)}, bf16[1024,1024]{1,0:T(8,128)(2,1)S(1)}, u32[]{:S(2)}, u32[]{:S(2)}) collective-permute-start(bf16[1024,1024]{1,0:T(8,128)(2,1)S(1)} %shard_map.60.mine_ref), channel_id=1, source_target_pairs={{0,16},{1,17},{2,18},{3,19},{4,20},{5,21},{6,22},{7,23},{8,24},{9,... | collective-permute-start | bytes 6291464 | tf_op jit(solution)/shard_map/ppermute | solution.py:39

commit v8 on v5

--- a/solution.py
+++ b/solution.py
@@ -10,7 +10,8 @@
 BF16 = jnp.bfloat16
 F32 = jnp.float32
 MIB = 2 ** 20
-UPPER = [(r, c) for r in range(4) for c in range(r, 4)]
+UPPER = [(r, c) for r in range(8) for c in range(r, 8)]
+PARTS = [UPPER[9 * i:9 * (i + 1)] for i in range(4)]
 SMEM = pl.BlockSpec(memory_space=pltpu.SMEM)
 VMEM = pl.BlockSpec(memory_space=pltpu.VMEM)
 
@@ -114,39 +115,39 @@
 
 
 def cov_kernel(scale, place_ref, *refs):
-    pieces, chunks, (all_ref, panel_ref) = refs[:4], refs[4:8], refs[8:]
+    pieces, chunks, (all_ref, full_ref, parts_ref) = refs[:4], refs[4:8], refs[8:]
     count, size = pieces[0].shape
-    tile, sub = size // 4, size // 16
+    tile, small = size // 4, size // 8
     for k, piece in enumerate(pieces):
         all_ref[k * count:(k + 1) * count, :] = piece[...]
     for r in range(4):
         cols = all_ref[:, r * tile:(r + 1) * tile]
-        panel_ref[:, r * tile:] = gram(cols, all_ref[:, r * tile:]) * scale
-        for k, chunk in enumerate(chunks):
-            start = pl.multiple_of(lax.rem(place_ref[0] + k * place_ref[1], 4) * sub, sub)
-            for t, (row, c) in enumerate(UPPER):
-                if row == r:
-                    chunk[t * sub:(t + 1) * sub, :] = panel_ref[
-                        pl.ds(start, sub), c * tile:(c + 1) * tile].astype(BF16)
+        full_ref[r * tile:(r + 1) * tile, r * tile:] = (gram(cols, all_ref[:, r * tile:]) * scale).astype(BF16)
+    for i, tiles in enumerate(PARTS):
+        for t, (r, c) in enumerate(tiles):
+            parts_ref[i, t * small:(t + 1) * small, :] = full_ref[
+                r * small:(r + 1) * small, c * small:(c + 1) * small]
+    for k, chunk in enumerate(chunks):
+        chunk[...] = parts_ref[lax.rem(place_ref[0] + k * place_ref[1], 4)]
 
 
 def cov(place, pieces, scale):
     count, size = pieces[0].shape
-    tile, sub = size // 4, size // 16
+    part = (len(PARTS[0]) * size // 8, size // 8)
     return pl.pallas_call(
         lambda *refs: cov_kernel(scale, *refs),
-        out_shape=(jax.ShapeDtypeStruct((len(UPPER) * sub, tile), BF16),) * 4,
+        out_shape=(jax.ShapeDtypeStruct(part, BF16),) * 4,
         in_specs=[SMEM] + [VMEM] * 4,
         out_specs=(VMEM,) * 4,
-        scratch_shapes=[pltpu.VMEM((4 * count, size), BF16), pltpu.VMEM((tile, size), F32)],
-        compiler_params=pltpu.CompilerParams(vmem_limit_bytes=16 * MIB),
+        scratch_shapes=[
+            pltpu.VMEM((4 * count, size), BF16), pltpu.VMEM((size, size), BF16), pltpu.VMEM((4,) + part, BF16)],
+        compiler_params=pltpu.CompilerParams(vmem_limit_bytes=20 * MIB),
     )(place, *pieces)
 
 
-def rounds_kernel(place_ref, damp_ref, p0, p1, p2, p3, out_ref, a_ref, x_ref, xb_ref, p_ref):
+def rounds_kernel(place_ref, damp_ref, p0, p1, p2, p3, out_ref, a_ref, x_ref, xb_ref, p_ref, parts_ref):
     size = out_ref.shape[0]
-    tile = size // 4
-    sub = tile // 4
+    tile, small = size // 4, size // 8
     base, damp = place_ref[0], damp_ref[0]
     blocks = [slice(i * tile, (i + 1) * tile) for i in range(4)]
 
@@ -156,22 +157,27 @@
             ref[blocks[c], blocks[r]] = value[blocks[r], :].T
 
     for k, piece in enumerate((p0, p1, p2, p3)):
-        start = pl.multiple_of(lax.rem(base + 4 - k, 4) * sub, sub)
-        for t, (r, c) in enumerate(UPPER):
-            a_ref[pl.ds(r * tile + start, sub), blocks[c]] = piece[t * sub:(t + 1) * sub, :]
+        parts_ref[lax.rem(base + 4 - k, 4)] = piece[...]
+    for i, tiles in enumerate(PARTS):
+        for t, (r, c) in enumerate(tiles):
+            value = parts_ref[i, t * small:(t + 1) * small, :]
+            rows, cols = slice(r * small, (r + 1) * small), slice(c * small, (c + 1) * small)
+            a_ref[rows, cols] = value
+            if r < c:
+                a_ref[cols, rows] = value.T
     row = lax.broadcasted_iota(jnp.int32, (tile, tile), 0)
     col = lax.broadcasted_iota(jnp.int32, (tile, tile), 1)
     eye = row == col
     total = jnp.zeros((1, 1), F32)
-    for r, c in UPPER:
-        value = a_ref[blocks[r], blocks[c]].astype(F32)
-        if r == c:
-            value = value + jnp.where(eye, damp, 0.0)
-            a_ref[blocks[r], blocks[c]] = value.astype(BF16)
-            total += jnp.sum(value * value, keepdims=True)
-        else:
-            total += 2.0 * jnp.sum(value * value, keepdims=True)
-            a_ref[blocks[c], blocks[r]] = a_ref[blocks[r], blocks[c]].T
+    for r in range(4):
+        for c in range(r, 4):
+            value = a_ref[blocks[r], blocks[c]].astype(F32)
+            if r == c:
+                value = value + jnp.where(eye, damp, 0.0)
+                a_ref[blocks[r], blocks[c]] = value.astype(BF16)
+                total += jnp.sum(value * value, keepdims=True)
+            else:
+                total += 2.0 * jnp.sum(value * value, keepdims=True)
     frob = jnp.sqrt(total)
     inv = 1.0 / frob
     inv_bf = inv.astype(BF16).astype(F32)
@@ -199,8 +205,7 @@
 
 
 def rounds(place, damp, pieces):
-    tile = pieces[0].shape[1]
-    size = tile * 4
+    size = pieces[0].shape[1] * 8
     return pl.pallas_call(
         rounds_kernel,
         out_shape=jax.ShapeDtypeStruct((size, size), BF16),
@@ -211,6 +216,7 @@
             pltpu.VMEM((size, size), F32),
             pltpu.VMEM((2, size, size), BF16),
             pltpu.VMEM((size, size), BF16),
+            pltpu.VMEM((4,) + pieces[0].shape, BF16),
         ],
         cost_estimate=pl.CostEstimate(flops=16 * size ** 3, transcendentals=0, bytes_accessed=4 * size * size),
         compiler_params=pltpu.CompilerParams(vmem_limit_bytes=24 * MIB),
@@ -247,15 +253,22 @@
 
 
 def last_kernel(place_ref, mine_ref, other_ref, out_ref):
-    tile = out_ref.shape[0]
+    tile, size = out_ref.shape
+
+    def put(rows, inverse):
+        for i in range(size // tile):
+            block = slice(i * tile, (i + 1) * tile)
+            value = lax.dot_general(
+                inverse[block, :], rows, (((1,), (1,)), ((), ())), preferred_element_type=F32)
+            out_ref[:, block] = value.astype(BF16).T
 
     @pl.when(place_ref[1] == 0)
     def _():
-        out_ref[...] = dot(other_ref[:tile, :], mine_ref[...]).astype(BF16)
+        put(other_ref[:tile, :], mine_ref)
 
     @pl.when(place_ref[1] == 1)
     def _():
-        out_ref[...] = dot(mine_ref[tile:2 * tile, :], other_ref[...]).astype(BF16)
+        put(mine_ref[tile:2 * tile, :], other_ref)
 
 
 def last(place, mine, other, rows):

time: 110 us -> 108 us (0.982)
  waiting for transfers between devices: 33.8 us -> 32 us
    ppermute x21, waiting for transfers between devices: 33.8 us -> 32 us  [moved(): return lax.ppermute(value, ('dp', 'owner'), pairs)]
where the time goes in v8:
time: 108 us
  starting transfers between devices  46.8 us (43%)
  waiting for transfers between devices  32 us (30%)
  Pallas kernels  23.8 us (22%)
  matrix products  3.28 us (3%)
  other arithmetic  1.39 us (1%)
    ppermute x21, starting transfers between devices, moved(): return lax.ppermute(value, ('dp', 'owner'), pairs)  46.8 us
    ppermute x21, waiting for transfers between devices, moved(): return lax.ppermute(value, ('dp', 'owner'), pairs)  32 us
    pallas_call x1, Pallas kernels, rounds(): pl.pallas_call(rounds_kernel, out_shape=jax.ShapeDtypeStruct((size, size)...  15.4 us
    dot_general x2, matrix products, dot(): return jnp.dot(a, b, preferred_element_type=F32)  3.28 us
    pallas_call x1, Pallas kernels, last(): pl.pallas_call(last_kernel, out_shape=jax.ShapeDtypeStruct((rows, mine.sh...  2.17 us
  transfers between devices with their start and end apart: 21, of which 9 were waited for; matrix products, arithmetic and copies ran while one was open for 2% of the time, Pallas kernels for 15%

profile of v8, /device:TPU:33, one launch (start us, length us, event | category | flops | bytes accessed | tf_op | source)
XLA Modules:
  0.0 108.1 jit_solution(18400683975435422289)
XLA Ops:
  0.0 3.0 %convolution_convert_fusion.g_ref.mine_ref = bf16[16,16384]{1,0:T(8,128)(2,1)S(1)} fusion(bf16[128,16384]{1,0:T(8,128)(2,1)} %param.6, s32[16]{0:T(128)} %param.7), kind=kOutput, calls=%fused_computation | convolution fusion | flops 67373056 | bytes 4718656 | tf_op jit(solution)/shard_map/dot_general | solution.py:20
  4.1 1.5 %collective-permute-done.other_ref = bf16[16,16384]{1,0:T(8,128)(2,1)S(1)} collective-permute-done((bf16[16,16384]{1,0:T(8,128)(2,1)S(1)}, bf16[16,16384]{1,0:T(8,128)(2,1)S(1)}, u32[]{:S(2)}, u32[]{:S(2)}) %collective-permute-start) | collective-permute-done | bytes 524320 | tf_op jit(solution)/shard_map/ppermute | solution.py:39
  5.7 7.0 %collective-permute-start.4 = (bf16[32,2048]{1,0:T(8,128)(2,1)S(1)}, bf16[32,2048]{1,0:T(8,128)(2,1)}, u32[]{:S(2)}, u32[]{:S(2)}) collective-permute-start(bf16[32,2048]{1,0:T(8,128)(2,1)S(1)} %get-tuple-element.43), channel_id=1, source_target_pairs={{0,0},{1,1},{2,2},{3,3},{4,4},{5,5},{6,6},{7,7},{8,8},{9,9},{10,10... | collective-permute-start | bytes 393224 | tf_op jit(solution)/shard_map/ppermute | solution.py:39
  12.8 0.9 shard_map.56
  13.7 1.6 %collective-permute-start.1 = (bf16[128,1024]{1,0:T(8,128)(2,1)}, bf16[128,1024]{1,0:T(8,128)(2,1)S(1)}, u32[]{:S(2)}, u32[]{:S(2)}) collective-permute-start(bf16[128,1024]{1,0:T(8,128)(2,1)} %get-tuple-element.25), channel_id=1, source_target_pairs={{0,4},{1,5},{2,6},{3,7},{4,8},{5,9},{6,10},{7,11},{8,12},{9,13},{1... | collective-permute-start | bytes 786440 | tf_op jit(solution)/shard_map/ppermute | solution.py:39
  15.2 1.6 %collective-permute-start.2 = (bf16[128,1024]{1,0:T(8,128)(2,1)}, bf16[128,1024]{1,0:T(8,128)(2,1)S(1)}, u32[]{:S(2)}, u32[]{:S(2)}) collective-permute-start(bf16[128,1024]{1,0:T(8,128)(2,1)} %get-tuple-element.26), channel_id=1, source_target_pairs={{0,8},{1,9},{2,10},{3,11},{4,12},{5,13},{6,14},{7,15},{8,0},{9,1},... | collective-permute-start | bytes 786440 | tf_op jit(solution)/shard_map/ppermute | solution.py:39
  17.6 0.9 fusion
  18.5 4.6 %collective-permute-start.5 = (bf16[64,1024]{1,0:T(8,128)(2,1)S(1)}, bf16[64,1024]{1,0:T(8,128)(2,1)S(1)}, u32[]{:S(2)}, u32[]{:S(2)}) collective-permute-start(bf16[64,1024]{1,0:T(8,128)(2,1)S(1)} %get-tuple-element.41), channel_id=1, source_target_pairs={{0,0},{1,1},{2,2},{3,3},{4,4},{5,5},{6,6},{7,7},{8,8},{9,9},{10,10... | collective-permute-start | bytes 393224 | tf_op jit(solution)/shard_map/ppermute | solution.py:39
  23.3 2.2 %collective-permute-done.5.come_ref = bf16[64,1024]{1,0:T(8,128)(2,1)S(1)} collective-permute-done((bf16[64,1024]{1,0:T(8,128)(2,1)S(1)}, bf16[64,1024]{1,0:T(8,128)(2,1)S(1)}, u32[]{:S(2)}, u32[]{:S(2)}) %collective-permute-start.5) | collective-permute-done | bytes 131104 | tf_op jit(solution)/shard_map/ppermute | solution.py:39
  25.5 1.4 %shard_map.57 = (bf16[128,1024]{1,0:T(8,128)(2,1)S(1)}, bf16[128,1024]{1,0:T(8,128)(2,1)}, bf16[128,1024]{1,0:T(8,128)(2,1)}, bf16[128,1024]{1,0:T(8,128)(2,1)S(1)}) custom-call(s32[2]{0:T(128)S(1)} %pad_add_fusion.2.place_ref, bf16[128,1024]{1,0:T(8,128)(2,1)S(1)} %get-tuple-element.24.h0, bf16[128,1024]{1,0:T(8,128)(2,1)S(1)} %collective-permute-done.1.h1, ...), custom_call_target="tpu_custom_call" | custom-call | tf_op jit(solution)/shard_map/pallas_call | solution.py:108
  26.9 1.2 %collective-permute-start.6 = (bf16[128,1024]{1,0:T(8,128)(2,1)}, bf16[128,1024]{1,0:T(8,128)(2,1)S(1)}, u32[]{:S(2)}, u32[]{:S(2)}) collective-permute-start(bf16[128,1024]{1,0:T(8,128)(2,1)} %get-tuple-element.29), channel_id=1, source_target_pairs={{0,1},{1,2},{2,3},{3,128},{4,5},{5,6},{6,7},{7,132},{8,9},{9,10},{... | collective-permute-start | bytes 786440 | tf_op jit(solution)/shard_map/ppermute | solution.py:39
  28.1 2.5 %collective-permute-start.7 = (bf16[128,1024]{1,0:T(8,128)(2,1)}, bf16[128,1024]{1,0:T(8,128)(2,1)S(1)}, u32[]{:S(2)}, u32[]{:S(2)}) collective-permute-start(bf16[128,1024]{1,0:T(8,128)(2,1)} %get-tuple-element.30), channel_id=1, source_target_pairs={{0,2},{1,131},{2,128},{3,1},{4,6},{5,135},{6,132},{7,5},{8,10},{9,... | collective-permute-start | bytes 786440 | tf_op jit(solution)/shard_map/ppermute | solution.py:39
  30.6 1.2 %collective-permute-start.8 = (bf16[128,1024]{1,0:T(8,128)(2,1)S(1)}, bf16[128,1024]{1,0:T(8,128)(2,1)S(1)}, u32[]{:S(2)}, u32[]{:S(2)}) collective-permute-start(bf16[128,1024]{1,0:T(8,128)(2,1)S(1)} %get-tuple-element.31), channel_id=1, source_target_pairs={{0,131},{1,0},{2,1},{3,2},{4,135},{5,4},{6,5},{7,6},{8,139},{9,8},... | collective-permute-start | bytes 786440 | tf_op jit(solution)/shard_map/ppermute | solution.py:39
  31.8 1.8 %collective-permute-done.6.refs_2_ = bf16[128,1024]{1,0:T(8,128)(2,1)S(1)} collective-permute-done((bf16[128,1024]{1,0:T(8,128)(2,1)}, bf16[128,1024]{1,0:T(8,128)(2,1)S(1)}, u32[]{:S(2)}, u32[]{:S(2)}) %collective-permute-start.6) | collective-permute-done | bytes 262176 | tf_op jit(solution)/shard_map/ppermute | solution.py:39
  33.5 3.8 %collective-permute-done.7.refs_3_ = bf16[128,1024]{1,0:T(8,128)(2,1)S(1)} collective-permute-done((bf16[128,1024]{1,0:T(8,128)(2,1)}, bf16[128,1024]{1,0:T(8,128)(2,1)S(1)}, u32[]{:S(2)}, u32[]{:S(2)}) %collective-permute-start.7) | collective-permute-done | bytes 262176 | tf_op jit(solution)/shard_map/ppermute | solution.py:39
  37.3 1.8 %shard_map.58 = (bf16[1152,128]{1,0:T(8,128)(2,1)S(1)}, bf16[1152,128]{1,0:T(8,128)(2,1)S(1)}, bf16[1152,128]{1,0:T(8,128)(2,1)S(1)}, bf16[1152,128]{1,0:T(8,128)(2,1)S(1)}) custom-call(s32[2]{0:T(128)S(1)} %pad_add_fusion.1.refs_0_, bf16[128,1024]{1,0:T(8,128)(2,1)S(1)} %get-tuple-element.28.refs_1_, bf16[128,1024]{1,0:T(8,128)(2,1)S(1)} %collective-permute-done.6.refs_2_, ...), custom_call_target="tpu_custom_call" | custom-call | tf_op jit(solution)/shard_map/pallas_call | solution.py:137
  39.2 0.8 collective-permute-start.9
  40.0 2.4 %collective-permute-start.10 = (bf16[1152,128]{1,0:T(8,128)(2,1)S(1)}, bf16[1152,128]{1,0:T(8,128)(2,1)S(1)}, u32[]{:S(2)}, u32[]{:S(2)}) collective-permute-start(bf16[1152,128]{1,0:T(8,128)(2,1)S(1)} %get-tuple-element.34), channel_id=1, source_target_pairs={{0,64},{1,65},{2,66},{3,67},{4,68},{5,69},{6,70},{7,71},{8,72},{9,... | collective-permute-start | bytes 884744 | tf_op jit(solution)/shard_map/ppermute | solution.py:39
  42.5 2.3 %collective-permute-done.9 = bf16[1152,128]{1,0:T(8,128)(2,1)S(1)} collective-permute-done((bf16[1152,128]{1,0:T(8,128)(2,1)S(1)}, bf16[1152,128]{1,0:T(8,128)(2,1)S(1)}, u32[]{:S(2)}, u32[]{:S(2)}) %collective-permute-start.9) | collective-permute-done | bytes 294944 | tf_op jit(solution)/shard_map/ppermute | solution.py:39
  44.8 8.3 %collective-permute-done.10 = bf16[1152,128]{1,0:T(8,128)(2,1)S(1)} collective-permute-done((bf16[1152,128]{1,0:T(8,128)(2,1)S(1)}, bf16[1152,128]{1,0:T(8,128)(2,1)S(1)}, u32[]{:S(2)}, u32[]{:S(2)}) %collective-permute-start.10) | collective-permute-done | bytes 294944 | tf_op jit(solution)/shard_map/ppermute | solution.py:39
  53.1 2.4 %collective-permute-done.11 = bf16[1152,128]{1,0:T(8,128)(2,1)S(1)} collective-permute-done((bf16[1152,128]{1,0:T(8,128)(2,1)S(1)}, bf16[1152,128]{1,0:T(8,128)(2,1)S(1)}, u32[]{:S(2)}, u32[]{:S(2)}) %collective-permute-start.11) | collective-permute-done | bytes 294944 | tf_op jit(solution)/shard_map/ppermute | solution.py:39
  56.5 5.8 %collective-permute-done.12 = bf16[1152,128]{1,0:T(8,128)(2,1)S(1)} collective-permute-done((bf16[1152,128]{1,0:T(8,128)(2,1)S(1)}, bf16[1152,128]{1,0:T(8,128)(2,1)S(1)}, u32[]{:S(2)}, u32[]{:S(2)}) %collective-permute-start.12) | collective-permute-done | bytes 294944 | tf_op jit(solution)/shard_map/ppermute | solution.py:39
  62.4 2.1 %collective-permute-start.16 = (bf16[1152,128]{1,0:T(8,128)(2,1)S(1)}, bf16[1152,128]{1,0:T(8,128)(2,1)S(1)}, u32[]{:S(2)}, u32[]{:S(2)}) collective-permute-start(bf16[1152,128]{1,0:T(8,128)(2,1)S(1)} %add_convert_fusion.p0), channel_id=1, source_target_pairs={{0,96},{1,97},{2,98},{3,99},{4,100},{5,101},{6,102},{7,103},{8,104... | collective-permute-start | bytes 884744 | tf_op jit(solution)/shard_map/ppermute | solution.py:39
  64.5 0.9 collective-permute-start.15
  66.6 1.9 %collective-permute-start.19 = (bf16[256,1024]{1,0:T(8,128)(2,1)S(1)}, bf16[256,1024]{1,0:T(8,128)(2,1)S(1)}, u32[]{:S(2)}, u32[]{:S(2)}) collective-permute-start(bf16[256,1024]{1,0:T(8,128)(2,1)S(1)} %copy-done.1), channel_id=1, source_target_pairs={{0,0},{1,1},{2,2},{3,3},{4,4},{5,5},{6,6},{7,7},{8,8},{9,9},{10,10... | collective-permute-start | bytes 1572872 | tf_op jit(solution)/shard_map/ppermute | solution.py:39
  68.6 8.6 %collective-permute-start.18 = (bf16[256,1024]{1,0:T(8,128)(2,1)S(1)}, bf16[256,1024]{1,0:T(8,128)(2,1)S(1)}, u32[]{:S(2)}, u32[]{:S(2)}) collective-permute-start(bf16[256,1024]{1,0:T(8,128)(2,1)S(1)} %copy-done.1), channel_id=1, source_target_pairs={{0,48},{1,49},{2,50},{3,51},{4,52},{5,53},{6,54},{7,55},{8,56},{9,... | collective-permute-start | bytes 1572872 | tf_op jit(solution)/shard_map/ppermute | solution.py:39
  77.1 3.3 %collective-permute-start.17 = (bf16[256,1024]{1,0:T(8,128)(2,1)S(1)}, bf16[256,1024]{1,0:T(8,128)(2,1)S(1)}, u32[]{:S(2)}, u32[]{:S(2)}) collective-permute-start(bf16[256,1024]{1,0:T(8,128)(2,1)S(1)} %copy-done.1), channel_id=1, source_target_pairs={{0,16},{1,17},{2,18},{3,19},{4,20},{5,21},{6,22},{7,23},{8,24},{9,... | collective-permute-start | bytes 1572872 | tf_op jit(solution)/shard_map/ppermute | solution.py:39
  80.4 15.4 %shard_map.59.s_ref = bf16[1024,1024]{1,0:T(8,128)(2,1)S(1)} custom-call(s32[3]{0:T(128)S(1)} %pad_add_fusion.place_ref, f32[1]{0:T(128)} %dynamic_slice.16.damp_ref, bf16[1152,128]{1,0:T(8,128)(2,1)S(1)} %add_convert_fusion.p0, bf16[1152,128]{1,0:T(8,128)(2,1)} %collective-permute-done.14.p1, bf16[1152,128]{1,0:T(8,128)(2,1)} %collective-permute-done.15.p2, ...), custom_call_target="tpu_custom_call" | custom-call | flops 17179869184 | bytes 4194304 | tf_op jit(solution)/shard_map/pallas_call | solution.py:209
  95.9 2.0 %shard_map.60.mine_ref = bf16[1024,1024]{1,0:T(8,128)(2,1)S(1)} custom-call(s32[3]{0:T(128)S(1)} %pad_add_fusion.place_ref, bf16[1024,1024]{1,0:T(8,128)(2,1)S(1)} %shard_map.59.s_ref, bf16[256,1024]{1,0:T(8,128)(2,1)S(1)} %collective-permute-done.17.w0, bf16[256,1024]{1,0:T(8,128)(2,1)S(1)} %copy-done.1, ...), custom_call_target="tpu_custom_call", output_to_operand_aliasing={{}: (1, {})} | custom-call | tf_op jit(solution)/shard_map/pallas_call | solution.py:244
  97.9 4.2 %collective-permute-start.20 = (bf16[1024,1024]{1,0:T(8,128)(2,1)S(1)}, bf16[1024,1024]{1,0:T(8,128)(2,1)S(1)}, u32[]{:S(2)}, u32[]{:S(2)}) collective-permute-start(bf16[1024,1024]{1,0:T(8,128)(2,1)S(1)} %shard_map.60.mine_ref), channel_id=1, source_target_pairs={{0,16},{1,17},{2,18},{3,19},{4,20},{5,21},{6,22},{7,23},{8,24},{9,... | collective-permute-start | bytes 6291464 | tf_op jit(solution)/shard_map/ppermute | solution.py:39
  102.1 3.8 %collective-permute-done.20.other_ref = bf16[1024,1024]{1,0:T(8,128)(2,1)S(1)} collective-permute-done((bf16[1024,1024]{1,0:T(8,128)(2,1)S(1)}, bf16[1024,1024]{1,0:T(8,128)(2,1)S(1)}, u32[]{:S(2)}, u32[]{:S(2)}) %collective-permute-start.20) | collective-permute-done | bytes 2097184 | tf_op jit(solution)/shard_map/ppermute | solution.py:39
  105.9 2.2 %shard_map.61 = bf16[256,1024]{1,0:T(8,128)(2,1)} custom-call(s32[3]{0:T(128)S(1)} %pad_add_fusion.place_ref, bf16[1024,1024]{1,0:T(8,128)(2,1)S(1)} %shard_map.60.mine_ref, bf16[1024,1024]{1,0:T(8,128)(2,1)S(1)} %collective-permute-done.20.other_ref), custom_call_target="tpu_custom_call" | custom-call | tf_op jit(solution)/shard_map/pallas_call | solution.py:275
  (36 shorter events, 4.4 us)
Async XLA Ops:
  0.0 3.0 %copy-start = (bf16[128,4096]{1,0:T(8,128)(2,1)S(1)}, bf16[128,4096]{1,0:T(8,128)(2,1)}, u32[]{:S(2)}) copy-start(bf16[128,4096]{1,0:T(8,128)(2,1)} %param.5) | copy-start | bytes 3145732
  0.0 3.0 %copy-start.2 = (s32[16]{0:T(128)S(1)}, s32[16]{0:T(128)}, u32[]{:S(2)}) copy-start(s32[16]{0:T(128)} %param.7) | copy-start | bytes 196
  3.3 62.7 %copy-start.3 = (f32[20]{0:T(128)S(1)}, f32[20]{0:T(128)}, u32[]{:S(2)}) copy-start(f32[20]{0:T(128)} %param.8) | copy-start | bytes 244
  3.3 63.3 %copy-start.1 = (bf16[256,1024]{1,0:T(8,128)(2,1)S(1)}, bf16[256,1024]{1,0:T(8,128)(2,1)}, u32[]{:S(2)}) copy-start(bf16[256,1024]{1,0:T(8,128)(2,1)} %w1.1) | copy-start | bytes 1572868
  3.4 2.3 %collective-permute-start = (bf16[16,16384]{1,0:T(8,128)(2,1)S(1)}, bf16[16,16384]{1,0:T(8,128)(2,1)S(1)}, u32[]{:S(2)}, u32[]{:S(2)}) collective-permute-start(bf16[16,16384]{1,0:T(8,128)(2,1)S(1)} %shard_map.55), channel_id=1, source_target_pairs={{0,16},{1,17},{2,18},{3,19},{4,20},{5,21},{6,22},{7,23},{8,24},{9,... | collective-permute-start | bytes 1572872 | tf_op jit(solution)/shard_map/ppermute | solution.py:39
  5.7 11.8 %collective-permute-start.4 = (bf16[32,2048]{1,0:T(8,128)(2,1)S(1)}, bf16[32,2048]{1,0:T(8,128)(2,1)}, u32[]{:S(2)}, u32[]{:S(2)}) collective-permute-start(bf16[32,2048]{1,0:T(8,128)(2,1)S(1)} %get-tuple-element.43), channel_id=1, source_target_pairs={{0,0},{1,1},{2,2},{3,3},{4,4},{5,5},{6,6},{7,7},{8,8},{9,9},{10,10... | collective-permute-start | bytes 393224 | tf_op jit(solution)/shard_map/ppermute | solution.py:39
  13.7 9.6 %collective-permute-start.1 = (bf16[128,1024]{1,0:T(8,128)(2,1)}, bf16[128,1024]{1,0:T(8,128)(2,1)S(1)}, u32[]{:S(2)}, u32[]{:S(2)}) collective-permute-start(bf16[128,1024]{1,0:T(8,128)(2,1)} %get-tuple-element.25), channel_id=1, source_target_pairs={{0,4},{1,5},{2,6},{3,7},{4,8},{5,9},{6,10},{7,11},{8,12},{9,13},{1... | collective-permute-start | bytes 786440 | tf_op jit(solution)/shard_map/ppermute | solution.py:39
  15.2 8.0 %collective-permute-start.2 = (bf16[128,1024]{1,0:T(8,128)(2,1)}, bf16[128,1024]{1,0:T(8,128)(2,1)S(1)}, u32[]{:S(2)}, u32[]{:S(2)}) collective-permute-start(bf16[128,1024]{1,0:T(8,128)(2,1)} %get-tuple-element.26), channel_id=1, source_target_pairs={{0,8},{1,9},{2,10},{3,11},{4,12},{5,13},{6,14},{7,15},{8,0},{9,1},... | collective-permute-start | bytes 786440 | tf_op jit(solution)/shard_map/ppermute | solution.py:39
  16.8 6.4 %collective-permute-start.3 = (bf16[128,1024]{1,0:T(8,128)(2,1)S(1)}, bf16[128,1024]{1,0:T(8,128)(2,1)S(1)}, u32[]{:S(2)}, u32[]{:S(2)}) collective-permute-start(bf16[128,1024]{1,0:T(8,128)(2,1)S(1)} %get-tuple-element.27), channel_id=1, source_target_pairs={{0,12},{1,13},{2,14},{3,15},{4,0},{5,1},{6,2},{7,3},{8,4},{9,5},{1... | collective-permute-start | bytes 786440 | tf_op jit(solution)/shard_map/ppermute | solution.py:39
  18.5 7.0 %collective-permute-start.5 = (bf16[64,1024]{1,0:T(8,128)(2,1)S(1)}, bf16[64,1024]{1,0:T(8,128)(2,1)S(1)}, u32[]{:S(2)}, u32[]{:S(2)}) collective-permute-start(bf16[64,1024]{1,0:T(8,128)(2,1)S(1)} %get-tuple-element.41), channel_id=1, source_target_pairs={{0,0},{1,1},{2,2},{3,3},{4,4},{5,5},{6,6},{7,7},{8,8},{9,9},{10,10... | collective-permute-start | bytes 393224 | tf_op jit(solution)/shard_map/ppermute | solution.py:39
  26.9 6.6 %collective-permute-start.6 = (bf16[128,1024]{1,0:T(8,128)(2,1)}, bf16[128,1024]{1,0:T(8,128)(2,1)S(1)}, u32[]{:S(2)}, u32[]{:S(2)}) collective-permute-start(bf16[128,1024]{1,0:T(8,128)(2,1)} %get-tuple-element.29), channel_id=1, source_target_pairs={{0,1},{1,2},{2,3},{3,128},{4,5},{5,6},{6,7},{7,132},{8,9},{9,10},{... | collective-permute-start | bytes 786440 | tf_op jit(solution)/shard_map/ppermute | solution.py:39
  28.1 9.2 %collective-permute-start.7 = (bf16[128,1024]{1,0:T(8,128)(2,1)}, bf16[128,1024]{1,0:T(8,128)(2,1)S(1)}, u32[]{:S(2)}, u32[]{:S(2)}) collective-permute-start(bf16[128,1024]{1,0:T(8,128)(2,1)} %get-tuple-element.30), channel_id=1, source_target_pairs={{0,2},{1,131},{2,128},{3,1},{4,6},{5,135},{6,132},{7,5},{8,10},{9,... | collective-permute-start | bytes 786440 | tf_op jit(solution)/shard_map/ppermute | solution.py:39
  30.6 6.8 %collective-permute-start.8 = (bf16[128,1024]{1,0:T(8,128)(2,1)S(1)}, bf16[128,1024]{1,0:T(8,128)(2,1)S(1)}, u32[]{:S(2)}, u32[]{:S(2)}) collective-permute-start(bf16[128,1024]{1,0:T(8,128)(2,1)S(1)} %get-tuple-element.31), channel_id=1, source_target_pairs={{0,131},{1,0},{2,1},{3,2},{4,135},{5,4},{6,5},{7,6},{8,139},{9,8},... | collective-permute-start | bytes 786440 | tf_op jit(solution)/shard_map/ppermute | solution.py:39
  39.2 5.7 %collective-permute-start.9 = (bf16[1152,128]{1,0:T(8,128)(2,1)S(1)}, bf16[1152,128]{1,0:T(8,128)(2,1)S(1)}, u32[]{:S(2)}, u32[]{:S(2)}) collective-permute-start(bf16[1152,128]{1,0:T(8,128)(2,1)S(1)} %get-tuple-element.33), channel_id=1, source_target_pairs={{0,32},{1,33},{2,34},{3,35},{4,36},{5,37},{6,38},{7,39},{8,40},{9,... | collective-permute-start | bytes 884744 | tf_op jit(solution)/shard_map/ppermute | solution.py:39
  40.0 13.1 %collective-permute-start.10 = (bf16[1152,128]{1,0:T(8,128)(2,1)S(1)}, bf16[1152,128]{1,0:T(8,128)(2,1)S(1)}, u32[]{:S(2)}, u32[]{:S(2)}) collective-permute-start(bf16[1152,128]{1,0:T(8,128)(2,1)S(1)} %get-tuple-element.34), channel_id=1, source_target_pairs={{0,64},{1,65},{2,66},{3,67},{4,68},{5,69},{6,70},{7,71},{8,72},{9,... | collective-permute-start | bytes 884744 | tf_op jit(solution)/shard_map/ppermute | solution.py:39
  42.3 13.2 %collective-permute-start.11 = (bf16[1152,128]{1,0:T(8,128)(2,1)S(1)}, bf16[1152,128]{1,0:T(8,128)(2,1)S(1)}, u32[]{:S(2)}, u32[]{:S(2)}) collective-permute-start(bf16[1152,128]{1,0:T(8,128)(2,1)S(1)} %get-tuple-element.35), channel_id=1, source_target_pairs={{0,96},{1,97},{2,98},{3,99},{4,100},{5,101},{6,102},{7,103},{8,104... | collective-permute-start | bytes 884744 | tf_op jit(solution)/shard_map/ppermute | solution.py:39
  55.7 0.8 collective-permute-start.13
  56.4 5.9 %collective-permute-start.12 = (bf16[1152,128]{1,0:T(8,128)(2,1)S(1)}, bf16[1152,128]{1,0:T(8,128)(2,1)S(1)}, u32[]{:S(2)}, u32[]{:S(2)}) collective-permute-start(bf16[1152,128]{1,0:T(8,128)(2,1)S(1)} %add_convert_fusion.1), channel_id=1, source_target_pairs={{0,2},{1,3},{2,128},{3,129},{4,6},{5,7},{6,132},{7,133},{8,10},{9,... | collective-permute-start | bytes 884744 | tf_op jit(solution)/shard_map/ppermute | solution.py:39
  62.4 14.7 %collective-permute-start.16 = (bf16[1152,128]{1,0:T(8,128)(2,1)S(1)}, bf16[1152,128]{1,0:T(8,128)(2,1)S(1)}, u32[]{:S(2)}, u32[]{:S(2)}) collective-permute-start(bf16[1152,128]{1,0:T(8,128)(2,1)S(1)} %add_convert_fusion.p0), channel_id=1, source_target_pairs={{0,96},{1,97},{2,98},{3,99},{4,100},{5,101},{6,102},{7,103},{8,104... | collective-permute-start | bytes 884744 | tf_op jit(solution)/shard_map/ppermute | solution.py:39
  64.5 15.9 %collective-permute-start.15 = (bf16[1152,128]{1,0:T(8,128)(2,1)S(1)}, bf16[1152,128]{1,0:T(8,128)(2,1)}, u32[]{:S(2)}, u32[]{:S(2)}) collective-permute-start(bf16[1152,128]{1,0:T(8,128)(2,1)S(1)} %add_convert_fusion.p0), channel_id=1, source_target_pairs={{0,64},{1,65},{2,66},{3,67},{4,68},{5,69},{6,70},{7,71},{8,72},{9,... | collective-permute-start | bytes 884744 | tf_op jit(solution)/shard_map/ppermute | solution.py:39
  65.4 15.0 %collective-permute-start.14 = (bf16[1152,128]{1,0:T(8,128)(2,1)S(1)}, bf16[1152,128]{1,0:T(8,128)(2,1)}, u32[]{:S(2)}, u32[]{:S(2)}) collective-permute-start(bf16[1152,128]{1,0:T(8,128)(2,1)S(1)} %add_convert_fusion.p0), channel_id=1, source_target_pairs={{0,32},{1,33},{2,34},{3,35},{4,36},{5,37},{6,38},{7,39},{8,40},{9,... | collective-permute-start | bytes 884744 | tf_op jit(solution)/shard_map/ppermute | solution.py:39
  66.6 29.2 %collective-permute-start.19 = (bf16[256,1024]{1,0:T(8,128)(2,1)S(1)}, bf16[256,1024]{1,0:T(8,128)(2,1)S(1)}, u32[]{:S(2)}, u32[]{:S(2)}) collective-permute-start(bf16[256,1024]{1,0:T(8,128)(2,1)S(1)} %copy-done.1), channel_id=1, source_target_pairs={{0,0},{1,1},{2,2},{3,3},{4,4},{5,5},{6,6},{7,7},{8,8},{9,9},{10,10... | collective-permute-start | bytes 1572872 | tf_op jit(solution)/shard_map/ppermute | solution.py:39
  68.6 27.3 %collective-permute-start.18 = (bf16[256,1024]{1,0:T(8,128)(2,1)S(1)}, bf16[256,1024]{1,0:T(8,128)(2,1)S(1)}, u32[]{:S(2)}, u32[]{:S(2)}) collective-permute-start(bf16[256,1024]{1,0:T(8,128)(2,1)S(1)} %copy-done.1), channel_id=1, source_target_pairs={{0,48},{1,49},{2,50},{3,51},{4,52},{5,53},{6,54},{7,55},{8,56},{9,... | collective-permute-start | bytes 1572872 | tf_op jit(solution)/shard_map/ppermute | solution.py:39
  77.1 18.7 %collective-permute-start.17 = (bf16[256,1024]{1,0:T(8,128)(2,1)S(1)}, bf16[256,1024]{1,0:T(8,128)(2,1)S(1)}, u32[]{:S(2)}, u32[]{:S(2)}) collective-permute-start(bf16[256,1024]{1,0:T(8,128)(2,1)S(1)} %copy-done.1), channel_id=1, source_target_pairs={{0,16},{1,17},{2,18},{3,19},{4,20},{5,21},{6,22},{7,23},{8,24},{9,... | collective-permute-start | bytes 1572872 | tf_op jit(solution)/shard_map/ppermute | solution.py:39
  97.9 8.0 %collective-permute-start.20 = (bf16[1024,1024]{1,0:T(8,128)(2,1)S(1)}, bf16[1024,1024]{1,0:T(8,128)(2,1)S(1)}, u32[]{:S(2)}, u32[]{:S(2)}) collective-permute-start(bf16[1024,1024]{1,0:T(8,128)(2,1)S(1)} %shard_map.60.mine_ref), channel_id=1, source_target_pairs={{0,16},{1,17},{2,18},{3,19},{4,20},{5,21},{6,22},{7,23},{8,24},{9,... | collective-permute-start | bytes 6291464 | tf_op jit(solution)/shard_map/ppermute | solution.py:39

commit v9 on v8

--- a/solution.py
+++ b/solution.py
@@ -39,10 +39,30 @@
     return lax.ppermute(value, ("dp", "owner"), pairs)
 
 
-def z_shift(zh, zl, k):
-    z = zh * 4 + zl
-    z = (z + {1: 1, 2: 2 if z % 2 == 0 else -2, 3: -1}[k]) % 8
-    return z // 4, z % 4
+def dealt(value, group_of):
+    groups = []
+    for device in range(256):
+        c, x, zl = device // 16 % 2, device // 4 % 4, device % 4
+        members = [linear(*member) for member in group_of(device // 128, device // 32 % 4, c, x, zl)]
+        assert device in members
+        if device == min(members):
+            groups.append(members)
+    assert sorted(sum(groups, [])) == list(range(256))
+    return lax.all_to_all(
+        value, ("dp", "owner"), split_axis=0, concat_axis=0, tiled=True, axis_index_groups=groups)
+
+
+def over_plane(zh, y, c, x, zl):
+    return [(zh, y, c, i, k) for i in range(4) for k in range(4)]
+
+
+def over_blocks(zh, y, c, x, zl):
+    z = (zh * 4 + zl + (-2 if zl < 2 else 2)) % 8
+    places = {zh: (zh, zl), 1 - zh: (z // 4, z % 4)}
+    return [
+        (places[h][0], y if y // 2 == g else 3 - y, c, i, places[h][1])
+        for i in range(4) for h in range(2) for g in range(2)
+    ]
 
 
 def offer_kernel(core_ref, x_ref, g_ref, out_ref):
@@ -66,60 +86,38 @@
     )(core, samp_x, samp_g)
 
 
-def pack_kernel(place_ref, mine_ref, other_ref, *outs):
-    count, size = mine_ref.shape[0], outs[0].shape[1]
-    for k, out in enumerate(outs):
-        for zl in range(4):
-            index = lax.rem(place_ref[0] + k, 4) * 4 + zl
-            cols = pl.ds(pl.multiple_of(index * size, size), size)
-            out[zl * 2 * count:(zl * 2 + 1) * count, :] = mine_ref[:, cols]
-            out[(zl * 2 + 1) * count:(zl * 2 + 2) * count, :] = other_ref[:, cols]
-
-
-def pack(place, mine, other, size):
+def pack_kernel(core_ref, x_ref, g_ref, other_ref, out_ref):
+    count, size = x_ref.shape[0], out_ref.shape[2]
+
+    def put(mine_ref, column):
+        for part in range(16):
+            cols = slice(column(part) * size, (column(part) + 1) * size)
+            out_ref[part, :count, :] = mine_ref[:, cols]
+            out_ref[part, count:, :] = other_ref[:, cols]
+
+    @pl.when(core_ref[0] == 0)
+    def _():
+        put(g_ref, lambda part: part // 4 * 4 + (part + 2) % 4)
+
+    @pl.when(core_ref[0] == 1)
+    def _():
+        put(x_ref, lambda part: part % 4)
+
+
+def pack(core, samp_x, samp_g, other, size):
     return pl.pallas_call(
         pack_kernel,
-        out_shape=(jax.ShapeDtypeStruct((8 * mine.shape[0], size), BF16),) * 4,
-        in_specs=[SMEM, VMEM, VMEM],
-        out_specs=(VMEM,) * 4,
+        out_shape=jax.ShapeDtypeStruct((16, 2 * samp_x.shape[0], size), BF16),
+        in_specs=[SMEM] + [VMEM] * 3,
+        out_specs=VMEM,
         compiler_params=pltpu.CompilerParams(vmem_limit_bytes=8 * MIB),
-    )(place, mine, other)
-
-
-def deal_kernel(place_ref, h0, h1, h2, h3, kept_ref, come_ref, *outs):
-    rows = h0.shape[0] // 4
-    half = kept_ref.shape[0]
-
-    @pl.when(place_ref[1] == 0)
-    def _():
-        for k, out in enumerate(outs):
-            start = pl.multiple_of(lax.rem(place_ref[0] + k, 4) * rows, rows)
-            for i, held in enumerate((h0, h1, h2, h3)):
-                out[i * rows:(i + 1) * rows, :] = held[pl.ds(start, rows), :]
-
-    @pl.when(place_ref[1] == 1)
-    def _():
-        for out in outs:
-            out[:half, :] = kept_ref[...]
-            out[half:, :] = come_ref[...]
-
-
-def deal(place, held, kept, come):
-    return pl.pallas_call(
-        deal_kernel,
-        out_shape=(jax.ShapeDtypeStruct(held[0].shape, BF16),) * 4,
-        in_specs=[SMEM] + [VMEM] * 6,
-        out_specs=(VMEM,) * 4,
-        compiler_params=pltpu.CompilerParams(vmem_limit_bytes=8 * MIB),
-    )(place, *held, kept, come)
+    )(core, samp_x, samp_g, other)
 
 
 def cov_kernel(scale, place_ref, *refs):
-    pieces, chunks, (all_ref, full_ref, parts_ref) = refs[:4], refs[4:8], refs[8:]
-    count, size = pieces[0].shape
+    all_ref, chunks, (full_ref, parts_ref) = refs[0], refs[1:5], refs[5:]
+    size = all_ref.shape[1]
     tile, small = size // 4, size // 8
-    for k, piece in enumerate(pieces):
-        all_ref[k * count:(k + 1) * count, :] = piece[...]
     for r in range(4):
         cols = all_ref[:, r * tile:(r + 1) * tile]
         full_ref[r * tile:(r + 1) * tile, r * tile:] = (gram(cols, all_ref[:, r * tile:]) * scale).astype(BF16)
@@ -131,18 +129,17 @@
         chunk[...] = parts_ref[lax.rem(place_ref[0] + k * place_ref[1], 4)]
 
 
-def cov(place, pieces, scale):
-    count, size = pieces[0].shape
+def cov(place, samples, scale):
+    size = samples.shape[1]
     part = (len(PARTS[0]) * size // 8, size // 8)
     return pl.pallas_call(
         lambda *refs: cov_kernel(scale, *refs),
         out_shape=(jax.ShapeDtypeStruct(part, BF16),) * 4,
-        in_specs=[SMEM] + [VMEM] * 4,
+        in_specs=[SMEM, VMEM],
         out_specs=(VMEM,) * 4,
-        scratch_shapes=[
-            pltpu.VMEM((4 * count, size), BF16), pltpu.VMEM((size, size), BF16), pltpu.VMEM((4,) + part, BF16)],
+        scratch_shapes=[pltpu.VMEM((size, size), BF16), pltpu.VMEM((4,) + part, BF16)],
         compiler_params=pltpu.CompilerParams(vmem_limit_bytes=20 * MIB),
-    )(place, *pieces)
+    )(place, samples)
 
 
 def rounds_kernel(place_ref, damp_ref, p0, p1, p2, p3, out_ref, a_ref, x_ref, xb_ref, p_ref, parts_ref):
@@ -299,31 +296,10 @@
     samp_x = dot(hot, activations).astype(BF16)
     other = moved(offer(core.reshape(1), samp_x, samp_g), lambda zh, y, c, x, zl: (zh, y, 1 - c, x, zl))
 
-    packed = pack(x.reshape(1), samp_g, other, size)
-    held = [packed[0]]
-    for k in (1, 2, 3):
-        held.append(moved(packed[k], lambda zh, y, c, x, zl: (zh, y, 0, (x + k) % 4, zl) if c == 0 else None))
-
-    both_x = jnp.concatenate([samp_x, other[:, :4 * size]])
-
-    def over_z(zh, y, c, x, zl):
-        z = (zh * 4 + zl + (-2 if zl < 2 else 2)) % 8
-        return (z // 4, y, 1, x, z % 4) if c == 1 else None
-
-    def columns(value, start, count):
-        return lax.dynamic_slice_in_dim(value, start * size, count * size, 1)
-
-    halves = jnp.concatenate([columns(both_x, zh * 2, 2), moved(columns(both_x, (1 - zh) * 2, 2), over_z)])
-    kept = columns(halves, y // 2, 1)
-    come = moved(columns(halves, 1 - y // 2, 1), lambda zh, y, c, x, zl: (zh, 3 - y, 1, x, zl) if c == 1 else None)
-
-    samples = list(deal(jnp.stack([(zl + 2) % 4, core]), held, kept, come))
-    for k in (1, 2, 3):
-        samples[k] = moved(
-            samples[k],
-            lambda zh, y, c, x, zl: (z_shift(zh, zl, k)[0], y, 0, x, z_shift(zh, zl, k)[1]) if c == 0
-            else (zh, y, 1, (x + k) % 4, zl),
-        )
+    samples = dealt(
+        pack(core.reshape(1), samp_x, samp_g, other, size),
+        lambda *place: over_plane(*place) if place[2] == 0 else over_blocks(*place),
+    ).reshape(-1, size)
 
     chunks = cov(jnp.stack([jnp.where(is_g, y, x), 1 - core]), samples, scale)
     total = chunks[0].astype(F32)

time: 108 us -> 104 us (0.963); the launches traced: 108 us -> 102 us
  starting transfers between devices: 46.8 us -> 24.2 us
  waiting for transfers between devices: 32 us -> 51 us
  Pallas kernels: 23.8 us -> 22.4 us
    ppermute x21 -> x13, starting transfers between devices: 46.8 us -> 12.8 us  [moved(): return lax.ppermute(value, ('dp', 'owner'), pairs)]
    all_to_all x0 -> x1, waiting for transfers between devices: none -> 16.5 us  [dealt(): lax.all_to_all(value, ('dp', 'owner'), split_axis=0, concat_axis=0, tiled...]
    all_to_all x0 -> x1, starting transfers between devices: none -> 11.4 us  [dealt(): lax.all_to_all(value, ('dp', 'owner'), split_axis=0, concat_axis=0, tiled...]
    ppermute x21 -> x13, waiting for transfers between devices: 32 us -> 34.5 us  [moved(): return lax.ppermute(value, ('dp', 'owner'), pairs)]
    pallas_call x2 -> x1, Pallas kernels: 2.27 us -> 1.05 us  [pack(): pl.pallas_call(pack_kernel, out_shape=jax.ShapeDtypeStruct((16, 2 * samp_...]
  transfers between devices with their start and end apart: 21 -> 14, of which waited for: 9 -> 10; matrix products, arithmetic and copies ran while one was open for 2% -> 1% of each run, Pallas kernels for 15% -> 15%
where the time goes in v9:
time: 104 us; the launch traced here: 102 us
  waiting for transfers between devices  51 us (49%)
  starting transfers between devices  24.2 us (23%)
  Pallas kernels  22.4 us (22%)
  matrix products  3.28 us (3%)
    ppermute x13, waiting for transfers between devices, moved(): return lax.ppermute(value, ('dp', 'owner'), pairs)  34.5 us
    all_to_all x1, waiting for transfers between devices, dealt(): lax.all_to_all(value, ('dp', 'owner'), split_axis=0, concat_axis=0, tiled...  16.5 us
    pallas_call x1, Pallas kernels, rounds(): pl.pallas_call(rounds_kernel, out_shape=jax.ShapeDtypeStruct((size, size)...  15.4 us
    ppermute x13, starting transfers between devices, moved(): return lax.ppermute(value, ('dp', 'owner'), pairs)  12.8 us
    all_to_all x1, starting transfers between devices, dealt(): lax.all_to_all(value, ('dp', 'owner'), split_axis=0, concat_axis=0, tiled...  11.4 us
    dot_general x2, matrix products, dot(): return jnp.dot(a, b, preferred_element_type=F32)  3.28 us
    pallas_call x1, Pallas kernels, last(): pl.pallas_call(last_kernel, out_shape=jax.ShapeDtypeStruct((rows, mine.sh...  2.16 us
  transfers between devices with their start and end apart: 14, of which 10 were waited for; matrix products, arithmetic and copies ran while one was open for 1% of the time, Pallas kernels for 15%

profile of v9, /device:TPU:33, one launch (start us, length us, event | category | flops | bytes accessed | tf_op | source)
XLA Modules:
  0.0 102.2 jit_solution(1064264155623393006)
XLA Ops:
  0.0 3.0 %convolution_convert_fusion.g_ref = bf16[16,16384]{1,0:T(8,128)(2,1)S(1)} fusion(bf16[128,16384]{1,0:T(8,128)(2,1)} %param.6, s32[16]{0:T(128)} %param.7), kind=kOutput, calls=%fused_computation | convolution fusion | flops 67373056 | bytes 4718656 | tf_op jit(solution)/shard_map/dot_general | solution.py:20
  3.0 0.3 convolution_convert_fusion.1.x_ref
  3.4 0.8 collective-permute-start
  4.2 1.5 %collective-permute-done.other_ref = bf16[16,16384]{1,0:T(8,128)(2,1)S(1)} collective-permute-done((bf16[16,16384]{1,0:T(8,128)(2,1)S(1)}, bf16[16,16384]{1,0:T(8,128)(2,1)S(1)}, u32[]{:S(2)}, u32[]{:S(2)}) %collective-permute-start) | collective-permute-done | bytes 524320 | tf_op jit(solution)/shard_map/ppermute | solution.py:39
  5.7 1.0 %shard_map.56 = bf16[16,32,1024]{2,1,0:T(8,128)(2,1)} custom-call(s32[1]{0:T(128)} %bitcast.1.core_ref, bf16[16,4096]{1,0:T(8,128)(2,1)S(1)} %convolution_convert_fusion.1.x_ref, bf16[16,16384]{1,0:T(8,128)(2,1)S(1)} %convolution_convert_fusion.g_ref, bf16[16,16384]{1,0:T(8,128)(2,1)S(1)} %collective-permute-done.other_ref), custom_call_target="tpu_custom_call" | custom-call | tf_op jit(solution)/shard_map/pallas_call | solution.py:108
  6.7 11.4 %all-to-all-start = ((bf16[16,32,1024]{2,1,0:T(8,128)(2,1)}), bf16[16,32,1024]{2,1,0:T(8,128)(2,1)S(1)}, u32[]{:S(2)}, u32[]{:S(2)}) async-start(bf16[16,32,1024]{2,1,0:T(8,128)(2,1)} %shard_map.56), calls=%async_computation | async-start | bytes 2097152 | tf_op jit(solution)/shard_map/all_to_all | solution.py:51
  18.3 16.5 %all-to-all-done = bf16[16,32,1024]{2,1,0:T(8,128)(2,1)S(1)} async-done(((bf16[16,32,1024]{2,1,0:T(8,128)(2,1)}), bf16[16,32,1024]{2,1,0:T(8,128)(2,1)S(1)}, u32[]{:S(2)}, u32[]{:S(2)}) %all-to-all-start) | async-done | bytes 1048608 | tf_op jit(solution)/shard_map/all_to_all | solution.py:51
  34.8 1.8 %shard_map.57 = (bf16[1152,128]{1,0:T(8,128)(2,1)S(1)}, bf16[1152,128]{1,0:T(8,128)(2,1)S(1)}, bf16[1152,128]{1,0:T(8,128)(2,1)S(1)}, bf16[1152,128]{1,0:T(8,128)(2,1)S(1)}) custom-call(s32[2]{0:T(128)S(1)} %pad_add_fusion.1.refs_0_, bf16[512,1024]{1,0:T(8,128)(2,1)S(1)} %bitcast.7), custom_call_target="tpu_custom_call" | custom-call | tf_op jit(solution)/shard_map/pallas_call | solution.py:135
  36.7 1.9 %collective-permute-start.1 = (bf16[1152,128]{1,0:T(8,128)(2,1)S(1)}, bf16[1152,128]{1,0:T(8,128)(2,1)S(1)}, u32[]{:S(2)}, u32[]{:S(2)}) collective-permute-start(bf16[1152,128]{1,0:T(8,128)(2,1)S(1)} %get-tuple-element.17), channel_id=1, source_target_pairs={{0,32},{1,33},{2,34},{3,35},{4,36},{5,37},{6,38},{7,39},{8,40},{9,... | collective-permute-start | bytes 884744 | tf_op jit(solution)/shard_map/ppermute | solution.py:39
  38.6 3.4 %collective-permute-start.2 = (bf16[1152,128]{1,0:T(8,128)(2,1)S(1)}, bf16[1152,128]{1,0:T(8,128)(2,1)S(1)}, u32[]{:S(2)}, u32[]{:S(2)}) collective-permute-start(bf16[1152,128]{1,0:T(8,128)(2,1)S(1)} %get-tuple-element.18), channel_id=1, source_target_pairs={{0,64},{1,65},{2,66},{3,67},{4,68},{5,69},{6,70},{7,71},{8,72},{9,... | collective-permute-start | bytes 884744 | tf_op jit(solution)/shard_map/ppermute | solution.py:39
  42.0 2.3 %collective-permute-done.1 = bf16[1152,128]{1,0:T(8,128)(2,1)S(1)} collective-permute-done((bf16[1152,128]{1,0:T(8,128)(2,1)S(1)}, bf16[1152,128]{1,0:T(8,128)(2,1)S(1)}, u32[]{:S(2)}, u32[]{:S(2)}) %collective-permute-start.1) | collective-permute-done | bytes 294944 | tf_op jit(solution)/shard_map/ppermute | solution.py:39
  44.3 7.7 %collective-permute-done.2 = bf16[1152,128]{1,0:T(8,128)(2,1)S(1)} collective-permute-done((bf16[1152,128]{1,0:T(8,128)(2,1)S(1)}, bf16[1152,128]{1,0:T(8,128)(2,1)S(1)}, u32[]{:S(2)}, u32[]{:S(2)}) %collective-permute-start.2) | collective-permute-done | bytes 294944 | tf_op jit(solution)/shard_map/ppermute | solution.py:39
  52.0 9.1 %collective-permute-done.3 = bf16[1152,128]{1,0:T(8,128)(2,1)S(1)} collective-permute-done((bf16[1152,128]{1,0:T(8,128)(2,1)S(1)}, bf16[1152,128]{1,0:T(8,128)(2,1)S(1)}, u32[]{:S(2)}, u32[]{:S(2)}) %collective-permute-start.3) | collective-permute-done | bytes 294944 | tf_op jit(solution)/shard_map/ppermute | solution.py:39
  61.0 0.2 add_convert_fusion.1
  61.2 0.7 collective-permute-start.5
  61.9 0.1 collective-permute-start.4
  62.0 5.5 %collective-permute-done.4 = bf16[1152,128]{1,0:T(8,128)(2,1)S(1)} collective-permute-done((bf16[1152,128]{1,0:T(8,128)(2,1)S(1)}, bf16[1152,128]{1,0:T(8,128)(2,1)S(1)}, u32[]{:S(2)}, u32[]{:S(2)}) %collective-permute-start.4) | collective-permute-done | bytes 294944 | tf_op jit(solution)/shard_map/ppermute | solution.py:39
  67.6 0.1 collective-permute-start.8
  67.7 2.0 %collective-permute-start.7 = (bf16[1152,128]{1,0:T(8,128)(2,1)S(1)}, bf16[1152,128]{1,0:T(8,128)(2,1)S(1)}, u32[]{:S(2)}, u32[]{:S(2)}) collective-permute-start(bf16[1152,128]{1,0:T(8,128)(2,1)S(1)} %add_convert_fusion.p0), channel_id=1, source_target_pairs={{0,64},{1,65},{2,66},{3,67},{4,68},{5,69},{6,70},{7,71},{8,72},{9,... | collective-permute-start | bytes 884744 | tf_op jit(solution)/shard_map/ppermute | solution.py:39
  69.7 0.5 collective-permute-start.6
  70.3 0.6 dynamic_slice.4.damp_ref
  71.0 1.9 %collective-permute-start.11 = (bf16[256,1024]{1,0:T(8,128)(2,1)S(1)}, bf16[256,1024]{1,0:T(8,128)(2,1)S(1)}, u32[]{:S(2)}, u32[]{:S(2)}) collective-permute-start(bf16[256,1024]{1,0:T(8,128)(2,1)S(1)} %copy-done.1), channel_id=1, source_target_pairs={{0,0},{1,1},{2,2},{3,3},{4,4},{5,5},{6,6},{7,7},{8,8},{9,9},{10,10... | collective-permute-start | bytes 1572872 | tf_op jit(solution)/shard_map/ppermute | solution.py:39
  72.9 0.1 collective-permute-start.10
  73.0 0.7 collective-permute-done.8.p3
  73.7 1.3 %collective-permute-start.9 = (bf16[256,1024]{1,0:T(8,128)(2,1)S(1)}, bf16[256,1024]{1,0:T(8,128)(2,1)S(1)}, u32[]{:S(2)}, u32[]{:S(2)}) collective-permute-start(bf16[256,1024]{1,0:T(8,128)(2,1)S(1)} %copy-done.1), channel_id=1, source_target_pairs={{0,16},{1,17},{2,18},{3,19},{4,20},{5,21},{6,22},{7,23},{8,24},{9,... | collective-permute-start | bytes 1572872 | tf_op jit(solution)/shard_map/ppermute | solution.py:39
  74.9 0.2 collective-permute-done.7.p2
  75.2 3.3 %collective-permute-done.6.p1 = bf16[1152,128]{1,0:T(8,128)(2,1)} collective-permute-done((bf16[1152,128]{1,0:T(8,128)(2,1)S(1)}, bf16[1152,128]{1,0:T(8,128)(2,1)}, u32[]{:S(2)}, u32[]{:S(2)}) %collective-permute-start.6) | collective-permute-done | bytes 294944 | tf_op jit(solution)/shard_map/ppermute | solution.py:39
  78.4 15.4 %shard_map.58.s_ref = bf16[1024,1024]{1,0:T(8,128)(2,1)S(1)} custom-call(s32[3]{0:T(128)S(1)} %pad_add_fusion.place_ref, f32[1]{0:T(128)} %dynamic_slice.4.damp_ref, bf16[1152,128]{1,0:T(8,128)(2,1)S(1)} %add_convert_fusion.p0, bf16[1152,128]{1,0:T(8,128)(2,1)} %collective-permute-done.6.p1, bf16[1152,128]{1,0:T(8,128)(2,1)S(1)} %collective-permute-done.7.p2, ...), custom_call_target="tpu_custom_call" | custom-call | flops 17179869184 | bytes 4194304 | tf_op jit(solution)/shard_map/pallas_call | solution.py:206
  93.9 1.8 %shard_map.59.mine_ref = bf16[1024,1024]{1,0:T(8,128)(2,1)S(1)} custom-call(s32[3]{0:T(128)S(1)} %pad_add_fusion.place_ref, bf16[1024,1024]{1,0:T(8,128)(2,1)S(1)} %shard_map.58.s_ref, bf16[256,1024]{1,0:T(8,128)(2,1)S(1)} %collective-permute-done.9.w0, bf16[256,1024]{1,0:T(8,128)(2,1)S(1)} %copy-done.1, ...), custom_call_target="tpu_custom_call", output_to_operand_aliasing={{}: (1, {})} | custom-call | tf_op jit(solution)/shard_map/pallas_call | solution.py:241
  95.8 0.1 collective-permute-start.12
  95.9 4.1 %collective-permute-done.12.other_ref = bf16[1024,1024]{1,0:T(8,128)(2,1)S(1)} collective-permute-done((bf16[1024,1024]{1,0:T(8,128)(2,1)S(1)}, bf16[1024,1024]{1,0:T(8,128)(2,1)S(1)}, u32[]{:S(2)}, u32[]{:S(2)}) %collective-permute-start.12) | collective-permute-done | bytes 2097184 | tf_op jit(solution)/shard_map/ppermute | solution.py:39
  100.0 2.2 %shard_map.60 = bf16[256,1024]{1,0:T(8,128)(2,1)} custom-call(s32[3]{0:T(128)S(1)} %pad_add_fusion.place_ref, bf16[1024,1024]{1,0:T(8,128)(2,1)S(1)} %shard_map.59.mine_ref, bf16[1024,1024]{1,0:T(8,128)(2,1)S(1)} %collective-permute-done.12.other_ref), custom_call_target="tpu_custom_call" | custom-call | tf_op jit(solution)/shard_map/pallas_call | solution.py:272
  (17 shorter events, 0.3 us)
Async XLA Ops:
  0.0 3.0 %copy-start = (bf16[128,4096]{1,0:T(8,128)(2,1)S(1)}, bf16[128,4096]{1,0:T(8,128)(2,1)}, u32[]{:S(2)}) copy-start(bf16[128,4096]{1,0:T(8,128)(2,1)} %param.5) | copy-start | bytes 3145732
  0.0 3.0 %copy-start.2 = (s32[16]{0:T(128)S(1)}, s32[16]{0:T(128)}, u32[]{:S(2)}) copy-start(s32[16]{0:T(128)} %param.7) | copy-start | bytes 196
  3.4 66.9 %copy-start.3 = (f32[20]{0:T(128)S(1)}, f32[20]{0:T(128)}, u32[]{:S(2)}) copy-start(f32[20]{0:T(128)} %param.8) | copy-start | bytes 244
  3.4 67.6 %copy-start.1 = (bf16[256,1024]{1,0:T(8,128)(2,1)S(1)}, bf16[256,1024]{1,0:T(8,128)(2,1)}, u32[]{:S(2)}) copy-start(bf16[256,1024]{1,0:T(8,128)(2,1)} %w1.1) | copy-start | bytes 1572868
  3.4 2.3 %collective-permute-start = (bf16[16,16384]{1,0:T(8,128)(2,1)S(1)}, bf16[16,16384]{1,0:T(8,128)(2,1)S(1)}, u32[]{:S(2)}, u32[]{:S(2)}) collective-permute-start(bf16[16,16384]{1,0:T(8,128)(2,1)S(1)} %shard_map.55), channel_id=1, source_target_pairs={{0,16},{1,17},{2,18},{3,19},{4,20},{5,21},{6,22},{7,23},{8,24},{9,... | collective-permute-start | bytes 1572872 | tf_op jit(solution)/shard_map/ppermute | solution.py:39
  6.7 28.1 %all-to-all-start = ((bf16[16,32,1024]{2,1,0:T(8,128)(2,1)}), bf16[16,32,1024]{2,1,0:T(8,128)(2,1)S(1)}, u32[]{:S(2)}, u32[]{:S(2)}) async-start(bf16[16,32,1024]{2,1,0:T(8,128)(2,1)} %shard_map.56), calls=%async_computation | async-start | bytes 2097152 | tf_op jit(solution)/shard_map/all_to_all | solution.py:51
  36.7 7.6 %collective-permute-start.1 = (bf16[1152,128]{1,0:T(8,128)(2,1)S(1)}, bf16[1152,128]{1,0:T(8,128)(2,1)S(1)}, u32[]{:S(2)}, u32[]{:S(2)}) collective-permute-start(bf16[1152,128]{1,0:T(8,128)(2,1)S(1)} %get-tuple-element.17), channel_id=1, source_target_pairs={{0,32},{1,33},{2,34},{3,35},{4,36},{5,37},{6,38},{7,39},{8,40},{9,... | collective-permute-start | bytes 884744 | tf_op jit(solution)/shard_map/ppermute | solution.py:39
  38.6 13.4 %collective-permute-start.2 = (bf16[1152,128]{1,0:T(8,128)(2,1)S(1)}, bf16[1152,128]{1,0:T(8,128)(2,1)S(1)}, u32[]{:S(2)}, u32[]{:S(2)}) collective-permute-start(bf16[1152,128]{1,0:T(8,128)(2,1)S(1)} %get-tuple-element.18), channel_id=1, source_target_pairs={{0,64},{1,65},{2,66},{3,67},{4,68},{5,69},{6,70},{7,71},{8,72},{9,... | collective-permute-start | bytes 884744 | tf_op jit(solution)/shard_map/ppermute | solution.py:39
  42.0 19.1 %collective-permute-start.3 = (bf16[1152,128]{1,0:T(8,128)(2,1)S(1)}, bf16[1152,128]{1,0:T(8,128)(2,1)S(1)}, u32[]{:S(2)}, u32[]{:S(2)}) collective-permute-start(bf16[1152,128]{1,0:T(8,128)(2,1)S(1)} %get-tuple-element.19), channel_id=1, source_target_pairs={{0,96},{1,97},{2,98},{3,99},{4,100},{5,101},{6,102},{7,103},{8,104... | collective-permute-start | bytes 884744 | tf_op jit(solution)/shard_map/ppermute | solution.py:39
  61.2 0.8 collective-permute-start.5
  61.9 5.7 %collective-permute-start.4 = (bf16[1152,128]{1,0:T(8,128)(2,1)S(1)}, bf16[1152,128]{1,0:T(8,128)(2,1)S(1)}, u32[]{:S(2)}, u32[]{:S(2)}) collective-permute-start(bf16[1152,128]{1,0:T(8,128)(2,1)S(1)} %add_convert_fusion.1), channel_id=1, source_target_pairs={{0,2},{1,3},{2,128},{3,129},{4,6},{5,7},{6,132},{7,133},{8,10},{9,... | collective-permute-start | bytes 884744 | tf_op jit(solution)/shard_map/ppermute | solution.py:39
  67.6 6.1 %collective-permute-start.8 = (bf16[1152,128]{1,0:T(8,128)(2,1)S(1)}, bf16[1152,128]{1,0:T(8,128)(2,1)S(1)}, u32[]{:S(2)}, u32[]{:S(2)}) collective-permute-start(bf16[1152,128]{1,0:T(8,128)(2,1)S(1)} %add_convert_fusion.p0), channel_id=1, source_target_pairs={{0,96},{1,97},{2,98},{3,99},{4,100},{5,101},{6,102},{7,103},{8,104... | collective-permute-start | bytes 884744 | tf_op jit(solution)/shard_map/ppermute | solution.py:39
  67.7 7.5 %collective-permute-start.7 = (bf16[1152,128]{1,0:T(8,128)(2,1)S(1)}, bf16[1152,128]{1,0:T(8,128)(2,1)S(1)}, u32[]{:S(2)}, u32[]{:S(2)}) collective-permute-start(bf16[1152,128]{1,0:T(8,128)(2,1)S(1)} %add_convert_fusion.p0), channel_id=1, source_target_pairs={{0,64},{1,65},{2,66},{3,67},{4,68},{5,69},{6,70},{7,71},{8,72},{9,... | collective-permute-start | bytes 884744 | tf_op jit(solution)/shard_map/ppermute | solution.py:39
  69.7 8.7 %collective-permute-start.6 = (bf16[1152,128]{1,0:T(8,128)(2,1)S(1)}, bf16[1152,128]{1,0:T(8,128)(2,1)}, u32[]{:S(2)}, u32[]{:S(2)}) collective-permute-start(bf16[1152,128]{1,0:T(8,128)(2,1)S(1)} %add_convert_fusion.p0), channel_id=1, source_target_pairs={{0,32},{1,33},{2,34},{3,35},{4,36},{5,37},{6,38},{7,39},{8,40},{9,... | collective-permute-start | bytes 884744 | tf_op jit(solution)/shard_map/ppermute | solution.py:39
  71.0 22.9 %collective-permute-start.11 = (bf16[256,1024]{1,0:T(8,128)(2,1)S(1)}, bf16[256,1024]{1,0:T(8,128)(2,1)S(1)}, u32[]{:S(2)}, u32[]{:S(2)}) collective-permute-start(bf16[256,1024]{1,0:T(8,128)(2,1)S(1)} %copy-done.1), channel_id=1, source_target_pairs={{0,0},{1,1},{2,2},{3,3},{4,4},{5,5},{6,6},{7,7},{8,8},{9,9},{10,10... | collective-permute-start | bytes 1572872 | tf_op jit(solution)/shard_map/ppermute | solution.py:39
  72.9 21.0 %collective-permute-start.10 = (bf16[256,1024]{1,0:T(8,128)(2,1)S(1)}, bf16[256,1024]{1,0:T(8,128)(2,1)S(1)}, u32[]{:S(2)}, u32[]{:S(2)}) collective-permute-start(bf16[256,1024]{1,0:T(8,128)(2,1)S(1)} %copy-done.1), channel_id=1, source_target_pairs={{0,48},{1,49},{2,50},{3,51},{4,52},{5,53},{6,54},{7,55},{8,56},{9,... | collective-permute-start | bytes 1572872 | tf_op jit(solution)/shard_map/ppermute | solution.py:39
  73.7 20.2 %collective-permute-start.9 = (bf16[256,1024]{1,0:T(8,128)(2,1)S(1)}, bf16[256,1024]{1,0:T(8,128)(2,1)S(1)}, u32[]{:S(2)}, u32[]{:S(2)}) collective-permute-start(bf16[256,1024]{1,0:T(8,128)(2,1)S(1)} %copy-done.1), channel_id=1, source_target_pairs={{0,16},{1,17},{2,18},{3,19},{4,20},{5,21},{6,22},{7,23},{8,24},{9,... | collective-permute-start | bytes 1572872 | tf_op jit(solution)/shard_map/ppermute | solution.py:39
  95.8 4.2 %collective-permute-start.12 = (bf16[1024,1024]{1,0:T(8,128)(2,1)S(1)}, bf16[1024,1024]{1,0:T(8,128)(2,1)S(1)}, u32[]{:S(2)}, u32[]{:S(2)}) collective-permute-start(bf16[1024,1024]{1,0:T(8,128)(2,1)S(1)} %shard_map.59.mine_ref), channel_id=1, source_target_pairs={{0,16},{1,17},{2,18},{3,19},{4,20},{5,21},{6,22},{7,23},{8,24},{9,... | collective-permute-start | bytes 6291464 | tf_op jit(solution)/shard_map/ppermute | solution.py:39

commit v10 on v9

--- a/solution.py
+++ b/solution.py
@@ -14,6 +14,7 @@
 PARTS = [UPPER[9 * i:9 * (i + 1)] for i in range(4)]
 SMEM = pl.BlockSpec(memory_space=pltpu.SMEM)
 VMEM = pl.BlockSpec(memory_space=pltpu.VMEM)
+ANY = pl.BlockSpec(memory_space=pl.ANY)
 
 
 def dot(a, b):
@@ -142,10 +143,14 @@
     )(place, samples)
 
 
-def rounds_kernel(place_ref, damp_ref, p0, p1, p2, p3, out_ref, a_ref, x_ref, xb_ref, p_ref, parts_ref):
+def rounds_kernel(place_ref, damp_ref, p0, p1, p2, p3, w0, w1, w2, w3, out_ref,
+                  a_ref, x_ref, xb_ref, p_ref, parts_ref, w_ref, sems):
     size = out_ref.shape[0]
     tile, small = size // 4, size // 8
-    base, damp = place_ref[0], damp_ref[0]
+    base, core, half, damp = place_ref[0], place_ref[1], place_ref[2], damp_ref[0]
+    loads = [pltpu.make_async_copy(w, w_ref.at[i], sems.at[i]) for i, w in enumerate((w0, w1, w2, w3))]
+    for load in loads:
+        load.start()
     blocks = [slice(i * tile, (i + 1) * tile) for i in range(4)]
 
     def mirrored(ref, c, value):
@@ -200,13 +205,27 @@
             else:
                 mirrored(out_ref, c, (value * (frob / 2.0 ** ITERS)).astype(BF16))
 
-
-def rounds(place, damp, pieces):
-    size = pieces[0].shape[1] * 8
+    for load in loads:
+        load.wait()
+
+    @pl.when(core == 1)
+    def _():
+        for i in range(2):
+            rows = pl.ds(pl.multiple_of((2 * half + i) * tile, tile), tile)
+            value = jnp.zeros((tile, size), F32)
+            for b in range(4):
+                cols = pl.ds(pl.multiple_of(lax.rem(2 * half + b, 4) * tile, tile), tile)
+                value += dot(out_ref[rows, cols], w_ref[b])
+            p_ref[blocks[i], :] = value.astype(BF16)
+        out_ref[:2 * tile, :] = p_ref[:2 * tile, :]
+
+
+def rounds(place, damp, pieces, weights):
+    tile, size = weights[0].shape
     return pl.pallas_call(
         rounds_kernel,
         out_shape=jax.ShapeDtypeStruct((size, size), BF16),
-        in_specs=[SMEM, SMEM] + [VMEM] * 4,
+        in_specs=[SMEM, SMEM] + [VMEM] * 4 + [ANY] * 4,
         out_specs=VMEM,
         scratch_shapes=[
             pltpu.VMEM((size, size), BF16),
@@ -214,39 +233,11 @@
             pltpu.VMEM((2, size, size), BF16),
             pltpu.VMEM((size, size), BF16),
             pltpu.VMEM((4,) + pieces[0].shape, BF16),
+            pltpu.VMEM((4, tile, size), BF16),
+            pltpu.SemaphoreType.DMA((4,)),
         ],
-        cost_estimate=pl.CostEstimate(flops=16 * size ** 3, transcendentals=0, bytes_accessed=4 * size * size),
-        compiler_params=pltpu.CompilerParams(vmem_limit_bytes=24 * MIB),
-    )(place, damp, *pieces)
-
-
-def mix_kernel(place_ref, s_ref, w0, w1, w2, w3, out_ref, t_ref):
-    tile, size = w0.shape
-    half = place_ref[2]
-
-    @pl.when(place_ref[1] == 1)
-    def _():
-        for i in range(2):
-            rows = pl.ds(pl.multiple_of((2 * half + i) * tile, tile), tile)
-            value = jnp.zeros((tile, size), F32)
-            for b, w in enumerate((w0, w1, w2, w3)):
-                cols = pl.ds(pl.multiple_of(lax.rem(2 * half + b, 4) * tile, tile), tile)
-                value += dot(s_ref[rows, cols], w[...])
-            t_ref[i * tile:(i + 1) * tile, :] = value.astype(BF16)
-        out_ref[:2 * tile, :] = t_ref[...]
-
-
-def mix(place, inverse, weights):
-    tile, size = weights[0].shape
-    return pl.pallas_call(
-        mix_kernel,
-        out_shape=jax.ShapeDtypeStruct(inverse.shape, BF16),
-        in_specs=[SMEM] + [VMEM] * 5,
-        out_specs=VMEM,
-        scratch_shapes=[pltpu.VMEM((2 * tile, size), BF16)],
-        input_output_aliases={1: 0},
-        compiler_params=pltpu.CompilerParams(vmem_limit_bytes=16 * MIB),
-    )(place, inverse, *weights)
+        compiler_params=pltpu.CompilerParams(vmem_limit_bytes=28 * MIB),
+    )(place, damp, *pieces, *weights)
 
 
 def last_kernel(place_ref, mine_ref, other_ref, out_ref):
@@ -296,10 +287,19 @@
     samp_x = dot(hot, activations).astype(BF16)
     other = moved(offer(core.reshape(1), samp_x, samp_g), lambda zh, y, c, x, zl: (zh, y, 1 - c, x, zl))
 
+    packed = pack(core.reshape(1), samp_x, samp_g, other, size)
     samples = dealt(
-        pack(core.reshape(1), samp_x, samp_g, other, size),
-        lambda *place: over_plane(*place) if place[2] == 0 else over_blocks(*place),
+        packed, lambda *place: over_plane(*place) if place[2] == 0 else over_blocks(*place),
     ).reshape(-1, size)
+
+    own_w, _ = lax.optimization_barrier((weight_grad, packed))
+    weights = [
+        moved(own_w, lambda zh, y, c, x, zl: (zh, y, 1 - c, x, zl)),
+        moved(own_w, lambda zh, y, c, x, zl: (zh, y ^ 1, 1, x, zl) if c == 0 else (zh, y, 0, x, zl)),
+        moved(own_w, lambda zh, y, c, x, zl: (zh, y ^ 1, 1, x, zl) if c == 1 else None),
+    ]
+    samples, weights = lax.optimization_barrier((samples, weights))
+    weights.insert(1, weight_grad)
 
     chunks = cov(jnp.stack([jnp.where(is_g, y, x), 1 - core]), samples, scale)
     total = chunks[0].astype(F32)
@@ -327,18 +327,9 @@
             lambda zh, y, c, x, zl: (zh, (y + k) % 4, 0, x, zl) if c == 0 else (zh, y, 1, (x + k) % 4, zl),
         ))
 
-    own_w, _ = lax.optimization_barrier((weight_grad, piece))
-    weights = [
-        moved(own_w, lambda zh, y, c, x, zl: (zh, y, 1 - c, x, zl)),
-        moved(own_w, lambda zh, y, c, x, zl: (zh, y ^ 1, 1, x, zl) if c == 0 else (zh, y, 0, x, zl)),
-        moved(own_w, lambda zh, y, c, x, zl: (zh, y ^ 1, 1, x, zl) if c == 1 else None),
-    ]
     damp = pick(damping, jnp.where(is_g, BLOCKS_A + o, zh * 2 + y // 2)).reshape(1)
     place = jnp.stack([jnp.where(is_g, y, x), core, y % 2])
-    inverse, *weights = lax.optimization_barrier((rounds(place, damp, pieces), *weights))
-    weights.insert(1, weight_grad)
-
-    mine = mix(place, inverse, weights)
+    mine = rounds(place, damp, pieces, weights)
     other = moved(mine, lambda zh, y, c, x, zl: (zh, y, 1 - c, x, zl))
     return last(place, mine, other, weight_grad.shape[0])
 

time: 104 us -> 102 us (0.981); the launches traced: 102 us -> 101 us
    all_to_all x1, waiting for transfers between devices: 16.5 us -> 0.82 us  [dealt(): lax.all_to_all(value, ('dp', 'owner'), split_axis=0, concat_axis=0, tiled...]
    ppermute x13, waiting for transfers between devices: 34.5 us -> 49.5 us  [moved(): return lax.ppermute(value, ('dp', 'owner'), pairs)]
    pallas_call x1 -> x0, Pallas kernels: 1.85 us -> none  [mix(): pl.pallas_call(mix_kernel, out_shape=jax.ShapeDtypeStruct(inverse.shape,...]
    pallas_call x1, Pallas kernels: 15.4 us -> 16.6 us  [rounds(): pl.pallas_call(rounds_kernel, out_shape=jax.ShapeDtypeStruct((size, size)...]
  transfers between devices with their start and end apart: 14 -> 14, of which waited for: 10 -> 12; matrix products, arithmetic and copies ran while one was open for 1% -> 1% of each run, Pallas kernels for 15% -> 0%
where the time goes in v10:
time: 102 us; the launch traced here: 101 us
  waiting for transfers between devices  50.4 us (49%)
  starting transfers between devices  24.8 us (24%)
  Pallas kernels  21.8 us (21%)
  matrix products  3.28 us (3%)
    ppermute x13, waiting for transfers between devices, moved(): return lax.ppermute(value, ('dp', 'owner'), pairs)  49.5 us
    pallas_call x1, Pallas kernels, rounds(): pl.pallas_call(rounds_kernel, out_shape=jax.ShapeDtypeStruct((size, size)...  16.6 us
    ppermute x13, starting transfers between devices, moved(): return lax.ppermute(value, ('dp', 'owner'), pairs)  13.4 us
    all_to_all x1, starting transfers between devices, dealt(): lax.all_to_all(value, ('dp', 'owner'), split_axis=0, concat_axis=0, tiled...  11.4 us
    dot_general x2, matrix products, dot(): return jnp.dot(a, b, preferred_element_type=F32)  3.28 us
    pallas_call x1, Pallas kernels, last(): pl.pallas_call(last_kernel, out_shape=jax.ShapeDtypeStruct((rows, mine.sh...  2.17 us
  transfers between devices with their start and end apart: 14, of which 12 were waited for; matrix products, arithmetic and copies ran while one was open for 1% of the time, Pallas kernels for 0%

profile of v10, /device:TPU:33, one launch (start us, length us, event | category | flops | bytes accessed | tf_op | source)
XLA Modules:
  0.0 101.4 jit_solution(6765813144669868056)
XLA Ops:
  0.0 3.0 %convolution_convert_fusion.g_ref = bf16[16,16384]{1,0:T(8,128)(2,1)S(1)} fusion(bf16[128,16384]{1,0:T(8,128)(2,1)} %param.6, s32[16]{0:T(128)} %param.7), kind=kOutput, calls=%fused_computation | convolution fusion | flops 67373056 | bytes 4718656 | tf_op jit(solution)/shard_map/dot_general | solution.py:21
  3.0 0.3 convolution_convert_fusion.1.x_ref
  3.4 0.8 collective-permute-start
  4.2 1.5 %collective-permute-done.other_ref = bf16[16,16384]{1,0:T(8,128)(2,1)S(1)} collective-permute-done((bf16[16,16384]{1,0:T(8,128)(2,1)S(1)}, bf16[16,16384]{1,0:T(8,128)(2,1)S(1)}, u32[]{:S(2)}, u32[]{:S(2)}) %collective-permute-start) | collective-permute-done | bytes 524320 | tf_op jit(solution)/shard_map/ppermute | solution.py:40
  5.7 1.0 %shard_map.56 = bf16[16,32,1024]{2,1,0:T(8,128)(2,1)} custom-call(s32[1]{0:T(128)} %bitcast.1.core_ref, bf16[16,4096]{1,0:T(8,128)(2,1)S(1)} %convolution_convert_fusion.1.x_ref, bf16[16,16384]{1,0:T(8,128)(2,1)S(1)} %convolution_convert_fusion.g_ref, bf16[16,16384]{1,0:T(8,128)(2,1)S(1)} %collective-permute-done.other_ref), custom_call_target="tpu_custom_call" | custom-call | tf_op jit(solution)/shard_map/pallas_call | solution.py:109
  6.7 11.4 %all-to-all-start = ((bf16[16,32,1024]{2,1,0:T(8,128)(2,1)}), bf16[16,32,1024]{2,1,0:T(8,128)(2,1)S(1)}, u32[]{:S(2)}, u32[]{:S(2)}) async-start(bf16[16,32,1024]{2,1,0:T(8,128)(2,1)} %shard_map.56), calls=%async_computation | async-start | bytes 2097152 | tf_op jit(solution)/shard_map/all_to_all | solution.py:52
  18.2 1.9 %collective-permute-start.3 = (bf16[256,1024]{1,0:T(8,128)(2,1)S(1)}, bf16[256,1024]{1,0:T(8,128)(2,1)S(1)}, u32[]{:S(2)}, u32[]{:S(2)}) collective-permute-start(bf16[256,1024]{1,0:T(8,128)(2,1)S(1)} %copy-done.1), channel_id=1, source_target_pairs={{0,0},{1,1},{2,2},{3,3},{4,4},{5,5},{6,6},{7,7},{8,8},{9,9},{10,10... | collective-permute-start | bytes 1572872 | tf_op jit(solution)/shard_map/ppermute | solution.py:40
  20.1 0.1 collective-permute-start.2
  20.2 1.8 %collective-permute-start.1 = (bf16[256,1024]{1,0:T(8,128)(2,1)S(1)}, bf16[256,1024]{1,0:T(8,128)(2,1)}, u32[]{:S(2)}, u32[]{:S(2)}) collective-permute-start(bf16[256,1024]{1,0:T(8,128)(2,1)S(1)} %copy-done.1), channel_id=1, source_target_pairs={{0,16},{1,17},{2,18},{3,19},{4,20},{5,21},{6,22},{7,23},{8,24},{9,... | collective-permute-start | bytes 1572872 | tf_op jit(solution)/shard_map/ppermute | solution.py:40
  22.1 11.0 %collective-permute-done.3.w3 = bf16[256,1024]{1,0:T(8,128)(2,1)S(1)} collective-permute-done((bf16[256,1024]{1,0:T(8,128)(2,1)S(1)}, bf16[256,1024]{1,0:T(8,128)(2,1)S(1)}, u32[]{:S(2)}, u32[]{:S(2)}) %collective-permute-start.3) | collective-permute-done | bytes 524320 | tf_op jit(solution)/shard_map/ppermute | solution.py:40
  33.1 0.9 collective-permute-done.2.w2
  34.0 0.8 all-to-all-done
  34.8 1.8 %shard_map.57 = (bf16[1152,128]{1,0:T(8,128)(2,1)S(1)}, bf16[1152,128]{1,0:T(8,128)(2,1)S(1)}, bf16[1152,128]{1,0:T(8,128)(2,1)S(1)}, bf16[1152,128]{1,0:T(8,128)(2,1)S(1)}) custom-call(s32[2]{0:T(128)S(1)} %pad_add_fusion.1.refs_0_, bf16[512,1024]{1,0:T(8,128)(2,1)S(1)} %bitcast.7), custom_call_target="tpu_custom_call" | custom-call | tf_op jit(solution)/shard_map/pallas_call | solution.py:136
  36.7 1.9 %collective-permute-start.4 = (bf16[1152,128]{1,0:T(8,128)(2,1)S(1)}, bf16[1152,128]{1,0:T(8,128)(2,1)S(1)}, u32[]{:S(2)}, u32[]{:S(2)}) collective-permute-start(bf16[1152,128]{1,0:T(8,128)(2,1)S(1)} %get-tuple-element.19), channel_id=1, source_target_pairs={{0,32},{1,33},{2,34},{3,35},{4,36},{5,37},{6,38},{7,39},{8,40},{9,... | collective-permute-start | bytes 884744 | tf_op jit(solution)/shard_map/ppermute | solution.py:40
  38.6 3.4 %collective-permute-start.5 = (bf16[1152,128]{1,0:T(8,128)(2,1)S(1)}, bf16[1152,128]{1,0:T(8,128)(2,1)S(1)}, u32[]{:S(2)}, u32[]{:S(2)}) collective-permute-start(bf16[1152,128]{1,0:T(8,128)(2,1)S(1)} %get-tuple-element.20), channel_id=1, source_target_pairs={{0,64},{1,65},{2,66},{3,67},{4,68},{5,69},{6,70},{7,71},{8,72},{9,... | collective-permute-start | bytes 884744 | tf_op jit(solution)/shard_map/ppermute | solution.py:40
  42.0 2.3 %collective-permute-done.4 = bf16[1152,128]{1,0:T(8,128)(2,1)S(1)} collective-permute-done((bf16[1152,128]{1,0:T(8,128)(2,1)S(1)}, bf16[1152,128]{1,0:T(8,128)(2,1)S(1)}, u32[]{:S(2)}, u32[]{:S(2)}) %collective-permute-start.4) | collective-permute-done | bytes 294944 | tf_op jit(solution)/shard_map/ppermute | solution.py:40
  44.3 7.7 %collective-permute-done.5 = bf16[1152,128]{1,0:T(8,128)(2,1)S(1)} collective-permute-done((bf16[1152,128]{1,0:T(8,128)(2,1)S(1)}, bf16[1152,128]{1,0:T(8,128)(2,1)S(1)}, u32[]{:S(2)}, u32[]{:S(2)}) %collective-permute-start.5) | collective-permute-done | bytes 294944 | tf_op jit(solution)/shard_map/ppermute | solution.py:40
  52.0 9.1 %collective-permute-done.6 = bf16[1152,128]{1,0:T(8,128)(2,1)S(1)} collective-permute-done((bf16[1152,128]{1,0:T(8,128)(2,1)S(1)}, bf16[1152,128]{1,0:T(8,128)(2,1)S(1)}, u32[]{:S(2)}, u32[]{:S(2)}) %collective-permute-start.6) | collective-permute-done | bytes 294944 | tf_op jit(solution)/shard_map/ppermute | solution.py:40
  61.0 0.2 add_convert_fusion.1
  61.2 0.7 collective-permute-start.8
  61.9 0.1 collective-permute-start.7
  62.0 5.5 %collective-permute-done.7 = bf16[1152,128]{1,0:T(8,128)(2,1)S(1)} collective-permute-done((bf16[1152,128]{1,0:T(8,128)(2,1)S(1)}, bf16[1152,128]{1,0:T(8,128)(2,1)S(1)}, u32[]{:S(2)}, u32[]{:S(2)}) %collective-permute-start.7) | collective-permute-done | bytes 294944 | tf_op jit(solution)/shard_map/ppermute | solution.py:40
  67.7 2.0 %collective-permute-start.10 = (bf16[1152,128]{1,0:T(8,128)(2,1)S(1)}, bf16[1152,128]{1,0:T(8,128)(2,1)S(1)}, u32[]{:S(2)}, u32[]{:S(2)}) collective-permute-start(bf16[1152,128]{1,0:T(8,128)(2,1)S(1)} %add_convert_fusion.p0), channel_id=1, source_target_pairs={{0,64},{1,65},{2,66},{3,67},{4,68},{5,69},{6,70},{7,71},{8,72},{9,... | collective-permute-start | bytes 884744 | tf_op jit(solution)/shard_map/ppermute | solution.py:40
  69.7 0.6 collective-permute-start.9
  70.3 0.7 dynamic_slice.4.damp_ref
  71.0 2.6 %collective-permute-done.11.p3 = bf16[1152,128]{1,0:T(8,128)(2,1)S(1)} collective-permute-done((bf16[1152,128]{1,0:T(8,128)(2,1)S(1)}, bf16[1152,128]{1,0:T(8,128)(2,1)S(1)}, u32[]{:S(2)}, u32[]{:S(2)}) %collective-permute-start.11) | collective-permute-done | bytes 294944 | tf_op jit(solution)/shard_map/ppermute | solution.py:40
  73.6 1.6 %collective-permute-done.10.p2 = bf16[1152,128]{1,0:T(8,128)(2,1)S(1)} collective-permute-done((bf16[1152,128]{1,0:T(8,128)(2,1)S(1)}, bf16[1152,128]{1,0:T(8,128)(2,1)S(1)}, u32[]{:S(2)}, u32[]{:S(2)}) %collective-permute-start.10) | collective-permute-done | bytes 294944 | tf_op jit(solution)/shard_map/ppermute | solution.py:40
  75.2 3.1 %collective-permute-done.9.p1 = bf16[1152,128]{1,0:T(8,128)(2,1)S(1)} collective-permute-done((bf16[1152,128]{1,0:T(8,128)(2,1)S(1)}, bf16[1152,128]{1,0:T(8,128)(2,1)S(1)}, u32[]{:S(2)}, u32[]{:S(2)}) %collective-permute-start.9) | collective-permute-done | bytes 294944 | tf_op jit(solution)/shard_map/ppermute | solution.py:40
  78.3 16.6 %shard_map.58.mine_ref = bf16[1024,1024]{1,0:T(8,128)(2,1)S(1)} custom-call(s32[3]{0:T(128)S(1)} %pad_add_fusion.place_ref, f32[1]{0:T(128)} %dynamic_slice.4.damp_ref, bf16[1152,128]{1,0:T(8,128)(2,1)S(1)} %add_convert_fusion.p0, bf16[1152,128]{1,0:T(8,128)(2,1)S(1)} %collective-permute-done.9.p1, bf16[1152,128]{1,0:T(8,128)(2,1)S(1)} %collective-permute-done.10.p2, ...), custom_call_target="tpu_custom_call" | custom-call | tf_op jit(solution)/shard_map/pallas_call | solution.py:225
  95.0 0.1 collective-permute-start.12
  95.1 4.1 %collective-permute-done.12.other_ref = bf16[1024,1024]{1,0:T(8,128)(2,1)S(1)} collective-permute-done((bf16[1024,1024]{1,0:T(8,128)(2,1)S(1)}, bf16[1024,1024]{1,0:T(8,128)(2,1)S(1)}, u32[]{:S(2)}, u32[]{:S(2)}) %collective-permute-start.12) | collective-permute-done | bytes 2097184 | tf_op jit(solution)/shard_map/ppermute | solution.py:40
  99.2 2.2 %shard_map.59 = bf16[256,1024]{1,0:T(8,128)(2,1)} custom-call(s32[3]{0:T(128)S(1)} %pad_add_fusion.place_ref, bf16[1024,1024]{1,0:T(8,128)(2,1)S(1)} %shard_map.58.mine_ref, bf16[1024,1024]{1,0:T(8,128)(2,1)S(1)} %collective-permute-done.12.other_ref), custom_call_target="tpu_custom_call" | custom-call | tf_op jit(solution)/shard_map/pallas_call | solution.py:263
  (16 shorter events, 0.4 us)
Async XLA Ops:
  0.0 3.0 %copy-start = (bf16[128,4096]{1,0:T(8,128)(2,1)S(1)}, bf16[128,4096]{1,0:T(8,128)(2,1)}, u32[]{:S(2)}) copy-start(bf16[128,4096]{1,0:T(8,128)(2,1)} %param.5) | copy-start | bytes 3145732
  0.0 3.0 %copy-start.2 = (s32[16]{0:T(128)S(1)}, s32[16]{0:T(128)}, u32[]{:S(2)}) copy-start(s32[16]{0:T(128)} %param.7) | copy-start | bytes 196
  3.0 15.1 %copy-start.1 = (bf16[256,1024]{1,0:T(8,128)(2,1)S(1)}, bf16[256,1024]{1,0:T(8,128)(2,1)}, u32[]{:S(2)}) copy-start(bf16[256,1024]{1,0:T(8,128)(2,1)} %w1.1) | copy-start | bytes 1572868
  3.4 66.9 %copy-start.3 = (f32[20]{0:T(128)S(1)}, f32[20]{0:T(128)}, u32[]{:S(2)}) copy-start(f32[20]{0:T(128)} %param.8) | copy-start | bytes 244
  3.4 2.3 %collective-permute-start = (bf16[16,16384]{1,0:T(8,128)(2,1)S(1)}, bf16[16,16384]{1,0:T(8,128)(2,1)S(1)}, u32[]{:S(2)}, u32[]{:S(2)}) collective-permute-start(bf16[16,16384]{1,0:T(8,128)(2,1)S(1)} %shard_map.55), channel_id=1, source_target_pairs={{0,16},{1,17},{2,18},{3,19},{4,20},{5,21},{6,22},{7,23},{8,24},{9,... | collective-permute-start | bytes 1572872 | tf_op jit(solution)/shard_map/ppermute | solution.py:40
  6.7 28.1 %all-to-all-start = ((bf16[16,32,1024]{2,1,0:T(8,128)(2,1)}), bf16[16,32,1024]{2,1,0:T(8,128)(2,1)S(1)}, u32[]{:S(2)}, u32[]{:S(2)}) async-start(bf16[16,32,1024]{2,1,0:T(8,128)(2,1)} %shard_map.56), calls=%async_computation | async-start | bytes 2097152 | tf_op jit(solution)/shard_map/all_to_all | solution.py:52
  18.2 14.9 %collective-permute-start.3 = (bf16[256,1024]{1,0:T(8,128)(2,1)S(1)}, bf16[256,1024]{1,0:T(8,128)(2,1)S(1)}, u32[]{:S(2)}, u32[]{:S(2)}) collective-permute-start(bf16[256,1024]{1,0:T(8,128)(2,1)S(1)} %copy-done.1), channel_id=1, source_target_pairs={{0,0},{1,1},{2,2},{3,3},{4,4},{5,5},{6,6},{7,7},{8,8},{9,9},{10,10... | collective-permute-start | bytes 1572872 | tf_op jit(solution)/shard_map/ppermute | solution.py:40
  20.1 13.9 %collective-permute-start.2 = (bf16[256,1024]{1,0:T(8,128)(2,1)S(1)}, bf16[256,1024]{1,0:T(8,128)(2,1)}, u32[]{:S(2)}, u32[]{:S(2)}) collective-permute-start(bf16[256,1024]{1,0:T(8,128)(2,1)S(1)} %copy-done.1), channel_id=1, source_target_pairs={{0,48},{1,49},{2,50},{3,51},{4,52},{5,53},{6,54},{7,55},{8,56},{9,... | collective-permute-start | bytes 1572872 | tf_op jit(solution)/shard_map/ppermute | solution.py:40
  20.2 13.8 %collective-permute-start.1 = (bf16[256,1024]{1,0:T(8,128)(2,1)S(1)}, bf16[256,1024]{1,0:T(8,128)(2,1)}, u32[]{:S(2)}, u32[]{:S(2)}) collective-permute-start(bf16[256,1024]{1,0:T(8,128)(2,1)S(1)} %copy-done.1), channel_id=1, source_target_pairs={{0,16},{1,17},{2,18},{3,19},{4,20},{5,21},{6,22},{7,23},{8,24},{9,... | collective-permute-start | bytes 1572872 | tf_op jit(solution)/shard_map/ppermute | solution.py:40
  36.7 7.6 %collective-permute-start.4 = (bf16[1152,128]{1,0:T(8,128)(2,1)S(1)}, bf16[1152,128]{1,0:T(8,128)(2,1)S(1)}, u32[]{:S(2)}, u32[]{:S(2)}) collective-permute-start(bf16[1152,128]{1,0:T(8,128)(2,1)S(1)} %get-tuple-element.19), channel_id=1, source_target_pairs={{0,32},{1,33},{2,34},{3,35},{4,36},{5,37},{6,38},{7,39},{8,40},{9,... | collective-permute-start | bytes 884744 | tf_op jit(solution)/shard_map/ppermute | solution.py:40
  38.6 13.4 %collective-permute-start.5 = (bf16[1152,128]{1,0:T(8,128)(2,1)S(1)}, bf16[1152,128]{1,0:T(8,128)(2,1)S(1)}, u32[]{:S(2)}, u32[]{:S(2)}) collective-permute-start(bf16[1152,128]{1,0:T(8,128)(2,1)S(1)} %get-tuple-element.20), channel_id=1, source_target_pairs={{0,64},{1,65},{2,66},{3,67},{4,68},{5,69},{6,70},{7,71},{8,72},{9,... | collective-permute-start | bytes 884744 | tf_op jit(solution)/shard_map/ppermute | solution.py:40
  42.0 19.1 %collective-permute-start.6 = (bf16[1152,128]{1,0:T(8,128)(2,1)S(1)}, bf16[1152,128]{1,0:T(8,128)(2,1)S(1)}, u32[]{:S(2)}, u32[]{:S(2)}) collective-permute-start(bf16[1152,128]{1,0:T(8,128)(2,1)S(1)} %get-tuple-element.21), channel_id=1, source_target_pairs={{0,96},{1,97},{2,98},{3,99},{4,100},{5,101},{6,102},{7,103},{8,104... | collective-permute-start | bytes 884744 | tf_op jit(solution)/shard_map/ppermute | solution.py:40
  61.2 0.8 collective-permute-start.8
  61.9 5.7 %collective-permute-start.7 = (bf16[1152,128]{1,0:T(8,128)(2,1)S(1)}, bf16[1152,128]{1,0:T(8,128)(2,1)S(1)}, u32[]{:S(2)}, u32[]{:S(2)}) collective-permute-start(bf16[1152,128]{1,0:T(8,128)(2,1)S(1)} %add_convert_fusion.1), channel_id=1, source_target_pairs={{0,2},{1,3},{2,128},{3,129},{4,6},{5,7},{6,132},{7,133},{8,10},{9,... | collective-permute-start | bytes 884744 | tf_op jit(solution)/shard_map/ppermute | solution.py:40
  67.6 5.9 %collective-permute-start.11 = (bf16[1152,128]{1,0:T(8,128)(2,1)S(1)}, bf16[1152,128]{1,0:T(8,128)(2,1)S(1)}, u32[]{:S(2)}, u32[]{:S(2)}) collective-permute-start(bf16[1152,128]{1,0:T(8,128)(2,1)S(1)} %add_convert_fusion.p0), channel_id=1, source_target_pairs={{0,96},{1,97},{2,98},{3,99},{4,100},{5,101},{6,102},{7,103},{8,104... | collective-permute-start | bytes 884744 | tf_op jit(solution)/shard_map/ppermute | solution.py:40
  67.7 7.5 %collective-permute-start.10 = (bf16[1152,128]{1,0:T(8,128)(2,1)S(1)}, bf16[1152,128]{1,0:T(8,128)(2,1)S(1)}, u32[]{:S(2)}, u32[]{:S(2)}) collective-permute-start(bf16[1152,128]{1,0:T(8,128)(2,1)S(1)} %add_convert_fusion.p0), channel_id=1, source_target_pairs={{0,64},{1,65},{2,66},{3,67},{4,68},{5,69},{6,70},{7,71},{8,72},{9,... | collective-permute-start | bytes 884744 | tf_op jit(solution)/shard_map/ppermute | solution.py:40
  69.7 8.7 %collective-permute-start.9 = (bf16[1152,128]{1,0:T(8,128)(2,1)S(1)}, bf16[1152,128]{1,0:T(8,128)(2,1)S(1)}, u32[]{:S(2)}, u32[]{:S(2)}) collective-permute-start(bf16[1152,128]{1,0:T(8,128)(2,1)S(1)} %add_convert_fusion.p0), channel_id=1, source_target_pairs={{0,32},{1,33},{2,34},{3,35},{4,36},{5,37},{6,38},{7,39},{8,40},{9,... | collective-permute-start | bytes 884744 | tf_op jit(solution)/shard_map/ppermute | solution.py:40
  95.0 4.2 %collective-permute-start.12 = (bf16[1024,1024]{1,0:T(8,128)(2,1)S(1)}, bf16[1024,1024]{1,0:T(8,128)(2,1)S(1)}, u32[]{:S(2)}, u32[]{:S(2)}) collective-permute-start(bf16[1024,1024]{1,0:T(8,128)(2,1)S(1)} %shard_map.58.mine_ref), channel_id=1, source_target_pairs={{0,16},{1,17},{2,18},{3,19},{4,20},{5,21},{6,22},{7,23},{8,24},{9,... | collective-permute-start | bytes 6291464 | tf_op jit(solution)/shard_map/ppermute | solution.py:40

commit v11 on v10

--- a/solution.py
+++ b/solution.py
@@ -11,6 +11,7 @@
 F32 = jnp.float32
 MIB = 2 ** 20
 UPPER = [(r, c) for r in range(8) for c in range(r, 8)]
+LARGE = [(r, c) for r in range(4) for c in range(r, 4)]
 PARTS = [UPPER[9 * i:9 * (i + 1)] for i in range(4)]
 SMEM = pl.BlockSpec(memory_space=pltpu.SMEM)
 VMEM = pl.BlockSpec(memory_space=pltpu.VMEM)
@@ -145,7 +146,7 @@
 
 def rounds_kernel(place_ref, damp_ref, p0, p1, p2, p3, w0, w1, w2, w3, out_ref,
                   a_ref, x_ref, xb_ref, p_ref, parts_ref, w_ref, sems):
-    size = out_ref.shape[0]
+    size = a_ref.shape[0]
     tile, small = size // 4, size // 8
     base, core, half, damp = place_ref[0], place_ref[1], place_ref[2], damp_ref[0]
     loads = [pltpu.make_async_copy(w, w_ref.at[i], sems.at[i]) for i, w in enumerate((w0, w1, w2, w3))]
@@ -203,7 +204,11 @@
                 x_ref[rows, blocks[c]] = value
                 mirrored(later, c, value.astype(BF16))
             else:
-                mirrored(out_ref, c, (value * (frob / 2.0 ** ITERS)).astype(BF16))
+                value = (value * (frob / 2.0 ** ITERS)).astype(BF16)
+                mirrored(later, c, value)
+                for r in range(c + 1):
+                    at = LARGE.index((r, c)) * tile
+                    out_ref[at:at + tile, :] = value[blocks[r], :]
 
     for load in loads:
         load.wait()
@@ -215,16 +220,17 @@
             value = jnp.zeros((tile, size), F32)
             for b in range(4):
                 cols = pl.ds(pl.multiple_of(lax.rem(2 * half + b, 4) * tile, tile), tile)
-                value += dot(out_ref[rows, cols], w_ref[b])
-            p_ref[blocks[i], :] = value.astype(BF16)
-        out_ref[:2 * tile, :] = p_ref[:2 * tile, :]
+                value += dot(xb_ref[(ITERS - 1) % 2, rows, cols], w_ref[b])
+            for b in range(4):
+                at = (i * 4 + b) * tile
+                out_ref[at:at + tile, :] = value[:, blocks[b]].astype(BF16)
 
 
 def rounds(place, damp, pieces, weights):
     tile, size = weights[0].shape
     return pl.pallas_call(
         rounds_kernel,
-        out_shape=jax.ShapeDtypeStruct((size, size), BF16),
+        out_shape=jax.ShapeDtypeStruct((len(LARGE) * tile, tile), BF16),
         in_specs=[SMEM, SMEM] + [VMEM] * 4 + [ANY] * 4,
         out_specs=VMEM,
         scratch_shapes=[
@@ -241,28 +247,32 @@
 
 
 def last_kernel(place_ref, mine_ref, other_ref, out_ref):
-    tile, size = out_ref.shape
-
-    def put(rows, inverse):
-        for i in range(size // tile):
-            block = slice(i * tile, (i + 1) * tile)
-            value = lax.dot_general(
-                inverse[block, :], rows, (((1,), (1,)), ((), ())), preferred_element_type=F32)
-            out_ref[:, block] = value.astype(BF16).T
+    tile = out_ref.shape[0]
+
+    def put(rows_ref, first, upper_ref):
+        for n in range(4):
+            value = jnp.zeros((tile, tile), F32)
+            for k in range(4):
+                at = LARGE.index((min(k, n), max(k, n))) * tile
+                contracted = 0 if k <= n else 1
+                value += lax.dot_general(
+                    rows_ref[(first + k) * tile:(first + k + 1) * tile, :], upper_ref[at:at + tile, :],
+                    (((1,), (contracted,)), ((), ())), preferred_element_type=F32)
+            out_ref[:, n * tile:(n + 1) * tile] = value.astype(BF16)
 
     @pl.when(place_ref[1] == 0)
     def _():
-        put(other_ref[:tile, :], mine_ref)
+        put(other_ref, 0, mine_ref)
 
     @pl.when(place_ref[1] == 1)
     def _():
-        put(mine_ref[tile:2 * tile, :], other_ref)
+        put(mine_ref, 4, other_ref)
 
 
 def last(place, mine, other, rows):
     return pl.pallas_call(
         last_kernel,
-        out_shape=jax.ShapeDtypeStruct((rows, mine.shape[1]), BF16),
+        out_shape=jax.ShapeDtypeStruct((rows, 4 * rows), BF16),
         in_specs=[SMEM] + [VMEM] * 2,
         out_specs=VMEM,
         compiler_params=pltpu.CompilerParams(vmem_limit_bytes=16 * MIB),

time: 102 us -> 101 us (level)
  waiting for transfers between devices: 50.4 us -> 49.2 us
    ppermute x13, waiting for transfers between devices: 49.5 us -> 48.4 us  [moved(): return lax.ppermute(value, ('dp', 'owner'), pairs)]
where the time goes in v11:
time: 101 us; the launch traced here: 100 us
  waiting for transfers between devices  49.2 us (49%)
  starting transfers between devices  24.8 us (25%)
  Pallas kernels  21.8 us (22%)
  matrix products  3.28 us (3%)
    ppermute x13, waiting for transfers between devices, moved(): return lax.ppermute(value, ('dp', 'owner'), pairs)  48.4 us
    pallas_call x1, Pallas kernels, rounds(): pl.pallas_call(rounds_kernel, out_shape=jax.ShapeDtypeStruct((len(LARGE)...  16.8 us
    ppermute x13, starting transfers between devices, moved(): return lax.ppermute(value, ('dp', 'owner'), pairs)  13.4 us
    all_to_all x1, starting transfers between devices, dealt(): lax.all_to_all(value, ('dp', 'owner'), split_axis=0, concat_axis=0, tiled...  11.4 us
    dot_general x2, matrix products, dot(): return jnp.dot(a, b, preferred_element_type=F32)  3.28 us
    pallas_call x1, Pallas kernels, last(): pl.pallas_call(last_kernel, out_shape=jax.ShapeDtypeStruct((rows, 4 * row...  2.07 us
  transfers between devices with their start and end apart: 14, of which 12 were waited for; matrix products, arithmetic and copies ran while one was open for 1% of the time, Pallas kernels for 0%

profile of v11, /device:TPU:33, one launch (start us, length us, event | category | flops | bytes accessed | tf_op | source)
XLA Modules:
  0.0 100.4 jit_solution(8376118193886475496)
XLA Ops:
  0.0 3.0 %convolution_convert_fusion.g_ref = bf16[16,16384]{1,0:T(8,128)(2,1)S(1)} fusion(bf16[128,16384]{1,0:T(8,128)(2,1)} %param.6, s32[16]{0:T(128)} %param.7), kind=kOutput, calls=%fused_computation | convolution fusion | flops 67373056 | bytes 4718656 | tf_op jit(solution)/shard_map/dot_general | solution.py:22
  3.0 0.3 convolution_convert_fusion.1.x_ref
  3.4 0.8 collective-permute-start
  4.2 1.5 %collective-permute-done.other_ref = bf16[16,16384]{1,0:T(8,128)(2,1)S(1)} collective-permute-done((bf16[16,16384]{1,0:T(8,128)(2,1)S(1)}, bf16[16,16384]{1,0:T(8,128)(2,1)S(1)}, u32[]{:S(2)}, u32[]{:S(2)}) %collective-permute-start) | collective-permute-done | bytes 524320 | tf_op jit(solution)/shard_map/ppermute | solution.py:41
  5.7 1.0 %shard_map.56 = bf16[16,32,1024]{2,1,0:T(8,128)(2,1)} custom-call(s32[1]{0:T(128)} %bitcast.1.core_ref, bf16[16,4096]{1,0:T(8,128)(2,1)S(1)} %convolution_convert_fusion.1.x_ref, bf16[16,16384]{1,0:T(8,128)(2,1)S(1)} %convolution_convert_fusion.g_ref, bf16[16,16384]{1,0:T(8,128)(2,1)S(1)} %collective-permute-done.other_ref), custom_call_target="tpu_custom_call" | custom-call | tf_op jit(solution)/shard_map/pallas_call | solution.py:110
  6.7 11.4 %all-to-all-start = ((bf16[16,32,1024]{2,1,0:T(8,128)(2,1)}), bf16[16,32,1024]{2,1,0:T(8,128)(2,1)S(1)}, u32[]{:S(2)}, u32[]{:S(2)}) async-start(bf16[16,32,1024]{2,1,0:T(8,128)(2,1)} %shard_map.56), calls=%async_computation | async-start | bytes 2097152 | tf_op jit(solution)/shard_map/all_to_all | solution.py:53
  18.2 1.9 %collective-permute-start.3 = (bf16[256,1024]{1,0:T(8,128)(2,1)S(1)}, bf16[256,1024]{1,0:T(8,128)(2,1)S(1)}, u32[]{:S(2)}, u32[]{:S(2)}) collective-permute-start(bf16[256,1024]{1,0:T(8,128)(2,1)S(1)} %copy-done.1), channel_id=1, source_target_pairs={{0,0},{1,1},{2,2},{3,3},{4,4},{5,5},{6,6},{7,7},{8,8},{9,9},{10,10... | collective-permute-start | bytes 1572872 | tf_op jit(solution)/shard_map/ppermute | solution.py:41
  20.1 0.1 collective-permute-start.2
  20.2 1.8 %collective-permute-start.1 = (bf16[256,1024]{1,0:T(8,128)(2,1)S(1)}, bf16[256,1024]{1,0:T(8,128)(2,1)}, u32[]{:S(2)}, u32[]{:S(2)}) collective-permute-start(bf16[256,1024]{1,0:T(8,128)(2,1)S(1)} %copy-done.1), channel_id=1, source_target_pairs={{0,16},{1,17},{2,18},{3,19},{4,20},{5,21},{6,22},{7,23},{8,24},{9,... | collective-permute-start | bytes 1572872 | tf_op jit(solution)/shard_map/ppermute | solution.py:41
  22.1 11.0 %collective-permute-done.3.w3 = bf16[256,1024]{1,0:T(8,128)(2,1)S(1)} collective-permute-done((bf16[256,1024]{1,0:T(8,128)(2,1)S(1)}, bf16[256,1024]{1,0:T(8,128)(2,1)S(1)}, u32[]{:S(2)}, u32[]{:S(2)}) %collective-permute-start.3) | collective-permute-done | bytes 524320 | tf_op jit(solution)/shard_map/ppermute | solution.py:41
  33.1 0.9 collective-permute-done.2.w2
  34.0 0.8 all-to-all-done
  34.8 1.8 %shard_map.57 = (bf16[1152,128]{1,0:T(8,128)(2,1)S(1)}, bf16[1152,128]{1,0:T(8,128)(2,1)S(1)}, bf16[1152,128]{1,0:T(8,128)(2,1)S(1)}, bf16[1152,128]{1,0:T(8,128)(2,1)S(1)}) custom-call(s32[2]{0:T(128)S(1)} %pad_add_fusion.1.refs_0_, bf16[512,1024]{1,0:T(8,128)(2,1)S(1)} %bitcast.7), custom_call_target="tpu_custom_call" | custom-call | tf_op jit(solution)/shard_map/pallas_call | solution.py:137
  36.7 1.9 %collective-permute-start.4 = (bf16[1152,128]{1,0:T(8,128)(2,1)S(1)}, bf16[1152,128]{1,0:T(8,128)(2,1)S(1)}, u32[]{:S(2)}, u32[]{:S(2)}) collective-permute-start(bf16[1152,128]{1,0:T(8,128)(2,1)S(1)} %get-tuple-element.19), channel_id=1, source_target_pairs={{0,32},{1,33},{2,34},{3,35},{4,36},{5,37},{6,38},{7,39},{8,40},{9,... | collective-permute-start | bytes 884744 | tf_op jit(solution)/shard_map/ppermute | solution.py:41
  38.6 3.4 %collective-permute-start.5 = (bf16[1152,128]{1,0:T(8,128)(2,1)S(1)}, bf16[1152,128]{1,0:T(8,128)(2,1)S(1)}, u32[]{:S(2)}, u32[]{:S(2)}) collective-permute-start(bf16[1152,128]{1,0:T(8,128)(2,1)S(1)} %get-tuple-element.20), channel_id=1, source_target_pairs={{0,64},{1,65},{2,66},{3,67},{4,68},{5,69},{6,70},{7,71},{8,72},{9,... | collective-permute-start | bytes 884744 | tf_op jit(solution)/shard_map/ppermute | solution.py:41
  42.0 2.3 %collective-permute-done.4 = bf16[1152,128]{1,0:T(8,128)(2,1)S(1)} collective-permute-done((bf16[1152,128]{1,0:T(8,128)(2,1)S(1)}, bf16[1152,128]{1,0:T(8,128)(2,1)S(1)}, u32[]{:S(2)}, u32[]{:S(2)}) %collective-permute-start.4) | collective-permute-done | bytes 294944 | tf_op jit(solution)/shard_map/ppermute | solution.py:41
  44.3 7.7 %collective-permute-done.5 = bf16[1152,128]{1,0:T(8,128)(2,1)S(1)} collective-permute-done((bf16[1152,128]{1,0:T(8,128)(2,1)S(1)}, bf16[1152,128]{1,0:T(8,128)(2,1)S(1)}, u32[]{:S(2)}, u32[]{:S(2)}) %collective-permute-start.5) | collective-permute-done | bytes 294944 | tf_op jit(solution)/shard_map/ppermute | solution.py:41
  52.0 9.1 %collective-permute-done.6 = bf16[1152,128]{1,0:T(8,128)(2,1)S(1)} collective-permute-done((bf16[1152,128]{1,0:T(8,128)(2,1)S(1)}, bf16[1152,128]{1,0:T(8,128)(2,1)S(1)}, u32[]{:S(2)}, u32[]{:S(2)}) %collective-permute-start.6) | collective-permute-done | bytes 294944 | tf_op jit(solution)/shard_map/ppermute | solution.py:41
  61.0 0.2 add_convert_fusion.1
  61.2 0.7 collective-permute-start.8
  61.9 0.1 collective-permute-start.7
  62.0 5.5 %collective-permute-done.7 = bf16[1152,128]{1,0:T(8,128)(2,1)S(1)} collective-permute-done((bf16[1152,128]{1,0:T(8,128)(2,1)S(1)}, bf16[1152,128]{1,0:T(8,128)(2,1)S(1)}, u32[]{:S(2)}, u32[]{:S(2)}) %collective-permute-start.7) | collective-permute-done | bytes 294944 | tf_op jit(solution)/shard_map/ppermute | solution.py:41
  67.7 2.0 %collective-permute-start.10 = (bf16[1152,128]{1,0:T(8,128)(2,1)S(1)}, bf16[1152,128]{1,0:T(8,128)(2,1)S(1)}, u32[]{:S(2)}, u32[]{:S(2)}) collective-permute-start(bf16[1152,128]{1,0:T(8,128)(2,1)S(1)} %add_convert_fusion.p0), channel_id=1, source_target_pairs={{0,64},{1,65},{2,66},{3,67},{4,68},{5,69},{6,70},{7,71},{8,72},{9,... | collective-permute-start | bytes 884744 | tf_op jit(solution)/shard_map/ppermute | solution.py:41
  69.7 0.6 collective-permute-start.9
  70.3 0.7 dynamic_slice.4.damp_ref
  71.0 2.6 %collective-permute-done.11.p3 = bf16[1152,128]{1,0:T(8,128)(2,1)S(1)} collective-permute-done((bf16[1152,128]{1,0:T(8,128)(2,1)S(1)}, bf16[1152,128]{1,0:T(8,128)(2,1)S(1)}, u32[]{:S(2)}, u32[]{:S(2)}) %collective-permute-start.11) | collective-permute-done | bytes 294944 | tf_op jit(solution)/shard_map/ppermute | solution.py:41
  73.6 1.6 %collective-permute-done.10.p2 = bf16[1152,128]{1,0:T(8,128)(2,1)S(1)} collective-permute-done((bf16[1152,128]{1,0:T(8,128)(2,1)S(1)}, bf16[1152,128]{1,0:T(8,128)(2,1)S(1)}, u32[]{:S(2)}, u32[]{:S(2)}) %collective-permute-start.10) | collective-permute-done | bytes 294944 | tf_op jit(solution)/shard_map/ppermute | solution.py:41
  75.2 3.1 %collective-permute-done.9.p1 = bf16[1152,128]{1,0:T(8,128)(2,1)S(1)} collective-permute-done((bf16[1152,128]{1,0:T(8,128)(2,1)S(1)}, bf16[1152,128]{1,0:T(8,128)(2,1)S(1)}, u32[]{:S(2)}, u32[]{:S(2)}) %collective-permute-start.9) | collective-permute-done | bytes 294944 | tf_op jit(solution)/shard_map/ppermute | solution.py:41
  78.3 16.8 %shard_map.58.mine_ref = bf16[2560,256]{1,0:T(8,128)(2,1)S(1)} custom-call(s32[3]{0:T(128)S(1)} %pad_add_fusion.place_ref, f32[1]{0:T(128)} %dynamic_slice.4.damp_ref, bf16[1152,128]{1,0:T(8,128)(2,1)S(1)} %add_convert_fusion.p0, bf16[1152,128]{1,0:T(8,128)(2,1)S(1)} %collective-permute-done.9.p1, bf16[1152,128]{1,0:T(8,128)(2,1)S(1)} %collective-permute-done.10.p2, ...), custom_call_target="tpu_custom_call" | custom-call | tf_op jit(solution)/shard_map/pallas_call | solution.py:231
  95.2 0.1 collective-permute-start.12
  95.3 3.0 %collective-permute-done.12.other_ref = bf16[2560,256]{1,0:T(8,128)(2,1)S(1)} collective-permute-done((bf16[2560,256]{1,0:T(8,128)(2,1)S(1)}, bf16[2560,256]{1,0:T(8,128)(2,1)S(1)}, u32[]{:S(2)}, u32[]{:S(2)}) %collective-permute-start.12) | collective-permute-done | bytes 1310752 | tf_op jit(solution)/shard_map/ppermute | solution.py:41
  98.3 2.1 %shard_map.59 = bf16[256,1024]{1,0:T(8,128)(2,1)} custom-call(s32[3]{0:T(128)S(1)} %pad_add_fusion.place_ref, bf16[2560,256]{1,0:T(8,128)(2,1)S(1)} %shard_map.58.mine_ref, bf16[2560,256]{1,0:T(8,128)(2,1)S(1)} %collective-permute-done.12.other_ref), custom_call_target="tpu_custom_call" | custom-call | tf_op jit(solution)/shard_map/pallas_call | solution.py:273
  (16 shorter events, 0.4 us)
Async XLA Ops:
  0.0 3.0 %copy-start = (bf16[128,4096]{1,0:T(8,128)(2,1)S(1)}, bf16[128,4096]{1,0:T(8,128)(2,1)}, u32[]{:S(2)}) copy-start(bf16[128,4096]{1,0:T(8,128)(2,1)} %param.5) | copy-start | bytes 3145732
  0.0 3.0 %copy-start.2 = (s32[16]{0:T(128)S(1)}, s32[16]{0:T(128)}, u32[]{:S(2)}) copy-start(s32[16]{0:T(128)} %param.7) | copy-start | bytes 196
  3.0 15.1 %copy-start.1 = (bf16[256,1024]{1,0:T(8,128)(2,1)S(1)}, bf16[256,1024]{1,0:T(8,128)(2,1)}, u32[]{:S(2)}) copy-start(bf16[256,1024]{1,0:T(8,128)(2,1)} %w1.1) | copy-start | bytes 1572868
  3.4 66.9 %copy-start.3 = (f32[20]{0:T(128)S(1)}, f32[20]{0:T(128)}, u32[]{:S(2)}) copy-start(f32[20]{0:T(128)} %param.8) | copy-start | bytes 244
  3.4 2.3 %collective-permute-start = (bf16[16,16384]{1,0:T(8,128)(2,1)S(1)}, bf16[16,16384]{1,0:T(8,128)(2,1)S(1)}, u32[]{:S(2)}, u32[]{:S(2)}) collective-permute-start(bf16[16,16384]{1,0:T(8,128)(2,1)S(1)} %shard_map.55), channel_id=1, source_target_pairs={{0,16},{1,17},{2,18},{3,19},{4,20},{5,21},{6,22},{7,23},{8,24},{9,... | collective-permute-start | bytes 1572872 | tf_op jit(solution)/shard_map/ppermute | solution.py:41
  6.7 28.1 %all-to-all-start = ((bf16[16,32,1024]{2,1,0:T(8,128)(2,1)}), bf16[16,32,1024]{2,1,0:T(8,128)(2,1)S(1)}, u32[]{:S(2)}, u32[]{:S(2)}) async-start(bf16[16,32,1024]{2,1,0:T(8,128)(2,1)} %shard_map.56), calls=%async_computation | async-start | bytes 2097152 | tf_op jit(solution)/shard_map/all_to_all | solution.py:53
  18.2 14.9 %collective-permute-start.3 = (bf16[256,1024]{1,0:T(8,128)(2,1)S(1)}, bf16[256,1024]{1,0:T(8,128)(2,1)S(1)}, u32[]{:S(2)}, u32[]{:S(2)}) collective-permute-start(bf16[256,1024]{1,0:T(8,128)(2,1)S(1)} %copy-done.1), channel_id=1, source_target_pairs={{0,0},{1,1},{2,2},{3,3},{4,4},{5,5},{6,6},{7,7},{8,8},{9,9},{10,10... | collective-permute-start | bytes 1572872 | tf_op jit(solution)/shard_map/ppermute | solution.py:41
  20.1 13.9 %collective-permute-start.2 = (bf16[256,1024]{1,0:T(8,128)(2,1)S(1)}, bf16[256,1024]{1,0:T(8,128)(2,1)}, u32[]{:S(2)}, u32[]{:S(2)}) collective-permute-start(bf16[256,1024]{1,0:T(8,128)(2,1)S(1)} %copy-done.1), channel_id=1, source_target_pairs={{0,48},{1,49},{2,50},{3,51},{4,52},{5,53},{6,54},{7,55},{8,56},{9,... | collective-permute-start | bytes 1572872 | tf_op jit(solution)/shard_map/ppermute | solution.py:41
  20.2 13.8 %collective-permute-start.1 = (bf16[256,1024]{1,0:T(8,128)(2,1)S(1)}, bf16[256,1024]{1,0:T(8,128)(2,1)}, u32[]{:S(2)}, u32[]{:S(2)}) collective-permute-start(bf16[256,1024]{1,0:T(8,128)(2,1)S(1)} %copy-done.1), channel_id=1, source_target_pairs={{0,16},{1,17},{2,18},{3,19},{4,20},{5,21},{6,22},{7,23},{8,24},{9,... | collective-permute-start | bytes 1572872 | tf_op jit(solution)/shard_map/ppermute | solution.py:41
  36.7 7.6 %collective-permute-start.4 = (bf16[1152,128]{1,0:T(8,128)(2,1)S(1)}, bf16[1152,128]{1,0:T(8,128)(2,1)S(1)}, u32[]{:S(2)}, u32[]{:S(2)}) collective-permute-start(bf16[1152,128]{1,0:T(8,128)(2,1)S(1)} %get-tuple-element.19), channel_id=1, source_target_pairs={{0,32},{1,33},{2,34},{3,35},{4,36},{5,37},{6,38},{7,39},{8,40},{9,... | collective-permute-start | bytes 884744 | tf_op jit(solution)/shard_map/ppermute | solution.py:41
  38.6 13.4 %collective-permute-start.5 = (bf16[1152,128]{1,0:T(8,128)(2,1)S(1)}, bf16[1152,128]{1,0:T(8,128)(2,1)S(1)}, u32[]{:S(2)}, u32[]{:S(2)}) collective-permute-start(bf16[1152,128]{1,0:T(8,128)(2,1)S(1)} %get-tuple-element.20), channel_id=1, source_target_pairs={{0,64},{1,65},{2,66},{3,67},{4,68},{5,69},{6,70},{7,71},{8,72},{9,... | collective-permute-start | bytes 884744 | tf_op jit(solution)/shard_map/ppermute | solution.py:41
  42.0 19.1 %collective-permute-start.6 = (bf16[1152,128]{1,0:T(8,128)(2,1)S(1)}, bf16[1152,128]{1,0:T(8,128)(2,1)S(1)}, u32[]{:S(2)}, u32[]{:S(2)}) collective-permute-start(bf16[1152,128]{1,0:T(8,128)(2,1)S(1)} %get-tuple-element.21), channel_id=1, source_target_pairs={{0,96},{1,97},{2,98},{3,99},{4,100},{5,101},{6,102},{7,103},{8,104... | collective-permute-start | bytes 884744 | tf_op jit(solution)/shard_map/ppermute | solution.py:41
  61.2 0.8 collective-permute-start.8
  61.9 5.7 %collective-permute-start.7 = (bf16[1152,128]{1,0:T(8,128)(2,1)S(1)}, bf16[1152,128]{1,0:T(8,128)(2,1)S(1)}, u32[]{:S(2)}, u32[]{:S(2)}) collective-permute-start(bf16[1152,128]{1,0:T(8,128)(2,1)S(1)} %add_convert_fusion.1), channel_id=1, source_target_pairs={{0,2},{1,3},{2,128},{3,129},{4,6},{5,7},{6,132},{7,133},{8,10},{9,... | collective-permute-start | bytes 884744 | tf_op jit(solution)/shard_map/ppermute | solution.py:41
  67.6 5.9 %collective-permute-start.11 = (bf16[1152,128]{1,0:T(8,128)(2,1)S(1)}, bf16[1152,128]{1,0:T(8,128)(2,1)S(1)}, u32[]{:S(2)}, u32[]{:S(2)}) collective-permute-start(bf16[1152,128]{1,0:T(8,128)(2,1)S(1)} %add_convert_fusion.p0), channel_id=1, source_target_pairs={{0,96},{1,97},{2,98},{3,99},{4,100},{5,101},{6,102},{7,103},{8,104... | collective-permute-start | bytes 884744 | tf_op jit(solution)/shard_map/ppermute | solution.py:41
  67.7 7.5 %collective-permute-start.10 = (bf16[1152,128]{1,0:T(8,128)(2,1)S(1)}, bf16[1152,128]{1,0:T(8,128)(2,1)S(1)}, u32[]{:S(2)}, u32[]{:S(2)}) collective-permute-start(bf16[1152,128]{1,0:T(8,128)(2,1)S(1)} %add_convert_fusion.p0), channel_id=1, source_target_pairs={{0,64},{1,65},{2,66},{3,67},{4,68},{5,69},{6,70},{7,71},{8,72},{9,... | collective-permute-start | bytes 884744 | tf_op jit(solution)/shard_map/ppermute | solution.py:41
  69.7 8.7 %collective-permute-start.9 = (bf16[1152,128]{1,0:T(8,128)(2,1)S(1)}, bf16[1152,128]{1,0:T(8,128)(2,1)S(1)}, u32[]{:S(2)}, u32[]{:S(2)}) collective-permute-start(bf16[1152,128]{1,0:T(8,128)(2,1)S(1)} %add_convert_fusion.p0), channel_id=1, source_target_pairs={{0,32},{1,33},{2,34},{3,35},{4,36},{5,37},{6,38},{7,39},{8,40},{9,... | collective-permute-start | bytes 884744 | tf_op jit(solution)/shard_map/ppermute | solution.py:41
  95.2 3.1 %collective-permute-start.12 = (bf16[2560,256]{1,0:T(8,128)(2,1)S(1)}, bf16[2560,256]{1,0:T(8,128)(2,1)S(1)}, u32[]{:S(2)}, u32[]{:S(2)}) collective-permute-start(bf16[2560,256]{1,0:T(8,128)(2,1)S(1)} %shard_map.58.mine_ref), channel_id=1, source_target_pairs={{0,16},{1,17},{2,18},{3,19},{4,20},{5,21},{6,22},{7,23},{8,24},{9,... | collective-permute-start | bytes 3932168 | tf_op jit(solution)/shard_map/ppermute | solution.py:41

commit v12 on v11

--- a/solution.py
+++ b/solution.py
@@ -324,11 +324,12 @@
         z = (zh * 4 + zl + by) % 8
         return z // 4, z % 4
 
-    here = moved(part, lambda zh, y, c, x, zl: (beside(zh, zl, 2)[0], y, 0, x, beside(zh, zl, 2)[1]) if c == 0
-                 else (zh, y ^ 1, 1, x, zl))
-    there = moved(part, lambda zh, y, c, x, zl: (beside(zh, zl, -2)[0], y, 0, x, beside(zh, zl, -2)[1]) if c == 0
-                  else None)
-    piece = (here.astype(F32) + there.astype(F32)).astype(BF16)
+    halves = jnp.split(part, 2)
+    here = [moved(half, lambda zh, y, c, x, zl: (beside(zh, zl, 2)[0], y, 0, x, beside(zh, zl, 2)[1]) if c == 0
+                  else (zh, y ^ 1, 1, x, zl)) for half in halves]
+    there = [moved(half, lambda zh, y, c, x, zl: (beside(zh, zl, -2)[0], y, 0, x, beside(zh, zl, -2)[1]) if c == 0
+                   else None) for half in halves]
+    piece = jnp.concatenate([(h.astype(F32) + t.astype(F32)).astype(BF16) for h, t in zip(here, there)])
 
     pieces = [piece]
     for k in (1, 2, 3):

time: 101 us -> 104 us (1.030); the launches traced: 100 us -> 102 us
  starting transfers between devices: 24.8 us -> 32.2 us
  waiting for transfers between devices: 49.2 us -> 43.6 us
    ppermute x13 -> x15, starting transfers between devices: 13.4 us -> 20.8 us  [moved(): return lax.ppermute(value, ('dp', 'owner'), pairs)]
    ppermute x13 -> x15, waiting for transfers between devices: 48.4 us -> 42.8 us  [moved(): return lax.ppermute(value, ('dp', 'owner'), pairs)]
  transfers between devices with their start and end apart: 14 -> 16, of which waited for: 12 -> 13; matrix products, arithmetic and copies ran while one was open for 1% -> 1% of each run, Pallas kernels for 0% -> 0%
where the time goes in v12:
time: 104 us; the launch traced here: 102 us
  waiting for transfers between devices  43.6 us (42%)
  starting transfers between devices  32.2 us (31%)
  Pallas kernels  21.8 us (21%)
  matrix products  3.28 us (3%)
    ppermute x15, waiting for transfers between devices, moved(): return lax.ppermute(value, ('dp', 'owner'), pairs)  42.8 us
    ppermute x15, starting transfers between devices, moved(): return lax.ppermute(value, ('dp', 'owner'), pairs)  20.8 us
    pallas_call x1, Pallas kernels, rounds(): pl.pallas_call(rounds_kernel, out_shape=jax.ShapeDtypeStruct((len(LARGE)...  16.8 us
    all_to_all x1, starting transfers between devices, dealt(): lax.all_to_all(value, ('dp', 'owner'), split_axis=0, concat_axis=0, tiled...  11.4 us
    dot_general x2, matrix products, dot(): return jnp.dot(a, b, preferred_element_type=F32)  3.28 us
  transfers between devices with their start and end apart: 16, of which 13 were waited for; matrix products, arithmetic and copies ran while one was open for 1% of the time, Pallas kernels for 0%

profile of v12, /device:TPU:33, one launch (start us, length us, event | category | flops | bytes accessed | tf_op | source)
XLA Modules:
  0.0 102.1 jit_solution(13209176980855549690)
XLA Ops:
  0.0 3.0 %convolution_convert_fusion.g_ref = bf16[16,16384]{1,0:T(8,128)(2,1)S(1)} fusion(bf16[128,16384]{1,0:T(8,128)(2,1)} %param.6, s32[16]{0:T(128)} %param.7), kind=kOutput, calls=%fused_computation | convolution fusion | flops 67373056 | bytes 4718656 | tf_op jit(solution)/shard_map/dot_general | solution.py:22
  3.4 0.8 collective-permute-start
  4.2 1.5 %collective-permute-done.other_ref = bf16[16,16384]{1,0:T(8,128)(2,1)S(1)} collective-permute-done((bf16[16,16384]{1,0:T(8,128)(2,1)S(1)}, bf16[16,16384]{1,0:T(8,128)(2,1)S(1)}, u32[]{:S(2)}, u32[]{:S(2)}) %collective-permute-start) | collective-permute-done | bytes 524320 | tf_op jit(solution)/shard_map/ppermute | solution.py:41
  5.7 1.1 %shard_map.56 = bf16[16,32,1024]{2,1,0:T(8,128)(2,1)} custom-call(s32[1]{0:T(128)} %bitcast.1.core_ref, bf16[16,4096]{1,0:T(8,128)(2,1)S(1)} %convolution_convert_fusion.1.x_ref, bf16[16,16384]{1,0:T(8,128)(2,1)S(1)} %convolution_convert_fusion.g_ref, bf16[16,16384]{1,0:T(8,128)(2,1)S(1)} %collective-permute-done.other_ref), custom_call_target="tpu_custom_call" | custom-call | tf_op jit(solution)/shard_map/pallas_call | solution.py:110
  6.8 11.4 %all-to-all-start = ((bf16[16,32,1024]{2,1,0:T(8,128)(2,1)}), bf16[16,32,1024]{2,1,0:T(8,128)(2,1)S(1)}, u32[]{:S(2)}, u32[]{:S(2)}) async-start(bf16[16,32,1024]{2,1,0:T(8,128)(2,1)} %shard_map.56), calls=%async_computation | async-start | bytes 2097152 | tf_op jit(solution)/shard_map/all_to_all | solution.py:53
  18.2 1.9 %collective-permute-start.3 = (bf16[256,1024]{1,0:T(8,128)(2,1)S(1)}, bf16[256,1024]{1,0:T(8,128)(2,1)S(1)}, u32[]{:S(2)}, u32[]{:S(2)}) collective-permute-start(bf16[256,1024]{1,0:T(8,128)(2,1)S(1)} %copy-done.1), channel_id=1, source_target_pairs={{0,0},{1,1},{2,2},{3,3},{4,4},{5,5},{6,6},{7,7},{8,8},{9,9},{10,10... | collective-permute-start | bytes 1572872 | tf_op jit(solution)/shard_map/ppermute | solution.py:41
  20.2 1.8 %collective-permute-start.1 = (bf16[256,1024]{1,0:T(8,128)(2,1)S(1)}, bf16[256,1024]{1,0:T(8,128)(2,1)}, u32[]{:S(2)}, u32[]{:S(2)}) collective-permute-start(bf16[256,1024]{1,0:T(8,128)(2,1)S(1)} %copy-done.1), channel_id=1, source_target_pairs={{0,16},{1,17},{2,18},{3,19},{4,20},{5,21},{6,22},{7,23},{8,24},{9,... | collective-permute-start | bytes 1572872 | tf_op jit(solution)/shard_map/ppermute | solution.py:41
  22.1 11.0 %collective-permute-done.3.w3 = bf16[256,1024]{1,0:T(8,128)(2,1)S(1)} collective-permute-done((bf16[256,1024]{1,0:T(8,128)(2,1)S(1)}, bf16[256,1024]{1,0:T(8,128)(2,1)S(1)}, u32[]{:S(2)}, u32[]{:S(2)}) %collective-permute-start.3) | collective-permute-done | bytes 524320 | tf_op jit(solution)/shard_map/ppermute | solution.py:41
  33.1 0.9 collective-permute-done.2.w2
  34.0 0.8 all-to-all-done
  34.9 1.8 %shard_map.57 = (bf16[1152,128]{1,0:T(8,128)(2,1)S(1)}, bf16[1152,128]{1,0:T(8,128)(2,1)S(1)}, bf16[1152,128]{1,0:T(8,128)(2,1)S(1)}, bf16[1152,128]{1,0:T(8,128)(2,1)S(1)}) custom-call(s32[2]{0:T(128)S(1)} %pad_add_fusion.1.refs_0_, bf16[512,1024]{1,0:T(8,128)(2,1)S(1)} %bitcast.7), custom_call_target="tpu_custom_call" | custom-call | tf_op jit(solution)/shard_map/pallas_call | solution.py:137
  36.7 1.9 %collective-permute-start.4 = (bf16[1152,128]{1,0:T(8,128)(2,1)S(1)}, bf16[1152,128]{1,0:T(8,128)(2,1)S(1)}, u32[]{:S(2)}, u32[]{:S(2)}) collective-permute-start(bf16[1152,128]{1,0:T(8,128)(2,1)S(1)} %get-tuple-element.19), channel_id=1, source_target_pairs={{0,32},{1,33},{2,34},{3,35},{4,36},{5,37},{6,38},{7,39},{8,40},{9,... | collective-permute-start | bytes 884744 | tf_op jit(solution)/shard_map/ppermute | solution.py:41
  38.6 3.4 %collective-permute-start.5 = (bf16[1152,128]{1,0:T(8,128)(2,1)S(1)}, bf16[1152,128]{1,0:T(8,128)(2,1)S(1)}, u32[]{:S(2)}, u32[]{:S(2)}) collective-permute-start(bf16[1152,128]{1,0:T(8,128)(2,1)S(1)} %get-tuple-element.20), channel_id=1, source_target_pairs={{0,64},{1,65},{2,66},{3,67},{4,68},{5,69},{6,70},{7,71},{8,72},{9,... | collective-permute-start | bytes 884744 | tf_op jit(solution)/shard_map/ppermute | solution.py:41
  42.0 2.3 %collective-permute-done.4 = bf16[1152,128]{1,0:T(8,128)(2,1)S(1)} collective-permute-done((bf16[1152,128]{1,0:T(8,128)(2,1)S(1)}, bf16[1152,128]{1,0:T(8,128)(2,1)S(1)}, u32[]{:S(2)}, u32[]{:S(2)}) %collective-permute-start.4) | collective-permute-done | bytes 294944 | tf_op jit(solution)/shard_map/ppermute | solution.py:41
  44.3 7.7 %collective-permute-done.5 = bf16[1152,128]{1,0:T(8,128)(2,1)S(1)} collective-permute-done((bf16[1152,128]{1,0:T(8,128)(2,1)S(1)}, bf16[1152,128]{1,0:T(8,128)(2,1)S(1)}, u32[]{:S(2)}, u32[]{:S(2)}) %collective-permute-start.5) | collective-permute-done | bytes 294944 | tf_op jit(solution)/shard_map/ppermute | solution.py:41
  52.0 6.0 %collective-permute-done.6 = bf16[1152,128]{1,0:T(8,128)(2,1)S(1)} collective-permute-done((bf16[1152,128]{1,0:T(8,128)(2,1)S(1)}, bf16[1152,128]{1,0:T(8,128)(2,1)S(1)}, u32[]{:S(2)}, u32[]{:S(2)}) %collective-permute-start.6) | collective-permute-done | bytes 294944 | tf_op jit(solution)/shard_map/ppermute | solution.py:41
  58.2 0.7 collective-permute-start.8
  58.9 0.7 collective-permute-start.10
  59.6 1.5 %collective-permute-start.9 = (bf16[576,128]{1,0:T(8,128)(2,1)S(1)}, bf16[576,128]{1,0:T(8,128)(2,1)S(1)}, u32[]{:S(2)}, u32[]{:S(2)}) collective-permute-start(bf16[576,128]{1,0:T(8,128)(2,1)S(1)} %get-tuple-element.26), channel_id=1, source_target_pairs={{0,2},{1,3},{2,128},{3,129},{4,6},{5,7},{6,132},{7,133},{8,10},{9,... | collective-permute-start | bytes 442376 | tf_op jit(solution)/shard_map/ppermute | solution.py:41
  61.1 2.1 %collective-permute-done.7 = bf16[576,128]{1,0:T(8,128)(2,1)S(1)} collective-permute-done((bf16[576,128]{1,0:T(8,128)(2,1)S(1)}, bf16[576,128]{1,0:T(8,128)(2,1)S(1)}, u32[]{:S(2)}, u32[]{:S(2)}) %collective-permute-start.7) | collective-permute-done | bytes 147488 | tf_op jit(solution)/shard_map/ppermute | solution.py:41
  63.3 1.2 %collective-permute-done.9 = bf16[576,128]{1,0:T(8,128)(2,1)S(1)} collective-permute-done((bf16[576,128]{1,0:T(8,128)(2,1)S(1)}, bf16[576,128]{1,0:T(8,128)(2,1)S(1)}, u32[]{:S(2)}, u32[]{:S(2)}) %collective-permute-start.9) | collective-permute-done | bytes 147488 | tf_op jit(solution)/shard_map/ppermute | solution.py:41
  64.6 0.9 collective-permute-start.13
  65.4 1.7 %collective-permute-start.12 = (bf16[1152,128]{1,0:T(8,128)(2,1)S(1)}, bf16[1152,128]{1,0:T(8,128)(2,1)S(1)}, u32[]{:S(2)}, u32[]{:S(2)}) collective-permute-start(bf16[1152,128]{1,0:T(8,128)(2,1)S(1)} %pad_maximum_fusion.p0), channel_id=1, source_target_pairs={{0,64},{1,65},{2,66},{3,67},{4,68},{5,69},{6,70},{7,71},{8,72},{9,... | collective-permute-start | bytes 884744 | tf_op jit(solution)/shard_map/ppermute | solution.py:41
  67.1 0.8 collective-permute-start.11
  67.9 0.6 dynamic_slice.4.damp_ref
  68.6 1.6 %collective-permute-done.13.p3 = bf16[1152,128]{1,0:T(8,128)(2,1)S(1)} collective-permute-done((bf16[1152,128]{1,0:T(8,128)(2,1)S(1)}, bf16[1152,128]{1,0:T(8,128)(2,1)S(1)}, u32[]{:S(2)}, u32[]{:S(2)}) %collective-permute-start.13) | collective-permute-done | bytes 294944 | tf_op jit(solution)/shard_map/ppermute | solution.py:41
  70.2 2.4 %collective-permute-done.12.p2 = bf16[1152,128]{1,0:T(8,128)(2,1)S(1)} collective-permute-done((bf16[1152,128]{1,0:T(8,128)(2,1)S(1)}, bf16[1152,128]{1,0:T(8,128)(2,1)S(1)}, u32[]{:S(2)}, u32[]{:S(2)}) %collective-permute-start.12) | collective-permute-done | bytes 294944 | tf_op jit(solution)/shard_map/ppermute | solution.py:41
  72.6 3.4 %collective-permute-done.11.p1 = bf16[1152,128]{1,0:T(8,128)(2,1)S(1)} collective-permute-done((bf16[1152,128]{1,0:T(8,128)(2,1)S(1)}, bf16[1152,128]{1,0:T(8,128)(2,1)S(1)}, u32[]{:S(2)}, u32[]{:S(2)}) %collective-permute-start.11) | collective-permute-done | bytes 294944 | tf_op jit(solution)/shard_map/ppermute | solution.py:41
  76.0 16.8 %shard_map.58.mine_ref = bf16[2560,256]{1,0:T(8,128)(2,1)S(1)} custom-call(s32[3]{0:T(128)S(1)} %pad_add_fusion.place_ref, f32[1]{0:T(128)} %dynamic_slice.4.damp_ref, bf16[1152,128]{1,0:T(8,128)(2,1)S(1)} %pad_maximum_fusion.p0, bf16[1152,128]{1,0:T(8,128)(2,1)S(1)} %collective-permute-done.11.p1, bf16[1152,128]{1,0:T(8,128)(2,1)S(1)} %collective-permute-done.12.p2, ...), custom_call_target="tpu_custom_call" | custom-call | tf_op jit(solution)/shard_map/pallas_call | solution.py:231
  92.8 4.6 %collective-permute-start.14 = (bf16[2560,256]{1,0:T(8,128)(2,1)S(1)}, bf16[2560,256]{1,0:T(8,128)(2,1)S(1)}, u32[]{:S(2)}, u32[]{:S(2)}) collective-permute-start(bf16[2560,256]{1,0:T(8,128)(2,1)S(1)} %shard_map.58.mine_ref), channel_id=1, source_target_pairs={{0,16},{1,17},{2,18},{3,19},{4,20},{5,21},{6,22},{7,23},{8,24},{9,... | collective-permute-start | bytes 3932168 | tf_op jit(solution)/shard_map/ppermute | solution.py:41
  97.4 2.7 %collective-permute-done.14.other_ref = bf16[2560,256]{1,0:T(8,128)(2,1)S(1)} collective-permute-done((bf16[2560,256]{1,0:T(8,128)(2,1)S(1)}, bf16[2560,256]{1,0:T(8,128)(2,1)S(1)}, u32[]{:S(2)}, u32[]{:S(2)}) %collective-permute-start.14) | collective-permute-done | bytes 1310752 | tf_op jit(solution)/shard_map/ppermute | solution.py:41
  100.0 2.1 %shard_map.59 = bf16[256,1024]{1,0:T(8,128)(2,1)} custom-call(s32[3]{0:T(128)S(1)} %pad_add_fusion.place_ref, bf16[2560,256]{1,0:T(8,128)(2,1)S(1)} %shard_map.58.mine_ref, bf16[2560,256]{1,0:T(8,128)(2,1)S(1)} %collective-permute-done.14.other_ref), custom_call_target="tpu_custom_call" | custom-call | tf_op jit(solution)/shard_map/pallas_call | solution.py:273
  (23 shorter events, 1.0 us)
Async XLA Ops:
  0.0 3.0 %copy-start = (bf16[128,4096]{1,0:T(8,128)(2,1)S(1)}, bf16[128,4096]{1,0:T(8,128)(2,1)}, u32[]{:S(2)}) copy-start(bf16[128,4096]{1,0:T(8,128)(2,1)} %param.5) | copy-start | bytes 3145732
  0.0 3.0 %copy-start.2 = (s32[16]{0:T(128)S(1)}, s32[16]{0:T(128)}, u32[]{:S(2)}) copy-start(s32[16]{0:T(128)} %param.7) | copy-start | bytes 196
  3.0 15.2 %copy-start.1 = (bf16[256,1024]{1,0:T(8,128)(2,1)S(1)}, bf16[256,1024]{1,0:T(8,128)(2,1)}, u32[]{:S(2)}) copy-start(bf16[256,1024]{1,0:T(8,128)(2,1)} %w1.1) | copy-start | bytes 1572868
  3.4 64.5 %copy-start.3 = (f32[20]{0:T(128)S(1)}, f32[20]{0:T(128)}, u32[]{:S(2)}) copy-start(f32[20]{0:T(128)} %param.8) | copy-start | bytes 244
  3.4 2.3 %collective-permute-start = (bf16[16,16384]{1,0:T(8,128)(2,1)S(1)}, bf16[16,16384]{1,0:T(8,128)(2,1)S(1)}, u32[]{:S(2)}, u32[]{:S(2)}) collective-permute-start(bf16[16,16384]{1,0:T(8,128)(2,1)S(1)} %shard_map.55), channel_id=1, source_target_pairs={{0,16},{1,17},{2,18},{3,19},{4,20},{5,21},{6,22},{7,23},{8,24},{9,... | collective-permute-start | bytes 1572872 | tf_op jit(solution)/shard_map/ppermute | solution.py:41
  6.8 28.1 %all-to-all-start = ((bf16[16,32,1024]{2,1,0:T(8,128)(2,1)}), bf16[16,32,1024]{2,1,0:T(8,128)(2,1)S(1)}, u32[]{:S(2)}, u32[]{:S(2)}) async-start(bf16[16,32,1024]{2,1,0:T(8,128)(2,1)} %shard_map.56), calls=%async_computation | async-start | bytes 2097152 | tf_op jit(solution)/shard_map/all_to_all | solution.py:53
  18.2 14.9 %collective-permute-start.3 = (bf16[256,1024]{1,0:T(8,128)(2,1)S(1)}, bf16[256,1024]{1,0:T(8,128)(2,1)S(1)}, u32[]{:S(2)}, u32[]{:S(2)}) collective-permute-start(bf16[256,1024]{1,0:T(8,128)(2,1)S(1)} %copy-done.1), channel_id=1, source_target_pairs={{0,0},{1,1},{2,2},{3,3},{4,4},{5,5},{6,6},{7,7},{8,8},{9,9},{10,10... | collective-permute-start | bytes 1572872 | tf_op jit(solution)/shard_map/ppermute | solution.py:41
  20.1 13.9 %collective-permute-start.2 = (bf16[256,1024]{1,0:T(8,128)(2,1)S(1)}, bf16[256,1024]{1,0:T(8,128)(2,1)}, u32[]{:S(2)}, u32[]{:S(2)}) collective-permute-start(bf16[256,1024]{1,0:T(8,128)(2,1)S(1)} %copy-done.1), channel_id=1, source_target_pairs={{0,48},{1,49},{2,50},{3,51},{4,52},{5,53},{6,54},{7,55},{8,56},{9,... | collective-permute-start | bytes 1572872 | tf_op jit(solution)/shard_map/ppermute | solution.py:41
  20.2 13.8 %collective-permute-start.1 = (bf16[256,1024]{1,0:T(8,128)(2,1)S(1)}, bf16[256,1024]{1,0:T(8,128)(2,1)}, u32[]{:S(2)}, u32[]{:S(2)}) collective-permute-start(bf16[256,1024]{1,0:T(8,128)(2,1)S(1)} %copy-done.1), channel_id=1, source_target_pairs={{0,16},{1,17},{2,18},{3,19},{4,20},{5,21},{6,22},{7,23},{8,24},{9,... | collective-permute-start | bytes 1572872 | tf_op jit(solution)/shard_map/ppermute | solution.py:41
  36.7 7.6 %collective-permute-start.4 = (bf16[1152,128]{1,0:T(8,128)(2,1)S(1)}, bf16[1152,128]{1,0:T(8,128)(2,1)S(1)}, u32[]{:S(2)}, u32[]{:S(2)}) collective-permute-start(bf16[1152,128]{1,0:T(8,128)(2,1)S(1)} %get-tuple-element.19), channel_id=1, source_target_pairs={{0,32},{1,33},{2,34},{3,35},{4,36},{5,37},{6,38},{7,39},{8,40},{9,... | collective-permute-start | bytes 884744 | tf_op jit(solution)/shard_map/ppermute | solution.py:41
  38.6 13.4 %collective-permute-start.5 = (bf16[1152,128]{1,0:T(8,128)(2,1)S(1)}, bf16[1152,128]{1,0:T(8,128)(2,1)S(1)}, u32[]{:S(2)}, u32[]{:S(2)}) collective-permute-start(bf16[1152,128]{1,0:T(8,128)(2,1)S(1)} %get-tuple-element.20), channel_id=1, source_target_pairs={{0,64},{1,65},{2,66},{3,67},{4,68},{5,69},{6,70},{7,71},{8,72},{9,... | collective-permute-start | bytes 884744 | tf_op jit(solution)/shard_map/ppermute | solution.py:41
  42.0 16.0 %collective-permute-start.6 = (bf16[1152,128]{1,0:T(8,128)(2,1)S(1)}, bf16[1152,128]{1,0:T(8,128)(2,1)S(1)}, u32[]{:S(2)}, u32[]{:S(2)}) collective-permute-start(bf16[1152,128]{1,0:T(8,128)(2,1)S(1)} %get-tuple-element.21), channel_id=1, source_target_pairs={{0,96},{1,97},{2,98},{3,99},{4,100},{5,101},{6,102},{7,103},{8,104... | collective-permute-start | bytes 884744 | tf_op jit(solution)/shard_map/ppermute | solution.py:41
  58.2 3.0 %collective-permute-start.8 = (bf16[576,128]{1,0:T(8,128)(2,1)S(1)}, bf16[576,128]{1,0:T(8,128)(2,1)S(1)}, u32[]{:S(2)}, u32[]{:S(2)}) collective-permute-start(bf16[576,128]{1,0:T(8,128)(2,1)S(1)} %get-tuple-element.25), channel_id=1, source_target_pairs={{0,130},{1,131},{2,0},{3,1},{4,134},{5,135},{6,4},{7,5},{8,138},{9... | collective-permute-start | bytes 442376 | tf_op jit(solution)/shard_map/ppermute | solution.py:41
  58.8 4.4 %collective-permute-start.7 = (bf16[576,128]{1,0:T(8,128)(2,1)S(1)}, bf16[576,128]{1,0:T(8,128)(2,1)S(1)}, u32[]{:S(2)}, u32[]{:S(2)}) collective-permute-start(bf16[576,128]{1,0:T(8,128)(2,1)S(1)} %get-tuple-element.25), channel_id=1, source_target_pairs={{0,2},{1,3},{2,128},{3,129},{4,6},{5,7},{6,132},{7,133},{8,10},{9,... | collective-permute-start | bytes 442376 | tf_op jit(solution)/shard_map/ppermute | solution.py:41
  58.9 4.3 %collective-permute-start.10 = (bf16[576,128]{1,0:T(8,128)(2,1)S(1)}, bf16[576,128]{1,0:T(8,128)(2,1)S(1)}, u32[]{:S(2)}, u32[]{:S(2)}) collective-permute-start(bf16[576,128]{1,0:T(8,128)(2,1)S(1)} %get-tuple-element.26), channel_id=1, source_target_pairs={{0,130},{1,131},{2,0},{3,1},{4,134},{5,135},{6,4},{7,5},{8,138},{9... | collective-permute-start | bytes 442376 | tf_op jit(solution)/shard_map/ppermute | solution.py:41
  59.6 4.9 %collective-permute-start.9 = (bf16[576,128]{1,0:T(8,128)(2,1)S(1)}, bf16[576,128]{1,0:T(8,128)(2,1)S(1)}, u32[]{:S(2)}, u32[]{:S(2)}) collective-permute-start(bf16[576,128]{1,0:T(8,128)(2,1)S(1)} %get-tuple-element.26), channel_id=1, source_target_pairs={{0,2},{1,3},{2,128},{3,129},{4,6},{5,7},{6,132},{7,133},{8,10},{9,... | collective-permute-start | bytes 442376 | tf_op jit(solution)/shard_map/ppermute | solution.py:41
  64.6 5.7 %collective-permute-start.13 = (bf16[1152,128]{1,0:T(8,128)(2,1)S(1)}, bf16[1152,128]{1,0:T(8,128)(2,1)S(1)}, u32[]{:S(2)}, u32[]{:S(2)}) collective-permute-start(bf16[1152,128]{1,0:T(8,128)(2,1)S(1)} %pad_maximum_fusion.p0), channel_id=1, source_target_pairs={{0,96},{1,97},{2,98},{3,99},{4,100},{5,101},{6,102},{7,103},{8,104... | collective-permute-start | bytes 884744 | tf_op jit(solution)/shard_map/ppermute | solution.py:41
  65.4 7.2 %collective-permute-start.12 = (bf16[1152,128]{1,0:T(8,128)(2,1)S(1)}, bf16[1152,128]{1,0:T(8,128)(2,1)S(1)}, u32[]{:S(2)}, u32[]{:S(2)}) collective-permute-start(bf16[1152,128]{1,0:T(8,128)(2,1)S(1)} %pad_maximum_fusion.p0), channel_id=1, source_target_pairs={{0,64},{1,65},{2,66},{3,67},{4,68},{5,69},{6,70},{7,71},{8,72},{9,... | collective-permute-start | bytes 884744 | tf_op jit(solution)/shard_map/ppermute | solution.py:41
  67.1 8.8 %collective-permute-start.11 = (bf16[1152,128]{1,0:T(8,128)(2,1)S(1)}, bf16[1152,128]{1,0:T(8,128)(2,1)S(1)}, u32[]{:S(2)}, u32[]{:S(2)}) collective-permute-start(bf16[1152,128]{1,0:T(8,128)(2,1)S(1)} %pad_maximum_fusion.p0), channel_id=1, source_target_pairs={{0,32},{1,33},{2,34},{3,35},{4,36},{5,37},{6,38},{7,39},{8,40},{9,... | collective-permute-start | bytes 884744 | tf_op jit(solution)/shard_map/ppermute | solution.py:41
  92.8 7.3 %collective-permute-start.14 = (bf16[2560,256]{1,0:T(8,128)(2,1)S(1)}, bf16[2560,256]{1,0:T(8,128)(2,1)S(1)}, u32[]{:S(2)}, u32[]{:S(2)}) collective-permute-start(bf16[2560,256]{1,0:T(8,128)(2,1)S(1)} %shard_map.58.mine_ref), channel_id=1, source_target_pairs={{0,16},{1,17},{2,18},{3,19},{4,20},{5,21},{6,22},{7,23},{8,24},{9,... | collective-permute-start | bytes 3932168 | tf_op jit(solution)/shard_map/ppermute | solution.py:41

commit v13 on v11

--- a/solution.py
+++ b/solution.py
@@ -308,10 +308,9 @@
         moved(own_w, lambda zh, y, c, x, zl: (zh, y ^ 1, 1, x, zl) if c == 0 else (zh, y, 0, x, zl)),
         moved(own_w, lambda zh, y, c, x, zl: (zh, y ^ 1, 1, x, zl) if c == 1 else None),
     ]
-    samples, weights = lax.optimization_barrier((samples, weights))
+    chunks = cov(jnp.stack([jnp.where(is_g, y, x), 1 - core]), samples, scale)
+    chunks, weights = lax.optimization_barrier((chunks, weights))
     weights.insert(1, weight_grad)
-
-    chunks = cov(jnp.stack([jnp.where(is_g, y, x), 1 - core]), samples, scale)
     total = chunks[0].astype(F32)
     for k in (1, 2, 3):
         total += moved(

time: 101 us -> 101 us (level)
    all_to_all x1, waiting for transfers between devices: 0.82 us -> 12.7 us  [dealt(): lax.all_to_all(value, ('dp', 'owner'), split_axis=0, concat_axis=0, tiled...]
    ppermute x13, waiting for transfers between devices: 48.4 us -> 36.5 us  [moved(): return lax.ppermute(value, ('dp', 'owner'), pairs)]
  transfers between devices with their start and end apart: 14 -> 14, of which waited for: 12 -> 10; matrix products, arithmetic and copies ran while one was open for 1% -> 1% of each run, Pallas kernels for 0% -> 2%
where the time goes in v13:
time: 101 us; the launch traced here: 100 us
  waiting for transfers between devices  49.2 us (49%)
  starting transfers between devices  24.8 us (25%)
  Pallas kernels  21.9 us (22%)
  matrix products  3.28 us (3%)
    ppermute x13, waiting for transfers between devices, moved(): return lax.ppermute(value, ('dp', 'owner'), pairs)  36.5 us
    pallas_call x1, Pallas kernels, rounds(): pl.pallas_call(rounds_kernel, out_shape=jax.ShapeDtypeStruct((len(LARGE)...  16.8 us
    ppermute x13, starting transfers between devices, moved(): return lax.ppermute(value, ('dp', 'owner'), pairs)  13.4 us
    all_to_all x1, waiting for transfers between devices, dealt(): lax.all_to_all(value, ('dp', 'owner'), split_axis=0, concat_axis=0, tiled...  12.7 us
    all_to_all x1, starting transfers between devices, dealt(): lax.all_to_all(value, ('dp', 'owner'), split_axis=0, concat_axis=0, tiled...  11.4 us
    dot_general x2, matrix products, dot(): return jnp.dot(a, b, preferred_element_type=F32)  3.28 us
    pallas_call x1, Pallas kernels, last(): pl.pallas_call(last_kernel, out_shape=jax.ShapeDtypeStruct((rows, 4 * row...  2.07 us
  transfers between devices with their start and end apart: 14, of which 10 were waited for; matrix products, arithmetic and copies ran while one was open for 1% of the time, Pallas kernels for 2%

profile of v13, /device:TPU:33, one launch (start us, length us, event | category | flops | bytes accessed | tf_op | source)
XLA Modules:
  0.0 100.4 jit_solution(10908531590230410168)
XLA Ops:
  0.0 3.0 %convolution_convert_fusion.g_ref = bf16[16,16384]{1,0:T(8,128)(2,1)S(1)} fusion(bf16[128,16384]{1,0:T(8,128)(2,1)} %param.6, s32[16]{0:T(128)} %param.7), kind=kOutput, calls=%fused_computation | convolution fusion | flops 67373056 | bytes 4718656 | tf_op jit(solution)/shard_map/dot_general | solution.py:22
  3.0 0.3 convolution_convert_fusion.1.x_ref
  3.4 0.8 collective-permute-start
  4.2 1.5 %collective-permute-done.other_ref = bf16[16,16384]{1,0:T(8,128)(2,1)S(1)} collective-permute-done((bf16[16,16384]{1,0:T(8,128)(2,1)S(1)}, bf16[16,16384]{1,0:T(8,128)(2,1)S(1)}, u32[]{:S(2)}, u32[]{:S(2)}) %collective-permute-start) | collective-permute-done | bytes 524320 | tf_op jit(solution)/shard_map/ppermute | solution.py:41
  5.7 1.0 %shard_map.56 = bf16[16,32,1024]{2,1,0:T(8,128)(2,1)} custom-call(s32[1]{0:T(128)} %bitcast.1.core_ref, bf16[16,4096]{1,0:T(8,128)(2,1)S(1)} %convolution_convert_fusion.1.x_ref, bf16[16,16384]{1,0:T(8,128)(2,1)S(1)} %convolution_convert_fusion.g_ref, bf16[16,16384]{1,0:T(8,128)(2,1)S(1)} %collective-permute-done.other_ref), custom_call_target="tpu_custom_call" | custom-call | tf_op jit(solution)/shard_map/pallas_call | solution.py:110
  6.7 11.4 %all-to-all-start = ((bf16[16,32,1024]{2,1,0:T(8,128)(2,1)}), bf16[16,32,1024]{2,1,0:T(8,128)(2,1)S(1)}, u32[]{:S(2)}, u32[]{:S(2)}) async-start(bf16[16,32,1024]{2,1,0:T(8,128)(2,1)} %shard_map.56), calls=%async_computation | async-start | bytes 2097152 | tf_op jit(solution)/shard_map/all_to_all | solution.py:53
  18.2 1.9 %collective-permute-start.3 = (bf16[256,1024]{1,0:T(8,128)(2,1)S(1)}, bf16[256,1024]{1,0:T(8,128)(2,1)S(1)}, u32[]{:S(2)}, u32[]{:S(2)}) collective-permute-start(bf16[256,1024]{1,0:T(8,128)(2,1)S(1)} %copy-done.1), channel_id=1, source_target_pairs={{0,0},{1,1},{2,2},{3,3},{4,4},{5,5},{6,6},{7,7},{8,8},{9,9},{10,10... | collective-permute-start | bytes 1572872 | tf_op jit(solution)/shard_map/ppermute | solution.py:41
  20.1 0.1 collective-permute-start.2
  20.2 1.8 %collective-permute-start.1 = (bf16[256,1024]{1,0:T(8,128)(2,1)S(1)}, bf16[256,1024]{1,0:T(8,128)(2,1)}, u32[]{:S(2)}, u32[]{:S(2)}) collective-permute-start(bf16[256,1024]{1,0:T(8,128)(2,1)S(1)} %copy-done.1), channel_id=1, source_target_pairs={{0,16},{1,17},{2,18},{3,19},{4,20},{5,21},{6,22},{7,23},{8,24},{9,... | collective-permute-start | bytes 1572872 | tf_op jit(solution)/shard_map/ppermute | solution.py:41
  22.1 12.7 %all-to-all-done = bf16[16,32,1024]{2,1,0:T(8,128)(2,1)S(1)} async-done(((bf16[16,32,1024]{2,1,0:T(8,128)(2,1)}), bf16[16,32,1024]{2,1,0:T(8,128)(2,1)S(1)}, u32[]{:S(2)}, u32[]{:S(2)}) %all-to-all-start) | async-done | bytes 1048608 | tf_op jit(solution)/shard_map/all_to_all | solution.py:53
  34.8 1.8 %shard_map.57 = (bf16[1152,128]{1,0:T(8,128)(2,1)S(1)}, bf16[1152,128]{1,0:T(8,128)(2,1)S(1)}, bf16[1152,128]{1,0:T(8,128)(2,1)S(1)}, bf16[1152,128]{1,0:T(8,128)(2,1)S(1)}) custom-call(s32[2]{0:T(128)S(1)} %pad_add_fusion.1.refs_0_, bf16[512,1024]{1,0:T(8,128)(2,1)S(1)} %bitcast.7), custom_call_target="tpu_custom_call" | custom-call | tf_op jit(solution)/shard_map/pallas_call | solution.py:137
  36.7 1.9 %collective-permute-start.4 = (bf16[1152,128]{1,0:T(8,128)(2,1)S(1)}, bf16[1152,128]{1,0:T(8,128)(2,1)S(1)}, u32[]{:S(2)}, u32[]{:S(2)}) collective-permute-start(bf16[1152,128]{1,0:T(8,128)(2,1)S(1)} %get-tuple-element.25), channel_id=1, source_target_pairs={{0,32},{1,33},{2,34},{3,35},{4,36},{5,37},{6,38},{7,39},{8,40},{9,... | collective-permute-start | bytes 884744 | tf_op jit(solution)/shard_map/ppermute | solution.py:41
  38.6 3.4 %collective-permute-start.5 = (bf16[1152,128]{1,0:T(8,128)(2,1)S(1)}, bf16[1152,128]{1,0:T(8,128)(2,1)S(1)}, u32[]{:S(2)}, u32[]{:S(2)}) collective-permute-start(bf16[1152,128]{1,0:T(8,128)(2,1)S(1)} %get-tuple-element.26), channel_id=1, source_target_pairs={{0,64},{1,65},{2,66},{3,67},{4,68},{5,69},{6,70},{7,71},{8,72},{9,... | collective-permute-start | bytes 884744 | tf_op jit(solution)/shard_map/ppermute | solution.py:41
  42.0 2.3 %collective-permute-done.4 = bf16[1152,128]{1,0:T(8,128)(2,1)S(1)} collective-permute-done((bf16[1152,128]{1,0:T(8,128)(2,1)S(1)}, bf16[1152,128]{1,0:T(8,128)(2,1)S(1)}, u32[]{:S(2)}, u32[]{:S(2)}) %collective-permute-start.4) | collective-permute-done | bytes 294944 | tf_op jit(solution)/shard_map/ppermute | solution.py:41
  44.3 7.7 %collective-permute-done.5 = bf16[1152,128]{1,0:T(8,128)(2,1)S(1)} collective-permute-done((bf16[1152,128]{1,0:T(8,128)(2,1)S(1)}, bf16[1152,128]{1,0:T(8,128)(2,1)S(1)}, u32[]{:S(2)}, u32[]{:S(2)}) %collective-permute-start.5) | collective-permute-done | bytes 294944 | tf_op jit(solution)/shard_map/ppermute | solution.py:41
  52.0 9.1 %collective-permute-done.6 = bf16[1152,128]{1,0:T(8,128)(2,1)S(1)} collective-permute-done((bf16[1152,128]{1,0:T(8,128)(2,1)S(1)}, bf16[1152,128]{1,0:T(8,128)(2,1)S(1)}, u32[]{:S(2)}, u32[]{:S(2)}) %collective-permute-start.6) | collective-permute-done | bytes 294944 | tf_op jit(solution)/shard_map/ppermute | solution.py:41
  61.1 0.2 add_convert_fusion.1
  61.2 0.7 collective-permute-start.8
  61.9 0.1 collective-permute-start.7
  62.0 5.5 %collective-permute-done.7 = bf16[1152,128]{1,0:T(8,128)(2,1)S(1)} collective-permute-done((bf16[1152,128]{1,0:T(8,128)(2,1)S(1)}, bf16[1152,128]{1,0:T(8,128)(2,1)S(1)}, u32[]{:S(2)}, u32[]{:S(2)}) %collective-permute-start.7) | collective-permute-done | bytes 294944 | tf_op jit(solution)/shard_map/ppermute | solution.py:41
  67.6 0.1 add_convert_fusion.p0
  67.6 0.1 collective-permute-start.11
  67.7 2.0 %collective-permute-start.10 = (bf16[1152,128]{1,0:T(8,128)(2,1)S(1)}, bf16[1152,128]{1,0:T(8,128)(2,1)S(1)}, u32[]{:S(2)}, u32[]{:S(2)}) collective-permute-start(bf16[1152,128]{1,0:T(8,128)(2,1)S(1)} %add_convert_fusion.p0), channel_id=1, source_target_pairs={{0,64},{1,65},{2,66},{3,67},{4,68},{5,69},{6,70},{7,71},{8,72},{9,... | collective-permute-start | bytes 884744 | tf_op jit(solution)/shard_map/ppermute | solution.py:41
  69.8 0.5 collective-permute-start.9
  70.3 0.7 dynamic_slice.4.damp_ref
  71.0 2.6 %collective-permute-done.11.p3 = bf16[1152,128]{1,0:T(8,128)(2,1)S(1)} collective-permute-done((bf16[1152,128]{1,0:T(8,128)(2,1)S(1)}, bf16[1152,128]{1,0:T(8,128)(2,1)S(1)}, u32[]{:S(2)}, u32[]{:S(2)}) %collective-permute-start.11) | collective-permute-done | bytes 294944 | tf_op jit(solution)/shard_map/ppermute | solution.py:41
  73.6 1.6 %collective-permute-done.10.p2 = bf16[1152,128]{1,0:T(8,128)(2,1)S(1)} collective-permute-done((bf16[1152,128]{1,0:T(8,128)(2,1)S(1)}, bf16[1152,128]{1,0:T(8,128)(2,1)S(1)}, u32[]{:S(2)}, u32[]{:S(2)}) %collective-permute-start.10) | collective-permute-done | bytes 294944 | tf_op jit(solution)/shard_map/ppermute | solution.py:41
  75.2 3.2 %collective-permute-done.9.p1 = bf16[1152,128]{1,0:T(8,128)(2,1)S(1)} collective-permute-done((bf16[1152,128]{1,0:T(8,128)(2,1)S(1)}, bf16[1152,128]{1,0:T(8,128)(2,1)S(1)}, u32[]{:S(2)}, u32[]{:S(2)}) %collective-permute-start.9) | collective-permute-done | bytes 294944 | tf_op jit(solution)/shard_map/ppermute | solution.py:41
  78.4 16.8 %shard_map.58.mine_ref = bf16[2560,256]{1,0:T(8,128)(2,1)S(1)} custom-call(s32[3]{0:T(128)S(1)} %pad_add_fusion.place_ref, f32[1]{0:T(128)} %dynamic_slice.4.damp_ref, bf16[1152,128]{1,0:T(8,128)(2,1)S(1)} %add_convert_fusion.p0, bf16[1152,128]{1,0:T(8,128)(2,1)S(1)} %collective-permute-done.9.p1, bf16[1152,128]{1,0:T(8,128)(2,1)S(1)} %collective-permute-done.10.p2, ...), custom_call_target="tpu_custom_call" | custom-call | tf_op jit(solution)/shard_map/pallas_call | solution.py:231
  95.2 0.1 collective-permute-start.12
  95.3 3.0 %collective-permute-done.12.other_ref = bf16[2560,256]{1,0:T(8,128)(2,1)S(1)} collective-permute-done((bf16[2560,256]{1,0:T(8,128)(2,1)S(1)}, bf16[2560,256]{1,0:T(8,128)(2,1)S(1)}, u32[]{:S(2)}, u32[]{:S(2)}) %collective-permute-start.12) | collective-permute-done | bytes 1310752 | tf_op jit(solution)/shard_map/ppermute | solution.py:41
  98.3 2.1 %shard_map.59 = bf16[256,1024]{1,0:T(8,128)(2,1)} custom-call(s32[3]{0:T(128)S(1)} %pad_add_fusion.place_ref, bf16[2560,256]{1,0:T(8,128)(2,1)S(1)} %shard_map.58.mine_ref, bf16[2560,256]{1,0:T(8,128)(2,1)S(1)} %collective-permute-done.12.other_ref), custom_call_target="tpu_custom_call" | custom-call | tf_op jit(solution)/shard_map/pallas_call | solution.py:273
  (16 shorter events, 0.2 us)
Async XLA Ops:
  0.0 3.0 %copy-start = (bf16[128,4096]{1,0:T(8,128)(2,1)S(1)}, bf16[128,4096]{1,0:T(8,128)(2,1)}, u32[]{:S(2)}) copy-start(bf16[128,4096]{1,0:T(8,128)(2,1)} %param.5) | copy-start | bytes 3145732
  0.0 3.0 %copy-start.2 = (s32[16]{0:T(128)S(1)}, s32[16]{0:T(128)}, u32[]{:S(2)}) copy-start(s32[16]{0:T(128)} %param.7) | copy-start | bytes 196
  3.0 15.1 %copy-start.1 = (bf16[256,1024]{1,0:T(8,128)(2,1)S(1)}, bf16[256,1024]{1,0:T(8,128)(2,1)}, u32[]{:S(2)}) copy-start(bf16[256,1024]{1,0:T(8,128)(2,1)} %w1.1) | copy-start | bytes 1572868
  3.4 66.9 %copy-start.3 = (f32[20]{0:T(128)S(1)}, f32[20]{0:T(128)}, u32[]{:S(2)}) copy-start(f32[20]{0:T(128)} %param.8) | copy-start | bytes 244
  3.4 2.3 %collective-permute-start = (bf16[16,16384]{1,0:T(8,128)(2,1)S(1)}, bf16[16,16384]{1,0:T(8,128)(2,1)S(1)}, u32[]{:S(2)}, u32[]{:S(2)}) collective-permute-start(bf16[16,16384]{1,0:T(8,128)(2,1)S(1)} %shard_map.55), channel_id=1, source_target_pairs={{0,16},{1,17},{2,18},{3,19},{4,20},{5,21},{6,22},{7,23},{8,24},{9,... | collective-permute-start | bytes 1572872 | tf_op jit(solution)/shard_map/ppermute | solution.py:41
  6.7 28.1 %all-to-all-start = ((bf16[16,32,1024]{2,1,0:T(8,128)(2,1)}), bf16[16,32,1024]{2,1,0:T(8,128)(2,1)S(1)}, u32[]{:S(2)}, u32[]{:S(2)}) async-start(bf16[16,32,1024]{2,1,0:T(8,128)(2,1)} %shard_map.56), calls=%async_computation | async-start | bytes 2097152 | tf_op jit(solution)/shard_map/all_to_all | solution.py:53
  18.2 18.5 %collective-permute-start.3 = (bf16[256,1024]{1,0:T(8,128)(2,1)S(1)}, bf16[256,1024]{1,0:T(8,128)(2,1)S(1)}, u32[]{:S(2)}, u32[]{:S(2)}) collective-permute-start(bf16[256,1024]{1,0:T(8,128)(2,1)S(1)} %copy-done.1), channel_id=1, source_target_pairs={{0,0},{1,1},{2,2},{3,3},{4,4},{5,5},{6,6},{7,7},{8,8},{9,9},{10,10... | collective-permute-start | bytes 1572872 | tf_op jit(solution)/shard_map/ppermute | solution.py:41
  20.1 16.6 %collective-permute-start.2 = (bf16[256,1024]{1,0:T(8,128)(2,1)S(1)}, bf16[256,1024]{1,0:T(8,128)(2,1)}, u32[]{:S(2)}, u32[]{:S(2)}) collective-permute-start(bf16[256,1024]{1,0:T(8,128)(2,1)S(1)} %copy-done.1), channel_id=1, source_target_pairs={{0,48},{1,49},{2,50},{3,51},{4,52},{5,53},{6,54},{7,55},{8,56},{9,... | collective-permute-start | bytes 1572872 | tf_op jit(solution)/shard_map/ppermute | solution.py:41
  20.2 16.5 %collective-permute-start.1 = (bf16[256,1024]{1,0:T(8,128)(2,1)S(1)}, bf16[256,1024]{1,0:T(8,128)(2,1)}, u32[]{:S(2)}, u32[]{:S(2)}) collective-permute-start(bf16[256,1024]{1,0:T(8,128)(2,1)S(1)} %copy-done.1), channel_id=1, source_target_pairs={{0,16},{1,17},{2,18},{3,19},{4,20},{5,21},{6,22},{7,23},{8,24},{9,... | collective-permute-start | bytes 1572872 | tf_op jit(solution)/shard_map/ppermute | solution.py:41
  36.7 7.6 %collective-permute-start.4 = (bf16[1152,128]{1,0:T(8,128)(2,1)S(1)}, bf16[1152,128]{1,0:T(8,128)(2,1)S(1)}, u32[]{:S(2)}, u32[]{:S(2)}) collective-permute-start(bf16[1152,128]{1,0:T(8,128)(2,1)S(1)} %get-tuple-element.25), channel_id=1, source_target_pairs={{0,32},{1,33},{2,34},{3,35},{4,36},{5,37},{6,38},{7,39},{8,40},{9,... | collective-permute-start | bytes 884744 | tf_op jit(solution)/shard_map/ppermute | solution.py:41
  38.6 13.4 %collective-permute-start.5 = (bf16[1152,128]{1,0:T(8,128)(2,1)S(1)}, bf16[1152,128]{1,0:T(8,128)(2,1)S(1)}, u32[]{:S(2)}, u32[]{:S(2)}) collective-permute-start(bf16[1152,128]{1,0:T(8,128)(2,1)S(1)} %get-tuple-element.26), channel_id=1, source_target_pairs={{0,64},{1,65},{2,66},{3,67},{4,68},{5,69},{6,70},{7,71},{8,72},{9,... | collective-permute-start | bytes 884744 | tf_op jit(solution)/shard_map/ppermute | solution.py:41
  42.0 19.1 %collective-permute-start.6 = (bf16[1152,128]{1,0:T(8,128)(2,1)S(1)}, bf16[1152,128]{1,0:T(8,128)(2,1)S(1)}, u32[]{:S(2)}, u32[]{:S(2)}) collective-permute-start(bf16[1152,128]{1,0:T(8,128)(2,1)S(1)} %get-tuple-element.27), channel_id=1, source_target_pairs={{0,96},{1,97},{2,98},{3,99},{4,100},{5,101},{6,102},{7,103},{8,104... | collective-permute-start | bytes 884744 | tf_op jit(solution)/shard_map/ppermute | solution.py:41
  61.2 0.8 collective-permute-start.8
  61.9 5.7 %collective-permute-start.7 = (bf16[1152,128]{1,0:T(8,128)(2,1)S(1)}, bf16[1152,128]{1,0:T(8,128)(2,1)S(1)}, u32[]{:S(2)}, u32[]{:S(2)}) collective-permute-start(bf16[1152,128]{1,0:T(8,128)(2,1)S(1)} %add_convert_fusion.1), channel_id=1, source_target_pairs={{0,2},{1,3},{2,128},{3,129},{4,6},{5,7},{6,132},{7,133},{8,10},{9,... | collective-permute-start | bytes 884744 | tf_op jit(solution)/shard_map/ppermute | solution.py:41
  67.6 5.9 %collective-permute-start.11 = (bf16[1152,128]{1,0:T(8,128)(2,1)S(1)}, bf16[1152,128]{1,0:T(8,128)(2,1)S(1)}, u32[]{:S(2)}, u32[]{:S(2)}) collective-permute-start(bf16[1152,128]{1,0:T(8,128)(2,1)S(1)} %add_convert_fusion.p0), channel_id=1, source_target_pairs={{0,96},{1,97},{2,98},{3,99},{4,100},{5,101},{6,102},{7,103},{8,104... | collective-permute-start | bytes 884744 | tf_op jit(solution)/shard_map/ppermute | solution.py:41
  67.7 7.5 %collective-permute-start.10 = (bf16[1152,128]{1,0:T(8,128)(2,1)S(1)}, bf16[1152,128]{1,0:T(8,128)(2,1)S(1)}, u32[]{:S(2)}, u32[]{:S(2)}) collective-permute-start(bf16[1152,128]{1,0:T(8,128)(2,1)S(1)} %add_convert_fusion.p0), channel_id=1, source_target_pairs={{0,64},{1,65},{2,66},{3,67},{4,68},{5,69},{6,70},{7,71},{8,72},{9,... | collective-permute-start | bytes 884744 | tf_op jit(solution)/shard_map/ppermute | solution.py:41
  69.8 8.6 %collective-permute-start.9 = (bf16[1152,128]{1,0:T(8,128)(2,1)S(1)}, bf16[1152,128]{1,0:T(8,128)(2,1)S(1)}, u32[]{:S(2)}, u32[]{:S(2)}) collective-permute-start(bf16[1152,128]{1,0:T(8,128)(2,1)S(1)} %add_convert_fusion.p0), channel_id=1, source_target_pairs={{0,32},{1,33},{2,34},{3,35},{4,36},{5,37},{6,38},{7,39},{8,40},{9,... | collective-permute-start | bytes 884744 | tf_op jit(solution)/shard_map/ppermute | solution.py:41
  95.2 3.1 %collective-permute-start.12 = (bf16[2560,256]{1,0:T(8,128)(2,1)S(1)}, bf16[2560,256]{1,0:T(8,128)(2,1)S(1)}, u32[]{:S(2)}, u32[]{:S(2)}) collective-permute-start(bf16[2560,256]{1,0:T(8,128)(2,1)S(1)} %shard_map.58.mine_ref), channel_id=1, source_target_pairs={{0,16},{1,17},{2,18},{3,19},{4,20},{5,21},{6,22},{7,23},{8,24},{9,... | collective-permute-start | bytes 3932168 | tf_op jit(solution)/shard_map/ppermute | solution.py:41
